TPU v7x, 32 devices: a whole 2x2x4 slice. The times are simulated.
32 devices in a mesh: wide: 8 (over y, x, core), narrow: 4 (over z).
Axes of the slice: x: 2, y: 2, z: 4, core: 2. Of those that a mesh axis runs over, the one named last changes fastest.
Arguments:
- tokens: bfloat16 [8192, 1536], P(('wide', 'narrow')), may hold values from -6 to 6
- gain_one: float32 [1536], replicated, may hold values from 0.5 to 1.5
- in_weight: bfloat16 [1536, 6216], P(('wide', 'narrow')), may hold values from -0.15625 to 0.15625
- forget_bias: float32 [24], replicated, may hold values from 1 to 7
- out_weight: bfloat16 [1536, 1536], P(('wide', 'narrow')), may hold values from -0.625 to 0.625
- gain_two: float32 [1536], replicated, may hold values from 0.5 to 1.5
- gate_up_weight: bfloat16 [1536, 8192], P(('wide', 'narrow')), may hold values from -0.15625 to 0.15625
- down_weight: bfloat16 [4096, 1536], P(('wide', 'narrow')), may hold values from -0.09375 to 0.09375
- segment_ids: int32 [8, 1024], P('wide'), may hold values from 0 to 2, as said below
- cotangent: bfloat16 [8192, 1536], P(('wide', 'narrow')), may hold values from -6 to 6
Outputs:
- output: bfloat16 [8192, 1536], P(('wide', 'narrow'))
- grad_tokens: float32 [8192, 1536], P(('wide', 'narrow'))
- grad_gain_one: float32 [1536], replicated
- grad_in_weight: float32 [1536, 6216], P('wide', 'narrow')
- grad_forget_bias: float32 [24], replicated
- grad_out_weight: float32 [1536, 1536], P('wide', 'narrow')
- grad_gain_two: float32 [1536], replicated
- grad_gate_up: float32 [1536, 8192], P('wide', 'narrow')
- grad_down: float32 [4096, 1536], P('wide', 'narrow')
Inputs may be any that keep to these rules, and one draw needn't show every extreme that they name: `segment_ids`: each slot holds three runs of rows with ids 0, 1, 2 in order: a first run (id 0), one whole sequence longer than 768 rows (id 1), and a last run (id 2); each run is attended as a sequence of its own, rows never attend across slots, and the first and last runs have at least one row each.
All inputs are finite; a program needn't handle non-finite values.
Results may differ from a plain program's by a relative error of at most 0.017.
Values may be sent and summed in bfloat16 or wider, within the bound.
A program may use at most 256 MiB of HBM per device.

v0:
```python
from functools import partial

import jax
import jax.numpy as jnp
from jax import lax
from jax.sharding import PartitionSpec as P

EPSILON = 1e-06
MASKED_SCORE = -1e30


def rms_norm(values, gain_vector):
    factor = lax.rsqrt(jnp.mean(values * values, axis=-1, keepdims=True) + EPSILON)
    return values * factor * gain_vector


def swiglu(gate_up, hidden_width):
    return jax.nn.silu(gate_up[:, :hidden_width]) * gate_up[:, hidden_width:]


def prepare(queries, keys_in, values_in, forget, key_shift, value_shift, continued):
    key_prev = (
        jnp.concatenate([jnp.zeros_like(keys_in[:1]), keys_in[:-1]], axis=0)
        * continued[:, None, None]
    )
    value_prev = (
        jnp.concatenate([jnp.zeros_like(values_in[:1]), values_in[:-1]], axis=0)
        * continued[:, None, None]
    )
    key_mix = jax.nn.sigmoid(key_shift)[:, :, None]
    value_mix = jax.nn.sigmoid(value_shift)[:, :, None]
    shifted_keys = keys_in + key_mix * (key_prev - keys_in)
    shifted_values = values_in + value_mix * (value_prev - values_in)
    query_norm = queries * lax.rsqrt(jnp.mean(queries * queries, axis=-1, keepdims=True) + EPSILON)
    key_norm = shifted_keys * lax.rsqrt(
        jnp.mean(shifted_keys * shifted_keys, axis=-1, keepdims=True) + EPSILON
    )
    decay = jnp.cumsum(jax.nn.log_sigmoid(forget), axis=0)
    return (query_norm, key_norm, shifted_values, decay)


def continuation(segments, dtype_like):
    joined = (segments[1:] == segments[:-1]).astype(dtype_like.dtype)
    return jnp.concatenate([jnp.zeros((1,), dtype_like.dtype), joined])


def block_scores(query_low, key_low, decay, segments, offset, block_rows, score_scale):
    row_index = offset + jnp.arange(block_rows, dtype=jnp.int32)
    col_index = jnp.arange(segments.shape[0], dtype=jnp.int32)
    query_block = lax.dynamic_slice_in_dim(query_low, offset, block_rows, 0)
    decay_block = lax.dynamic_slice_in_dim(decay, offset, block_rows, 0)
    segment_block = lax.dynamic_slice_in_dim(segments, offset, block_rows, 0)
    scores = (
        jnp.einsum("qhd,khd->hqk", query_block, key_low, preferred_element_type=jnp.float32)
        * score_scale
    )
    scores = scores + decay_block.T[:, :, None] - decay.T[:, None, :]
    visible = (col_index[None, :] <= row_index[:, None]) & (
        segment_block[:, None] == segments[None, :]
    )
    return (jnp.where(visible[None], scores, MASKED_SCORE), query_block)


def attend_forward(query_low, key_low, value_low, decay, segments, block_rows, score_scale):
    slot_rows = query_low.shape[0]
    offsets = jnp.arange(slot_rows // block_rows, dtype=jnp.int32) * block_rows

    def forward_block(offset):
        scores, unused = block_scores(
            query_low, key_low, decay, segments, offset, block_rows, score_scale
        )
        largest = jnp.max(scores, axis=-1, keepdims=True)
        exponent_terms = jnp.exp(scores - largest)
        denominator = jnp.sum(exponent_terms, axis=-1, keepdims=True)
        weights_low = (exponent_terms / denominator).astype(jnp.bfloat16)
        result = jnp.einsum(
            "hqk,khd->qhd", weights_low, value_low, preferred_element_type=jnp.float32
        )
        return (result, (largest + jnp.log(denominator))[..., 0])

    results, log_total = lax.map(forward_block, offsets)
    return (results.reshape(slot_rows, query_low.shape[1], query_low.shape[2]), log_total)


def attend_backward(
    query_low, key_low, value_low, decay, segments, log_total, grad_low, block_rows, score_scale
):
    slot_rows = query_low.shape[0]
    offsets = jnp.arange(slot_rows // block_rows, dtype=jnp.int32) * block_rows

    def backward_block(running, packed):
        grad_keys, grad_values, grad_decay = running
        offset, block_total = packed
        scores, query_block = block_scores(
            query_low, key_low, decay, segments, offset, block_rows, score_scale
        )
        exact = jnp.exp(scores - block_total[:, :, None])
        grad_block = lax.dynamic_slice_in_dim(grad_low, offset, block_rows, 0)
        grad_probs = jnp.einsum(
            "qhd,khd->hqk", grad_block, value_low, preferred_element_type=jnp.float32
        )
        inner = jnp.sum(exact * grad_probs, axis=-1, keepdims=True)
        grad_scores = (exact * (grad_probs - inner)).astype(jnp.bfloat16)
        grad_queries = (
            jnp.einsum("hqk,khd->qhd", grad_scores, key_low, preferred_element_type=jnp.float32)
            * score_scale
        )
        grad_keys = (
            grad_keys
            + jnp.einsum(
                "hqk,qhd->khd", grad_scores, query_block, preferred_element_type=jnp.float32
            )
            * score_scale
        )
        grad_values = grad_values + jnp.einsum(
            "hqk,qhd->khd",
            exact.astype(jnp.bfloat16),
            grad_block,
            preferred_element_type=jnp.float32,
        )
        score_float = grad_scores.astype(jnp.float32)
        row_totals = jnp.sum(score_float, axis=-1)
        col_totals = jnp.sum(score_float, axis=1)
        grad_decay = grad_decay - col_totals.T
        current = lax.dynamic_slice_in_dim(grad_decay, offset, block_rows, 0)
        grad_decay = lax.dynamic_update_slice_in_dim(grad_decay, current + row_totals.T, offset, 0)
        return ((grad_keys, grad_values, grad_decay), grad_queries)

    zeros_heads = jnp.zeros(query_low.shape, jnp.float32)
    zeros_decay = jnp.zeros(decay.shape, jnp.float32)
    finals, grad_queries = lax.scan(
        backward_block, (zeros_heads, zeros_heads, zeros_decay), (offsets, log_total)
    )
    return (grad_queries.reshape(query_low.shape), finals[0], finals[1], finals[2])


def on_device(
    tokens,
    gain_one,
    in_weight,
    forget_bias,
    out_weight,
    gain_two,
    gate_up_weight,
    down_weight,
    segment_ids,
    cotangent,
):
    inputs = tokens.astype(jnp.float32)
    token_rows = inputs.shape[0]
    width = inputs.shape[1]
    heads = forget_bias.shape[0]
    head_size = width // heads
    local_heads = heads // lax.axis_size("narrow")
    base = 4 * width
    full_in, full_out = (
        lax.all_gather(in_weight, ("wide", "narrow"), axis=0, tiled=True),
        lax.all_gather(out_weight, ("wide", "narrow"), axis=0, tiled=True),
    )
    normed_one = rms_norm(inputs, gain_one).astype(jnp.bfloat16)
    projected = jnp.dot(normed_one, full_in, preferred_element_type=jnp.float32)
    qkv_low = (
        projected[:, : 3 * width].astype(jnp.bfloat16).reshape(token_rows, 3, heads, head_size)
    )
    gate_logit = projected[:, 3 * width : base]
    gate_low = jnp.stack(
        [
            projected[:, base : base + heads] + forget_bias,
            projected[:, base + heads : base + 2 * heads],
            projected[:, base + 2 * heads : base + 3 * heads],
        ],
        axis=1,
    ).astype(jnp.bfloat16)
    head_qkv, head_gates = (
        lax.all_to_all(qkv_low, "narrow", split_axis=2, concat_axis=0, tiled=True),
        lax.all_to_all(gate_low, "narrow", split_axis=2, concat_axis=0, tiled=True),
    )
    segments = segment_ids[0]
    continued = continuation(segments, inputs)
    head_floats = head_qkv.astype(jnp.float32)
    gate_floats = head_gates.astype(jnp.float32)
    prepare_slot = partial(prepare, continued=continued)
    prepared, prepare_back = jax.vjp(
        prepare_slot,
        head_floats[:, 0],
        head_floats[:, 1],
        head_floats[:, 2],
        gate_floats[:, 0],
        gate_floats[:, 1],
        gate_floats[:, 2],
    )
    query_low = prepared[0].astype(jnp.bfloat16)
    key_low = prepared[1].astype(jnp.bfloat16)
    value_low = prepared[2].astype(jnp.bfloat16)
    decay = prepared[3]
    slot_rows = query_low.shape[0]
    block_rows = min(512, slot_rows)
    score_scale = head_size ** (-0.5)
    attended_heads, log_total = attend_forward(
        query_low, key_low, value_low, decay, segments, block_rows, score_scale
    )
    attended = lax.all_to_all(
        attended_heads.astype(jnp.bfloat16), "narrow", split_axis=0, concat_axis=1, tiled=True
    ).reshape(token_rows, width)
    attended_float = attended.astype(jnp.float32)
    gate_open = jax.nn.sigmoid(gate_logit)
    mixed = (attended_float * gate_open).astype(jnp.bfloat16)
    middle = inputs + jnp.dot(mixed, full_out, preferred_element_type=jnp.float32)
    full_gate_up, full_down = (
        lax.all_gather(gate_up_weight, ("wide", "narrow"), axis=0, tiled=True),
        lax.all_gather(down_weight, ("wide", "narrow"), axis=0, tiled=True),
    )
    normed_two = rms_norm(middle, gain_two).astype(jnp.bfloat16)
    gate_up = jnp.dot(normed_two, full_gate_up, preferred_element_type=jnp.float32)
    hidden_width = full_down.shape[0]
    hidden = swiglu(gate_up, hidden_width).astype(jnp.bfloat16)
    output = (middle + jnp.dot(hidden, full_down, preferred_element_type=jnp.float32)).astype(
        jnp.bfloat16
    )
    upstream = cotangent.astype(jnp.float32)
    branch_two_grad = upstream.astype(jnp.bfloat16)
    grad_hidden = jnp.einsum(
        "td,fd->tf", branch_two_grad, full_down, preferred_element_type=jnp.float32
    )
    unused_value, swiglu_back = jax.vjp(partial(swiglu, hidden_width=hidden_width), gate_up)
    gate_up_grad = swiglu_back(grad_hidden)[0].astype(jnp.bfloat16)
    grad_normed_two = jnp.einsum(
        "tc,dc->td", gate_up_grad, full_gate_up, preferred_element_type=jnp.float32
    )
    unused_two, norm_two_back = jax.vjp(rms_norm, middle, gain_two)
    grad_middle_norm, grad_gain_two = norm_two_back(grad_normed_two)
    slot_normed_two, slot_hidden = (
        lax.all_gather(normed_two, "narrow", axis=0, tiled=True),
        lax.all_gather(hidden, "narrow", axis=0, tiled=True),
    )
    cols_gate_up, cols_down = (
        lax.all_to_all(gate_up_grad, "narrow", split_axis=1, concat_axis=0, tiled=True),
        lax.all_to_all(branch_two_grad, "narrow", split_axis=1, concat_axis=0, tiled=True),
    )
    grad_gate_up = jnp.einsum(
        "td,tc->dc", slot_normed_two, cols_gate_up, preferred_element_type=jnp.float32
    )
    grad_down = jnp.einsum("tf,td->fd", slot_hidden, cols_down, preferred_element_type=jnp.float32)
    ffn_shard_up, ffn_shard_down = (
        lax.psum_scatter(
            grad_gate_up.astype(jnp.bfloat16), "wide", scatter_dimension=0, tiled=True
        ).astype(jnp.float32),
        lax.psum_scatter(
            grad_down.astype(jnp.bfloat16), "wide", scatter_dimension=0, tiled=True
        ).astype(jnp.float32),
    )
    grad_middle = upstream + grad_middle_norm
    branch_one_grad = grad_middle.astype(jnp.bfloat16)
    grad_mixed = jnp.einsum(
        "te,de->td", branch_one_grad, full_out, preferred_element_type=jnp.float32
    )
    grad_attended = (
        (grad_mixed * gate_open).astype(jnp.bfloat16).reshape(token_rows, heads, head_size)
    )
    grad_gate_logit = grad_mixed * attended_float * gate_open * (1.0 - gate_open)
    head_grad = lax.all_to_all(grad_attended, "narrow", split_axis=1, concat_axis=0, tiled=True)
    slot_normed_one, slot_mixed = (
        lax.all_gather(normed_one, "narrow", axis=0, tiled=True),
        lax.all_gather(mixed, "narrow", axis=0, tiled=True),
    )
    grad_queries, grad_keys, grad_values, grad_decay = attend_backward(
        query_low,
        key_low,
        value_low,
        decay,
        segments,
        log_total,
        head_grad,
        block_rows,
        score_scale,
    )
    grads_in = prepare_back((grad_queries, grad_keys, grad_values, grad_decay))
    local_bias = jnp.sum(grads_in[3], axis=0)
    grad_bias = lax.dynamic_update_slice(
        jnp.zeros((heads,), jnp.float32), local_bias, (lax.axis_index("narrow") * local_heads,)
    )
    back_qkv = jnp.stack([grads_in[0], grads_in[1], grads_in[2]], axis=1).astype(jnp.bfloat16)
    back_gates = jnp.stack([grads_in[3], grads_in[4], grads_in[5]], axis=1).astype(jnp.bfloat16)
    seq_qkv, seq_gates = (
        lax.all_to_all(back_qkv, "narrow", split_axis=0, concat_axis=2, tiled=True),
        lax.all_to_all(back_gates, "narrow", split_axis=0, concat_axis=2, tiled=True),
    )
    projected_grad = jnp.concatenate(
        [
            seq_qkv.reshape(token_rows, 3 * width),
            grad_gate_logit.astype(jnp.bfloat16),
            seq_gates.reshape(token_rows, 3 * heads),
        ],
        axis=1,
    )
    grad_normed_one = jnp.einsum(
        "tc,dc->td", projected_grad, full_in, preferred_element_type=jnp.float32
    )
    unused_one, norm_one_back = jax.vjp(rms_norm, inputs, gain_one)
    grad_inputs_norm, grad_gain_one = norm_one_back(grad_normed_one)
    grad_tokens = grad_middle + grad_inputs_norm
    cols_projected, cols_branch = (
        lax.all_to_all(projected_grad, "narrow", split_axis=1, concat_axis=0, tiled=True),
        lax.all_to_all(branch_one_grad, "narrow", split_axis=1, concat_axis=0, tiled=True),
    )
    grad_in = jnp.einsum(
        "td,tc->dc", slot_normed_one, cols_projected, preferred_element_type=jnp.float32
    )
    grad_out = jnp.einsum("td,te->de", slot_mixed, cols_branch, preferred_element_type=jnp.float32)
    attention_shard_in, attention_shard_out = (
        lax.psum_scatter(
            grad_in.astype(jnp.bfloat16), "wide", scatter_dimension=0, tiled=True
        ).astype(jnp.float32),
        lax.psum_scatter(
            grad_out.astype(jnp.bfloat16), "wide", scatter_dimension=0, tiled=True
        ).astype(jnp.float32),
    )
    gain_one_total, gain_two_total, bias_total = lax.psum(
        (grad_gain_one, grad_gain_two, grad_bias), ("wide", "narrow")
    )
    return (
        output,
        grad_tokens,
        gain_one_total,
        attention_shard_in,
        bias_total,
        attention_shard_out,
        gain_two_total,
        ffn_shard_up,
        ffn_shard_down,
    )


def solution(mesh):
    in_specs = (
        P(("wide", "narrow"), None),
        P(),
        P(("wide", "narrow"), None),
        P(),
        P(("wide", "narrow"), None),
        P(),
        P(("wide", "narrow"), None),
        P(("wide", "narrow"), None),
        P("wide", None),
        P(("wide", "narrow"), None),
    )
    out_specs = (
        P(("wide", "narrow"), None),
        P(("wide", "narrow"), None),
        P(),
        P("wide", "narrow"),
        P(),
        P("wide", "narrow"),
        P(),
        P("wide", "narrow"),
        P("wide", "narrow"),
    )
    return jax.shard_map(
        on_device, mesh=mesh, in_specs=in_specs, out_specs=out_specs, check_vma=False
    )
```

profile of v0, /device:TPU:0, one launch (start us, length us, event | category | flops | bytes accessed | tf_op | source)
XLA Modules:
  0.0 1237.0 jit_solution(6587978566074906406)
XLA Ops:
  11.6 128.4 %all-gather.9.cloned.1.call-done = bf16[1536,6216]{1,0:T(8,128)(2,1)} async-done(((bf16[48,6216]{1,0:T(8,128)(2,1)}), bf16[1536,6216]{1,0:T(8,128)(2,1)}) %all-gather.9.cloned.1.call-update) | async-done | bytes 19095568 | tf_op jit(solution)/shard_map/all_gather | solution.py:157
  140.0 15.4 %fusion.79 = (bf16[256,6216]{0,1:T(8,128)(2,1)}, f32[256,6216]{0,1:T(8,128)}) fusion(bf16[256,1536]{1,0:T(8,128)(2,1)S(1)} %fusion.32, bf16[1536,6216]{1,0:T(8,128)(2,1)} %all-gather.9.cloned.1.call-done), kind=kOutput, calls=%fused_computation.188 | convolution fusion | flops 4890052608 | bytes 29429760 | tf_op jit(solution)/shard_map/dot_general | solution.py:161
  172.7 67.6 %all-to-all-done = bf16[256,3,24,64]{0,3,1,2:T(8,128)(2,1)S(1)} async-done(((bf16[256,3,24,64]{0,3,1,2:T(8,128)(2,1)}), bf16[256,3,24,64]{0,3,1,2:T(8,128)(2,1)S(1)}, u32[]{:S(2)}, u32[]{:S(2)}) %all-to-all-start) | async-done | bytes 2359328 | tf_op jit(solution)/shard_map/all_to_all | solution.py:175
  260.9 40.5 %while.29 = (s32[]{:T(128)}, bf16[2,512,6,64]{1,3,2,0:T(8,128)(2,1)S(1)}, f32[2,6,512]{2,1,0:T(8,128)}, s32[2]{0:T(128)S(1)}, s32[1024]{0:T(1024)S(1)}, /*index=...) while((s32[]{:T(128)}, ...), condition=%wide.region_8.9_spmd, body=%wide.region_5.8_spmd.sunk | while | flops 863499776 | bytes 42883776 | solution.py:81
  307.6 42.4 %all_to_all.151 = bf16[4,2,49152]{2,1,0:T(2,128)(2,1)S(1)} all-to-all(bf16[4,2,49152]{2,1,0:T(2,128)(2,1)} %reshape.367), channel_id=1, replica_groups=mesh['wide'=8,'narrow'=4] {'narrow'}, dimensions={0} | all-to-all | bytes 1572864 | tf_op jit(solution)/shard_map/all_to_all | solution.py:202
  357.7 9.7 all-gather.21.cloned.1.call-start
  373.6 28.4 %all-gather.13.cloned.1.call-done = bf16[1536,8192]{1,0:T(8,128)(2,1)} async-done(((bf16[48,8192]{1,0:T(8,128)(2,1)}), bf16[1536,8192]{1,0:T(8,128)(2,1)}) %all-gather.13.cloned.1.call-update) | async-done | bytes 25165840 | tf_op jit(solution)/shard_map/all_gather | solution.py:210
  402.0 13.8 %fusion.80 = f32[256,8192]{1,0:T(8,128)} fusion(bf16[256,1536]{1,0:T(8,128)(2,1)} %multiply_convert_fusion.3, bf16[1536,8192]{1,0:T(8,128)(2,1)} %all-gather.13.cloned.1.call-done), kind=kOutput, calls=%fused_computation.189 | convolution fusion | flops 6442450944 | bytes 34340864 | tf_op jit(solution)/shard_map/dot_general | solution.py:214
  415.8 83.5 %all-gather.15.cloned.1.call-done = bf16[4096,1536]{1,0:T(8,128)(2,1)} async-done(((bf16[128,1536]{1,0:T(8,128)(2,1)}), bf16[4096,1536]{1,0:T(8,128)(2,1)}) %all-gather.15.cloned.1.call-update) | async-done | bytes 12582928 | tf_op jit(solution)/shard_map/all_gather | solution.py:211
  499.3 11.3 fusion.51
  515.4 14.5 %multiply_reduce_fusion.1 = (f32[1536]{0:T(1024)}, f32[256]{0:T(256)S(1)}, f32[256,1536]{1,0:T(8,128)}) fusion(f32[256,1536]{1,0:T(8,128)S(1)} %get-tuple-element.295, f32[256]{0:T(256)S(1)} %fusion.74, f32[1536]{0:T(1024)S(1)} %copy-done.48, bf16[256,8192]{1,0:T(8,128)(2,1)} %add_convert_fusion, bf16[1536,8192]{1,0:T(8,128)(2,1)} %all-gather.13.cloned.1.call-done), kind=kOutput, calls=%fused_computation.103 | convolution fusion | flops 6444808192 | bytes 32520192 | tf_op jit(solution)/shard_map/tc,dc->td/dot_general | solution.py:227
  543.0 35.2 %all-to-all-done.3 = bf16[256,24,64]{0,2,1:T(8,128)(2,1)S(1)} async-done(((bf16[256,24,64]{0,2,1:T(8,128)(2,1)}), bf16[256,24,64]{0,2,1:T(8,128)(2,1)S(1)}, u32[]{:S(2)}, u32[]{:S(2)}) %all-to-all-start.3) | async-done | bytes 786464 | tf_op jit(solution)/shard_map/all_to_all | solution.py:261
  584.5 107.8 %while.30 = (s32[]{:T(128)}, f32[1024,6,64]{0,2,1:T(8,128)}, f32[1024,6,64]{0,2,1:T(8,128)}, f32[1024,6]{0,1:T(8,128)S(1)}, f32[2,512,6,64]{1,0,3,2:T(2,128)}, /...) while((s32[]{:T(128)}, f32[1024,6,64]{0,2,1:T(8,128)}, ...), condition=%wide.region_15.16_spmd.clone, body=%wide.region_11.15_spmd.clone.sunk | while | flops 2061039104 | bytes 226384272 | solution.py:131
  612.6 15.0 %dynamic_update_slice.30 = f32[2,512,6,64]{1,0,3,2:T(2,128)} dynamic-update-slice(f32[2,512,6,64]{1,0,3,2:T(2,128)} %get-tuple-element.519, f32[1,512,6,64]{1,0,3,2:T(1,128)S(1)} %copy.180, s32[]{:T(128)} %get-tuple-element.515, s32[]{:T(128)} %constant.54.clone.1..sunk.1, s32[]{:T(128)} %constant.54.clone.1..sunk.1, s32[]{:T(128)} %constant.54.clone.1..sunk.1) | dynamic-update-slice | bytes 1572868 | tf_op jit(solution)/shard_map/while/body/jit(dynamic_update_index_in_dim)/dynamic_update_slice | solution.py:81
  666.1 15.0 %dynamic_update_slice.30 = f32[2,512,6,64]{1,0,3,2:T(2,128)} dynamic-update-slice(f32[2,512,6,64]{1,0,3,2:T(2,128)} %get-tuple-element.519, f32[1,512,6,64]{1,0,3,2:T(1,128)S(1)} %copy.180, s32[]{:T(128)} %get-tuple-element.515, s32[]{:T(128)} %constant.54.clone.1..sunk.1, s32[]{:T(128)} %constant.54.clone.1..sunk.1, s32[]{:T(128)} %constant.54.clone.1..sunk.1) | dynamic-update-slice | bytes 1572868 | tf_op jit(solution)/shard_map/while/body/jit(dynamic_update_index_in_dim)/dynamic_update_slice | solution.py:81
  753.1 181.5 %all-to-all-done.8 = bf16[256,4,2048]{2,0,1:T(8,128)(2,1)} async-done(((bf16[256,4,2048]{2,0,1:T(8,128)(2,1)}), bf16[256,4,2048]{2,0,1:T(8,128)(2,1)}, u32[]{:S(2)}, u32[]{:S(2)}) %all-to-all-start.8) | async-done | bytes 4194336 | tf_op jit(solution)/shard_map/all_to_all | solution.py:237
  938.3 11.3 convolution_convert_fusion.1
  951.2 56.3 %all-to-all-done.4 = bf16[4,2,147456]{2,1,0:T(2,128)(2,1)S(1)} async-done(((bf16[4,2,147456]{2,1,0:T(2,128)(2,1)}), bf16[4,2,147456]{2,1,0:T(2,128)(2,1)S(1)}, u32[]{:S(2)}, u32[]{:S(2)}) %all-to-all-start.4) | async-done | bytes 2359328 | tf_op jit(solution)/shard_map/all_to_all | solution.py:285
  1025.9 74.7 %all_to_all.152 = bf16[256,4,1554]{0,2,1:T(8,128)(2,1)S(1)} all-to-all(bf16[256,4,1554]{0,2,1:T(8,128)(2,1)S(1)} %all_to_all.125), channel_id=1, replica_groups=mesh['wide'=8,'narrow'=4] {'narrow'}, dimensions={1} | all-to-all | bytes 6365184 | tf_op jit(solution)/shard_map/all_to_all | solution.py:303
  1111.2 10.4 convolution_convert_fusion
  1123.0 22.4 %all_to_all.153 = bf16[256,4,384]{0,2,1:T(8,128)(2,1)S(1)} all-to-all(bf16[256,4,384]{0,2,1:T(8,128)(2,1)S(1)} %bitcast.302), channel_id=1, replica_groups=mesh['wide'=8,'narrow'=4] {'narrow'}, dimensions={1} | all-to-all | bytes 1572864 | tf_op jit(solution)/shard_map/all_to_all | solution.py:238
  1156.7 9.8 fusion.29
  1168.3 11.6 fusion.33
  1179.9 39.2 %all-reduce.6 = (f32[1536]{0:T(1024)}, f32[24]{0:T(128)}, f32[1536]{0:T(1024)}) all-reduce(f32[1536]{0:T(1024)S(1)} %get-tuple-element.209, f32[24]{0:T(128)S(1)} %negate_dynamic-update-slice_fusion, f32[1536]{0:T(1024)S(1)} %copy-done.64), channel_id=1, replica_groups=mesh['wide'=8,'narrow'=4] {'wide','narrow'}, use_global_device_ids=true, to_apply=%region_24.25 | all-reduce | flops 3096 | bytes 24768 | tf_op jit(solution)/shard_map/psum | solution.py:318
  (343 shorter events, 315.5 us)
Async XLA Ops:
  7.2 132.8 %all-gather.9.cloned.1.call-start = ((), (), s32[]{:S(2)}) async-start(), calls=%async_computation.14 | async-start | bytes 19869696 | tf_op jit(solution)/shard_map/all_gather | solution.py:157
  7.9 359.5 %all-gather.11.cloned.1.call-start = ((), (), s32[]{:S(2)}) async-start(), calls=%async_computation.15 | async-start | bytes 4866048 | tf_op jit(solution)/shard_map/all_gather | solution.py:158
  8.7 393.3 %all-gather.13.cloned.1.call-start = ((), (), s32[]{:S(2)}) async-start(), calls=%async_computation.16 | async-start | bytes 25952256 | tf_op jit(solution)/shard_map/all_gather | solution.py:210
  9.4 489.9 %all-gather.15.cloned.1.call-start = ((), (), s32[]{:S(2)}) async-start(), calls=%async_computation.17 | async-start | bytes 12976128 | tf_op jit(solution)/shard_map/all_gather | solution.py:211
  11.6 143.8 %copy-start.29 = (bf16[256,1536]{1,0:T(8,128)(2,1)}, bf16[256,1536]{1,0:T(8,128)(2,1)S(1)}, u32[]{:S(2)}) copy-start(bf16[256,1536]{1,0:T(8,128)(2,1)S(1)} %fusion.32) | copy-start | bytes 2359300
  11.6 144.5 %copy-start.65 = (f32[24]{0:T(128)S(1)}, f32[24]{0:T(128)}, u32[]{:S(2)}) copy-start(f32[24]{0:T(128)} %param.17) | copy-start | bytes 292
  157.6 8.9 all-to-all-start.1
  166.5 73.8 %all-to-all-start = ((bf16[256,3,24,64]{0,3,1,2:T(8,128)(2,1)}), bf16[256,3,24,64]{0,3,1,2:T(8,128)(2,1)S(1)}, u32[]{:S(2)}, u32[]{:S(2)}) async-start(bf16[256,3,24,64]{0,3,1,2:T(8,128)(2,1)} %copy.101), calls=%async_computation | async-start | bytes 4718592 | tf_op jit(solution)/shard_map/all_to_all | solution.py:175
  170.2 578.0 %all-gather.19.cloned.1.call-start = ((), (), s32[]{:S(2)}) async-start(), calls=%async_computation.20 | async-start | bytes 3932160 | tf_op jit(solution)/shard_map/all_gather | solution.py:264
  357.7 580.6 %all-gather.21.cloned.1.call-start = ((), (), s32[]{:S(2)}) async-start(), calls=%async_computation.22 | async-start | bytes 3932160 | tf_op jit(solution)/shard_map/all_gather | solution.py:233
  371.5 158.5 %copy-start.7 = (f32[256,1536]{1,0:T(8,128)}, f32[256,1536]{1,0:T(8,128)S(1)}, u32[]{:S(2)}) copy-start(f32[256,1536]{1,0:T(8,128)S(1)} %get-tuple-element.295) | copy-start | bytes 4718596
  371.5 158.4 %copy-start.55 = (f32[256]{0:T(256)}, f32[256]{0:T(256)S(1)}, u32[]{:S(2)}) copy-start(f32[256]{0:T(256)S(1)} %fusion.74) | copy-start | bytes 3076
  372.8 738.3 %all-gather.17.cloned.1.call-start = ((), (), s32[]{:S(2)}) async-start(), calls=%async_computation.18 | async-start | bytes 3932160 | tf_op jit(solution)/shard_map/all_gather | solution.py:263
  373.6 125.7 %copy-start.21 = (bf16[256,1536]{1,0:T(8,128)(2,1)S(1)}, bf16[256,1536]{1,0:T(8,128)(2,1)}, u32[]{:S(2)}) copy-start(bf16[256,1536]{1,0:T(8,128)(2,1)} %param.23) | copy-start | bytes 2359300
  537.7 40.5 %all-to-all-start.3 = ((bf16[256,24,64]{0,2,1:T(8,128)(2,1)}), bf16[256,24,64]{0,2,1:T(8,128)(2,1)S(1)}, u32[]{:S(2)}, u32[]{:S(2)}) async-start(bf16[256,24,64]{0,2,1:T(8,128)(2,1)} %bitcast.30), calls=%async_computation.3 | async-start | bytes 1572864 | tf_op jit(solution)/shard_map/all_to_all | solution.py:261
  541.2 604.6 %all-gather.23.cloned.1.call-start = ((), (), s32[]{:S(2)}) async-start(), calls=%async_computation.24 | async-start | bytes 10485760 | tf_op jit(solution)/shard_map/all_gather | solution.py:234
  578.2 136.9 %all-to-all-start.7 = ((bf16[256,4,384]{2,0,1:T(8,128)(2,1)}), bf16[256,4,384]{2,0,1:T(8,128)(2,1)}, u32[]{:S(2)}, u32[]{:S(2)}) async-start(bf16[256,4,384]{2,0,1:T(8,128)(2,1)} %bitcast.223), calls=%async_computation.8 | async-start | bytes 1572864 | tf_op jit(solution)/shard_map/all_to_all | solution.py:304
  715.1 10.8 all-to-all-start.5
  725.8 208.8 %all-to-all-start.8 = ((bf16[256,4,2048]{2,0,1:T(8,128)(2,1)}), bf16[256,4,2048]{2,0,1:T(8,128)(2,1)}, u32[]{:S(2)}, u32[]{:S(2)}) async-start(bf16[256,4,2048]{2,0,1:T(8,128)(2,1)} %bitcast.281), calls=%async_computation.10 | async-start | bytes 8388608 | tf_op jit(solution)/shard_map/all_to_all | solution.py:237
  731.0 435.6 %reduce-scatter.7.cloned.1.call-start = ((), (), s32[]{:S(2)}) async-start(), calls=%async_computation.21 | async-start | bytes 1327104 | tf_op jit(solution)/shard_map/reduce_scatter | solution.py:314
  934.6 72.9 %all-to-all-start.4 = ((bf16[4,2,147456]{2,1,0:T(2,128)(2,1)}), bf16[4,2,147456]{2,1,0:T(2,128)(2,1)S(1)}, u32[]{:S(2)}, u32[]{:S(2)}) async-start(bf16[4,2,147456]{2,1,0:T(2,128)(2,1)} %reshape.371), calls=%async_computation.4 | async-start | bytes 4718592 | tf_op jit(solution)/shard_map/all_to_all | solution.py:285
  938.2 284.8 %reduce-scatter.9.cloned.1.call-start = ((), (), s32[]{:S(2)}) async-start(), calls=%async_computation.23 | async-start | bytes 7077888 | tf_op jit(solution)/shard_map/reduce_scatter | solution.py:245
  949.7 275.8 %reduce-scatter.5.cloned.1.call-start = ((), (), s32[]{:S(2)}) async-start(), calls=%async_computation.19 | async-start | bytes 5750784 | tf_op jit(solution)/shard_map/reduce_scatter | solution.py:311
  1121.6 106.1 %reduce-scatter.11.cloned.1.call-start = ((), (), s32[]{:S(2)}) async-start(), calls=%async_computation.25 | async-start | bytes 3538944 | tf_op jit(solution)/shard_map/reduce_scatter | solution.py:248
  (69 other events, 876.7 us)
Sparse Core Ops, SparseCore 0:
  10.8 129.1 all-gather.8
  142.8 90.1 all-gather.10
  235.9 166.0 all-gather.12
  404.7 94.5 all-gather.14
  501.3 78.4 all-gather.18
  581.3 72.6 all-gather.20
  655.5 62.3 all-gather.16
  719.5 277.7 all-gather.22
  1001.0 34.9 reduce-scatter.6
  1039.6 61.7 reduce-scatter.8
  1121.7 54.8 reduce-scatter.4
  1179.8 46.3 reduce-scatter.10
where the time goes:
time: 1250 us; the launch traced here: 1240 us
  waiting for transfers between devices  588 us (47%)
  matrix products  192 us (15%)
  blocking collectives  179 us (14%)
  local copies, waits for them, and re-layouts  139 us (11%)
  other arithmetic  77.6 us (6%)
  starting transfers between devices  38.5 us (3%)
  between operations  15.8 us (1%)
    all_to_all x1, waiting for transfers between devices, on_device(): lax.all_to_all(gate_up_grad, 'narrow', split_axis=1, concat_axis=0, tiled...  182 us
    all_gather x1, waiting for transfers between devices, on_device(): lax.all_gather(in_weight, ('wide', 'narrow'), axis=0, tiled=True)  128 us
    all_gather x1, waiting for transfers between devices, on_device(): lax.all_gather(down_weight, ('wide', 'narrow'), axis=0, tiled=True)  83.5 us
    all_to_all x1, blocking collectives, on_device(): lax.all_to_all(projected_grad, 'narrow', split_axis=1, concat_axis=0, til...  74.7 us
    all_to_all x1, waiting for transfers between devices, on_device(): lax.all_to_all(qkv_low, 'narrow', split_axis=2, concat_axis=0, tiled=True)  67.6 us
    all_to_all x1, waiting for transfers between devices, on_device(): lax.all_to_all(back_qkv, 'narrow', split_axis=0, concat_axis=2, tiled=True)  56.3 us
    all_to_all x1, blocking collectives, on_device(): lax.all_to_all(attended_heads.astype(jnp.bfloat16), 'narrow', split_axis=...  42.4 us
    psum x1, blocking collectives, on_device(): lax.psum((grad_gain_one, grad_gain_two, grad_bias), ('wide', 'narrow'))  39.2 us
  transfers between devices with their start and end apart: 19, of which 9 were waited for; matrix products, arithmetic and copies ran while one was open for 31% of the time, Pallas kernels for 0%

commit v1 on v0

v1 whole, which is shorter than its diff:
```python
import functools

import jax
import jax.numpy as jnp
from jax import lax
from jax.experimental import pallas as pl
from jax.experimental.pallas import tpu as pltpu
from jax.sharding import PartitionSpec as P

EPSILON = 1e-06
SEPARATE = 128.0
F32 = jnp.float32
BF16 = jnp.bfloat16
LANES = 128
EXACT = lax.Precision.HIGHEST
ANY = pl.BlockSpec(memory_space=pl.ANY)


def dot_f32(left, right, dims=((1,), (0,))):
    return lax.dot_general(left, right, (dims, ((), ())), preferred_element_type=F32)


def along_narrow(block, step, narrow):
    pairs = [(i, (i + step) % narrow) for i in range(narrow)]
    return lax.ppermute(block, "narrow", pairs)


def along_wide(block, flip, wide):
    return lax.ppermute(block, "wide", [(i, i ^ flip) for i in range(wide)])


def gather_narrow(block, narrow, slot, shape):
    me = lambda: lax.axis_index("narrow")
    if narrow != 4:
        pieces = [block] + [along_narrow(block, k, narrow) for k in range(1, narrow)]
        return assemble(pieces, lambda k, t: slot(lax.rem(me() + narrow - k, narrow), t), shape)
    two = lax.ppermute(block, "narrow", [(0, 2), (2, 0), (1, 3), (3, 1)])
    one = lax.ppermute(block, "narrow", [(0, 1), (1, 0), (2, 3), (3, 2)])
    middle = lax.ppermute(block, "narrow", [(1, 2), (2, 1)])
    end = lax.ppermute(two, "narrow", [(2, 3), (1, 0)])
    is_middle = lambda: (me() == 1) | (me() == 2)

    def plan(sources, targets):
        t = targets[0]
        far = slot(flipped(me(), 3), t)
        return [
            (sources[0], slot(me(), t)),
            (sources[1], slot(flipped(me(), 1), t)),
            (sources[2], slot(flipped(me(), 2), t)),
            (sources[3], far, is_middle()),
            (sources[4], far, jnp.logical_not(is_middle())),
        ]

    whole = jax.ShapeDtypeStruct(shape, block.dtype)
    return local_copies(plan, 5, [block, one, two, middle, end], [whole], True)[0]


def from_wide(block, wide):
    even = [block] + [along_wide(block, k, wide) for k in range(2, wide, 2)]
    pieces = []
    for piece in even:
        pieces += [piece, along_wide(piece, 1, wide)]
    return pieces


def copy_kernel(plan, count, *refs):
    sources, targets, sems = refs[:count], refs[count:-1], refs[-1]
    copies = plan(sources, targets)

    def each(act):
        for n, (src, dst, *when) in enumerate(copies):
            copy = pltpu.make_async_copy(src, dst, sems.at[n])
            if when:
                pl.when(when[0])(functools.partial(act, copy))
            else:
                act(copy)

    each(lambda copy: copy.start())
    each(lambda copy: copy.wait())


def local_copies(plan, copies, sources, shapes, gather):
    moved = sum(s.size * s.dtype.itemsize for s in shapes)
    inside = pl.BlockSpec(memory_space=pltpu.VMEM)
    out = pl.pallas_call(
        functools.partial(copy_kernel, plan, len(sources)),
        out_shape=shapes,
        in_specs=[ANY if gather else inside] * len(sources),
        out_specs=[inside if gather else ANY] * len(shapes),
        compiler_params=pltpu.CompilerParams(vmem_limit_bytes=16 * 2**20),
        scratch_shapes=[pltpu.SemaphoreType.DMA((copies,))],
        cost_estimate=pl.CostEstimate(flops=0, bytes_accessed=2 * moved, transcendentals=0),
    )(*sources)
    return out


def assemble(pieces, place, shape):
    def plan(sources, targets):
        return [(src, place(k, targets[0])) for k, src in enumerate(sources)]

    whole = jax.ShapeDtypeStruct(shape, pieces[0].dtype)
    return local_copies(plan, len(pieces), pieces, [whole], True)[0]


def narrow_order(k, narrow):
    return lax.rem(lax.axis_index("narrow") + narrow - k, narrow)


def narrow_target(k, narrow):
    return lax.rem(lax.axis_index("narrow") + k, narrow)


def flipped(me, k):
    out = me
    bit = 1
    while bit <= k:
        if k & bit:
            out = out + bit - 2 * bit * lax.rem(lax.div(out, bit), 2)
        bit *= 2
    return out


def wide_order(k):
    return flipped(lax.axis_index("wide"), k)


def nothing_kernel(*refs):
    pass


def follow(array, *earlier):
    return pl.pallas_call(
        nothing_kernel,
        out_shape=jax.ShapeDtypeStruct(array.shape, array.dtype),
        in_specs=[ANY] * (1 + len(earlier)),
        out_specs=ANY,
        input_output_aliases={0: 0},
    )(array, *earlier)


def rms_factor(values):
    return lax.rsqrt(jnp.mean(values * values, axis=-1, keepdims=True) + EPSILON)


def rms_back(values, gain, grad):
    factor = rms_factor(values)
    normed = values * factor
    grad_gain = jnp.sum(grad * normed, axis=0)
    scaled = grad * gain
    inner = jnp.mean(scaled * normed, axis=-1, keepdims=True)
    return (factor * (scaled - normed * inner), grad_gain)


def log_sigmoid(v):
    return jnp.minimum(v, 0.0) - jnp.log1p(jnp.exp(-jnp.abs(v)))


def iota(shape, dim):
    return lax.broadcasted_iota(jnp.int32, shape, dim)


def running_sum(v, reverse):
    rows = v.shape[0]
    index = iota(v.shape, 0)
    step = 1
    while step < rows:
        if reverse:
            v = v + jnp.where(index < rows - step, pltpu.roll(v, rows - step, 0), 0.0)
        else:
            v = v + jnp.where(index >= step, pltpu.roll(v, step, 0), 0.0)
        step *= 2
    return v


def half_of(lane, head_size):
    return (lane >= head_size).astype(jnp.int32)


def spread(first, head_size):
    row, lane = iota((LANES, LANES), 0), iota((LANES, LANES), 1)
    return row == first + half_of(lane, head_size)


def collect(first, head_size):
    row, lane = iota((LANES, LANES), 0), iota((LANES, LANES), 1)
    return lane == first + half_of(row, head_size)


def same_head(head_size):
    row, lane = iota((LANES, LANES), 0), iota((LANES, LANES), 1)
    return (half_of(row, head_size) == half_of(lane, head_size)).astype(F32)


def exact_dot(left, right):
    return lax.dot_general(
        left, right, (((1,), (0,)), ((), ())), precision=EXACT, preferred_element_type=F32
    )


def head_mean(v, head_size):
    return exact_dot(v, same_head(head_size)) * (1.0 / head_size)


def prologue(pair, heads, head_size, q_ref, k_ref, v_ref, small_low, cont):
    spot = lambda group: spread(group * heads + 2 * pair, head_size).astype(BF16)
    key_mix = jax.nn.sigmoid(dot_f32(small_low, spot(1)))
    value_mix = jax.nn.sigmoid(dot_f32(small_low, spot(2)))
    queries = q_ref[...].astype(BF16).astype(F32)
    keys = k_ref[...].astype(BF16).astype(F32)
    values = v_ref[...].astype(BF16).astype(F32)
    key_step = pltpu.roll(keys, 1, 0) * cont - keys
    value_step = pltpu.roll(values, 1, 0) * cont - values
    shifted = keys + key_mix * key_step
    value_low = (values + value_mix * value_step).astype(BF16)
    query_factor = lax.rsqrt(head_mean(queries * queries, head_size) + EPSILON)
    key_factor = lax.rsqrt(head_mean(shifted * shifted, head_size) + EPSILON)
    return (
        queries * query_factor,
        shifted * key_factor,
        value_low,
        query_factor,
        key_factor,
        key_mix,
        value_mix,
        key_step,
        value_step,
    )


def small_columns(small_ref, bias_ref):
    return (small_ref[...] + bias_ref[0:1, :]).astype(BF16)


def decay_of(small_low, cont):
    return running_sum(log_sigmoid(small_low.astype(F32)) - SEPARATE * (1.0 - cont), False)


def forward_kernel(
    heads, head_size, block, q_ref, k_ref, v_ref, gate_ref, small_ref, bias_ref, cont_ref,
    mixed_ref, att_ref, log_ref, decay_scr,
):
    pair = pl.program_id(0)
    cont = cont_ref[...]
    small_low = small_columns(small_ref, bias_ref)

    @pl.when(pair == 0)
    def _():
        decay_scr[...] = decay_of(small_low, cont)

    query, key, value_low, *unused = prologue(
        pair, heads, head_size, q_ref, k_ref, v_ref, small_low, cont
    )
    rows = query.shape[0]
    query = query.astype(BF16) * BF16(head_size**-0.5)
    key = key.astype(BF16)
    decay = exact_dot(decay_scr[...], spread(2 * pair, head_size).astype(F32))
    decay_rows = decay.T
    lane = iota((1, LANES), 1)
    ones = jnp.ones((rows, LANES), BF16)
    value_wide = jnp.concatenate([value_low, ones], axis=1)
    for i in range(rows // block):
        lo, hi = i * block, (i + 1) * block
        row_index = iota((block, hi), 0) + lo
        visible = iota((block, hi), 1) <= row_index
        outs, sums = [], []
        for head in range(2):
            mine = (lane >= head_size) if head else (lane < head_size)
            at = head * head_size
            left = jnp.where(mine, query[lo:hi], BF16(0.0))
            scores = dot_f32(left, key[:hi], ((1,), (1,)))
            scores = scores + decay[lo:hi, at : at + 1] - decay_rows[at : at + 1, :hi]
            weights = jnp.where(visible, jnp.exp(scores), 0.0).astype(BF16)
            both = dot_f32(weights, value_wide[:hi])
            outs.append(both[:, :LANES])
            sums.append(both[:, LANES:])
        first = lane < head_size
        total = jnp.where(first, sums[0], sums[1])
        attended = (jnp.where(first, outs[0], outs[1]) / total).astype(BF16)
        att_ref[lo:hi, :] = attended
        log_ref[lo:hi, :] = jnp.log(total)
        opened = jax.nn.sigmoid(gate_ref[lo:hi, :])
        mixed_ref[lo:hi, :] = (attended.astype(F32) * opened).astype(BF16)


def backward_kernel(
    heads, head_size, block, q_ref, k_ref, v_ref, gate_ref, small_ref, bias_ref, cont_ref,
    att_ref, log_ref, grad_ref, out_ref, bias_grad_ref, decay_scr, small_scr, dq_scr,
):
    pair = pl.program_id(0)
    cont = cont_ref[...]
    small_low = small_columns(small_ref, bias_ref)
    rows = cont.shape[0]
    width = heads * head_size

    @pl.when(pair == 0)
    def _():
        decay_scr[...] = decay_of(small_low, cont)
        small_scr[...] = jnp.zeros_like(small_scr)

    (
        query_norm, key_norm, value_low, query_factor, key_factor, key_mix, value_mix, key_step,
        value_step,
    ) = prologue(pair, heads, head_size, q_ref, k_ref, v_ref, small_low, cont)
    query = query_norm.astype(BF16) * BF16(head_size**-0.5)
    key = key_norm.astype(BF16)
    opened = jax.nn.sigmoid(gate_ref[...])
    attended = att_ref[...].astype(F32)
    grad_mixed = grad_ref[...].astype(F32)
    grad_low = (grad_mixed * opened).astype(BF16)
    grad_gate = grad_mixed * attended * opened * (1.0 - opened)

    def columns(group):
        at = group * width + pair * LANES
        return pl.ds(pl.multiple_of(at, LANES), LANES)

    out_ref[:, columns(3)] = grad_gate.astype(BF16)
    inner = exact_dot(grad_low.astype(F32) * attended, same_head(head_size))
    decay = exact_dot(decay_scr[...], spread(2 * pair, head_size).astype(F32))
    level_rows = (decay - log_ref[...]).T
    inner_rows = inner.T
    lane = iota((1, LANES), 1)
    ones = jnp.ones((rows, LANES), BF16)
    query_wide = jnp.concatenate([query, ones], axis=1)
    key_wide = jnp.concatenate([key, ones], axis=1)
    key_parts, value_parts, query_parts = [], [], []
    for head in range(2):
        mine = (lane >= head_size) if head else (lane < head_size)
        at = head * head_size
        keys_out, values_out = [], []
        for j in range(rows // block):
            lo, hi = j * block, (j + 1) * block
            span = rows - lo
            visible = iota((block, span), 0) <= iota((block, span), 1)
            scores = dot_f32(
                jnp.where(mine, key[lo:hi], BF16(0.0)), query[lo:], ((1,), (1,))
            )
            scores = scores + level_rows[at : at + 1, lo:] - decay[lo:hi, at : at + 1]
            probs = jnp.where(visible, jnp.exp(scores), 0.0)
            grad_probs = dot_f32(
                jnp.where(mine, value_low[lo:hi], BF16(0.0)), grad_low[lo:], ((1,), (1,))
            )
            grad_scores = (probs * (grad_probs - inner_rows[at : at + 1, lo:])).astype(BF16)
            values_out.append(dot_f32(probs.astype(BF16), grad_low[lo:]))
            keys_out.append(dot_f32(grad_scores, query_wide[lo:]))
            part = dot_f32(grad_scores, key_wide[lo:hi], ((0,), (0,)))
            if j == 0:
                dq_scr[...] = part
            else:
                dq_scr[lo:, :] += part
        key_parts.append(jnp.concatenate(keys_out, axis=0))
        value_parts.append(jnp.concatenate(values_out, axis=0))
        query_parts.append(dq_scr[...])
    first = lane < head_size

    def join(parts):
        return jnp.where(first, parts[0], parts[1])

    grad_query = join([p[:, :LANES] for p in query_parts]) * head_size**-0.5
    grad_key = join([p[:, :LANES] for p in key_parts])
    grad_value = join(value_parts)
    grad_decay = join([p[:, LANES:] for p in query_parts]) - join([p[:, LANES:] for p in key_parts])

    def norm_back(grad, normed, factor):
        return factor * (grad - normed * head_mean(grad * normed, head_size))

    def shift_back(grad, mix):
        return grad * (1.0 - mix) + pltpu.roll(grad * mix * cont, rows - 1, 0)

    grad_query = norm_back(grad_query, query_norm, query_factor)
    grad_shifted = norm_back(grad_key, key_norm, key_factor)
    out_ref[:, columns(0)] = grad_query.astype(BF16)
    out_ref[:, columns(1)] = shift_back(grad_shifted, key_mix).astype(BF16)
    out_ref[:, columns(2)] = shift_back(grad_value, value_mix).astype(BF16)
    key_logit = grad_shifted * key_step * key_mix * (1.0 - key_mix)
    value_logit = grad_value * value_step * value_mix * (1.0 - value_mix)
    single = (lax.rem(lane, head_size) == 0).astype(F32)
    small_scr[...] += (
        exact_dot(grad_decay * single, collect(2 * pair, head_size).astype(F32))
        + exact_dot(key_logit, collect(heads + 2 * pair, head_size).astype(F32))
        + exact_dot(value_logit, collect(2 * heads + 2 * pair, head_size).astype(F32))
    )

    @pl.when(pair == pl.num_programs(0) - 1)
    def _():
        grads = small_scr[...]
        forget = running_sum(grads, True) * jax.nn.sigmoid(-small_low.astype(F32))
        result = jnp.where(lane < heads, forget, grads)
        out_ref[:, 4 * width :] = result.astype(BF16)
        bias_grad_ref[...] = jnp.broadcast_to(
            jnp.sum(result, axis=0, keepdims=True), bias_grad_ref.shape
        )


def attention_specs(rows, pairs):
    def block_at(group):
        return pl.BlockSpec((rows, LANES), lambda p: (0, group * pairs + p))

    def fixed(height, column=0):
        return pl.BlockSpec((height, LANES), lambda p: (0, column))

    base = [block_at(0), block_at(1), block_at(2), block_at(3), fixed(rows, 4 * pairs), fixed(8), fixed(rows)]
    return base, pl.BlockSpec((rows, LANES), lambda p: (0, p))


def attention_forward(projected, bias, cont, heads, head_size, block):
    rows = projected.shape[0]
    pairs = heads * head_size // LANES
    base, own = attention_specs(rows, pairs)
    wide = jax.ShapeDtypeStruct((rows, heads * head_size), BF16)
    return pl.pallas_call(
        functools.partial(forward_kernel, heads, head_size, block),
        grid=(pairs,),
        in_specs=base,
        out_specs=[own] * 3,
        out_shape=[wide, wide, jax.ShapeDtypeStruct(wide.shape, F32)],
        scratch_shapes=[pltpu.VMEM((rows, LANES), F32)],
        compiler_params=pltpu.CompilerParams(vmem_limit_bytes=48 * 2**20),
        cost_estimate=pl.CostEstimate(
            flops=heads * rows * rows * 400, bytes_accessed=rows * 1664 * 6, transcendentals=heads * rows * rows // 2
        ),
    )(*([projected] * 5), bias, cont)


def attention_backward(projected, bias, cont, attended, logs, grad, heads, head_size, block):
    rows = projected.shape[0]
    pairs = heads * head_size // LANES
    base, own = attention_specs(rows, pairs)
    columns = 4 * heads * head_size + LANES
    return pl.pallas_call(
        functools.partial(backward_kernel, heads, head_size, block),
        grid=(pairs,),
        in_specs=base + [own] * 3,
        out_specs=[
            pl.BlockSpec((rows, columns), lambda p: (0, 0)),
            pl.BlockSpec((8, LANES), lambda p: (0, 0)),
        ],
        out_shape=[
            jax.ShapeDtypeStruct((rows, columns), BF16),
            jax.ShapeDtypeStruct((8, LANES), F32),
        ],
        scratch_shapes=[
            pltpu.VMEM((rows, LANES), F32),
            pltpu.VMEM((rows, LANES), F32),
            pltpu.VMEM((rows, 2 * LANES), F32),
        ],
        compiler_params=pltpu.CompilerParams(vmem_limit_bytes=56 * 2**20),
        cost_estimate=pl.CostEstimate(
            flops=heads * rows * rows * 1000, bytes_accessed=rows * 1664 * 8, transcendentals=heads * rows * rows // 2
        ),
    )(*([projected] * 5), bias, cont, attended, logs, grad)


def reduce_wide(pieces, wide):
    received = along_wide(jnp.stack(pieces[1::2]), 1, wide)
    summed = [
        (pieces[2 * n].astype(F32) + received[n].astype(F32)).astype(BF16) for n in range(wide // 2)
    ]
    total = summed[0].astype(F32)
    for n in range(1, wide // 2):
        total = total + along_wide(summed[n], 2 * n, wide).astype(F32)
    return total


def reduce_narrow(share, narrow):
    me = lax.axis_index("narrow")
    if narrow != 4:
        total = share(me).astype(F32)
        for k in range(1, narrow):
            total = total + along_narrow(share(lax.rem(me + k, narrow)), k, narrow).astype(F32)
        return total
    far = share(flipped(me, 3))
    joined = lax.ppermute(far, "narrow", [(0, 1), (3, 2)])
    middle = lax.ppermute(far, "narrow", [(1, 2), (2, 1)])
    one = lax.ppermute(share(flipped(me, 1)), "narrow", [(0, 1), (1, 0), (2, 3), (3, 2)])
    two = (share(flipped(me, 2)).astype(F32) + joined.astype(F32)).astype(BF16)
    two = lax.ppermute(two, "narrow", [(0, 2), (2, 0), (1, 3), (3, 1)])
    total = share(me).astype(F32) + one.astype(F32)
    return total + middle.astype(F32) + two.astype(F32)


def total_of(values, wide, narrow):
    bit = 1
    while bit < wide:
        values = values + along_wide(values, bit, wide)
        bit *= 2
    bit = 1
    while bit < narrow:
        values = values + lax.ppermute(values, "narrow", [(i, i ^ bit) for i in range(narrow)])
        bit *= 2
    return values


def on_device(
    tokens, gain_one, in_weight, forget_bias, out_weight, gain_two, gate_up_weight, down_weight,
    segment_ids, cotangent,
):
    wide, narrow = lax.axis_size("wide"), lax.axis_size("narrow")
    w, z = lax.axis_index("wide"), lax.axis_index("narrow")
    rows, width = tokens.shape
    slot = rows * narrow
    heads = forget_bias.shape[0]
    head_size = width // heads
    own_heads = heads // narrow
    own_width = own_heads * head_size
    part_rows = in_weight.shape[0]
    hidden_all = down_weight.shape[0] * wide * narrow
    unit = hidden_all // (2 * wide)
    columns = 4 * own_width + LANES
    base = 4 * width

    small = in_weight[:, base:].reshape(part_rows, 3, narrow, own_heads)
    small = jnp.moveaxis(small, 2, 0).reshape(narrow, part_rows, 3 * own_heads)
    small = jnp.pad(small, ((0, 0), (0, 0), (0, LANES - 3 * own_heads)))

    def split_in(sources, targets):
        copies = []
        for k, target in enumerate(targets):
            to = narrow_target(k, narrow)
            for group in range(4):
                at = pl.multiple_of(group * width + to * own_width, LANES)
                copies.append(
                    (
                        sources[0].at[:, pl.ds(at, own_width)],
                        target.at[:, pl.ds(group * own_width, own_width)],
                    )
                )
            copies.append((sources[1].at[to], target.at[:, pl.ds(4 * own_width, LANES)]))
        return copies

    in_parts = local_copies(
        split_in, 5 * narrow, [in_weight, small],
        [jax.ShapeDtypeStruct((part_rows, columns), BF16)] * narrow, False,
    )
    in_pieces = [in_parts[0]] + [along_narrow(in_parts[k], k, narrow) for k in range(1, narrow)]
    in_block = assemble(
        in_pieces, lambda k, t: t.at[narrow_order(k, narrow)], (narrow, part_rows, columns)
    )

    slot_tokens = gather_narrow(
        tokens, narrow, lambda n, t: t.at[n], (narrow, rows, width)
    ).reshape(slot, width)
    in_full = assemble(
        from_wide(in_block, wide), lambda k, t: t.at[wide_order(k)],
        (wide, narrow, part_rows, columns),
    ).reshape(width, columns)
    slot_floats = slot_tokens.astype(F32)
    normed_one = (slot_floats * rms_factor(slot_floats) * gain_one).astype(BF16)
    projected = dot_f32(normed_one, in_full)

    out_block = gather_narrow(
        follow(out_weight, slot_tokens), narrow, lambda n, t: t.at[n], (narrow,) + out_weight.shape
    )
    out_full = assemble(
        from_wide(out_block, wide), lambda k, t: t.at[wide_order(k)], (wide,) + out_block.shape
    ).reshape(width, width)

    def split_up(sources, targets):
        copies = []
        for k, target in enumerate(targets):
            to = wide_order(k)
            for group in range(4):
                at = pl.multiple_of((group * wide + to) * unit, 64)
                copies.append(
                    (
                        sources[0].at[:, pl.ds(at, unit)],
                        target.at[:, pl.ds(group * unit, unit)],
                    )
                )
        return copies

    if unit % LANES == 0:
        up_parts = local_copies(
            split_up, 4 * wide, [gate_up_weight],
            [jax.ShapeDtypeStruct((part_rows, 4 * unit), BF16)] * wide, False,
        )
    else:
        grouped = jnp.moveaxis(gate_up_weight.reshape(part_rows, 4, wide, unit), 2, 0)
        grouped = grouped.reshape(wide, part_rows, 4 * unit)
        up_parts = [
            lax.dynamic_index_in_dim(grouped, wide_order(k), 0, False) for k in range(wide)
        ]
    up_pieces = [up_parts[0]] + [along_wide(up_parts[k], k, wide) for k in range(1, wide)]
    up_block = assemble(up_pieces, lambda k, t: t.at[wide_order(k)], (wide, part_rows, 4 * unit))
    up_full = gather_narrow(
        follow(up_block, out_block), narrow, lambda n, t: t.at[:, n],
        (wide, narrow, part_rows, 4 * unit),
    ).reshape(width, 4 * unit)
    down_rows = down_weight.shape[0]
    pairs = []
    for i in range(wide * narrow):
        to_wide = (i % (2 * wide)) // 2
        to_narrow = i % 2 + 2 * (i // (2 * wide))
        pairs.append((i, to_wide * narrow + to_narrow))
    down_block = lax.ppermute(follow(down_weight, slot_tokens), ("wide", "narrow"), pairs)
    down_full = gather_narrow(
        follow(down_block, up_full), narrow, lambda n, t: t.at[n], (narrow, down_rows, width)
    ).reshape(2 * unit, width)

    segments = segment_ids[0]
    joined = (segments[1:] == segments[:-1]).astype(F32)
    cont = jnp.concatenate([jnp.zeros((1,), F32), joined])
    cont = jnp.broadcast_to(cont[:, None], (slot, LANES))
    own_bias = lax.dynamic_slice_in_dim(forget_bias, z * own_heads, own_heads)
    bias = jnp.broadcast_to(jnp.pad(own_bias, (0, LANES - own_heads))[None], (8, LANES))
    block = min(256, slot)
    mixed, attended, logs = attention_forward(
        projected, bias, cont, own_heads, head_size, block
    )

    def rows_of(k, array):
        return lax.dynamic_slice_in_dim(array, lax.rem(z + k, narrow) * rows, rows, 0)

    def columns_of(k, array, size):
        return lax.dynamic_slice_in_dim(array, lax.rem(z + k, narrow) * size, size, 1)

    def share_columns(array, size):
        return lambda n: lax.dynamic_slice_in_dim(array, n * size, size, 1)

    mixed_pieces = [rows_of(0, mixed)] + [
        along_narrow(rows_of(k, mixed), k, narrow) for k in range(1, narrow)
    ]

    def at_columns(k, target):
        at = pl.multiple_of(narrow_order(k, narrow) * own_width, LANES)
        return target.at[:, pl.ds(at, own_width)]

    mixed_rows = assemble(mixed_pieces, at_columns, (rows, width))
    inputs = tokens.astype(F32)
    middle = inputs + dot_f32(mixed_rows, out_full)
    normed_two = (middle * rms_factor(middle) * gain_two).astype(BF16)

    plane_normed = jnp.concatenate(from_wide(normed_two, wide), axis=0)
    plane_grad = jnp.concatenate(from_wide(follow(cotangent, in_full), wide), axis=0)
    gate_up = dot_f32(plane_normed, up_full)
    gate, up = gate_up[:, : 2 * unit], gate_up[:, 2 * unit :]
    opened = jax.nn.sigmoid(gate)
    hidden = (gate * opened * up).astype(BF16)
    grad_hidden = dot_f32(plane_grad, down_full, ((1,), (1,)))
    gate_up_grad = jnp.concatenate(
        [
            grad_hidden * up * (opened * (1.0 + gate * (1.0 - opened))),
            grad_hidden * gate * opened,
        ],
        axis=1,
    ).astype(BF16)
    grad_normed_two = dot_f32(gate_up_grad, up_full, ((1,), (1,))).astype(BF16)
    grad_up_full = dot_f32(plane_normed, gate_up_grad, ((0,), (0,))).astype(BF16)
    grad_down_full = dot_f32(hidden, plane_grad, ((0,), (0,))).astype(BF16)

    def row_pieces(array):
        return [array[k * rows : (k + 1) * rows] for k in range(wide)]

    grad_normed_two = reduce_wide(row_pieces(grad_normed_two), wide)
    upstream = cotangent.astype(F32)
    grad_middle_norm, grad_gain_two = rms_back(middle, gain_two, grad_normed_two)
    grad_middle = upstream + grad_middle_norm
    branch_one_grad = grad_middle.astype(BF16)
    grad_mixed = dot_f32(branch_one_grad, out_full, ((1,), (1,))).astype(BF16)
    grad_pieces = [columns_of(0, grad_mixed, own_width)] + [
        along_narrow(columns_of(k, grad_mixed, own_width), k, narrow) for k in range(1, narrow)
    ]
    slot_grad = assemble(
        grad_pieces, lambda k, t: t.at[narrow_order(k, narrow)], (narrow, rows, own_width)
    ).reshape(slot, own_width)
    branch_two = dot_f32(follow(hidden, grad_normed_two), down_full).astype(BF16)
    output = (middle + reduce_wide(row_pieces(branch_two), wide)).astype(BF16)

    projected_grad, bias_grad = attention_backward(
        projected, bias, cont, attended, logs, slot_grad, own_heads, head_size, block
    )
    grad_normed_one_part = dot_f32(projected_grad, in_full, ((1,), (1,))).astype(BF16)
    grad_normed_one = reduce_narrow(
        lambda n: lax.dynamic_slice_in_dim(grad_normed_one_part, n * rows, rows, 0), narrow
    )
    grad_inputs, grad_gain_one = rms_back(inputs, gain_one, grad_normed_one)
    grad_tokens = grad_middle + grad_inputs

    grad_up = reduce_narrow(share_columns(grad_up_full, unit), narrow)
    grad_up = grad_up.astype(BF16)
    wide_rows = width // wide
    grad_up_pieces = []
    for k in range(wide):
        piece = lax.dynamic_slice_in_dim(grad_up, wide_order(k) * wide_rows, wide_rows, 0)
        grad_up_pieces.append(along_wide(piece, k, wide) if k else piece)
    if unit % LANES == 0:
        grad_up = assemble(
            grad_up_pieces,
            lambda k, t: t.at[:, pl.ds(pl.multiple_of(wide_order(k) * unit, LANES), unit)],
            (wide_rows, wide * unit),
        )
    else:
        grad_up = assemble(
            grad_up_pieces, lambda k, t: t.at[wide_order(k)], (wide, wide_rows, unit)
        )
        grad_up = jnp.moveaxis(grad_up, 0, 1).reshape(wide_rows, wide * unit)
    grad_up = grad_up.astype(F32)

    narrow_width = width // narrow
    grad_down = reduce_narrow(share_columns(grad_down_full, narrow_width), narrow).astype(BF16)
    low_half, high_half = grad_down[:unit], grad_down[unit:]
    is_odd = lax.rem(w, 2) == 1
    first_send = jnp.where(is_odd, high_half, low_half)
    second_send = jnp.where(is_odd, low_half, high_half)
    half = wide // 2
    first_got = lax.ppermute(
        first_send, "wide", [(i, i // 2 + (half if i % 2 else 0)) for i in range(wide)]
    )
    second_got = lax.ppermute(
        second_send, "wide", [(i, i // 2 + (0 if i % 2 else half)) for i in range(wide)]
    )
    in_low = w < half
    grad_down = jnp.concatenate(
        [
            jnp.where(in_low, first_got, second_got),
            jnp.where(in_low, second_got, first_got),
        ],
        axis=0,
    ).astype(F32)

    grad_out_full = dot_f32(mixed_rows, branch_one_grad, ((0,), (0,))).astype(BF16)

    def wide_pieces(array):
        return [
            lax.dynamic_slice_in_dim(array, wide_order(k) * wide_rows, wide_rows, 0)
            for k in range(wide)
        ]

    grad_out = reduce_wide(wide_pieces(grad_out_full), wide).astype(BF16)
    grad_out = reduce_narrow(share_columns(grad_out, narrow_width), narrow)
    grad_in_full = dot_f32(normed_one, projected_grad, ((0,), (0,))).astype(BF16)
    grad_in = reduce_wide(wide_pieces(grad_in_full), wide).astype(BF16)
    grad_small = grad_in[:, 4 * own_width :]
    sections = []
    for j in range(4):
        own = grad_in[:, j * own_width : (j + 1) * own_width]
        after = grad_in[:, (j + 1) * own_width : (j + 1) * own_width + LANES]
        sections.append(jnp.concatenate([own, after], axis=1))
    sections = jnp.stack(sections)
    got = []
    for k in range(narrow):
        piece = lax.dynamic_index_in_dim(sections, lax.rem(z + k, narrow), 0, False)
        got.append(along_narrow(piece, k, narrow) if k else piece)
    got = assemble(
        got, lambda k, t: t.at[narrow_order(k, narrow)],
        (narrow, wide_rows, own_width + LANES),
    )
    extra = 3 * heads
    section = jnp.concatenate([got[n, :, :own_width] for n in range(narrow)], axis=1)
    small_all = jnp.stack([got[n, :, own_width : own_width + 3 * own_heads] for n in range(narrow)])
    small_all = small_all.reshape(narrow, wide_rows, 3, own_heads)
    small_all = jnp.transpose(small_all, (1, 2, 0, 3)).reshape(wide_rows, extra)
    next_first = got[0, :, own_width : own_width + extra]
    tail = jnp.where(z == narrow - 1, small_all, next_first)
    joined_columns = jnp.concatenate([section, tail], axis=1)
    shard = (base + extra) // narrow
    grad_in = lax.dynamic_slice_in_dim(joined_columns, z * (shard - width), shard, 1).astype(F32)

    all_bias = lax.dynamic_update_slice(
        jnp.zeros((heads,), F32), bias_grad[0, :own_heads], (z * own_heads,)
    )
    packed = jnp.concatenate([grad_gain_one, grad_gain_two, all_bias])
    packed = total_of(packed, wide, narrow)
    return (
        output,
        grad_tokens,
        packed[:width],
        grad_in,
        packed[2 * width :],
        grad_out,
        packed[width : 2 * width],
        grad_up,
        grad_down,
    )


def solution(mesh):
    both = ("wide", "narrow")
    in_specs = (
        P(both, None), P(), P(both, None), P(), P(both, None), P(), P(both, None), P(both, None),
        P("wide", None), P(both, None),
    )
    out_specs = (
        P(both, None), P(both, None), P(), P("wide", "narrow"), P(), P("wide", "narrow"), P(),
        P("wide", "narrow"), P("wide", "narrow"),
    )
    return jax.shard_map(
        on_device, mesh=mesh, in_specs=in_specs, out_specs=out_specs, check_vma=False
    )
```

time: 1250 us -> 752 us (0.60)
  waiting for transfers between devices: 588 us -> 339 us
  blocking collectives: 179 us -> 0 us
  matrix products: 192 us -> 73 us
  starting transfers between devices: 38.5 us -> 140 us
  Pallas kernels: 0 us -> 66.7 us
  local copies, waits for them, and re-layouts: 139 us -> 72.9 us
  other arithmetic: 77.6 us -> 45.2 us
  between operations: 15.8 us -> 2.48 us
    all_to_all x7 -> x0, waiting for transfers between devices: 344 us -> none  [the longest x1 182 us: on_device(): lax.all_to_all(gate_up_grad, 'narrow', split_axis=1, concat_axis=0, tiled...]
    ppermute x0 -> x110, waiting for transfers between devices: none -> 339 us  [the longest x61 140 us: along_wide(): return lax.ppermute(block, 'wide', [(i, i ^ flip) for i in range(wide)])]
    all_gather x8 -> x0, waiting for transfers between devices: 240 us -> none  [the longest x1 128 us: on_device(): lax.all_gather(in_weight, ('wide', 'narrow'), axis=0, tiled=True)]
    ppermute x0 -> x110, starting transfers between devices: none -> 140 us  [the longest x61 58.7 us: along_wide(): return lax.ppermute(block, 'wide', [(i, i ^ flip) for i in range(wide)])]
    all_to_all x3 -> x0, blocking collectives: 140 us -> none  [the longest x1 74.7 us: on_device(): lax.all_to_all(projected_grad, 'narrow', split_axis=1, concat_axis=0, til...]
    dot_general x26 -> x12, matrix products: 192 us -> 73 us  [dot_f32(): lax.dot_general(left, right, (dims, ((), ())), preferred_element_type=F32)]
    pallas_call x0 -> x22, Pallas kernels: none -> 66.7 us  [the longest x1 37.5 us: attention_backward(): pl.pallas_call(functools.partial(backward_kernel, heads, head_size, block...]
    psum x1 -> x0, blocking collectives: 39.2 us -> none  [on_device(): lax.psum((grad_gain_one, grad_gain_two, grad_bias), ('wide', 'narrow'))]
  transfers between devices with their start and end apart: 19 -> 110, of which waited for: 9 -> 46; matrix products, arithmetic and copies ran while one was open for 31% -> 15% of each run, Pallas kernels for 0% -> 9%
where the time goes in v1:
time: 752 us; the launch traced here: 740 us
  waiting for transfers between devices  339 us (45%)
  starting transfers between devices  140 us (19%)
  matrix products  73 us (10%)
  local copies, waits for them, and re-layouts  72.9 us (10%)
  Pallas kernels  66.7 us (9%)
  other arithmetic  45.2 us (6%)
    ppermute x61, waiting for transfers between devices, along_wide(): return lax.ppermute(block, 'wide', [(i, i ^ flip) for i in range(wide)])  140 us
    dot_general x12, matrix products, dot_f32(): lax.dot_general(left, right, (dims, ((), ())), preferred_element_type=F32)  73 us
    unnamed x205, local copies, waits for them, and re-layouts  61.4 us
    ppermute x61, starting transfers between devices, along_wide(): return lax.ppermute(block, 'wide', [(i, i ^ flip) for i in range(wide)])  58.7 us
    ppermute x4, waiting for transfers between devices, reduce_narrow(): lax.ppermute(share(flipped(me, 1)), 'narrow', [(0, 1), (1, 0), (2, 3), (3...  43.7 us
    pallas_call x1, Pallas kernels, attention_backward(): pl.pallas_call(functools.partial(backward_kernel, heads, head_size, block...  37.5 us
    ppermute x4, waiting for transfers between devices, gather_narrow(): end = lax.ppermute(two, 'narrow', [(2, 3), (1, 0)])  33.7 us
    ppermute x12, waiting for transfers between devices, along_narrow(): return lax.ppermute(block, 'narrow', pairs)  30.8 us
  transfers between devices with their start and end apart: 110, of which 46 were waited for; matrix products, arithmetic and copies ran while one was open for 15% of the time, Pallas kernels for 9%

profile of v1, /device:TPU:0, one launch (start us, length us, event | category | flops | bytes accessed | tf_op | source)
XLA Modules:
  0.0 739.7 jit_solution(9303968577371688485)
XLA Ops:
  29.9 23.6 %collective-permute-done.10.refs_4_ = bf16[4,48,1664]{2,1,0:T(8,128)(2,1)S(1)} collective-permute-done((bf16[4,48,1664]{2,1,0:T(8,128)(2,1)S(1)}, bf16[4,48,1664]{2,1,0:T(8,128)(2,1)S(1)}, u32[]{:S(2)}, u32[]{:S(2)}) %collective-permute-start.10) | collective-permute-done | bytes 639008 | tf_op jit(solution)/shard_map/ppermute | solution.py:29
  83.2 14.5 %collective-permute-done.3.refs_4_ = bf16[256,1536]{1,0:T(8,128)(2,1)} collective-permute-done((bf16[256,1536]{1,0:T(8,128)(2,1)S(1)}, bf16[256,1536]{1,0:T(8,128)(2,1)}, u32[]{:S(2)}, u32[]{:S(2)}) %collective-permute-start.3) | collective-permute-done | bytes 786464 | tf_op jit(solution)/shard_map/ppermute | solution.py:40
  107.3 10.4 %fusion.42.q_ref.k_ref.v_ref.gate_ref.small_ref = f32[1024,1664]{1,0:T(8,128)} fusion(bf16[1024,1536]{1,0:T(8,128)(2,1)S(1)} %bitcast.211, bf16[1536,1664]{1,0:T(8,128)(2,1)} %bitcast.194), kind=kOutput, calls=%fused_computation.199 | convolution fusion | flops 5234491392 | bytes 15073280 | tf_op jit(solution)/shard_map/dot_general | solution.py:20
  117.9 15.1 %shard_map.173 = (bf16[1024,384]{1,0:T(8,128)(2,1)S(1)}, bf16[1024,384]{1,0:T(8,128)(2,1)S(1)}, f32[1024,384]{1,0:T(8,128)S(1)}) custom-call(f32[1024,1664]{1,0:T(8,128)} %fusion.42.q_ref.k_ref.v_ref.gate_ref.small_ref, f32[1024,1664]{1,0:T(8,128)} %fusion.42.q_ref.k_ref.v_ref.gate_ref.small_ref, f32[1024,1664]{1,0:T(8,128)} %fusion.42.q_ref.k_ref.v_ref.gate_ref.small_ref, ...), custom_call_target="tpu_custom_call" | custom-call | flops 2516582400 | bytes 10223616 | tf_op jit(solution)/shard_map/pallas_call | solution.py:410
  168.7 13.3 %collective-permute-done.24.refs_4_ = bf16[4,48,1536]{2,1,0:T(8,128)(2,1)S(1)} collective-permute-done((bf16[4,48,1536]{2,1,0:T(8,128)(2,1)S(1)}, bf16[4,48,1536]{2,1,0:T(8,128)(2,1)S(1)}, u32[]{:S(2)}, u32[]{:S(2)}) %collective-permute-start.24) | collective-permute-done | bytes 589856 | tf_op jit(solution)/shard_map/ppermute | solution.py:29
  203.5 16.2 %collective-permute-done.49 = bf16[256,1536]{1,0:T(8,128)(2,1)} collective-permute-done((bf16[256,1536]{1,0:T(8,128)(2,1)}, bf16[256,1536]{1,0:T(8,128)(2,1)}, u32[]{:S(2)}, u32[]{:S(2)}) %collective-permute-start.49) | collective-permute-done | bytes 786464 | tf_op jit(solution)/shard_map/ppermute | solution.py:29
  239.8 10.8 %collective-permute-done.45.refs_4_ = bf16[8,48,1024]{2,1,0:T(8,128)(2,1)S(1)} collective-permute-done((bf16[8,48,1024]{2,1,0:T(8,128)(2,1)S(1)}, bf16[8,48,1024]{2,1,0:T(8,128)(2,1)S(1)}, u32[]{:S(2)}, u32[]{:S(2)}) %collective-permute-start.45) | collective-permute-done | bytes 786464 | tf_op jit(solution)/shard_map/ppermute | solution.py:40
  253.7 9.5 %collective-permute-start.55 = (bf16[128,1536]{1,0:T(8,128)(2,1)}, bf16[128,1536]{1,0:T(8,128)(2,1)S(1)}, u32[]{:S(2)}, u32[]{:S(2)}) collective-permute-start(bf16[128,1536]{1,0:T(8,128)(2,1)} %shard_map.184.refs_0_), channel_id=1, source_target_pairs={{0,2},{2,0},{1,3},{3,1},{4,6},{6,4},{5,7},{7,5},{8,10},{10,8},{9,1... | collective-permute-start | bytes 1179656 | tf_op jit(solution)/shard_map/ppermute | solution.py:37
  269.8 10.7 %collective-permute-done.55.refs_2_ = bf16[128,1536]{1,0:T(8,128)(2,1)S(1)} collective-permute-done((bf16[128,1536]{1,0:T(8,128)(2,1)}, bf16[128,1536]{1,0:T(8,128)(2,1)S(1)}, u32[]{:S(2)}, u32[]{:S(2)}) %collective-permute-start.55) | collective-permute-done | bytes 393248 | tf_op jit(solution)/shard_map/ppermute | solution.py:37
  297.5 8.4 %collective-permute-done.57.refs_4_ = bf16[128,1536]{1,0:T(8,128)(2,1)S(1)} collective-permute-done((bf16[128,1536]{1,0:T(8,128)(2,1)S(1)}, bf16[128,1536]{1,0:T(8,128)(2,1)S(1)}, u32[]{:S(2)}, u32[]{:S(2)}) %collective-permute-start.57) | collective-permute-done | bytes 393248 | tf_op jit(solution)/shard_map/ppermute | solution.py:40
  312.6 8.9 %fusion.43 = f32[2048,1024]{1,0:T(8,128)S(1)} fusion(bf16[2048,1536]{1,0:T(8,128)(2,1)} %constant_dynamic-update-slice_fusion, bf16[1536,1024]{1,0:T(8,128)(2,1)S(1)} %bitcast.200), kind=kOutput, calls=%fused_computation.200 | convolution fusion | flops 6442450944 | bytes 17825792 | tf_op jit(solution)/shard_map/dot_general | solution.py:20
  359.4 9.5 %collective-permute-done.59 = bf16[256,1536]{1,0:T(8,128)(2,1)S(1)} collective-permute-done((bf16[256,1536]{1,0:T(8,128)(2,1)S(1)}, bf16[256,1536]{1,0:T(8,128)(2,1)S(1)}, u32[]{:S(2)}, u32[]{:S(2)}) %collective-permute-start.59) | collective-permute-done | bytes 786464 | tf_op jit(solution)/shard_map/ppermute | solution.py:29
  368.9 17.5 %collective-permute-done.60 = bf16[256,1536]{1,0:T(8,128)(2,1)S(1)} collective-permute-done((bf16[256,1536]{1,0:T(8,128)(2,1)S(1)}, bf16[256,1536]{1,0:T(8,128)(2,1)S(1)}, u32[]{:S(2)}, u32[]{:S(2)}) %collective-permute-start.60) | collective-permute-done | bytes 786464 | tf_op jit(solution)/shard_map/ppermute | solution.py:29
  400.9 8.8 %convolution_convert_fusion.4 = bf16[1536,1024]{1,0:T(8,128)(2,1)S(1)} fusion(bf16[2048,1536]{1,0:T(8,128)(2,1)} %constant_dynamic-update-slice_fusion, bf16[2048,512]{1,0:T(8,128)(2,1)S(1)} %copy-done.83, bf16[2048,512]{1,0:T(8,128)(2,1)S(1)} %copy-done.81), kind=kOutput, calls=%fused_computation.15 | convolution fusion | flops 6452412416 | bytes 13631488 | tf_op jit(solution)/shard_map/dot_general | solution.py:20
  420.5 19.1 %collective-permute-done.106 = bf16[512,384]{1,0:T(8,128)(2,1)} collective-permute-done((bf16[512,384]{1,0:T(8,128)(2,1)}, bf16[512,384]{1,0:T(8,128)(2,1)}, u32[]{:S(2)}, u32[]{:S(2)}) %collective-permute-start.106) | collective-permute-done | bytes 393248 | tf_op jit(solution)/shard_map/ppermute | solution.py:472
  445.2 11.1 %collective-permute-done.104 = bf16[512,384]{1,0:T(8,128)(2,1)S(1)} collective-permute-done((bf16[512,384]{1,0:T(8,128)(2,1)}, bf16[512,384]{1,0:T(8,128)(2,1)S(1)}, u32[]{:S(2)}, u32[]{:S(2)}) %collective-permute-start.104) | collective-permute-done | bytes 393248 | tf_op jit(solution)/shard_map/ppermute | solution.py:474
  469.1 20.3 %collective-permute-done.93 = bf16[1536,256]{1,0:T(8,128)(2,1)S(1)} collective-permute-done((bf16[1536,256]{1,0:T(8,128)(2,1)}, bf16[1536,256]{1,0:T(8,128)(2,1)S(1)}, u32[]{:S(2)}, u32[]{:S(2)}) %collective-permute-start.93) | collective-permute-done | bytes 786464 | tf_op jit(solution)/shard_map/ppermute | solution.py:474
  498.8 8.0 %collective-permute-done.65 = bf16[256,1536]{1,0:T(8,128)(2,1)S(1)} collective-permute-done((bf16[256,1536]{1,0:T(8,128)(2,1)S(1)}, bf16[256,1536]{1,0:T(8,128)(2,1)S(1)}, u32[]{:S(2)}, u32[]{:S(2)}) %collective-permute-start.65) | collective-permute-done | bytes 786464 | tf_op jit(solution)/shard_map/ppermute | solution.py:29
  529.1 37.5 %shard_map.188 = (bf16[1024,1664]{1,0:T(8,128)(2,1)}, f32[8,128]{1,0:T(8,128)}) custom-call(f32[1024,1664]{1,0:T(8,128)} %fusion.42.q_ref.k_ref.v_ref.gate_ref.small_ref, f32[1024,1664]{1,0:T(8,128)} %fusion.42.q_ref.k_ref.v_ref.gate_ref.small_ref, f32[1024,1664]{1,0:T(8,128)} %fusion.42.q_ref.k_ref.v_ref.gate_ref.small_ref, ...), custom_call_target="tpu_custom_call" | custom-call | flops 6291456000 | bytes 13631488 | tf_op jit(solution)/shard_map/pallas_call | solution.py:429
  589.3 9.9 %collective-permute-done.71 = bf16[256,1536]{1,0:T(8,128)(2,1)S(1)} collective-permute-done((bf16[256,1536]{1,0:T(8,128)(2,1)S(1)}, bf16[256,1536]{1,0:T(8,128)(2,1)S(1)}, u32[]{:S(2)}, u32[]{:S(2)}) %collective-permute-start.71) | collective-permute-done | bytes 786464 | tf_op jit(solution)/shard_map/ppermute | solution.py:472
  603.8 12.3 %collective-permute-done.69 = bf16[256,1536]{1,0:T(8,128)(2,1)S(1)} collective-permute-done((bf16[256,1536]{1,0:T(8,128)(2,1)S(1)}, bf16[256,1536]{1,0:T(8,128)(2,1)S(1)}, u32[]{:S(2)}, u32[]{:S(2)}) %collective-permute-start.69) | collective-permute-done | bytes 786464 | tf_op jit(solution)/shard_map/ppermute | solution.py:474
  617.1 17.5 %collective-permute-done.72 = bf16[256,1536]{1,0:T(8,128)(2,1)S(1)} collective-permute-done((bf16[256,1536]{1,0:T(8,128)(2,1)S(1)}, bf16[256,1536]{1,0:T(8,128)(2,1)S(1)}, u32[]{:S(2)}, u32[]{:S(2)}) %collective-permute-start.72) | collective-permute-done | bytes 786464 | tf_op jit(solution)/shard_map/ppermute | solution.py:476
  683.1 11.1 %collective-permute-done.87 = bf16[192,1536]{1,0:T(8,128)(2,1)S(1)} collective-permute-done((bf16[192,1536]{1,0:T(8,128)(2,1)S(1)}, bf16[192,1536]{1,0:T(8,128)(2,1)S(1)}, u32[]{:S(2)}, u32[]{:S(2)}) %collective-permute-start.87) | collective-permute-done | bytes 589856 | tf_op jit(solution)/shard_map/ppermute | solution.py:29
  709.5 10.3 %collective-permute-done.80 = bf16[192,1664]{1,0:T(8,128)(2,1)S(1)} collective-permute-done((bf16[192,1664]{1,0:T(8,128)(2,1)S(1)}, bf16[192,1664]{1,0:T(8,128)(2,1)S(1)}, u32[]{:S(2)}, u32[]{:S(2)}) %collective-permute-start.80) | collective-permute-done | bytes 639008 | tf_op jit(solution)/shard_map/ppermute | solution.py:29
  (518 shorter events, 403.0 us)
Async XLA Ops:
  25.1 37.1 %collective-permute-start.1 = (bf16[256,1536]{1,0:T(8,128)(2,1)S(1)}, bf16[256,1536]{1,0:T(8,128)(2,1)S(1)}, u32[]{:S(2)}, u32[]{:S(2)}) collective-permute-start(bf16[256,1536]{1,0:T(8,128)(2,1)S(1)} %copy-done.6), channel_id=1, source_target_pairs={{0,2},{2,0},{1,3},{3,1},{4,6},{6,4},{5,7},{7,5},{8,10},{10,8},{9,1... | collective-permute-start | bytes 2359304 | tf_op jit(solution)/shard_map/ppermute | solution.py:37
  29.9 35.9 %collective-permute-start.7 = (bf16[4,48,1664]{2,1,0:T(8,128)(2,1)S(1)}, bf16[4,48,1664]{2,1,0:T(8,128)(2,1)S(1)}, u32[]{:S(2)}, u32[]{:S(2)}) collective-permute-start(bf16[4,48,1664]{2,1,0:T(8,128)(2,1)S(1)} %shard_map.171.refs_0_), channel_id=1, source_target_pairs={{0,4},{4,0},{8,12},{12,8},{16,20},{20,16},{24,28},{28,24},{1,5},{5... | collective-permute-start | bytes 1916936 | tf_op jit(solution)/shard_map/ppermute | solution.py:29
  73.6 60.5 %collective-permute-start.35 = (bf16[48,1024]{1,0:T(8,128)(2,1)}, bf16[48,1024]{1,0:T(8,128)(2,1)S(1)}, u32[]{:S(2)}, u32[]{:S(2)}) collective-permute-start(bf16[48,1024]{1,0:T(8,128)(2,1)} %get-tuple-element.32), channel_id=1, source_target_pairs={{0,4},{4,0},{8,12},{12,8},{16,20},{20,16},{24,28},{28,24},{1,5},{5... | collective-permute-start | bytes 294920 | tf_op jit(solution)/shard_map/ppermute | solution.py:29
  73.7 61.1 %collective-permute-start.36 = (bf16[48,1024]{1,0:T(8,128)(2,1)}, bf16[48,1024]{1,0:T(8,128)(2,1)S(1)}, u32[]{:S(2)}, u32[]{:S(2)}) collective-permute-start(bf16[48,1024]{1,0:T(8,128)(2,1)} %get-tuple-element.33), channel_id=1, source_target_pairs={{0,8},{4,12},{8,0},{12,4},{16,24},{20,28},{24,16},{28,20},{1,9},{5... | collective-permute-start | bytes 294920 | tf_op jit(solution)/shard_map/ppermute | solution.py:29
  82.9 51.9 %collective-permute-start.37 = (bf16[48,1024]{1,0:T(8,128)(2,1)}, bf16[48,1024]{1,0:T(8,128)(2,1)}, u32[]{:S(2)}, u32[]{:S(2)}) collective-permute-start(bf16[48,1024]{1,0:T(8,128)(2,1)} %get-tuple-element.34), channel_id=1, source_target_pairs={{0,12},{4,8},{8,4},{12,0},{16,28},{20,24},{24,20},{28,16},{1,13},{... | collective-permute-start | bytes 294920 | tf_op jit(solution)/shard_map/ppermute | solution.py:29
  103.2 40.0 %collective-permute-start.17 = (bf16[48,1536]{1,0:T(8,128)(2,1)}, bf16[48,1536]{1,0:T(8,128)(2,1)S(1)}, u32[]{:S(2)}, u32[]{:S(2)}) collective-permute-start(bf16[48,1536]{1,0:T(8,128)(2,1)} %shard_map.175.refs_0_), channel_id=1, source_target_pairs={{0,1},{1,0},{2,3},{3,2},{4,5},{5,4},{6,7},{7,6},{8,9},{9,8},{10,11... | collective-permute-start | bytes 442376 | tf_op jit(solution)/shard_map/ppermute | solution.py:38
  142.2 39.8 %collective-permute-start.46 = (bf16[256,1536]{1,0:T(8,128)(2,1)}, bf16[256,1536]{1,0:T(8,128)(2,1)S(1)}, u32[]{:S(2)}, u32[]{:S(2)}) collective-permute-start(bf16[256,1536]{1,0:T(8,128)(2,1)} %shard_map.182), channel_id=1, source_target_pairs={{0,4},{4,0},{8,12},{12,8},{16,20},{20,16},{24,28},{28,24},{1,5},{5... | collective-permute-start | bytes 2359304 | tf_op jit(solution)/shard_map/ppermute | solution.py:29
  183.6 36.0 %collective-permute-start.49 = (bf16[256,1536]{1,0:T(8,128)(2,1)}, bf16[256,1536]{1,0:T(8,128)(2,1)}, u32[]{:S(2)}, u32[]{:S(2)}) collective-permute-start(bf16[256,1536]{1,0:T(8,128)(2,1)} %shard_map.182), channel_id=1, source_target_pairs={{0,16},{4,20},{8,24},{12,28},{16,0},{20,4},{24,8},{28,12},{1,17},{... | collective-permute-start | bytes 2359304 | tf_op jit(solution)/shard_map/ppermute | solution.py:29
  191.7 37.6 %collective-permute-start.43 = (bf16[8,48,1024]{2,1,0:T(8,128)(2,1)}, bf16[8,48,1024]{2,1,0:T(8,128)(2,1)S(1)}, u32[]{:S(2)}, u32[]{:S(2)}) collective-permute-start(bf16[8,48,1024]{2,1,0:T(8,128)(2,1)} %shard_map.180.refs_0_), channel_id=1, source_target_pairs={{0,2},{2,0},{1,3},{3,1},{4,6},{6,4},{5,7},{7,5},{8,10},{10,8},{9,1... | collective-permute-start | bytes 2359304 | tf_op jit(solution)/shard_map/ppermute | solution.py:37
  194.0 38.0 %collective-permute-start.42 = (bf16[8,48,1024]{2,1,0:T(8,128)(2,1)}, bf16[8,48,1024]{2,1,0:T(8,128)(2,1)S(1)}, u32[]{:S(2)}, u32[]{:S(2)}) collective-permute-start(bf16[8,48,1024]{2,1,0:T(8,128)(2,1)} %shard_map.180.refs_0_), channel_id=1, source_target_pairs={{0,1},{1,0},{2,3},{3,2},{4,5},{5,4},{6,7},{7,6},{8,9},{9,8},{10,11... | collective-permute-start | bytes 2359304 | tf_op jit(solution)/shard_map/ppermute | solution.py:38
  235.9 45.0 %collective-permute-start.29 = (bf16[256,1536]{1,0:T(8,128)(2,1)}, bf16[256,1536]{1,0:T(8,128)(2,1)}, u32[]{:S(2)}, u32[]{:S(2)}) collective-permute-start(bf16[256,1536]{1,0:T(8,128)(2,1)} %get-tuple-element.50), channel_id=1, source_target_pairs={{0,8},{4,12},{8,0},{12,4},{16,24},{20,28},{24,16},{28,20},{1,9},{5... | collective-permute-start | bytes 2359304 | tf_op jit(solution)/shard_map/ppermute | solution.py:29
  250.6 42.0 %collective-permute-start.28 = (bf16[256,1536]{1,0:T(8,128)(2,1)}, bf16[256,1536]{1,0:T(8,128)(2,1)S(1)}, u32[]{:S(2)}, u32[]{:S(2)}) collective-permute-start(bf16[256,1536]{1,0:T(8,128)(2,1)} %get-tuple-element.50), channel_id=1, source_target_pairs={{0,4},{4,0},{8,12},{12,8},{16,20},{20,16},{24,28},{28,24},{1,5},{5... | collective-permute-start | bytes 2359304 | tf_op jit(solution)/shard_map/ppermute | solution.py:29
  252.6 41.3 %collective-permute-start.31 = (bf16[256,1536]{1,0:T(8,128)(2,1)}, bf16[256,1536]{1,0:T(8,128)(2,1)}, u32[]{:S(2)}, u32[]{:S(2)}) collective-permute-start(bf16[256,1536]{1,0:T(8,128)(2,1)} %get-tuple-element.50), channel_id=1, source_target_pairs={{0,16},{4,20},{8,24},{12,28},{16,0},{20,4},{24,8},{28,12},{1,17},{... | collective-permute-start | bytes 2359304 | tf_op jit(solution)/shard_map/ppermute | solution.py:29
  350.3 36.2 %collective-permute-start.60 = (bf16[256,1536]{1,0:T(8,128)(2,1)S(1)}, bf16[256,1536]{1,0:T(8,128)(2,1)S(1)}, u32[]{:S(2)}, u32[]{:S(2)}) collective-permute-start(bf16[256,1536]{1,0:T(8,128)(2,1)S(1)} %get-tuple-element.58), channel_id=1, source_target_pairs={{0,16},{4,20},{8,24},{12,28},{16,0},{20,4},{24,8},{28,12},{1,17},{... | collective-permute-start | bytes 2359304 | tf_op jit(solution)/shard_map/ppermute | solution.py:29
  399.5 65.5 %collective-permute-start.62 = (bf16[4,256,1536]{2,1,0:T(8,128)(2,1)}, bf16[4,256,1536]{2,1,0:T(8,128)(2,1)}, u32[]{:S(2)}, u32[]{:S(2)}) collective-permute-start(bf16[4,256,1536]{2,1,0:T(8,128)(2,1)} %pad_maximum_fusion.2), channel_id=1, source_target_pairs={{0,4},{4,0},{8,12},{12,8},{16,20},{20,16},{24,28},{28,24},{1,5},{5... | collective-permute-start | bytes 9437192 | tf_op jit(solution)/shard_map/ppermute | solution.py:29
  418.8 37.5 %collective-permute-start.105 = (bf16[512,384]{1,0:T(8,128)(2,1)}, bf16[512,384]{1,0:T(8,128)(2,1)S(1)}, u32[]{:S(2)}, u32[]{:S(2)}) collective-permute-start(bf16[512,384]{1,0:T(8,128)(2,1)} %get-tuple-element.87), channel_id=1, source_target_pairs={{1,2},{2,1},{5,6},{6,5},{9,10},{10,9},{13,14},{14,13},{17,18},{18,... | collective-permute-start | bytes 1179656 | tf_op jit(solution)/shard_map/ppermute | solution.py:473
  419.7 72.1 %collective-permute-start.94 = (bf16[1536,256]{1,0:T(8,128)(2,1)}, bf16[1536,256]{1,0:T(8,128)(2,1)S(1)}, u32[]{:S(2)}, u32[]{:S(2)}) collective-permute-start(bf16[1536,256]{1,0:T(8,128)(2,1)} %get-tuple-element.83), channel_id=1, source_target_pairs={{1,2},{2,1},{5,6},{6,5},{9,10},{10,9},{13,14},{14,13},{17,18},{18,... | collective-permute-start | bytes 2359304 | tf_op jit(solution)/shard_map/ppermute | solution.py:473
  456.4 39.9 %collective-permute-start.96 = (bf16[1536,256]{1,0:T(8,128)(2,1)S(1)}, bf16[1536,256]{1,0:T(8,128)(2,1)S(1)}, u32[]{:S(2)}, u32[]{:S(2)}) collective-permute-start(bf16[1536,256]{1,0:T(8,128)(2,1)S(1)} %add_convert_fusion.1), channel_id=1, source_target_pairs={{0,2},{2,0},{1,3},{3,1},{4,6},{6,4},{5,7},{7,5},{8,10},{10,8},{9,1... | collective-permute-start | bytes 2359304 | tf_op jit(solution)/shard_map/ppermute | solution.py:476
  491.8 145.8 %collective-permute-start.108 = (bf16[256,384]{1,0:T(8,128)(2,1)}, bf16[256,384]{1,0:T(8,128)(2,1)}, u32[]{:S(2)}, u32[]{:S(2)}) collective-permute-start(bf16[256,384]{1,0:T(8,128)(2,1)} %get-tuple-element.118), channel_id=1, source_target_pairs={{0,0},{4,16},{8,4},{12,20},{16,8},{20,24},{24,12},{28,28},{1,1},{5... | collective-permute-start | bytes 589832 | tf_op jit(solution)/shard_map/ppermute | solution.py:705
  519.5 142.4 %collective-permute-start.85 = (bf16[4,192,1536]{2,1,0:T(8,128)(2,1)}, bf16[4,192,1536]{2,1,0:T(8,128)(2,1)}, u32[]{:S(2)}, u32[]{:S(2)}) collective-permute-start(bf16[4,192,1536]{2,1,0:T(8,128)(2,1)} %pad_maximum_fusion.6), channel_id=1, source_target_pairs={{0,4},{4,0},{8,12},{12,8},{16,20},{20,16},{24,28},{28,24},{1,5},{5... | collective-permute-start | bytes 7077896 | tf_op jit(solution)/shard_map/ppermute | solution.py:29
  581.3 35.9 %collective-permute-start.70 = (bf16[256,1536]{1,0:T(8,128)(2,1)S(1)}, bf16[256,1536]{1,0:T(8,128)(2,1)S(1)}, u32[]{:S(2)}, u32[]{:S(2)}) collective-permute-start(bf16[256,1536]{1,0:T(8,128)(2,1)S(1)} %get-tuple-element.85), channel_id=1, source_target_pairs={{1,2},{2,1},{5,6},{6,5},{9,10},{10,9},{13,14},{14,13},{17,18},{18,... | collective-permute-start | bytes 2359304 | tf_op jit(solution)/shard_map/ppermute | solution.py:473
  617.1 52.8 %collective-permute-start.78 = (bf16[4,192,1664]{2,1,0:T(8,128)(2,1)}, bf16[4,192,1664]{2,1,0:T(8,128)(2,1)}, u32[]{:S(2)}, u32[]{:S(2)}) collective-permute-start(bf16[4,192,1664]{2,1,0:T(8,128)(2,1)} %pad_maximum_fusion.5), channel_id=1, source_target_pairs={{0,4},{4,0},{8,12},{12,8},{16,20},{20,16},{24,28},{28,24},{1,5},{5... | collective-permute-start | bytes 7667720 | tf_op jit(solution)/shard_map/ppermute | solution.py:29
  673.1 46.7 %collective-permute-start.80 = (bf16[192,1664]{1,0:T(8,128)(2,1)S(1)}, bf16[192,1664]{1,0:T(8,128)(2,1)S(1)}, u32[]{:S(2)}, u32[]{:S(2)}) collective-permute-start(bf16[192,1664]{1,0:T(8,128)(2,1)S(1)} %get-tuple-element.62), channel_id=1, source_target_pairs={{0,16},{4,20},{8,24},{12,28},{16,0},{20,4},{24,8},{28,12},{1,17},{... | collective-permute-start | bytes 1916936 | tf_op jit(solution)/shard_map/ppermute | solution.py:29
  680.6 39.2 %collective-permute-start.81 = (bf16[192,1664]{1,0:T(8,128)(2,1)S(1)}, bf16[192,1664]{1,0:T(8,128)(2,1)S(1)}, u32[]{:S(2)}, u32[]{:S(2)}) collective-permute-start(bf16[192,1664]{1,0:T(8,128)(2,1)S(1)} %get-tuple-element.61), channel_id=1, source_target_pairs={{0,24},{4,28},{8,16},{12,20},{16,8},{20,12},{24,0},{28,4},{1,25},{... | collective-permute-start | bytes 1916936 | tf_op jit(solution)/shard_map/ppermute | solution.py:29
  (178 other events, 2660.6 us)

commit v2 on v1

--- a/solution.py
+++ b/solution.py
@@ -20,47 +20,8 @@
     return lax.dot_general(left, right, (dims, ((), ())), preferred_element_type=F32)
 
 
-def along_narrow(block, step, narrow):
-    pairs = [(i, (i + step) % narrow) for i in range(narrow)]
-    return lax.ppermute(block, "narrow", pairs)
-
-
 def along_wide(block, flip, wide):
     return lax.ppermute(block, "wide", [(i, i ^ flip) for i in range(wide)])
-
-
-def gather_narrow(block, narrow, slot, shape):
-    me = lambda: lax.axis_index("narrow")
-    if narrow != 4:
-        pieces = [block] + [along_narrow(block, k, narrow) for k in range(1, narrow)]
-        return assemble(pieces, lambda k, t: slot(lax.rem(me() + narrow - k, narrow), t), shape)
-    two = lax.ppermute(block, "narrow", [(0, 2), (2, 0), (1, 3), (3, 1)])
-    one = lax.ppermute(block, "narrow", [(0, 1), (1, 0), (2, 3), (3, 2)])
-    middle = lax.ppermute(block, "narrow", [(1, 2), (2, 1)])
-    end = lax.ppermute(two, "narrow", [(2, 3), (1, 0)])
-    is_middle = lambda: (me() == 1) | (me() == 2)
-
-    def plan(sources, targets):
-        t = targets[0]
-        far = slot(flipped(me(), 3), t)
-        return [
-            (sources[0], slot(me(), t)),
-            (sources[1], slot(flipped(me(), 1), t)),
-            (sources[2], slot(flipped(me(), 2), t)),
-            (sources[3], far, is_middle()),
-            (sources[4], far, jnp.logical_not(is_middle())),
-        ]
-
-    whole = jax.ShapeDtypeStruct(shape, block.dtype)
-    return local_copies(plan, 5, [block, one, two, middle, end], [whole], True)[0]
-
-
-def from_wide(block, wide):
-    even = [block] + [along_wide(block, k, wide) for k in range(2, wide, 2)]
-    pieces = []
-    for piece in even:
-        pieces += [piece, along_wide(piece, 1, wide)]
-    return pieces
 
 
 def copy_kernel(plan, count, *refs):
@@ -82,7 +43,7 @@
 def local_copies(plan, copies, sources, shapes, gather):
     moved = sum(s.size * s.dtype.itemsize for s in shapes)
     inside = pl.BlockSpec(memory_space=pltpu.VMEM)
-    out = pl.pallas_call(
+    return pl.pallas_call(
         functools.partial(copy_kernel, plan, len(sources)),
         out_shape=shapes,
         in_specs=[ANY if gather else inside] * len(sources),
@@ -91,23 +52,6 @@
         scratch_shapes=[pltpu.SemaphoreType.DMA((copies,))],
         cost_estimate=pl.CostEstimate(flops=0, bytes_accessed=2 * moved, transcendentals=0),
     )(*sources)
-    return out
-
-
-def assemble(pieces, place, shape):
-    def plan(sources, targets):
-        return [(src, place(k, targets[0])) for k, src in enumerate(sources)]
-
-    whole = jax.ShapeDtypeStruct(shape, pieces[0].dtype)
-    return local_copies(plan, len(pieces), pieces, [whole], True)[0]
-
-
-def narrow_order(k, narrow):
-    return lax.rem(lax.axis_index("narrow") + narrow - k, narrow)
-
-
-def narrow_target(k, narrow):
-    return lax.rem(lax.axis_index("narrow") + k, narrow)
 
 
 def flipped(me, k):
@@ -120,22 +64,747 @@
     return out
 
 
-def wide_order(k):
-    return flipped(lax.axis_index("wide"), k)
-
-
-def nothing_kernel(*refs):
-    pass
+LINE_TWO = [(0, 2), (2, 0), (1, 3), (3, 1)]
+LINE_ONE = [(0, 1), (1, 0), (2, 3), (3, 2)]
+LINE_MIDDLE = [(1, 2), (2, 1)]
+LINE_OUT = [(2, 3), (1, 0)]
+LINE_IN = [(0, 1), (3, 2)]
+
+
+def on_line(block, pairs):
+    return lax.ppermute(block, "narrow", pairs)
 
 
 def follow(array, *earlier):
+    return lax.optimization_barrier((array, *earlier))[0]
+
+
+MESH = pl.DeviceIdType.MESH
+VMEM = pl.BlockSpec(memory_space=pltpu.VMEM)
+DMA = pltpu.SemaphoreType.DMA
+
+
+def greet(devices):
+    barrier = pltpu.get_barrier_semaphore()
+    for device in devices:
+        pl.semaphore_signal(barrier, inc=1, device_id=device, device_id_type=MESH)
+    pl.semaphore_wait(barrier, len(devices))
+
+
+class Sender:
+    def __init__(self, send, recv):
+        self.send, self.recv, self.used = send, recv, 0
+
+    def plan(self, src, dst, device):
+        n = self.used
+        self.used += 1
+        return pltpu.make_async_remote_copy(
+            src_ref=src, dst_ref=dst, send_sem=self.send.at[n], recv_sem=self.recv.at[n],
+            device_id=device, device_id_type=MESH,
+        )
+
+
+def narrow_device(n):
+    return {"narrow": n}
+
+
+def wide_device(n):
+    return {"wide": n}
+
+
+def wide_steps(wide):
+    return [1] + list(range(2, wide, 2))
+
+
+def by_device(ref, w):
+    return (lambda k: ref.at[flipped(w, k)]), (lambda k, to: ref.at[flipped(w, k)])
+
+
+class WideGather:
+    def __init__(self, sender, w, wide, part, target):
+        self.far = list(range(2, wide, 2))
+        self.first = {
+            k: sender.plan(part(0), target(0, k), wide_device(flipped(w, k)))
+            for k in wide_steps(wide)
+        }
+        sibling = wide_device(flipped(w, 1))
+        self.second = {k: sender.plan(part(k), target(k, 1), sibling) for k in self.far}
+
+    def start(self):
+        for k in self.far + [1]:
+            self.first[k].start()
+
+    def pass_on(self):
+        for k in self.far:
+            self.first[k].wait_recv()
+            self.second[k].start()
+
+    def finish(self):
+        self.first[1].wait_recv()
+        for k in self.far:
+            self.second[k].wait_recv()
+        for copy in list(self.first.values()) + list(self.second.values()):
+            copy.wait_send()
+
+
+def gather_kernel(
+    wide, x_ref, in_ref, out_ref, up_ref, slot_ref, in_full, out_full, up_block, send, recv, local
+):
+    w, z = lax.axis_index("wide"), lax.axis_index("narrow")
+    line = [flipped(z, k) for k in range(4)]
+    sender = Sender(send, recv)
+    own = [
+        pltpu.make_async_copy(in_ref.at[z], in_full.at[w, z], local.at[0]),
+        pltpu.make_async_copy(out_ref, out_full.at[w, z], local.at[1]),
+        pltpu.make_async_copy(x_ref, slot_ref.at[z], local.at[2]),
+        pltpu.make_async_copy(up_ref.at[w], up_block.at[w], local.at[3]),
+    ]
+    for copy in own:
+        copy.start()
+    greet(
+        [narrow_device(line[k]) for k in (1, 2, 3)]
+        + [wide_device(flipped(w, k)) for k in range(1, wide)]
+    )
+    ups = [
+        sender.plan(up_ref.at[flipped(w, k)], up_block.at[w], wide_device(flipped(w, k)))
+        for k in range(1, wide)
+    ]
+    is_middle = (z == 1) | (z == 2)
+    is_end = (z == 0) | (z == 3)
+    ins = [
+        sender.plan(in_ref.at[line[k]], in_full.at[w, z], narrow_device(line[k])) for k in (2, 3, 1)
+    ]
+    outs = [sender.plan(out_ref, out_full.at[w, z], narrow_device(line[k])) for k in (2, 3, 1)]
+    two = sender.plan(x_ref, slot_ref.at[z], narrow_device(line[2]))
+    one = sender.plan(x_ref, slot_ref.at[z], narrow_device(line[1]))
+    middle = sender.plan(x_ref, slot_ref.at[z], narrow_device(line[3]))
+    relay = sender.plan(slot_ref.at[line[2]], slot_ref.at[line[2]], narrow_device(line[1]))
+    in_wide = WideGather(sender, w, wide, *by_device(in_full, w))
+    out_wide = WideGather(sender, w, wide, *by_device(out_full, w))
+    for copy in ins + outs + ups:
+        copy.start()
+    own[0].wait()
+    for copy in ins:
+        copy.wait_recv()
+    in_wide.start()
+    two.start()
+    one.start()
+    own[1].wait()
+    for copy in outs:
+        copy.wait_recv()
+    out_wide.start()
+    in_wide.pass_on()
+    two.wait_recv()
+
+    @pl.when(is_middle)
+    def _():
+        relay.start()
+        middle.start()
+
+    out_wide.pass_on()
+    one.wait_recv()
+    own[2].wait()
+    own[3].wait()
+    for copy in ups:
+        copy.wait()
+
+    @pl.when(is_middle)
+    def _():
+        middle.wait_recv()
+        middle.wait_send()
+        relay.wait_send()
+
+    @pl.when(is_end)
+    def _():
+        relay.wait_recv()
+
+    for copy in ins + outs + [two, one]:
+        copy.wait_send()
+    in_wide.finish()
+    out_wide.finish()
+
+
+def gather_all(tokens, in_parts, out_weight, up_parts):
+    narrow, wide = in_parts.shape[0], up_parts.shape[0]
+    steps = 10 + 4 * wide
+    shapes = [
+        (narrow,) + tokens.shape, (wide,) + in_parts.shape, (wide, narrow) + out_weight.shape,
+        up_parts.shape,
+    ]
     return pl.pallas_call(
-        nothing_kernel,
-        out_shape=jax.ShapeDtypeStruct(array.shape, array.dtype),
-        in_specs=[ANY] * (1 + len(earlier)),
-        out_specs=ANY,
-        input_output_aliases={0: 0},
-    )(array, *earlier)
+        functools.partial(gather_kernel, wide),
+        out_shape=[jax.ShapeDtypeStruct(shape, BF16) for shape in shapes],
+        in_specs=[ANY] * 4,
+        out_specs=[VMEM] * 4,
+        scratch_shapes=[DMA((steps,)), DMA((steps,)), DMA((4,))],
+        compiler_params=pltpu.CompilerParams(
+            collective_id=0, has_side_effects=True, vmem_limit_bytes=32 * 2**20
+        ),
+    )(tokens, in_parts, out_weight, up_parts)
+
+
+def exchange_kernel(source, target, src_ref, dst_ref, send, recv, local):
+    z = lax.axis_index("narrow")
+    line = [flipped(z, k) for k in range(4)]
+    sender = Sender(send, recv)
+    own = pltpu.make_async_copy(source(src_ref, z), target(dst_ref, z), local.at[0])
+    own.start()
+    greet([narrow_device(line[k]) for k in (1, 2, 3)])
+    copies = [
+        sender.plan(source(src_ref, line[k]), target(dst_ref, z), narrow_device(line[k]))
+        for k in (2, 3, 1)
+    ]
+    for copy in copies:
+        copy.start()
+    own.wait()
+    for copy in copies:
+        copy.wait()
+
+
+def exchange(array, source, target, shape, collective_id):
+    return pl.pallas_call(
+        functools.partial(exchange_kernel, source, target),
+        out_shape=jax.ShapeDtypeStruct(shape, array.dtype),
+        in_specs=[ANY],
+        out_specs=VMEM,
+        scratch_shapes=[DMA((3,)), DMA((3,)), DMA((1,))],
+        compiler_params=pltpu.CompilerParams(
+            collective_id=collective_id, has_side_effects=True, vmem_limit_bytes=16 * 2**20
+        ),
+    )(array)
+
+
+def place_of(k, wide):
+    return k // 2 + (k % 2) * (wide // 2)
+
+
+def rows_kernel(wide, *refs):
+    half = wide // 2
+    grads = refs[:half]
+    (
+        src_ref, up_ref, up_two, up_one, down_ref, dst_ref, grad_ref, up_full, down_full, send,
+        recv, local,
+    ) = refs[half:]
+    w, z = lax.axis_index("wide"), lax.axis_index("narrow")
+    line = [flipped(z, k) for k in range(4)]
+    is_middle = (z == 1) | (z == 2)
+    is_end = (z == 0) | (z == 3)
+    sender = Sender(send, recv)
+    up_at = lambda n: up_full.at[:, n]
+    down_at = lambda n: down_full.at[n]
+    moves = [
+        (src_ref, dst_ref.at[0]), (down_ref, down_at(z)),
+        (up_ref, up_at(z)), (up_two, up_at(line[2])), (up_one, up_at(line[1])),
+    ] + [(grads[n], grad_ref.at[n]) for n in range(half)]
+    own = [pltpu.make_async_copy(src, dst, local.at[n]) for n, (src, dst) in enumerate(moves)]
+    for copy in own:
+        copy.start()
+    greet(
+        [wide_device(flipped(w, k)) for k in wide_steps(wide)]
+        + [narrow_device(line[k]) for k in (1, 2, 3)]
+    )
+    gather = WideGather(
+        sender, w, wide, lambda k: src_ref if k == 0 else dst_ref.at[place_of(k, wide)],
+        lambda k, to: dst_ref.at[place_of(k ^ to, wide)],
+    )
+    middle = sender.plan(up_ref, up_at(z), narrow_device(line[3]))
+    relay = sender.plan(up_two, up_at(line[2]), narrow_device(line[1]))
+    down_two = sender.plan(down_ref, down_at(z), narrow_device(line[2]))
+    down_one = sender.plan(down_ref, down_at(z), narrow_device(line[1]))
+    down_middle = sender.plan(down_ref, down_at(z), narrow_device(line[3]))
+    down_relay = sender.plan(down_at(line[2]), down_at(line[2]), narrow_device(line[1]))
+    gather.start()
+    down_two.start()
+
+    @pl.when(is_middle)
+    def _():
+        relay.start()
+
+    down_two.wait_recv()
+
+    @pl.when(is_middle)
+    def _():
+        down_relay.start()
+        middle.start()
+        down_middle.start()
+
+    down_one.start()
+    sibling = wide_device(flipped(w, 1))
+    copies = [sender.plan(grads[n], grad_ref.at[half + n], sibling) for n in range(half)]
+    for copy in copies:
+        copy.start()
+    gather.pass_on()
+
+    @pl.when(is_middle)
+    def _():
+        middle.wait()
+        down_middle.wait()
+        relay.wait_send()
+        down_relay.wait_send()
+
+    @pl.when(is_end)
+    def _():
+        relay.wait_recv()
+        down_relay.wait_recv()
+
+    down_two.wait_send()
+    for copy in own + copies + [down_one]:
+        copy.wait()
+    gather.finish()
+
+
+def gather_rows(array, grads, ups, down, collective_id):
+    half = len(grads)
+    wide = 2 * half
+    whole = jax.ShapeDtypeStruct((wide,) + array.shape, array.dtype)
+    up_shape = ups[0].shape
+    full = jax.ShapeDtypeStruct((up_shape[0], 4) + up_shape[1:], BF16)
+    return pl.pallas_call(
+        functools.partial(rows_kernel, wide),
+        out_shape=[whole, whole, full, jax.ShapeDtypeStruct((4,) + down.shape, BF16)],
+        in_specs=[ANY] * (half + 5),
+        out_specs=[VMEM, ANY if wide > 8 else VMEM, VMEM, VMEM],
+        scratch_shapes=[DMA((2 * wide + 6,)), DMA((2 * wide + 6,)), DMA((half + 5,))],
+        compiler_params=pltpu.CompilerParams(
+            collective_id=collective_id, has_side_effects=True, vmem_limit_bytes=48 * 2**20
+        ),
+    )(*grads, array, *ups, down)
+
+
+def hidden_kernel(
+    half, normed_ref, grad_ref, up_ref, down_ref, hidden_ref, mid_ref, even_ref, odd_ref, branch_ref
+):
+    size = down_ref.shape[0]
+    gate_up = dot_f32(normed_ref[...], up_ref[...])
+    grad_hidden = dot_f32(grad_ref[...], down_ref[...], ((1,), (1,)))
+    gate, up = gate_up[:, :size], gate_up[:, size:]
+    opened = jax.nn.sigmoid(gate)
+    acted = gate * opened
+    hidden_ref[...] = (acted * up).astype(BF16)
+    mid_ref[:, :size] = (grad_hidden * up * (opened * (1.0 + gate * (1.0 - opened)))).astype(BF16)
+    mid_ref[:, size:] = (grad_hidden * acted).astype(BF16)
+    grad_normed = dot_f32(mid_ref[...], up_ref[...], ((1,), (1,))).astype(BF16)
+    branch_ref[...] = dot_f32(hidden_ref[...], down_ref[...]).astype(BF16)
+    step = pl.program_id(0)
+
+    @pl.when(step < half)
+    def _():
+        even_ref[...] = grad_normed
+
+    @pl.when(step >= half)
+    def _():
+        odd_ref[...] = grad_normed
+
+
+def feed_forward(normed, grad, up_full, down_full, rows):
+    total, width = normed.shape
+    blocks = total // rows
+    half = blocks // 2
+    size = down_full.shape[0]
+    row_block = lambda columns: pl.BlockSpec((rows, columns), lambda i: (i, 0))
+    fixed = lambda array: pl.BlockSpec(array.shape, lambda i: (0, 0))
+    return pl.pallas_call(
+        functools.partial(hidden_kernel, half),
+        grid=(blocks,),
+        in_specs=[row_block(width), row_block(width), fixed(up_full), fixed(down_full)],
+        out_specs=[
+            row_block(size), row_block(2 * size),
+            pl.BlockSpec((rows, width), lambda i: (jnp.minimum(i, half - 1), 0)),
+            pl.BlockSpec((rows, width), lambda i: (jnp.maximum(i - half, 0), 0)),
+            row_block(width),
+        ],
+        out_shape=[
+            jax.ShapeDtypeStruct((total, size), BF16),
+            jax.ShapeDtypeStruct((total, 2 * size), BF16),
+            jax.ShapeDtypeStruct((total // 2, width), BF16),
+            jax.ShapeDtypeStruct((total // 2, width), BF16),
+            jax.ShapeDtypeStruct((total, width), BF16),
+        ],
+        compiler_params=pltpu.CompilerParams(vmem_limit_bytes=48 * 2**20),
+    )(normed, grad, up_full, down_full)
+
+
+def middle_kernel(
+    wide, even_ref, odd_ref, branch_ref, up_ref, down_ref, norm_sum, branch_sum, up_src, down_src,
+    up_acc, down_acc, core_buf, own_buf, far_buf, branch_buf, up_join, up_one, up_mid, down_join,
+    down_one, down_mid, up_own, down_own, send, recv, local,
+):
+    w, z = lax.axis_index("wide"), lax.axis_index("narrow")
+    line = [flipped(z, k) for k in range(4)]
+    half = wide // 2
+    unit = up_src.shape[1]
+    part = down_src.shape[1]
+    sender = Sender(send, recv)
+    is_middle = (z == 1) | (z == 2)
+    is_end = (z == 0) | (z == 3)
+
+    def up_share(n):
+        return up_ref.at[:, pl.ds(pl.multiple_of(n * unit, unit), unit)]
+
+    def down_share(n):
+        return down_ref.at[:, pl.ds(pl.multiple_of(n * part, part), part)]
+
+    moves = [
+        (up_share(line[2]), up_src), (down_share(line[2]), down_src),
+        (up_share(z), up_own), (down_share(z), down_own),
+    ]
+    moves += [(even_ref.at[n], own_buf.at[n]) for n in range(half)]
+    pairs = branch_sum.shape[0]
+    moves += [(branch_ref.at[n], branch_sum.at[n]) for n in range(pairs)]
+    own = [pltpu.make_async_copy(src, dst, local.at[n]) for n, (src, dst) in enumerate(moves)]
+    for copy in own:
+        copy.start()
+    greet(
+        [wide_device(flipped(w, k)) for k in wide_steps(wide)]
+        + [narrow_device(line[k]) for k in (1, 3)]
+    )
+    sibling = wide_device(flipped(w, 1))
+    core = [sender.plan(odd_ref.at[n], core_buf.at[n], sibling) for n in range(half)]
+    far = [
+        sender.plan(own_buf.at[n], far_buf.at[n - 1], wide_device(flipped(w, 2 * n)))
+        for n in range(1, half)
+    ]
+    branch_core = [
+        sender.plan(branch_ref.at[pairs + n], branch_buf.at[n], sibling) for n in range(pairs)
+    ]
+    joins = [
+        sender.plan(up_share(line[3]), up_join, narrow_device(line[1])),
+        sender.plan(down_share(line[3]), down_join, narrow_device(line[1])),
+    ]
+    mids = [
+        sender.plan(up_share(line[3]), up_mid, narrow_device(line[3])),
+        sender.plan(down_share(line[3]), down_mid, narrow_device(line[3])),
+    ]
+    ones = [
+        sender.plan(up_share(line[1]), up_one, narrow_device(line[1])),
+        sender.plan(down_share(line[1]), down_one, narrow_device(line[1])),
+    ]
+    order = list(range(1, half)) + [0]
+    for n in order:
+        core[n].start()
+
+    @pl.when(is_end)
+    def _():
+        for copy in joins:
+            copy.start()
+
+    @pl.when(is_middle)
+    def _():
+        for copy in mids:
+            copy.start()
+
+    for copy in ones:
+        copy.start()
+    for n in order:
+        core[n].wait_recv()
+        own[4 + n].wait()
+        total = own_buf[n].astype(F32) + core_buf[n].astype(F32)
+        own_buf[n] = total.astype(BF16)
+        if n > 0:
+            far[n - 1].start()
+    for copy in branch_core:
+        copy.start()
+    for n in range(pairs):
+        branch_core[n].wait_recv()
+        own[4 + half + n].wait()
+        total = branch_sum[n].astype(F32) + branch_buf[n].astype(F32)
+        branch_sum[n] = total.astype(BF16)
+    for n in range(4):
+        own[n].wait()
+
+    @pl.when(is_middle)
+    def _():
+        for copy in joins:
+            copy.wait_recv()
+        up_src[...] = (up_src[...].astype(F32) + up_join[...].astype(F32)).astype(BF16)
+        down_src[...] = (down_src[...].astype(F32) + down_join[...].astype(F32)).astype(BF16)
+
+    total = own_buf[0].astype(F32)
+    for n in range(1, half):
+        far[n - 1].wait_recv()
+        total = total + far_buf[n - 1].astype(F32)
+    norm_sum[...] = total
+    for copy in ones:
+        copy.wait_recv()
+    up_acc[...] = up_own[...].astype(F32) + up_one[...].astype(F32)
+    down_acc[...] = down_own[...].astype(F32) + down_one[...].astype(F32)
+
+    @pl.when(is_middle)
+    def _():
+        for copy in mids:
+            copy.wait()
+        up_acc[...] += up_mid[...].astype(F32)
+        down_acc[...] += down_mid[...].astype(F32)
+
+    @pl.when(is_end)
+    def _():
+        for copy in joins:
+            copy.wait_send()
+
+    for copy in core + far + branch_core + ones:
+        copy.wait_send()
+
+
+def middle_sums(even, odd, branch, grad_up, grad_down, collective_id):
+    half, rows, width = even.shape
+    wide = 2 * half
+    unit, part = grad_up.shape[1] // 4, grad_down.shape[1] // 4
+    up_shape, down_shape = (grad_up.shape[0], unit), (grad_down.shape[0], part)
+    steps = 4 * half + 6
+    rows_buf = pltpu.VMEM((half, rows, width), BF16)
+    pairs = branch.shape[0] // 2
+    return pl.pallas_call(
+        functools.partial(middle_kernel, wide),
+        out_shape=[
+            jax.ShapeDtypeStruct((rows, width), F32),
+            jax.ShapeDtypeStruct((pairs,) + branch.shape[1:], BF16),
+            jax.ShapeDtypeStruct(up_shape, BF16),
+            jax.ShapeDtypeStruct(down_shape, BF16),
+            jax.ShapeDtypeStruct(up_shape, F32),
+            jax.ShapeDtypeStruct(down_shape, F32),
+        ],
+        in_specs=[ANY] * 5,
+        out_specs=[VMEM] * 6,
+        scratch_shapes=[
+            rows_buf, rows_buf, pltpu.VMEM((half - 1, rows, width), BF16),
+            pltpu.VMEM((pairs,) + branch.shape[1:], BF16),
+            *[pltpu.VMEM(up_shape, BF16)] * 3, *[pltpu.VMEM(down_shape, BF16)] * 3,
+            pltpu.VMEM(up_shape, BF16), pltpu.VMEM(down_shape, BF16),
+            DMA((steps,)), DMA((steps,)), DMA((4 + 2 * half,)),
+        ],
+        compiler_params=pltpu.CompilerParams(
+            collective_id=collective_id, has_side_effects=True, vmem_limit_bytes=56 * 2**20
+        ),
+    )(even, odd, branch, grad_up, grad_down)
+
+
+def last_kernel(
+    wide, rows, own_width, norm_ref, in_ref, out_ref, up_ref, norm_sum, in_got, out_sum, up_got,
+    join_buf, one_buf, mid_buf, two_buf, two_src, own_norm, in_core, in_own, in_far, in_sum,
+    out_core, out_own, out_far, out_low, out_buf, send, recv, local,
+):
+    w, z = lax.axis_index("wide"), lax.axis_index("narrow")
+    line = [flipped(z, k) for k in range(4)]
+    half = wide // 2
+    unit = up_ref.shape[1]
+    wide_rows = up_got.shape[0]
+    sender = Sender(send, recv)
+    is_middle = (z == 1) | (z == 2)
+    is_end = (z == 0) | (z == 3)
+
+    def norm_block(n):
+        return norm_ref.at[pl.ds(pl.multiple_of(n * rows, rows), rows), :]
+
+    def out_columns(n):
+        return pl.ds(pl.multiple_of(n * own_width, LANES), own_width)
+
+    def up_rows(n):
+        return up_ref.at[pl.ds(pl.multiple_of(n * wide_rows, 16), wide_rows), :]
+
+    def up_columns(n):
+        return up_got.at[:, pl.ds(pl.multiple_of(n * unit, LANES), unit)]
+
+    def section(n):
+        return in_sum.at[:, pl.ds(pl.multiple_of(n * own_width, LANES), own_width + LANES)]
+
+    moves = [
+        (norm_block(line[2]), two_src), (norm_block(z), own_norm), (up_rows(w), up_columns(w)),
+    ]
+    moves += [(in_ref.at[flipped(w, 2 * n)], in_own.at[n]) for n in range(half)]
+    moves += [(out_ref.at[flipped(w, 2 * n)], out_own.at[n]) for n in range(half)]
+    own = [pltpu.make_async_copy(src, dst, local.at[n]) for n, (src, dst) in enumerate(moves)]
+    for copy in own:
+        copy.start()
+    greet(
+        [narrow_device(line[k]) for k in (1, 2, 3)]
+        + [wide_device(flipped(w, k)) for k in range(1, wide)]
+    )
+    sibling = wide_device(flipped(w, 1))
+
+    def over_wide(ref, core_buf, own_buf, far_buf):
+        core = [
+            sender.plan(ref.at[flipped(w, 2 * n + 1)], core_buf.at[n], sibling)
+            for n in range(half)
+        ]
+        far = [
+            sender.plan(own_buf.at[n], far_buf.at[n - 1], wide_device(flipped(w, 2 * n)))
+            for n in range(1, half)
+        ]
+        return core, far
+
+    joined = sender.plan(norm_block(line[3]), join_buf, narrow_device(line[1]))
+    one = sender.plan(norm_block(line[1]), one_buf, narrow_device(line[1]))
+    middle = sender.plan(norm_block(line[3]), mid_buf, narrow_device(line[3]))
+    two = sender.plan(two_src, two_buf, narrow_device(line[2]))
+    in_steps = over_wide(in_ref, in_core, in_own, in_far)
+    out_steps = over_wide(out_ref, out_core, out_own, out_far)
+    sections = [
+        sender.plan(section(line[k]), in_got.at[z], narrow_device(line[k])) for k in (2, 3, 1)
+    ]
+    outs = [
+        sender.plan(out_low.at[:, out_columns(line[k])], out_buf.at[k - 1], narrow_device(line[k]))
+        for k in (1, 2, 3)
+    ]
+    ups = [
+        sender.plan(up_rows(flipped(w, k)), up_columns(w), wide_device(flipped(w, k)))
+        for k in range(1, wide)
+    ]
+    order = list(range(1, half)) + [0]
+    for core in (in_steps[0], out_steps[0]):
+        for n in order:
+            core[n].start()
+
+    @pl.when(is_end)
+    def _():
+        joined.start()
+
+    def between_cores(steps, core_buf, own_buf, first):
+        core, far = steps
+        for n in order:
+            core[n].wait_recv()
+            own[first + n].wait()
+            total = own_buf[n].astype(F32) + core_buf[n].astype(F32)
+            own_buf[n] = total.astype(BF16)
+            if n > 0:
+                far[n - 1].start()
+
+    def between_chips(steps, own_buf, far_buf):
+        total = own_buf[0].astype(F32)
+        for n in range(1, half):
+            steps[1][n - 1].wait_recv()
+            total = total + far_buf[n - 1].astype(F32)
+        return total.astype(BF16)
+
+    between_cores(in_steps, in_core, in_own, 3)
+    own[0].wait()
+
+    @pl.when(is_middle)
+    def _():
+        joined.wait_recv()
+        two_src[...] = (two_src[...].astype(F32) + join_buf[...].astype(F32)).astype(BF16)
+        middle.start()
+
+    two.start()
+    one.start()
+    between_cores(out_steps, out_core, out_own, 3 + half)
+    in_sum[...] = between_chips(in_steps, in_own, in_far)
+    mine = pltpu.make_async_copy(section(z), in_got.at[z], local.at[3 + 2 * half])
+    mine.start()
+    for copy in sections:
+        copy.start()
+    out_low[...] = between_chips(out_steps, out_own, out_far)
+    for copy in outs + ups:
+        copy.start()
+    own[1].wait()
+    own[2].wait()
+    one.wait_recv()
+    norm_sum[...] = own_norm[...].astype(F32) + one_buf[...].astype(F32)
+
+    @pl.when(is_middle)
+    def _():
+        middle.wait()
+        norm_sum[...] += mid_buf[...].astype(F32)
+
+    two.wait_recv()
+    norm_sum[...] += two_buf[...].astype(F32)
+    total = out_low[:, out_columns(z)].astype(F32)
+    for n in range(3):
+        outs[n].wait_recv()
+        total = total + out_buf[n].astype(F32)
+    out_sum[...] = total
+    for copy in sections + ups:
+        copy.wait_recv()
+    mine.wait()
+
+    @pl.when(is_end)
+    def _():
+        joined.wait_send()
+
+    sent = [one, two] + in_steps[0] + in_steps[1] + out_steps[0] + out_steps[1]
+    for copy in sent + sections + outs + ups:
+        copy.wait_send()
+
+
+def last_transfers(norm_part, in_part, out_part, up_part, rows, own_width, collective_id):
+    wide, wide_rows, columns = in_part.shape
+    half = wide // 2
+    width = norm_part.shape[1]
+    unit = up_part.shape[1]
+    steps = 4 + 4 * half + 6 + wide
+    block = pltpu.VMEM((rows, width), BF16)
+    sums = lambda size: [
+        pltpu.VMEM((half, wide_rows, size), BF16), pltpu.VMEM((half, wide_rows, size), BF16),
+        pltpu.VMEM((half - 1, wide_rows, size), BF16), pltpu.VMEM((wide_rows, size), BF16),
+    ]
+    return pl.pallas_call(
+        functools.partial(last_kernel, wide, rows, own_width),
+        out_shape=[
+            jax.ShapeDtypeStruct((rows, width), F32),
+            jax.ShapeDtypeStruct((4, wide_rows, own_width + LANES), BF16),
+            jax.ShapeDtypeStruct((wide_rows, own_width), F32),
+            jax.ShapeDtypeStruct((wide_rows, wide * unit), BF16),
+        ],
+        in_specs=[ANY] * 4,
+        out_specs=[VMEM] * 4,
+        scratch_shapes=[
+            *[block] * 6, *sums(columns), *sums(width),
+            pltpu.VMEM((3, wide_rows, own_width), BF16),
+            DMA((steps,)), DMA((steps,)), DMA((4 + 2 * half,)),
+        ],
+        compiler_params=pltpu.CompilerParams(
+            collective_id=collective_id, has_side_effects=True, vmem_limit_bytes=48 * 2**20
+        ),
+    )(norm_part, in_part, out_part, up_part)
+
+
+def total_kernel(wide, v_ref, out_ref, narrow_buf, wide_buf, sum_buf, send, recv):
+    w, z = lax.axis_index("wide"), lax.axis_index("narrow")
+    greet(
+        [narrow_device(flipped(z, k)) for k in (1, 2, 3)]
+        + [wide_device(flipped(w, k)) for k in range(1, wide)]
+    )
+    sender = Sender(send, recv)
+    first = [
+        sender.plan(v_ref, narrow_buf.at[z], narrow_device(flipped(z, k))) for k in (1, 2, 3)
+    ]
+    second = [
+        sender.plan(sum_buf, wide_buf.at[w], wide_device(flipped(w, k))) for k in range(1, wide)
+    ]
+    for copy in first:
+        copy.start()
+    narrow_buf[z] = v_ref[...]
+    for copy in first:
+        copy.wait()
+    sum_buf[...] = narrow_buf[0] + narrow_buf[1] + narrow_buf[2] + narrow_buf[3]
+    for copy in second:
+        copy.start()
+    wide_buf[w] = sum_buf[...]
+    for copy in second:
+        copy.wait()
+    total = wide_buf[0]
+    for n in range(1, wide):
+        total = total + wide_buf[n]
+    out_ref[...] = total
+
+
+def total_of(values, wide, collective_id):
+    size = values.shape[0]
+    height = -(-size // (8 * LANES)) * 8
+    padded = jnp.pad(values, (0, height * LANES - size)).reshape(height, LANES)
+    total = pl.pallas_call(
+        functools.partial(total_kernel, wide),
+        out_shape=jax.ShapeDtypeStruct(padded.shape, F32),
+        in_specs=[VMEM],
+        out_specs=VMEM,
+        scratch_shapes=[
+            pltpu.VMEM((4,) + padded.shape, F32),
+            pltpu.VMEM((wide,) + padded.shape, F32),
+            pltpu.VMEM(padded.shape, F32),
+            DMA((wide + 2,)), DMA((wide + 2,)),
+        ],
+        compiler_params=pltpu.CompilerParams(collective_id=collective_id, has_side_effects=True),
+    )(padded)
+    return total.reshape(-1)[:size]
 
 
 def rms_factor(values):
@@ -415,9 +1084,6 @@
         out_shape=[wide, wide, jax.ShapeDtypeStruct(wide.shape, F32)],
         scratch_shapes=[pltpu.VMEM((rows, LANES), F32)],
         compiler_params=pltpu.CompilerParams(vmem_limit_bytes=48 * 2**20),
-        cost_estimate=pl.CostEstimate(
-            flops=heads * rows * rows * 400, bytes_accessed=rows * 1664 * 6, transcendentals=heads * rows * rows // 2
-        ),
     )(*([projected] * 5), bias, cont)
 
 
@@ -444,50 +1110,14 @@
             pltpu.VMEM((rows, 2 * LANES), F32),
         ],
         compiler_params=pltpu.CompilerParams(vmem_limit_bytes=56 * 2**20),
-        cost_estimate=pl.CostEstimate(
-            flops=heads * rows * rows * 1000, bytes_accessed=rows * 1664 * 8, transcendentals=heads * rows * rows // 2
-        ),
     )(*([projected] * 5), bias, cont, attended, logs, grad)
 
 
-def reduce_wide(pieces, wide):
-    received = along_wide(jnp.stack(pieces[1::2]), 1, wide)
-    summed = [
-        (pieces[2 * n].astype(F32) + received[n].astype(F32)).astype(BF16) for n in range(wide // 2)
-    ]
-    total = summed[0].astype(F32)
-    for n in range(1, wide // 2):
-        total = total + along_wide(summed[n], 2 * n, wide).astype(F32)
+def add_up(parts):
+    total = parts[0].astype(F32)
+    for part in parts[1:]:
+        total = total + part.astype(F32)
     return total
-
-
-def reduce_narrow(share, narrow):
-    me = lax.axis_index("narrow")
-    if narrow != 4:
-        total = share(me).astype(F32)
-        for k in range(1, narrow):
-            total = total + along_narrow(share(lax.rem(me + k, narrow)), k, narrow).astype(F32)
-        return total
-    far = share(flipped(me, 3))
-    joined = lax.ppermute(far, "narrow", [(0, 1), (3, 2)])
-    middle = lax.ppermute(far, "narrow", [(1, 2), (2, 1)])
-    one = lax.ppermute(share(flipped(me, 1)), "narrow", [(0, 1), (1, 0), (2, 3), (3, 2)])
-    two = (share(flipped(me, 2)).astype(F32) + joined.astype(F32)).astype(BF16)
-    two = lax.ppermute(two, "narrow", [(0, 2), (2, 0), (1, 3), (3, 1)])
-    total = share(me).astype(F32) + one.astype(F32)
-    return total + middle.astype(F32) + two.astype(F32)
-
-
-def total_of(values, wide, narrow):
-    bit = 1
-    while bit < wide:
-        values = values + along_wide(values, bit, wide)
-        bit *= 2
-    bit = 1
-    while bit < narrow:
-        values = values + lax.ppermute(values, "narrow", [(i, i ^ bit) for i in range(narrow)])
-        bit *= 2
-    return values
 
 
 def on_device(
@@ -511,90 +1141,64 @@
     small = in_weight[:, base:].reshape(part_rows, 3, narrow, own_heads)
     small = jnp.moveaxis(small, 2, 0).reshape(narrow, part_rows, 3 * own_heads)
     small = jnp.pad(small, ((0, 0), (0, 0), (0, LANES - 3 * own_heads)))
-
-    def split_in(sources, targets):
-        copies = []
-        for k, target in enumerate(targets):
-            to = narrow_target(k, narrow)
+    aligned = unit % LANES == 0
+
+    def split_weights(sources, targets):
+        copies = [(sources[1], targets[0].at[:, :, pl.ds(4 * own_width, LANES)])]
+        for n in range(narrow):
             for group in range(4):
-                at = pl.multiple_of(group * width + to * own_width, LANES)
                 copies.append(
                     (
-                        sources[0].at[:, pl.ds(at, own_width)],
-                        target.at[:, pl.ds(group * own_width, own_width)],
+                        sources[0].at[:, pl.ds(group * width + n * own_width, own_width)],
+                        targets[0].at[n, :, pl.ds(group * own_width, own_width)],
                     )
                 )
-            copies.append((sources[1].at[to], target.at[:, pl.ds(4 * own_width, LANES)]))
+        if aligned:
+            for n in range(wide):
+                for group in range(4):
+                    copies.append(
+                        (
+                            sources[2].at[:, pl.ds((group * wide + n) * unit, unit)],
+                            targets[1].at[n, :, pl.ds(group * unit, unit)],
+                        )
+                    )
         return copies
 
-    in_parts = local_copies(
-        split_in, 5 * narrow, [in_weight, small],
-        [jax.ShapeDtypeStruct((part_rows, columns), BF16)] * narrow, False,
-    )
-    in_pieces = [in_parts[0]] + [along_narrow(in_parts[k], k, narrow) for k in range(1, narrow)]
-    in_block = assemble(
-        in_pieces, lambda k, t: t.at[narrow_order(k, narrow)], (narrow, part_rows, columns)
-    )
-
-    slot_tokens = gather_narrow(
-        tokens, narrow, lambda n, t: t.at[n], (narrow, rows, width)
-    ).reshape(slot, width)
-    in_full = assemble(
-        from_wide(in_block, wide), lambda k, t: t.at[wide_order(k)],
-        (wide, narrow, part_rows, columns),
-    ).reshape(width, columns)
-    slot_floats = slot_tokens.astype(F32)
-    normed_one = (slot_floats * rms_factor(slot_floats) * gain_one).astype(BF16)
-    projected = dot_f32(normed_one, in_full)
-
-    out_block = gather_narrow(
-        follow(out_weight, slot_tokens), narrow, lambda n, t: t.at[n], (narrow,) + out_weight.shape
-    )
-    out_full = assemble(
-        from_wide(out_block, wide), lambda k, t: t.at[wide_order(k)], (wide,) + out_block.shape
-    ).reshape(width, width)
-
-    def split_up(sources, targets):
-        copies = []
-        for k, target in enumerate(targets):
-            to = wide_order(k)
-            for group in range(4):
-                at = pl.multiple_of((group * wide + to) * unit, 64)
-                copies.append(
-                    (
-                        sources[0].at[:, pl.ds(at, unit)],
-                        target.at[:, pl.ds(group * unit, unit)],
-                    )
-                )
-        return copies
-
-    if unit % LANES == 0:
-        up_parts = local_copies(
-            split_up, 4 * wide, [gate_up_weight],
-            [jax.ShapeDtypeStruct((part_rows, 4 * unit), BF16)] * wide, False,
+    shapes = [
+        jax.ShapeDtypeStruct((narrow, part_rows, columns), BF16),
+        jax.ShapeDtypeStruct((wide, part_rows, 4 * unit), BF16),
+    ]
+    copies = 4 * narrow + 1
+    if aligned:
+        in_parts, up_parts = local_copies(
+            split_weights, copies + 4 * wide, [in_weight, small, gate_up_weight], shapes, False
         )
     else:
-        grouped = jnp.moveaxis(gate_up_weight.reshape(part_rows, 4, wide, unit), 2, 0)
-        grouped = grouped.reshape(wide, part_rows, 4 * unit)
-        up_parts = [
-            lax.dynamic_index_in_dim(grouped, wide_order(k), 0, False) for k in range(wide)
-        ]
-    up_pieces = [up_parts[0]] + [along_wide(up_parts[k], k, wide) for k in range(1, wide)]
-    up_block = assemble(up_pieces, lambda k, t: t.at[wide_order(k)], (wide, part_rows, 4 * unit))
-    up_full = gather_narrow(
-        follow(up_block, out_block), narrow, lambda n, t: t.at[:, n],
-        (wide, narrow, part_rows, 4 * unit),
-    ).reshape(width, 4 * unit)
+        in_parts = local_copies(split_weights, copies, [in_weight, small], shapes[:1], False)[0]
+        up_parts = jnp.moveaxis(gate_up_weight.reshape(part_rows, 4, wide, unit), 2, 0)
+        up_parts = up_parts.reshape(wide, part_rows, 4 * unit)
+
+    grads = [cotangent] + [along_wide(cotangent, k, wide) for k in range(2, wide, 2)]
     down_rows = down_weight.shape[0]
     pairs = []
     for i in range(wide * narrow):
         to_wide = (i % (2 * wide)) // 2
         to_narrow = i % 2 + 2 * (i // (2 * wide))
         pairs.append((i, to_wide * narrow + to_narrow))
-    down_block = lax.ppermute(follow(down_weight, slot_tokens), ("wide", "narrow"), pairs)
-    down_full = gather_narrow(
-        follow(down_block, up_full), narrow, lambda n, t: t.at[n], (narrow, down_rows, width)
-    ).reshape(2 * unit, width)
+    down_block = lax.ppermute(down_weight, ("wide", "narrow"), pairs)
+
+    slot_tokens, in_full, out_full, up_block = gather_all(tokens, in_parts, out_weight, up_parts)
+    slot_tokens = slot_tokens.reshape(slot, width)
+    in_full = in_full.reshape(width, columns)
+    out_full = out_full.reshape(width, width)
+    grads = [cotangent] + [follow(piece, slot_tokens) for piece in grads[1:]]
+
+    up_two = on_line(up_block, LINE_TWO)
+    up_one = on_line(up_block, LINE_ONE)
+
+    slot_floats = slot_tokens.astype(F32)
+    normed_one = (slot_floats * rms_factor(slot_floats) * gain_one).astype(BF16)
+    projected = dot_f32(normed_one, in_full)
 
     segments = segment_ids[0]
     joined = (segments[1:] == segments[:-1]).astype(F32)
@@ -607,107 +1211,88 @@
         projected, bias, cont, own_heads, head_size, block
     )
 
-    def rows_of(k, array):
-        return lax.dynamic_slice_in_dim(array, lax.rem(z + k, narrow) * rows, rows, 0)
-
-    def columns_of(k, array, size):
-        return lax.dynamic_slice_in_dim(array, lax.rem(z + k, narrow) * size, size, 1)
-
-    def share_columns(array, size):
-        return lambda n: lax.dynamic_slice_in_dim(array, n * size, size, 1)
-
-    mixed_pieces = [rows_of(0, mixed)] + [
-        along_narrow(rows_of(k, mixed), k, narrow) for k in range(1, narrow)
-    ]
-
-    def at_columns(k, target):
-        at = pl.multiple_of(narrow_order(k, narrow) * own_width, LANES)
-        return target.at[:, pl.ds(at, own_width)]
-
-    mixed_rows = assemble(mixed_pieces, at_columns, (rows, width))
+    def row_block(ref, n):
+        return ref.at[pl.ds(pl.multiple_of(n * rows, rows), rows), :]
+
+    def column_block(ref, n):
+        return ref.at[:, pl.ds(pl.multiple_of(n * own_width, LANES), own_width)]
+
+    mixed_rows = exchange(mixed, row_block, column_block, (rows, width), 1)
     inputs = tokens.astype(F32)
     middle = inputs + dot_f32(mixed_rows, out_full)
     normed_two = (middle * rms_factor(middle) * gain_two).astype(BF16)
 
-    plane_normed = jnp.concatenate(from_wide(normed_two, wide), axis=0)
-    plane_grad = jnp.concatenate(from_wide(follow(cotangent, in_full), wide), axis=0)
-    gate_up = dot_f32(plane_normed, up_full)
-    gate, up = gate_up[:, : 2 * unit], gate_up[:, 2 * unit :]
-    opened = jax.nn.sigmoid(gate)
-    hidden = (gate * opened * up).astype(BF16)
-    grad_hidden = dot_f32(plane_grad, down_full, ((1,), (1,)))
-    gate_up_grad = jnp.concatenate(
-        [
-            grad_hidden * up * (opened * (1.0 + gate * (1.0 - opened))),
-            grad_hidden * gate * opened,
-        ],
-        axis=1,
-    ).astype(BF16)
-    grad_normed_two = dot_f32(gate_up_grad, up_full, ((1,), (1,))).astype(BF16)
+    half = wide // 2
+    ups = [up_block] + [follow(piece, normed_two) for piece in (up_two, up_one)]
+    plane_normed, plane_grad, up_full, down_full = gather_rows(
+        normed_two, grads, ups, follow(down_block, normed_two), 2
+    )
+    plane_normed = plane_normed.reshape(wide * rows, width)
+    plane_grad = plane_grad.reshape(wide * rows, width)
+    up_full = up_full.reshape(width, 4 * unit)
+    down_full = down_full.reshape(2 * unit, width)
+    hidden, gate_up_grad, norm_even, norm_odd, branch = feed_forward(
+        plane_normed, plane_grad, up_full, down_full, rows
+    )
     grad_up_full = dot_f32(plane_normed, gate_up_grad, ((0,), (0,))).astype(BF16)
     grad_down_full = dot_f32(hidden, plane_grad, ((0,), (0,))).astype(BF16)
-
-    def row_pieces(array):
-        return [array[k * rows : (k + 1) * rows] for k in range(wide)]
-
-    grad_normed_two = reduce_wide(row_pieces(grad_normed_two), wide)
+    if unit % LANES:
+        grouped = grad_up_full.reshape(width, 4, unit)
+        grad_up_full = jnp.pad(grouped, ((0, 0), (0, 0), (0, LANES - unit))).reshape(width, -1)
+    branch = branch.reshape(wide, rows, width)
+    fits = wide <= 8
+    grad_normed_two, branch_sum, up_src, down_src, up_acc, down_acc = middle_sums(
+        norm_even.reshape(half, rows, width), norm_odd.reshape(half, rows, width),
+        branch if fits else branch[:2, :16], grad_up_full, grad_down_full, 6,
+    )
+    if not fits:
+        received = along_wide(branch[half:], 1, wide)
+        branch_sum = (branch[:half].astype(F32) + received.astype(F32)).astype(BF16)
+    branch_parts = [branch_sum[0]] + [
+        along_wide(branch_sum[n], 2 * n, wide) for n in range(1, half)
+    ]
     upstream = cotangent.astype(F32)
     grad_middle_norm, grad_gain_two = rms_back(middle, gain_two, grad_normed_two)
     grad_middle = upstream + grad_middle_norm
     branch_one_grad = grad_middle.astype(BF16)
     grad_mixed = dot_f32(branch_one_grad, out_full, ((1,), (1,))).astype(BF16)
-    grad_pieces = [columns_of(0, grad_mixed, own_width)] + [
-        along_narrow(columns_of(k, grad_mixed, own_width), k, narrow) for k in range(1, narrow)
-    ]
-    slot_grad = assemble(
-        grad_pieces, lambda k, t: t.at[narrow_order(k, narrow)], (narrow, rows, own_width)
-    ).reshape(slot, own_width)
-    branch_two = dot_f32(follow(hidden, grad_normed_two), down_full).astype(BF16)
-    output = (middle + reduce_wide(row_pieces(branch_two), wide)).astype(BF16)
+    slot_grad = exchange(grad_mixed, column_block, row_block, (slot, own_width), 3)
+    up_two = on_line(follow(up_src, slot_grad), LINE_TWO)
+    down_two = on_line(follow(down_src, slot_grad), LINE_TWO)
 
     projected_grad, bias_grad = attention_backward(
         projected, bias, cont, attended, logs, slot_grad, own_heads, head_size, block
     )
-    grad_normed_one_part = dot_f32(projected_grad, in_full, ((1,), (1,))).astype(BF16)
-    grad_normed_one = reduce_narrow(
-        lambda n: lax.dynamic_slice_in_dim(grad_normed_one_part, n * rows, rows, 0), narrow
-    )
-    grad_inputs, grad_gain_one = rms_back(inputs, gain_one, grad_normed_one)
-    grad_tokens = grad_middle + grad_inputs
-
-    grad_up = reduce_narrow(share_columns(grad_up_full, unit), narrow)
-    grad_up = grad_up.astype(BF16)
+    norm_part = dot_f32(projected_grad, in_full, ((1,), (1,))).astype(BF16)
+    in_part = dot_f32(normed_one, projected_grad, ((0,), (0,))).astype(BF16)
+
     wide_rows = width // wide
-    grad_up_pieces = []
-    for k in range(wide):
-        piece = lax.dynamic_slice_in_dim(grad_up, wide_order(k) * wide_rows, wide_rows, 0)
-        grad_up_pieces.append(along_wide(piece, k, wide) if k else piece)
-    if unit % LANES == 0:
-        grad_up = assemble(
-            grad_up_pieces,
-            lambda k, t: t.at[:, pl.ds(pl.multiple_of(wide_order(k) * unit, LANES), unit)],
-            (wide_rows, wide * unit),
-        )
-    else:
-        grad_up = assemble(
-            grad_up_pieces, lambda k, t: t.at[wide_order(k)], (wide, wide_rows, unit)
-        )
-        grad_up = jnp.moveaxis(grad_up, 0, 1).reshape(wide_rows, wide * unit)
-    grad_up = grad_up.astype(F32)
-
-    narrow_width = width // narrow
-    grad_down = reduce_narrow(share_columns(grad_down_full, narrow_width), narrow).astype(BF16)
+    out_part = dot_f32(mixed_rows, branch_one_grad, ((0,), (0,))).astype(BF16)
+    branch_parts = [follow(part, in_part, norm_part) for part in branch_parts]
+    output = (middle + add_up(branch_parts)).astype(BF16)
+    up_part = (up_acc + follow(up_two, in_part, norm_part).astype(F32)).astype(BF16)
+    grad_down = (down_acc + follow(down_two, in_part, norm_part).astype(F32)).astype(BF16)
     low_half, high_half = grad_down[:unit], grad_down[unit:]
     is_odd = lax.rem(w, 2) == 1
     first_send = jnp.where(is_odd, high_half, low_half)
     second_send = jnp.where(is_odd, low_half, high_half)
-    half = wide // 2
     first_got = lax.ppermute(
         first_send, "wide", [(i, i // 2 + (half if i % 2 else 0)) for i in range(wide)]
     )
     second_got = lax.ppermute(
         second_send, "wide", [(i, i // 2 + (0 if i % 2 else half)) for i in range(wide)]
     )
+    norm_sum, got, grad_out, grad_up = last_transfers(
+        norm_part, in_part.reshape(wide, wide_rows, columns),
+        out_part.reshape(wide, wide_rows, width), up_part, rows, own_width, 4,
+    )
+    if not aligned:
+        grad_up = grad_up.reshape(wide_rows, wide, LANES)[:, :, :unit]
+        grad_up = grad_up.reshape(wide_rows, wide * unit)
+    first_got, second_got = follow(first_got, norm_sum), follow(second_got, norm_sum)
+    grad_up = grad_up.astype(F32)
+    grad_inputs, grad_gain_one = rms_back(inputs, gain_one, norm_sum)
+    grad_tokens = grad_middle + grad_inputs
     in_low = w < half
     grad_down = jnp.concatenate(
         [
@@ -717,33 +1302,6 @@
         axis=0,
     ).astype(F32)
 
-    grad_out_full = dot_f32(mixed_rows, branch_one_grad, ((0,), (0,))).astype(BF16)
-
-    def wide_pieces(array):
-        return [
-            lax.dynamic_slice_in_dim(array, wide_order(k) * wide_rows, wide_rows, 0)
-            for k in range(wide)
-        ]
-
-    grad_out = reduce_wide(wide_pieces(grad_out_full), wide).astype(BF16)
-    grad_out = reduce_narrow(share_columns(grad_out, narrow_width), narrow)
-    grad_in_full = dot_f32(normed_one, projected_grad, ((0,), (0,))).astype(BF16)
-    grad_in = reduce_wide(wide_pieces(grad_in_full), wide).astype(BF16)
-    grad_small = grad_in[:, 4 * own_width :]
-    sections = []
-    for j in range(4):
-        own = grad_in[:, j * own_width : (j + 1) * own_width]
-        after = grad_in[:, (j + 1) * own_width : (j + 1) * own_width + LANES]
-        sections.append(jnp.concatenate([own, after], axis=1))
-    sections = jnp.stack(sections)
-    got = []
-    for k in range(narrow):
-        piece = lax.dynamic_index_in_dim(sections, lax.rem(z + k, narrow), 0, False)
-        got.append(along_narrow(piece, k, narrow) if k else piece)
-    got = assemble(
-        got, lambda k, t: t.at[narrow_order(k, narrow)],
-        (narrow, wide_rows, own_width + LANES),
-    )
     extra = 3 * heads
     section = jnp.concatenate([got[n, :, :own_width] for n in range(narrow)], axis=1)
     small_all = jnp.stack([got[n, :, own_width : own_width + 3 * own_heads] for n in range(narrow)])
@@ -759,7 +1317,7 @@
         jnp.zeros((heads,), F32), bias_grad[0, :own_heads], (z * own_heads,)
     )
     packed = jnp.concatenate([grad_gain_one, grad_gain_two, all_bias])
-    packed = total_of(packed, wide, narrow)
+    packed = total_of(packed, wide, 5)
     return (
         output,
         grad_tokens,

time: 752 us -> 612 us (0.81); the launches traced: 740 us -> 608 us
  Pallas kernels: 66.7 us -> 441 us
  waiting for transfers between devices: 339 us -> 31.9 us
  starting transfers between devices: 140 us -> 30.3 us
  local copies, waits for them, and re-layouts: 72.9 us -> 27.2 us
  other arithmetic: 45.2 us -> 23.7 us
  matrix products: 73 us -> 52.8 us
    pallas_call x6 -> x8, Pallas kernels: 0.01 us -> 387 us  [the longest x1 100 us: last_transfers(): pl.pallas_call(functools.partial(last_kernel, wide, rows, own_width), out...]
    ppermute x47 -> x5, waiting for transfers between devices: 199 us -> 22.7 us  [the longest x4 22.7 us: on_line(): return lax.ppermute(block, 'narrow', pairs)]
    ppermute x61 -> x6, waiting for transfers between devices: 140 us -> 9.21 us  [along_wide(): return lax.ppermute(block, 'wide', [(i, i ^ flip) for i in range(wide)])]
    ppermute x47 -> x5, starting transfers between devices: 77.3 us -> 12.2 us  [the longest x4 10.6 us: on_line(): return lax.ppermute(block, 'narrow', pairs)]
    ppermute x61 -> x6, starting transfers between devices: 58.7 us -> 14.3 us  [along_wide(): return lax.ppermute(block, 'wide', [(i, i ^ flip) for i in range(wide)])]
    unnamed x205 -> x96, local copies, waits for them, and re-layouts: 61.4 us -> 18.9 us
    dot_general x12 -> x8, matrix products: 73 us -> 52.8 us  [dot_f32(): lax.dot_general(left, right, (dims, ((), ())), preferred_element_type=F32)]
    convert_element_type x12 -> x3, other arithmetic: 18.3 us -> 1.93 us  [the longest x1 1.61 us: on_device(): normed_two = (middle * rms_factor(middle) * gain_two).astype(BF16)]
  transfers between devices with their start and end apart: 110 -> 13, of which waited for: 46 -> 2; matrix products, arithmetic and copies ran while one was open for 15% -> 9% of each run, Pallas kernels for 9% -> 32%
where the time goes in v2:
time: 612 us; the launch traced here: 608 us
  Pallas kernels  441 us (72%)
  matrix products  52.8 us (9%)
  waiting for transfers between devices  31.9 us (5%)
  starting transfers between devices  30.3 us (5%)
  local copies, waits for them, and re-layouts  27.2 us (4%)
  other arithmetic  23.7 us (4%)
    pallas_call x1, Pallas kernels, last_transfers(): pl.pallas_call(functools.partial(last_kernel, wide, rows, own_width), out...  100 us
    pallas_call x1, Pallas kernels, gather_all(): pl.pallas_call(functools.partial(gather_kernel, wide), out_shape=[jax.Sha...  86.9 us
    pallas_call x1, Pallas kernels, middle_sums(): pl.pallas_call(functools.partial(middle_kernel, wide), out_shape=[jax.Sha...  56.3 us
    pallas_call x1, Pallas kernels, gather_rows(): pl.pallas_call(functools.partial(rows_kernel, wide), out_shape=[whole, wh...  55.1 us
    dot_general x8, matrix products, dot_f32(): lax.dot_general(left, right, (dims, ((), ())), preferred_element_type=F32)  52.8 us
    pallas_call x2, Pallas kernels, exchange(): pl.pallas_call(functools.partial(exchange_kernel, source, target), out_sh...  48.5 us
    pallas_call x1, Pallas kernels, attention_backward(): pl.pallas_call(functools.partial(backward_kernel, heads, head_size, block...  37.6 us
    pallas_call x1, Pallas kernels, feed_forward(): pl.pallas_call(functools.partial(hidden_kernel, half), grid=(blocks,), in...  27 us
  transfers between devices with their start and end apart: 13, of which 2 were waited for; matrix products, arithmetic and copies ran while one was open for 9% of the time, Pallas kernels for 32%

profile of v2, /device:TPU:0, one launch (start us, length us, event | category | flops | bytes accessed | tf_op | source)
XLA Modules:
  0.0 607.8 jit_solution(8616612393551721771)
XLA Ops:
  6.7 86.9 %shard_map.170 = (bf16[4,256,1536]{2,1,0:T(8,128)(2,1)S(1)}, bf16[8,4,48,1664]{3,2,1,0:T(8,128)(2,1)S(1)}, bf16[8,4,48,1536]{3,2,1,0:T(8,128)(2,1)S(1)}, bf16[8,48,1024]{2,1,0:T(8,128)(2,1)}) custom-call(bf16[256,1536]{1,0:T(8,128)(2,1)S(1)} %copy-done, bf16[4,48,1664]{2,1,0:T(8,128)(2,1)S(1)} %get-tuple-element.55.in_ref, bf16[48,1536]{1,0:T(8,128)(2,1)S(1)} %copy-done.13, ...), custom_call_target="tpu_custom_call" | custom-call | tf_op jit(solution)/shard_map/pallas_call | solution.py:234
  98.1 4.0 collective-permute-start.4
  106.2 4.0 collective-permute-start.2
  116.3 8.0 %fusion.19.q_ref.k_ref.v_ref.gate_ref.small_ref = f32[1024,1664]{1,0:T(8,128)} fusion(bf16[1024,1536]{1,0:T(8,128)(2,1)S(1)} %bitcast.84, bf16[1536,1664]{1,0:T(8,128)(2,1)S(1)} %bitcast.70), kind=kOutput, calls=%fused_computation.67 | convolution fusion | flops 5234491392 | bytes 15073280 | tf_op jit(solution)/shard_map/dot_general | solution.py:20
  124.7 15.0 %shard_map.171 = (bf16[1024,384]{1,0:T(8,128)(2,1)S(1)}, bf16[1024,384]{1,0:T(8,128)(2,1)S(1)}, f32[1024,384]{1,0:T(8,128)S(1)}) custom-call(f32[1024,1664]{1,0:T(8,128)} %fusion.19.q_ref.k_ref.v_ref.gate_ref.small_ref, f32[1024,1664]{1,0:T(8,128)} %fusion.19.q_ref.k_ref.v_ref.gate_ref.small_ref, f32[1024,1664]{1,0:T(8,128)} %fusion.19.q_ref.k_ref.v_ref.gate_ref.small_ref, ...), custom_call_target="tpu_custom_call" | custom-call | tf_op jit(solution)/shard_map/pallas_call | solution.py:1079
  139.7 30.5 %shard_map.172 = bf16[256,1536]{1,0:T(8,128)(2,1)S(1)} custom-call(bf16[1024,384]{1,0:T(8,128)(2,1)S(1)} %get-tuple-element.59.src_ref), custom_call_target="tpu_custom_call" | custom-call | tf_op jit(solution)/shard_map/pallas_call | solution.py:265
  170.3 5.2 multiply_reduce_fusion.2
  176.0 5.1 collective-permute-start
  185.5 9.2 %collective-permute-done.refs_1_ = bf16[256,1536]{1,0:T(8,128)(2,1)} collective-permute-done((bf16[256,1536]{1,0:T(8,128)(2,1)}, bf16[256,1536]{1,0:T(8,128)(2,1)}, u32[]{:S(2)}, u32[]{:S(2)}) %collective-permute-start) | collective-permute-done | bytes 786464 | tf_op jit(solution)/shard_map/ppermute | solution.py:24
  194.7 55.1 %shard_map.173 = (bf16[8,256,1536]{2,1,0:T(8,128)(2,1)}, bf16[8,256,1536]{2,1,0:T(8,128)(2,1)}, bf16[8,4,48,1024]{3,2,1,0:T(8,128)(2,1)}, bf16[4,128,1536]{2,1,0:T(8,128)(2,1)}) custom-call(bf16[256,1536]{1,0:T(8,128)(2,1)} %refs_0_.3, bf16[256,1536]{1,0:T(8,128)(2,1)} %collective-permute-done.refs_1_, bf16[256,1536]{1,0:T(8,128)(2,1)} %collective-permute-done.1.refs_2_, ...), custom_call_target="tpu_custom_call" | custom-call | tf_op jit(solution)/shard_map/pallas_call | solution.py:362
  251.2 27.0 %shard_map.174 = (bf16[2048,512]{1,0:T(8,128)(2,1)S(1)}, bf16[2048,1024]{1,0:T(8,128)(2,1)}, bf16[1024,1536]{1,0:T(8,128)(2,1)}, bf16[1024,1536]{1,0:T(8,128)(2,1)}, bf16[2048,1536]{1,0:T(8,128)(2,1)}) custom-call(bf16[2048,1536]{1,0:T(8,128)(2,1)} %bitcast.76, bf16[2048,1536]{1,0:T(8,128)(2,1)} %bitcast.80, bf16[1536,1024]{1,0:T(8,128)(2,1)} %bitcast.85, ...), custom_call_target="tpu_custom_call" | custom-call | tf_op jit(solution)/shard_map/pallas_call | solution.py:406
  278.2 7.7 %convolution_convert_fusion.4.down_ref = bf16[512,1536]{1,0:T(8,128)(2,1)} fusion(bf16[2048,512]{1,0:T(8,128)(2,1)S(1)} %get-tuple-element.76, bf16[2048,1536]{1,0:T(8,128)(2,1)} %bitcast.81), kind=kOutput, calls=%fused_computation.12 | convolution fusion | flops 3222011904 | bytes 9961472 | tf_op jit(solution)/shard_map/dot_general | solution.py:20
  285.9 8.2 %convolution_convert_fusion.2.up_ref = bf16[1536,1024]{1,0:T(8,128)(2,1)} fusion(bf16[2048,1536]{1,0:T(8,128)(2,1)S(1)} %bitcast.79, bf16[2048,1024]{1,0:T(8,128)(2,1)S(1)} %copy-done.37), kind=kOutput, calls=%fused_computation.8 | convolution fusion | flops 6444023808 | bytes 13631488 | tf_op jit(solution)/shard_map/dot_general | solution.py:20
  294.1 56.3 %shard_map.175 = (f32[256,1536]{1,0:T(8,128)}, bf16[4,256,1536]{2,1,0:T(8,128)(2,1)}, bf16[1536,256]{1,0:T(8,128)(2,1)}, bf16[512,384]{1,0:T(8,128)(2,1)}, f32[1536,256]{1,0:T(8,128)}, /*index=5*/f32[512,384]{1,0:T(8,128)}) custom-call(bf16[4,256,1536]{2,1,0:T(8,128)(2,1)} %bitcast.86, bf16[4,256,1536]{2,1,0:T(8,128)(2,1)} %bitcast.87, ...), custom_call_target="tpu_custom_call" | custom-call | tf_op jit(solution)/shard_map/pallas_call | solution.py:556
  356.3 18.0 %shard_map.176.grad_ref = bf16[1024,384]{1,0:T(8,128)(2,1)S(1)} custom-call(bf16[256,1536]{1,0:T(8,128)(2,1)S(1)} %convolution_convert_fusion.5.src_ref), custom_call_target="tpu_custom_call" | custom-call | tf_op jit(solution)/shard_map/pallas_call | solution.py:265
  375.2 3.4 collective-permute-start.10
  378.7 37.6 %shard_map.177 = (bf16[1024,1664]{1,0:T(8,128)(2,1)}, f32[8,128]{1,0:T(8,128)}) custom-call(f32[1024,1664]{1,0:T(8,128)} %fusion.19.q_ref.k_ref.v_ref.gate_ref.small_ref, f32[1024,1664]{1,0:T(8,128)} %fusion.19.q_ref.k_ref.v_ref.gate_ref.small_ref, f32[1024,1664]{1,0:T(8,128)} %fusion.19.q_ref.k_ref.v_ref.gate_ref.small_ref, ...), custom_call_target="tpu_custom_call" | custom-call | tf_op jit(solution)/shard_map/pallas_call | solution.py:1095
  416.3 10.7 %convolution_convert_fusion.3.norm_ref = bf16[1024,1536]{1,0:T(8,128)(2,1)} fusion(bf16[1024,1664]{1,0:T(8,128)(2,1)} %get-tuple-element.81, bf16[1536,1664]{1,0:T(8,128)(2,1)} %bitcast.69), kind=kOutput, calls=%fused_computation.9 | convolution fusion | flops 5236064256 | bytes 11665408 | tf_op jit(solution)/shard_map/dot_general | solution.py:20
  427.0 8.0 %convolution_convert_fusion = bf16[1536,1664]{1,0:T(8,128)(2,1)} fusion(bf16[1024,1664]{1,0:T(8,128)(2,1)S(1)} %copy-done.38, bf16[1024,1536]{1,0:T(8,128)(2,1)S(1)} %bitcast.67, f32[1536]{0:T(1024)S(1)} %copy-done.30, f32[1024]{0:T(1024)S(1)} %bitcast.92), kind=kOutput, calls=%fused_computation.2 | convolution fusion | flops 5243338752 | bytes 11675648 | tf_op jit(solution)/shard_map/dot_general | solution.py:20
  437.8 3.6 convolution_convert_fusion.1
  448.1 22.7 %collective-permute-done.9 = bf16[1536,256]{1,0:T(8,128)(2,1)S(1)} collective-permute-done((bf16[1536,256]{1,0:T(8,128)(2,1)S(1)}, bf16[1536,256]{1,0:T(8,128)(2,1)S(1)}, u32[]{:S(2)}, u32[]{:S(2)}) %collective-permute-start.9) | collective-permute-done | bytes 786464 | tf_op jit(solution)/shard_map/ppermute | solution.py:75
  474.0 100.4 %shard_map.178 = (f32[256,1536]{1,0:T(8,128)S(1)}, bf16[4,192,512]{2,1,0:T(8,128)(2,1)S(1)}, f32[192,384]{1,0:T(8,128)S(1)}, bf16[192,2048]{1,0:T(8,128)(2,1)S(1)}) custom-call(bf16[1024,1536]{1,0:T(8,128)(2,1)} %convolution_convert_fusion.3.norm_ref, bf16[8,192,1664]{2,1,0:T(8,128)(2,1)} %bitcast.83, bf16[8,192,1536]{2,1,0:T(8,128)(2,1)} %bitcast.75, ...), custom_call_target="tpu_custom_call" | custom-call | tf_op jit(solution)/shard_map/pallas_call | solution.py:739
  576.4 13.0 %shard_map.179 = f32[32,128]{1,0:T(8,128)} custom-call(f32[32,128]{1,0:T(8,128)} %fusion.17.v_ref), custom_call_target="tpu_custom_call" | custom-call | tf_op jit(solution)/shard_map/pallas_call | solution.py:794
  602.8 4.1 fusion.11
  (163 shorter events, 62.9 us)
Async XLA Ops:
  98.1 15.8 %copy-start.30 = (f32[1536]{0:T(1024)S(1)}, f32[1536]{0:T(1024)}, u32[]{:S(2)}) copy-start(f32[1536]{0:T(1024)} %param.11) | copy-start | bytes 18436
  98.1 87.4 %collective-permute-start.4 = (bf16[8,48,1024]{2,1,0:T(8,128)(2,1)}, bf16[8,48,1024]{2,1,0:T(8,128)(2,1)}, u32[]{:S(2)}, u32[]{:S(2)}) collective-permute-start(bf16[8,48,1024]{2,1,0:T(8,128)(2,1)} %get-tuple-element.64.refs_5_), channel_id=1, source_target_pairs={{0,1},{1,0},{2,3},{3,2},{4,5},{5,4},{6,7},{7,6},{8,9},{9,8},{10,11... | collective-permute-start | bytes 2359304 | tf_op jit(solution)/shard_map/ppermute | solution.py:75
  102.1 83.4 %collective-permute-start.3 = (bf16[8,48,1024]{2,1,0:T(8,128)(2,1)}, bf16[8,48,1024]{2,1,0:T(8,128)(2,1)}, u32[]{:S(2)}, u32[]{:S(2)}) collective-permute-start(bf16[8,48,1024]{2,1,0:T(8,128)(2,1)} %get-tuple-element.64.refs_5_), channel_id=1, source_target_pairs={{0,2},{2,0},{1,3},{3,1},{4,6},{6,4},{5,7},{7,5},{8,10},{10,8},{9,1... | collective-permute-start | bytes 2359304 | tf_op jit(solution)/shard_map/ppermute | solution.py:75
  105.2 80.3 %collective-permute-start.1 = (bf16[256,1536]{1,0:T(8,128)(2,1)}, bf16[256,1536]{1,0:T(8,128)(2,1)}, u32[]{:S(2)}, u32[]{:S(2)}) collective-permute-start(bf16[256,1536]{1,0:T(8,128)(2,1)} %refs_0_.3), channel_id=1, source_target_pairs={{0,16},{4,20},{8,24},{12,28},{16,0},{20,4},{24,8},{28,12},{1,17},{... | collective-permute-start | bytes 2359304 | tf_op jit(solution)/shard_map/ppermute | solution.py:24
  106.2 79.2 %collective-permute-start.2 = (bf16[256,1536]{1,0:T(8,128)(2,1)}, bf16[256,1536]{1,0:T(8,128)(2,1)}, u32[]{:S(2)}, u32[]{:S(2)}) collective-permute-start(bf16[256,1536]{1,0:T(8,128)(2,1)} %refs_0_.3), channel_id=1, source_target_pairs={{0,24},{4,28},{8,16},{12,20},{16,8},{20,12},{24,0},{28,4},{1,25},{... | collective-permute-start | bytes 2359304 | tf_op jit(solution)/shard_map/ppermute | solution.py:24
  110.2 65.8 %collective-permute-start.5 = (bf16[128,1536]{1,0:T(8,128)(2,1)}, bf16[128,1536]{1,0:T(8,128)(2,1)S(1)}, u32[]{:S(2)}, u32[]{:S(2)}) collective-permute-start(bf16[128,1536]{1,0:T(8,128)(2,1)} %param.17), channel_id=1, source_target_pairs={{0,0},{1,1},{2,4},{3,5},{4,8},{5,9},{6,12},{7,13},{8,16},{9,17},{1... | collective-permute-start | bytes 1179656 | tf_op jit(solution)/shard_map/ppermute | solution.py:1188
  124.7 45.6 %copy-start.1 = (bf16[256,1536]{1,0:T(8,128)(2,1)S(1)}, bf16[256,1536]{1,0:T(8,128)(2,1)}, u32[]{:S(2)}) copy-start(bf16[256,1536]{1,0:T(8,128)(2,1)} %x_ref.1) | copy-start | bytes 2359300
  139.7 35.7 %copy-start.7 = (f32[1024,384]{1,0:T(8,128)}, f32[1024,384]{1,0:T(8,128)S(1)}, u32[]{:S(2)}) copy-start(f32[1024,384]{1,0:T(8,128)S(1)} %get-tuple-element.79.log_ref) | copy-start | bytes 4718596
  139.7 35.7 %copy-start.11 = (bf16[1024,384]{1,0:T(8,128)(2,1)}, bf16[1024,384]{1,0:T(8,128)(2,1)S(1)}, u32[]{:S(2)}) copy-start(bf16[1024,384]{1,0:T(8,128)(2,1)S(1)} %get-tuple-element.78.att_ref) | copy-start | bytes 2359300
  176.0 18.7 %collective-permute-start = (bf16[256,1536]{1,0:T(8,128)(2,1)}, bf16[256,1536]{1,0:T(8,128)(2,1)}, u32[]{:S(2)}, u32[]{:S(2)}) collective-permute-start(bf16[256,1536]{1,0:T(8,128)(2,1)} %refs_0_.3), channel_id=1, source_target_pairs={{0,8},{4,12},{8,0},{12,4},{16,24},{20,28},{24,16},{28,20},{1,9},{5... | collective-permute-start | bytes 2359304 | tf_op jit(solution)/shard_map/ppermute | solution.py:24
  183.8 391.4 %copy-start.33 = (f32[256]{0:T(256)}, f32[256]{0:T(256)S(1)}, u32[]{:S(2)}) copy-start(f32[256]{0:T(256)S(1)} %add_rsqrt_fusion.1) | copy-start | bytes 3076
  251.2 34.7 %slice-start.2 = ((s8[6291456]{0:T(1024)(128)(4,1)}), s8[2097152]{0:T(1024)(128)(4,1)S(1)}, s32[]{:S(2)}) async-start(s8[6291456]{0:T(1024)(128)(4,1)} %bitcast.77), calls=%async_computation.2 | async-start | bytes 4194304
  285.9 69.0 %slice-start = ((s8[4718592]{0:T(1024)(128)(4,1)}), s8[4194304]{0:T(1024)(128)(4,1)S(1)}, s32[]{:S(2)}) async-start(s8[4718592]{0:T(1024)(128)(4,1)} %bitcast.72), calls=%async_computation | async-start | bytes 8388608
  294.1 56.3 %copy-start.31 = (f32[256]{0:T(256)S(1)}, f32[256]{0:T(256)}, u32[]{:S(2)}) copy-start(f32[256]{0:T(256)} %add_rsqrt_fusion.2) | copy-start | bytes 3076
  294.1 60.8 %slice-start.1 = ((s8[4718592]{0:T(1024)(128)(4,1)}), s8[524288]{0:T(1024)(128)(4,1)S(1)}, s32[]{:S(2)}) async-start(s8[4718592]{0:T(1024)(128)(4,1)} %bitcast.72), calls=%async_computation.1 | async-start | bytes 1048576
  375.2 71.1 %collective-permute-start.10 = (bf16[512,384]{1,0:T(8,128)(2,1)}, bf16[512,384]{1,0:T(8,128)(2,1)S(1)}, u32[]{:S(2)}, u32[]{:S(2)}) collective-permute-start(bf16[512,384]{1,0:T(8,128)(2,1)} %get-tuple-element.97), channel_id=1, source_target_pairs={{0,2},{2,0},{1,3},{3,1},{4,6},{6,4},{5,7},{7,5},{8,10},{10,8},{9,1... | collective-permute-start | bytes 1179656 | tf_op jit(solution)/shard_map/ppermute | solution.py:75
  435.0 35.7 %collective-permute-start.9 = (bf16[1536,256]{1,0:T(8,128)(2,1)S(1)}, bf16[1536,256]{1,0:T(8,128)(2,1)S(1)}, u32[]{:S(2)}, u32[]{:S(2)}) collective-permute-start(bf16[1536,256]{1,0:T(8,128)(2,1)S(1)} %copy-done.39), channel_id=1, source_target_pairs={{0,2},{2,0},{1,3},{3,1},{4,6},{6,4},{5,7},{7,5},{8,10},{10,8},{9,1... | collective-permute-start | bytes 2359304 | tf_op jit(solution)/shard_map/ppermute | solution.py:75
  441.4 32.3 %copy-start.26 = (f32[1536,256]{1,0:T(8,128)S(1)}, f32[1536,256]{1,0:T(8,128)}, u32[]{:S(2)}) copy-start(f32[1536,256]{1,0:T(8,128)} %get-tuple-element.86) | copy-start | bytes 4718596
  441.4 153.3 %collective-permute-start.6 = (bf16[256,1536]{1,0:T(8,128)(2,1)}, bf16[256,1536]{1,0:T(8,128)(2,1)}, u32[]{:S(2)}, u32[]{:S(2)}) collective-permute-start(bf16[256,1536]{1,0:T(8,128)(2,1)} %get-tuple-element.108), channel_id=1, source_target_pairs={{0,8},{4,12},{8,0},{12,4},{16,24},{20,28},{24,16},{28,20},{1,9},{5... | collective-permute-start | bytes 2359304 | tf_op jit(solution)/shard_map/ppermute | solution.py:24
  444.1 150.6 %collective-permute-start.7 = (bf16[256,1536]{1,0:T(8,128)(2,1)}, bf16[256,1536]{1,0:T(8,128)(2,1)}, u32[]{:S(2)}, u32[]{:S(2)}) collective-permute-start(bf16[256,1536]{1,0:T(8,128)(2,1)} %get-tuple-element.107), channel_id=1, source_target_pairs={{0,16},{4,20},{8,24},{12,28},{16,0},{20,4},{24,8},{28,12},{1,17},{... | collective-permute-start | bytes 2359304 | tf_op jit(solution)/shard_map/ppermute | solution.py:24
  444.1 152.7 %collective-permute-start.8 = (bf16[256,1536]{1,0:T(8,128)(2,1)}, bf16[256,1536]{1,0:T(8,128)(2,1)}, u32[]{:S(2)}, u32[]{:S(2)}) collective-permute-start(bf16[256,1536]{1,0:T(8,128)(2,1)} %get-tuple-element.106), channel_id=1, source_target_pairs={{0,24},{4,28},{8,16},{12,20},{16,8},{20,12},{24,0},{28,4},{1,25},{... | collective-permute-start | bytes 2359304 | tf_op jit(solution)/shard_map/ppermute | solution.py:24
  447.2 145.0 %collective-permute-start.12 = (bf16[256,384]{1,0:T(8,128)(2,1)}, bf16[256,384]{1,0:T(8,128)(2,1)}, u32[]{:S(2)}, u32[]{:S(2)}) collective-permute-start(bf16[256,384]{1,0:T(8,128)(2,1)} %get-tuple-element.112), channel_id=1, source_target_pairs={{0,16},{4,0},{8,20},{12,4},{16,24},{20,8},{24,28},{28,12},{1,17},{... | collective-permute-start | bytes 589832 | tf_op jit(solution)/shard_map/ppermute | solution.py:1282
  470.7 121.5 %collective-permute-start.11 = (bf16[256,384]{1,0:T(8,128)(2,1)}, bf16[256,384]{1,0:T(8,128)(2,1)}, u32[]{:S(2)}, u32[]{:S(2)}) collective-permute-start(bf16[256,384]{1,0:T(8,128)(2,1)} %get-tuple-element.111), channel_id=1, source_target_pairs={{0,0},{4,16},{8,4},{12,20},{16,8},{20,24},{24,12},{28,28},{1,1},{5... | collective-permute-start | bytes 589832 | tf_op jit(solution)/shard_map/ppermute | solution.py:1279
  473.9 101.3 %copy-start.2 = (bf16[256,1536]{1,0:T(8,128)(2,1)S(1)}, bf16[256,1536]{1,0:T(8,128)(2,1)}, u32[]{:S(2)}) copy-start(bf16[256,1536]{1,0:T(8,128)(2,1)} %x_ref.1) | copy-start | bytes 2359300
  (34 other events, 186.2 us)

commit v3 on v2

--- a/solution.py
+++ b/solution.py
@@ -116,6 +116,14 @@
     return [1] + list(range(2, wide, 2))
 
 
+def straight_steps(wide):
+    return [k for k in range(2, wide, 2) if k & (k - 1) == 0]
+
+
+def diagonal_steps(wide):
+    return [k for k in range(2, wide, 2) if k & (k - 1)]
+
+
 def by_device(ref, w):
     return (lambda k: ref.at[flipped(w, k)]), (lambda k, to: ref.at[flipped(w, k)])
 
@@ -148,7 +156,8 @@
 
 
 def gather_kernel(
-    wide, x_ref, in_ref, out_ref, up_ref, slot_ref, in_full, out_full, up_block, send, recv, local
+    wide, x_ref, in_ref, out_ref, up_ref, grad_ref, slot_ref, in_full, out_full, up_block, grad_far,
+    send, recv, local,
 ):
     w, z = lax.axis_index("wide"), lax.axis_index("narrow")
     line = [flipped(z, k) for k in range(4)]
@@ -168,6 +177,10 @@
     ups = [
         sender.plan(up_ref.at[flipped(w, k)], up_block.at[w], wide_device(flipped(w, k)))
         for k in range(1, wide)
+    ]
+    grads = [
+        sender.plan(grad_ref, grad_far.at[n], wide_device(flipped(w, k)))
+        for n, k in enumerate(diagonal_steps(wide))
     ]
     is_middle = (z == 1) | (z == 2)
     is_end = (z == 0) | (z == 3)
@@ -194,6 +207,8 @@
         copy.wait_recv()
     out_wide.start()
     in_wide.pass_on()
+    for copy in grads:
+        copy.start()
     two.wait_recv()
 
     @pl.when(is_middle)
@@ -205,7 +220,7 @@
     one.wait_recv()
     own[2].wait()
     own[3].wait()
-    for copy in ups:
+    for copy in ups + grads:
         copy.wait()
 
     @pl.when(is_middle)
@@ -224,35 +239,44 @@
     out_wide.finish()
 
 
-def gather_all(tokens, in_parts, out_weight, up_parts):
+def gather_all(tokens, in_parts, out_weight, up_parts, cotangent):
     narrow, wide = in_parts.shape[0], up_parts.shape[0]
     steps = 10 + 4 * wide
     shapes = [
         (narrow,) + tokens.shape, (wide,) + in_parts.shape, (wide, narrow) + out_weight.shape,
-        up_parts.shape,
+        up_parts.shape, (len(diagonal_steps(wide)),) + cotangent.shape,
     ]
     return pl.pallas_call(
         functools.partial(gather_kernel, wide),
         out_shape=[jax.ShapeDtypeStruct(shape, BF16) for shape in shapes],
-        in_specs=[ANY] * 4,
-        out_specs=[VMEM] * 4,
+        in_specs=[ANY] * 5,
+        out_specs=[VMEM] * 5,
         scratch_shapes=[DMA((steps,)), DMA((steps,)), DMA((4,))],
         compiler_params=pltpu.CompilerParams(
-            collective_id=0, has_side_effects=True, vmem_limit_bytes=32 * 2**20
+            collective_id=0, has_side_effects=True, vmem_limit_bytes=40 * 2**20
         ),
-    )(tokens, in_parts, out_weight, up_parts)
-
-
-def exchange_kernel(source, target, src_ref, dst_ref, send, recv, local):
-    z = lax.axis_index("narrow")
+    )(tokens, in_parts, out_weight, up_parts, cotangent)
+
+
+def exchange_kernel(source, target, steps, *refs):
+    count = len(steps)
+    src_ref, sides, dst_ref = refs[0], refs[1 : 1 + count], refs[1 + count]
+    got = refs[2 + count : 2 + 2 * count]
+    send, recv, local = refs[2 + 2 * count :]
+    w, z = lax.axis_index("wide"), lax.axis_index("narrow")
     line = [flipped(z, k) for k in range(4)]
     sender = Sender(send, recv)
     own = pltpu.make_async_copy(source(src_ref, z), target(dst_ref, z), local.at[0])
     own.start()
-    greet([narrow_device(line[k]) for k in (1, 2, 3)])
+    greet(
+        [narrow_device(line[k]) for k in (1, 2, 3)] + [wide_device(flipped(w, k)) for k in steps]
+    )
     copies = [
         sender.plan(source(src_ref, line[k]), target(dst_ref, z), narrow_device(line[k]))
         for k in (2, 3, 1)
+    ]
+    copies += [
+        sender.plan(sides[n], got[n], wide_device(flipped(w, k))) for n, k in enumerate(steps)
     ]
     for copy in copies:
         copy.start()
@@ -261,17 +285,19 @@
         copy.wait()
 
 
-def exchange(array, source, target, shape, collective_id):
+def exchange(array, source, target, shape, steps, sides, collective_id):
+    count = len(steps) + 4
     return pl.pallas_call(
-        functools.partial(exchange_kernel, source, target),
-        out_shape=jax.ShapeDtypeStruct(shape, array.dtype),
-        in_specs=[ANY],
-        out_specs=VMEM,
-        scratch_shapes=[DMA((3,)), DMA((3,)), DMA((1,))],
+        functools.partial(exchange_kernel, source, target, steps),
+        out_shape=[jax.ShapeDtypeStruct(shape, array.dtype)]
+        + [jax.ShapeDtypeStruct(side.shape, side.dtype) for side in sides],
+        in_specs=[ANY] * (1 + len(sides)),
+        out_specs=[VMEM] * (1 + len(sides)),
+        scratch_shapes=[DMA((count,)), DMA((count,)), DMA((1,))],
         compiler_params=pltpu.CompilerParams(
             collective_id=collective_id, has_side_effects=True, vmem_limit_bytes=16 * 2**20
         ),
-    )(array)
+    )(array, *sides)
 
 
 def place_of(k, wide):
@@ -282,8 +308,8 @@
     half = wide // 2
     grads = refs[:half]
     (
-        src_ref, up_ref, up_two, up_one, down_ref, dst_ref, grad_ref, up_full, down_full, send,
-        recv, local,
+        src_ref, up_ref, up_two, up_one, down_ref, down_two, down_one, dst_ref, grad_ref, up_full,
+        down_full, send, recv, local,
     ) = refs[half:]
     w, z = lax.axis_index("wide"), lax.axis_index("narrow")
     line = [flipped(z, k) for k in range(4)]
@@ -293,7 +319,8 @@
     up_at = lambda n: up_full.at[:, n]
     down_at = lambda n: down_full.at[n]
     moves = [
-        (src_ref, dst_ref.at[0]), (down_ref, down_at(z)),
+        (src_ref, dst_ref.at[0]),
+        (down_ref, down_at(z)), (down_two, down_at(line[2])), (down_one, down_at(line[1])),
         (up_ref, up_at(z)), (up_two, up_at(line[2])), (up_one, up_at(line[1])),
     ] + [(grads[n], grad_ref.at[n]) for n in range(half)]
     own = [pltpu.make_async_copy(src, dst, local.at[n]) for n, (src, dst) in enumerate(moves)]
@@ -301,34 +328,27 @@
         copy.start()
     greet(
         [wide_device(flipped(w, k)) for k in wide_steps(wide)]
-        + [narrow_device(line[k]) for k in (1, 2, 3)]
+        + [narrow_device(line[k]) for k in (1, 3)]
     )
     gather = WideGather(
         sender, w, wide, lambda k: src_ref if k == 0 else dst_ref.at[place_of(k, wide)],
         lambda k, to: dst_ref.at[place_of(k ^ to, wide)],
     )
-    middle = sender.plan(up_ref, up_at(z), narrow_device(line[3]))
-    relay = sender.plan(up_two, up_at(line[2]), narrow_device(line[1]))
-    down_two = sender.plan(down_ref, down_at(z), narrow_device(line[2]))
-    down_one = sender.plan(down_ref, down_at(z), narrow_device(line[1]))
-    down_middle = sender.plan(down_ref, down_at(z), narrow_device(line[3]))
-    down_relay = sender.plan(down_at(line[2]), down_at(line[2]), narrow_device(line[1]))
+    middles = [
+        sender.plan(up_ref, up_at(z), narrow_device(line[3])),
+        sender.plan(down_ref, down_at(z), narrow_device(line[3])),
+    ]
+    relays = [
+        sender.plan(up_two, up_at(line[2]), narrow_device(line[1])),
+        sender.plan(down_two, down_at(line[2]), narrow_device(line[1])),
+    ]
     gather.start()
-    down_two.start()
 
     @pl.when(is_middle)
     def _():
-        relay.start()
-
-    down_two.wait_recv()
-
-    @pl.when(is_middle)
-    def _():
-        down_relay.start()
-        middle.start()
-        down_middle.start()
-
-    down_one.start()
+        for copy in middles + relays:
+            copy.start()
+
     sibling = wide_device(flipped(w, 1))
     copies = [sender.plan(grads[n], grad_ref.at[half + n], sibling) for n in range(half)]
     for copy in copies:
@@ -337,23 +357,22 @@
 
     @pl.when(is_middle)
     def _():
-        middle.wait()
-        down_middle.wait()
-        relay.wait_send()
-        down_relay.wait_send()
+        for copy in middles:
+            copy.wait()
+        for copy in relays:
+            copy.wait_send()
 
     @pl.when(is_end)
     def _():
-        relay.wait_recv()
-        down_relay.wait_recv()
-
-    down_two.wait_send()
-    for copy in own + copies + [down_one]:
+        for copy in relays:
+            copy.wait_recv()
+
+    for copy in own + copies:
         copy.wait()
     gather.finish()
 
 
-def gather_rows(array, grads, ups, down, collective_id):
+def gather_rows(array, grads, ups, downs, collective_id):
     half = len(grads)
     wide = 2 * half
     whole = jax.ShapeDtypeStruct((wide,) + array.shape, array.dtype)
@@ -361,14 +380,14 @@
     full = jax.ShapeDtypeStruct((up_shape[0], 4) + up_shape[1:], BF16)
     return pl.pallas_call(
         functools.partial(rows_kernel, wide),
-        out_shape=[whole, whole, full, jax.ShapeDtypeStruct((4,) + down.shape, BF16)],
-        in_specs=[ANY] * (half + 5),
+        out_shape=[whole, whole, full, jax.ShapeDtypeStruct((4,) + downs[0].shape, BF16)],
+        in_specs=[ANY] * (half + 7),
         out_specs=[VMEM, ANY if wide > 8 else VMEM, VMEM, VMEM],
-        scratch_shapes=[DMA((2 * wide + 6,)), DMA((2 * wide + 6,)), DMA((half + 5,))],
+        scratch_shapes=[DMA((2 * wide + 4,)), DMA((2 * wide + 4,)), DMA((half + 7,))],
         compiler_params=pltpu.CompilerParams(
             collective_id=collective_id, has_side_effects=True, vmem_limit_bytes=48 * 2**20
         ),
-    )(*grads, array, *ups, down)
+    )(*grads, array, *ups, *downs)
 
 
 def hidden_kernel(
@@ -425,9 +444,9 @@
 
 
 def middle_kernel(
-    wide, even_ref, odd_ref, branch_ref, up_ref, down_ref, norm_sum, branch_sum, up_src, down_src,
-    up_acc, down_acc, core_buf, own_buf, far_buf, branch_buf, up_join, up_one, up_mid, down_join,
-    down_one, down_mid, up_own, down_own, send, recv, local,
+    wide, even_ref, got_ref, branch_ref, up_ref, down_ref, norm_sum, branch_sum, up_src, down_src,
+    up_one, down_one, up_acc, down_acc, core_buf, own_buf, far_buf, branch_buf, up_join, up_mid,
+    down_join, down_mid, up_own, down_own, send, recv, local,
 ):
     w, z = lax.axis_index("wide"), lax.axis_index("narrow")
     line = [flipped(z, k) for k in range(4)]
@@ -447,7 +466,9 @@
     moves = [
         (up_share(line[2]), up_src), (down_share(line[2]), down_src),
         (up_share(z), up_own), (down_share(z), down_own),
-    ]
+        (up_share(line[1]), up_one), (down_share(line[1]), down_one),
+    ]
+    moves += [(got_ref.at[n], core_buf.at[n]) for n in range(half)]
     moves += [(even_ref.at[n], own_buf.at[n]) for n in range(half)]
     pairs = branch_sum.shape[0]
     moves += [(branch_ref.at[n], branch_sum.at[n]) for n in range(pairs)]
@@ -459,7 +480,6 @@
         + [narrow_device(line[k]) for k in (1, 3)]
     )
     sibling = wide_device(flipped(w, 1))
-    core = [sender.plan(odd_ref.at[n], core_buf.at[n], sibling) for n in range(half)]
     far = [
         sender.plan(own_buf.at[n], far_buf.at[n - 1], wide_device(flipped(w, 2 * n)))
         for n in range(1, half)
@@ -475,13 +495,7 @@
         sender.plan(up_share(line[3]), up_mid, narrow_device(line[3])),
         sender.plan(down_share(line[3]), down_mid, narrow_device(line[3])),
     ]
-    ones = [
-        sender.plan(up_share(line[1]), up_one, narrow_device(line[1])),
-        sender.plan(down_share(line[1]), down_one, narrow_device(line[1])),
-    ]
     order = list(range(1, half)) + [0]
-    for n in order:
-        core[n].start()
 
     @pl.when(is_end)
     def _():
@@ -493,11 +507,9 @@
         for copy in mids:
             copy.start()
 
-    for copy in ones:
-        copy.start()
     for n in order:
-        core[n].wait_recv()
-        own[4 + n].wait()
+        own[6 + n].wait()
+        own[6 + half + n].wait()
         total = own_buf[n].astype(F32) + core_buf[n].astype(F32)
         own_buf[n] = total.astype(BF16)
         if n > 0:
@@ -506,10 +518,10 @@
         copy.start()
     for n in range(pairs):
         branch_core[n].wait_recv()
-        own[4 + half + n].wait()
+        own[6 + 2 * half + n].wait()
         total = branch_sum[n].astype(F32) + branch_buf[n].astype(F32)
         branch_sum[n] = total.astype(BF16)
-    for n in range(4):
+    for n in range(6):
         own[n].wait()
 
     @pl.when(is_middle)
@@ -524,10 +536,8 @@
         far[n - 1].wait_recv()
         total = total + far_buf[n - 1].astype(F32)
     norm_sum[...] = total
-    for copy in ones:
-        copy.wait_recv()
-    up_acc[...] = up_own[...].astype(F32) + up_one[...].astype(F32)
-    down_acc[...] = down_own[...].astype(F32) + down_one[...].astype(F32)
+    up_acc[...] = up_own[...].astype(F32)
+    down_acc[...] = down_own[...].astype(F32)
 
     @pl.when(is_middle)
     def _():
@@ -541,11 +551,11 @@
         for copy in joins:
             copy.wait_send()
 
-    for copy in core + far + branch_core + ones:
+    for copy in far + branch_core:
         copy.wait_send()
 
 
-def middle_sums(even, odd, branch, grad_up, grad_down, collective_id):
+def middle_sums(even, got, branch, grad_up, grad_down, collective_id):
     half, rows, width = even.shape
     wide = 2 * half
     unit, part = grad_up.shape[1] // 4, grad_down.shape[1] // 4
@@ -558,28 +568,28 @@
         out_shape=[
             jax.ShapeDtypeStruct((rows, width), F32),
             jax.ShapeDtypeStruct((pairs,) + branch.shape[1:], BF16),
-            jax.ShapeDtypeStruct(up_shape, BF16),
-            jax.ShapeDtypeStruct(down_shape, BF16),
+            *[jax.ShapeDtypeStruct(up_shape, BF16), jax.ShapeDtypeStruct(down_shape, BF16)] * 2,
             jax.ShapeDtypeStruct(up_shape, F32),
             jax.ShapeDtypeStruct(down_shape, F32),
         ],
         in_specs=[ANY] * 5,
-        out_specs=[VMEM] * 6,
+        out_specs=[VMEM] * 8,
         scratch_shapes=[
             rows_buf, rows_buf, pltpu.VMEM((half - 1, rows, width), BF16),
             pltpu.VMEM((pairs,) + branch.shape[1:], BF16),
-            *[pltpu.VMEM(up_shape, BF16)] * 3, *[pltpu.VMEM(down_shape, BF16)] * 3,
+            *[pltpu.VMEM(up_shape, BF16)] * 2, *[pltpu.VMEM(down_shape, BF16)] * 2,
             pltpu.VMEM(up_shape, BF16), pltpu.VMEM(down_shape, BF16),
-            DMA((steps,)), DMA((steps,)), DMA((4 + 2 * half,)),
+            DMA((steps,)), DMA((steps,)), DMA((6 + 3 * half,)),
         ],
         compiler_params=pltpu.CompilerParams(
-            collective_id=collective_id, has_side_effects=True, vmem_limit_bytes=56 * 2**20
+            collective_id=collective_id, has_side_effects=True, vmem_limit_bytes=58 * 2**20
         ),
-    )(even, odd, branch, grad_up, grad_down)
+    )(even, got, branch, grad_up, grad_down)
 
 
 def last_kernel(
-    wide, rows, own_width, norm_ref, in_ref, out_ref, up_ref, norm_sum, in_got, out_sum, up_got,
+    wide, rows, own_width, norm_ref, in_ref, out_ref, up_ref, branch_ref, norm_sum, in_got, out_sum,
+    up_got, branch_got,
     join_buf, one_buf, mid_buf, two_buf, two_src, own_norm, in_core, in_own, in_far, in_sum,
     out_core, out_own, out_far, out_low, out_buf, send, recv, local,
 ):
@@ -649,6 +659,10 @@
         sender.plan(up_rows(flipped(w, k)), up_columns(w), wide_device(flipped(w, k)))
         for k in range(1, wide)
     ]
+    branches = [
+        sender.plan(branch_ref.at[n], branch_got.at[n], wide_device(flipped(w, k)))
+        for n, k in enumerate(diagonal_steps(wide))
+    ]
     order = list(range(1, half)) + [0]
     for core in (in_steps[0], out_steps[0]):
         for n in order:
@@ -657,6 +671,10 @@
     @pl.when(is_end)
     def _():
         joined.start()
+
+    @pl.when(is_middle)
+    def _():
+        middle.start()
 
     def between_cores(steps, core_buf, own_buf, first):
         core, far = steps
@@ -682,11 +700,12 @@
     def _():
         joined.wait_recv()
         two_src[...] = (two_src[...].astype(F32) + join_buf[...].astype(F32)).astype(BF16)
-        middle.start()
 
     two.start()
     one.start()
     between_cores(out_steps, out_core, out_own, 3 + half)
+    for copy in branches:
+        copy.start()
     in_sum[...] = between_chips(in_steps, in_own, in_far)
     mine = pltpu.make_async_copy(section(z), in_got.at[z], local.at[3 + 2 * half])
     mine.start()
@@ -712,7 +731,7 @@
         outs[n].wait_recv()
         total = total + out_buf[n].astype(F32)
     out_sum[...] = total
-    for copy in sections + ups:
+    for copy in sections + ups + branches:
         copy.wait_recv()
     mine.wait()
 
@@ -721,16 +740,16 @@
         joined.wait_send()
 
     sent = [one, two] + in_steps[0] + in_steps[1] + out_steps[0] + out_steps[1]
-    for copy in sent + sections + outs + ups:
+    for copy in sent + sections + outs + ups + branches:
         copy.wait_send()
 
 
-def last_transfers(norm_part, in_part, out_part, up_part, rows, own_width, collective_id):
+def last_transfers(norm_part, in_part, out_part, up_part, branches, rows, own_width, collective_id):
     wide, wide_rows, columns = in_part.shape
     half = wide // 2
     width = norm_part.shape[1]
     unit = up_part.shape[1]
-    steps = 4 + 4 * half + 6 + wide
+    steps = 4 + 4 * half + 6 + 2 * wide
     block = pltpu.VMEM((rows, width), BF16)
     sums = lambda size: [
         pltpu.VMEM((half, wide_rows, size), BF16), pltpu.VMEM((half, wide_rows, size), BF16),
@@ -743,9 +762,10 @@
             jax.ShapeDtypeStruct((4, wide_rows, own_width + LANES), BF16),
             jax.ShapeDtypeStruct((wide_rows, own_width), F32),
             jax.ShapeDtypeStruct((wide_rows, wide * unit), BF16),
+            jax.ShapeDtypeStruct(branches.shape, BF16),
         ],
-        in_specs=[ANY] * 4,
-        out_specs=[VMEM] * 4,
+        in_specs=[ANY] * 5,
+        out_specs=[VMEM] * 5,
         scratch_shapes=[
             *[block] * 6, *sums(columns), *sums(width),
             pltpu.VMEM((3, wide_rows, own_width), BF16),
@@ -754,7 +774,7 @@
         compiler_params=pltpu.CompilerParams(
             collective_id=collective_id, has_side_effects=True, vmem_limit_bytes=48 * 2**20
         ),
-    )(norm_part, in_part, out_part, up_part)
+    )(norm_part, in_part, out_part, up_part, branches)
 
 
 def total_kernel(wide, v_ref, out_ref, narrow_buf, wide_buf, sum_buf, send, recv):
@@ -953,9 +973,25 @@
 
 def backward_kernel(
     heads, head_size, block, q_ref, k_ref, v_ref, gate_ref, small_ref, bias_ref, cont_ref,
-    att_ref, log_ref, grad_ref, out_ref, bias_grad_ref, decay_scr, small_scr, dq_scr,
+    att_ref, log_ref, grad_ref, up_src, down_src, up_one, down_one, out_ref, bias_grad_ref,
+    up_two_got, down_two_got, up_one_got, down_one_got, decay_scr, small_scr, dq_scr, send, recv,
 ):
     pair = pl.program_id(0)
+    z = lax.axis_index("narrow")
+    sender = Sender(send, recv)
+    copies = [
+        sender.plan(up_src, up_two_got, narrow_device(flipped(z, 2))),
+        sender.plan(down_src, down_two_got, narrow_device(flipped(z, 2))),
+        sender.plan(up_one, up_one_got, narrow_device(flipped(z, 1))),
+        sender.plan(down_one, down_one_got, narrow_device(flipped(z, 1))),
+    ]
+
+    @pl.when(pair == 0)
+    def _():
+        greet([narrow_device(flipped(z, 1)), narrow_device(flipped(z, 2))])
+        for copy in copies:
+            copy.start()
+
     cont = cont_ref[...]
     small_low = small_columns(small_ref, bias_ref)
     rows = cont.shape[0]
@@ -1058,6 +1094,8 @@
         bias_grad_ref[...] = jnp.broadcast_to(
             jnp.sum(result, axis=0, keepdims=True), bias_grad_ref.shape
         )
+        for copy in copies:
+            copy.wait()
 
 
 def attention_specs(rows, pairs):
@@ -1087,7 +1125,9 @@
     )(*([projected] * 5), bias, cont)
 
 
-def attention_backward(projected, bias, cont, attended, logs, grad, heads, head_size, block):
+def attention_backward(
+    projected, bias, cont, attended, logs, grad, shares, heads, head_size, block, collective_id
+):
     rows = projected.shape[0]
     pairs = heads * head_size // LANES
     base, own = attention_specs(rows, pairs)
@@ -1095,22 +1135,28 @@
     return pl.pallas_call(
         functools.partial(backward_kernel, heads, head_size, block),
         grid=(pairs,),
-        in_specs=base + [own] * 3,
+        in_specs=base + [own] * 3 + [ANY] * 4,
         out_specs=[
             pl.BlockSpec((rows, columns), lambda p: (0, 0)),
             pl.BlockSpec((8, LANES), lambda p: (0, 0)),
-        ],
+        ]
+        + [ANY] * 4,
         out_shape=[
             jax.ShapeDtypeStruct((rows, columns), BF16),
             jax.ShapeDtypeStruct((8, LANES), F32),
-        ],
+        ]
+        + [jax.ShapeDtypeStruct(share.shape, BF16) for share in shares],
         scratch_shapes=[
             pltpu.VMEM((rows, LANES), F32),
             pltpu.VMEM((rows, LANES), F32),
             pltpu.VMEM((rows, 2 * LANES), F32),
+            DMA((4,)),
+            DMA((4,)),
         ],
-        compiler_params=pltpu.CompilerParams(vmem_limit_bytes=56 * 2**20),
-    )(*([projected] * 5), bias, cont, attended, logs, grad)
+        compiler_params=pltpu.CompilerParams(
+            collective_id=collective_id, has_side_effects=True, vmem_limit_bytes=56 * 2**20
+        ),
+    )(*([projected] * 5), bias, cont, attended, logs, grad, *shares)
 
 
 def add_up(parts):
@@ -1178,7 +1224,6 @@
         up_parts = jnp.moveaxis(gate_up_weight.reshape(part_rows, 4, wide, unit), 2, 0)
         up_parts = up_parts.reshape(wide, part_rows, 4 * unit)
 
-    grads = [cotangent] + [along_wide(cotangent, k, wide) for k in range(2, wide, 2)]
     down_rows = down_weight.shape[0]
     pairs = []
     for i in range(wide * narrow):
@@ -1187,11 +1232,12 @@
         pairs.append((i, to_wide * narrow + to_narrow))
     down_block = lax.ppermute(down_weight, ("wide", "narrow"), pairs)
 
-    slot_tokens, in_full, out_full, up_block = gather_all(tokens, in_parts, out_weight, up_parts)
+    slot_tokens, in_full, out_full, up_block, grad_far = gather_all(
+        tokens, in_parts, out_weight, up_parts, cotangent
+    )
     slot_tokens = slot_tokens.reshape(slot, width)
     in_full = in_full.reshape(width, columns)
     out_full = out_full.reshape(width, width)
-    grads = [cotangent] + [follow(piece, slot_tokens) for piece in grads[1:]]
 
     up_two = on_line(up_block, LINE_TWO)
     up_one = on_line(up_block, LINE_ONE)
@@ -1217,7 +1263,17 @@
     def column_block(ref, n):
         return ref.at[:, pl.ds(pl.multiple_of(n * own_width, LANES), own_width)]
 
-    mixed_rows = exchange(mixed, row_block, column_block, (rows, width), 1)
+    straight, diagonal = straight_steps(wide), diagonal_steps(wide)
+    mixed_rows, *grad_near = exchange(
+        mixed, row_block, column_block, (rows, width), straight, [cotangent] * len(straight), 1
+    )
+    grads = {0: cotangent}
+    grads.update({k: grad_near[n] for n, k in enumerate(straight)})
+    grads.update({k: grad_far[n] for n, k in enumerate(diagonal)})
+    grads = [grads[k] for k in range(0, wide, 2)]
+    down_block = follow(down_block, mixed_rows)
+    down_two = on_line(down_block, LINE_TWO)
+    down_one = on_line(down_block, LINE_ONE)
     inputs = tokens.astype(F32)
     middle = inputs + dot_f32(mixed_rows, out_full)
     normed_two = (middle * rms_factor(middle) * gain_two).astype(BF16)
@@ -1225,7 +1281,7 @@
     half = wide // 2
     ups = [up_block] + [follow(piece, normed_two) for piece in (up_two, up_one)]
     plane_normed, plane_grad, up_full, down_full = gather_rows(
-        normed_two, grads, ups, follow(down_block, normed_two), 2
+        normed_two, grads, ups, [down_block, down_two, down_one], 2
     )
     plane_normed = plane_normed.reshape(wide * rows, width)
     plane_grad = plane_grad.reshape(wide * rows, width)
@@ -1241,37 +1297,38 @@
         grad_up_full = jnp.pad(grouped, ((0, 0), (0, 0), (0, LANES - unit))).reshape(width, -1)
     branch = branch.reshape(wide, rows, width)
     fits = wide <= 8
-    grad_normed_two, branch_sum, up_src, down_src, up_acc, down_acc = middle_sums(
-        norm_even.reshape(half, rows, width), norm_odd.reshape(half, rows, width),
+    norm_got = along_wide(norm_odd.reshape(half, rows, width), 1, wide)
+    (
+        grad_normed_two, branch_sum, up_src, down_src, up_one, down_one, up_acc, down_acc,
+    ) = middle_sums(
+        norm_even.reshape(half, rows, width), norm_got,
         branch if fits else branch[:2, :16], grad_up_full, grad_down_full, 6,
     )
     if not fits:
         received = along_wide(branch[half:], 1, wide)
         branch_sum = (branch[:half].astype(F32) + received.astype(F32)).astype(BF16)
-    branch_parts = [branch_sum[0]] + [
-        along_wide(branch_sum[n], 2 * n, wide) for n in range(1, half)
-    ]
     upstream = cotangent.astype(F32)
     grad_middle_norm, grad_gain_two = rms_back(middle, gain_two, grad_normed_two)
     grad_middle = upstream + grad_middle_norm
     branch_one_grad = grad_middle.astype(BF16)
     grad_mixed = dot_f32(branch_one_grad, out_full, ((1,), (1,))).astype(BF16)
-    slot_grad = exchange(grad_mixed, column_block, row_block, (slot, own_width), 3)
-    up_two = on_line(follow(up_src, slot_grad), LINE_TWO)
-    down_two = on_line(follow(down_src, slot_grad), LINE_TWO)
-
-    projected_grad, bias_grad = attention_backward(
-        projected, bias, cont, attended, logs, slot_grad, own_heads, head_size, block
+    slot_grad, *branch_near = exchange(
+        grad_mixed, column_block, row_block, (slot, own_width), straight,
+        [branch_sum[k // 2] for k in straight], 3,
+    )
+
+    projected_grad, bias_grad, up_two, down_two, up_one, down_one = attention_backward(
+        projected, bias, cont, attended, logs, slot_grad, [up_src, down_src, up_one, down_one],
+        own_heads, head_size, block, 7,
     )
     norm_part = dot_f32(projected_grad, in_full, ((1,), (1,))).astype(BF16)
     in_part = dot_f32(normed_one, projected_grad, ((0,), (0,))).astype(BF16)
 
     wide_rows = width // wide
     out_part = dot_f32(mixed_rows, branch_one_grad, ((0,), (0,))).astype(BF16)
-    branch_parts = [follow(part, in_part, norm_part) for part in branch_parts]
-    output = (middle + add_up(branch_parts)).astype(BF16)
-    up_part = (up_acc + follow(up_two, in_part, norm_part).astype(F32)).astype(BF16)
-    grad_down = (down_acc + follow(down_two, in_part, norm_part).astype(F32)).astype(BF16)
+    late = lambda part: part.astype(F32)
+    up_part = (up_acc + late(up_one) + late(up_two)).astype(BF16)
+    grad_down = (down_acc + late(down_one) + late(down_two)).astype(BF16)
     low_half, high_half = grad_down[:unit], grad_down[unit:]
     is_odd = lax.rem(w, 2) == 1
     first_send = jnp.where(is_odd, high_half, low_half)
@@ -1282,10 +1339,13 @@
     second_got = lax.ppermute(
         second_send, "wide", [(i, i // 2 + (0 if i % 2 else half)) for i in range(wide)]
     )
-    norm_sum, got, grad_out, grad_up = last_transfers(
+    norm_sum, got, grad_out, grad_up, branch_far = last_transfers(
         norm_part, in_part.reshape(wide, wide_rows, columns),
-        out_part.reshape(wide, wide_rows, width), up_part, rows, own_width, 4,
-    )
+        out_part.reshape(wide, wide_rows, width), up_part,
+        jnp.stack([branch_sum[k // 2] for k in diagonal]), rows, own_width, 4,
+    )
+    branch_far = [branch_far[n] for n in range(len(diagonal))]
+    output = (middle + add_up([branch_sum[0]] + branch_near + branch_far)).astype(BF16)
     if not aligned:
         grad_up = grad_up.reshape(wide_rows, wide, LANES)[:, :, :unit]
         grad_up = grad_up.reshape(wide_rows, wide * unit)

time: 612 us -> 594 us (0.971)
  waiting for transfers between devices: 31.9 us -> 17.1 us
  starting transfers between devices: 30.3 us -> 22.2 us
    pallas_call x1, Pallas kernels: 37.6 us -> 57.9 us  [attention_backward(): pl.pallas_call(functools.partial(backward_kernel, heads, head_size, block...]
    ppermute x6 -> x1, starting transfers between devices: 14.3 us -> 0.38 us  [along_wide(): return lax.ppermute(block, 'wide', [(i, i ^ flip) for i in range(wide)])]
    pallas_call x1, Pallas kernels: 100 us -> 90.3 us  [last_transfers(): pl.pallas_call(functools.partial(last_kernel, wide, rows, own_width), out...]
    pallas_call x1, Pallas kernels: 56.3 us -> 46.4 us  [middle_sums(): pl.pallas_call(functools.partial(middle_kernel, wide), out_shape=[jax.Sha...]
    ppermute x6 -> x1, waiting for transfers between devices: 9.21 us -> 0.01 us  [along_wide(): return lax.ppermute(block, 'wide', [(i, i ^ flip) for i in range(wide)])]
    pallas_call x1, Pallas kernels: 86.9 us -> 94.9 us  [gather_all(): pl.pallas_call(functools.partial(gather_kernel, wide), out_shape=[jax.Sha...]
    unnamed x96 -> x108, local copies, waits for them, and re-layouts: 18.9 us -> 16.4 us
  transfers between devices with their start and end apart: 13 -> 8, of which waited for: 2 -> 2; matrix products, arithmetic and copies ran while one was open for 9% -> 9% of each run, Pallas kernels for 32% -> 10%
where the time goes in v3:
time: 594 us; the launch traced here: 589 us
  Pallas kernels  445 us (75%)
  matrix products  56.4 us (9%)
  other arithmetic  24.8 us (4%)
  local copies, waits for them, and re-layouts  22.4 us (4%)
  starting transfers between devices  22.2 us (4%)
  waiting for transfers between devices  17.1 us (3%)
    pallas_call x1, Pallas kernels, gather_all(): pl.pallas_call(functools.partial(gather_kernel, wide), out_shape=[jax.Sha...  94.9 us
    pallas_call x1, Pallas kernels, last_transfers(): pl.pallas_call(functools.partial(last_kernel, wide, rows, own_width), out...  90.3 us
    pallas_call x1, Pallas kernels, attention_backward(): pl.pallas_call(functools.partial(backward_kernel, heads, head_size, block...  57.9 us
    dot_general x8, matrix products, dot_f32(): lax.dot_general(left, right, (dims, ((), ())), preferred_element_type=F32)  56.4 us
    pallas_call x1, Pallas kernels, gather_rows(): pl.pallas_call(functools.partial(rows_kernel, wide), out_shape=[whole, wh...  50.8 us
    pallas_call x2, Pallas kernels, exchange(): pl.pallas_call(functools.partial(exchange_kernel, source, target, steps),...  50.3 us
    pallas_call x1, Pallas kernels, middle_sums(): pl.pallas_call(functools.partial(middle_kernel, wide), out_shape=[jax.Sha...  46.4 us
    pallas_call x1, Pallas kernels, feed_forward(): pl.pallas_call(functools.partial(hidden_kernel, half), grid=(blocks,), in...  26.9 us
  transfers between devices with their start and end apart: 8, of which 2 were waited for; matrix products, arithmetic and copies ran while one was open for 9% of the time, Pallas kernels for 10%

profile of v3, /device:TPU:0, one launch (start us, length us, event | category | flops | bytes accessed | tf_op | source)
XLA Modules:
  0.0 589.4 jit_solution(2696876050831077488)
XLA Ops:
  7.8 94.9 %shard_map.170 = (bf16[4,256,1536]{2,1,0:T(8,128)(2,1)S(1)}, bf16[8,4,48,1664]{3,2,1,0:T(8,128)(2,1)}, bf16[8,4,48,1536]{3,2,1,0:T(8,128)(2,1)S(1)}, bf16[8,48,1...) custom-call(bf16[256,1536]{1,0:T(8,128)(2,1)S(1)} %copy-done.2, bf16[4,48,1664]{2,1,0:T(8,128)(2,1)S(1)} %get-tuple-element.58.in_ref, ...), custom_call_target="tpu_custom_call" | custom-call | tf_op jit(solution)/shard_map/pallas_call | solution.py:249
  103.6 12.9 %collective-permute-start.1 = (bf16[8,48,1024]{2,1,0:T(8,128)(2,1)}, bf16[8,48,1024]{2,1,0:T(8,128)(2,1)}, u32[]{:S(2)}, u32[]{:S(2)}) collective-permute-start(bf16[8,48,1024]{2,1,0:T(8,128)(2,1)} %get-tuple-element.68.refs_5_), channel_id=1, source_target_pairs={{0,1},{1,0},{2,3},{3,2},{4,5},{5,4},{6,7},{7,6},{8,9},{9,8},{10,11... | collective-permute-start | bytes 2359304 | tf_op jit(solution)/shard_map/ppermute | solution.py:75
  116.5 2.8 collective-permute-start
  126.8 11.4 %fusion.20.q_ref.k_ref.v_ref.gate_ref.small_ref = f32[1024,1664]{1,0:T(8,128)} fusion(bf16[1024,1536]{1,0:T(8,128)(2,1)} %bitcast.91, bf16[1536,1664]{1,0:T(8,128)(2,1)} %bitcast.99), kind=kOutput, calls=%fused_computation.67 | convolution fusion | flops 5234491392 | bytes 15073280 | tf_op jit(solution)/shard_map/dot_general | solution.py:20
  138.4 15.0 %shard_map.171 = (bf16[1024,384]{1,0:T(8,128)(2,1)S(1)}, bf16[1024,384]{1,0:T(8,128)(2,1)S(1)}, f32[1024,384]{1,0:T(8,128)S(1)}) custom-call(f32[1024,1664]{1,0:T(8,128)} %fusion.20.q_ref.k_ref.v_ref.gate_ref.small_ref, f32[1024,1664]{1,0:T(8,128)} %fusion.20.q_ref.k_ref.v_ref.gate_ref.small_ref, f32[1024,1664]{1,0:T(8,128)} %fusion.20.q_ref.k_ref.v_ref.gate_ref.small_ref, ...), custom_call_target="tpu_custom_call" | custom-call | tf_op jit(solution)/shard_map/pallas_call | solution.py:1117
  154.3 30.5 %shard_map.172 = (bf16[256,1536]{1,0:T(8,128)(2,1)S(1)}, bf16[256,1536]{1,0:T(8,128)(2,1)S(1)}, bf16[256,1536]{1,0:T(8,128)(2,1)S(1)}) custom-call(bf16[1024,384]{1,0:T(8,128)(2,1)S(1)} %get-tuple-element.62.refs_0_, bf16[256,1536]{1,0:T(8,128)(2,1)S(1)} %copy-done.1, bf16[256,1536]{1,0:T(8,128)(2,1)S(1)} %copy-done.1), custom_call_target="tpu_custom_call" | custom-call | tf_op jit(solution)/shard_map/pallas_call | solution.py:290
  185.8 3.1 multiply_reduce_fusion.3
  191.6 14.7 %collective-permute-done.4.refs_10_ = bf16[128,1536]{1,0:T(8,128)(2,1)S(1)} collective-permute-done((bf16[128,1536]{1,0:T(8,128)(2,1)S(1)}, bf16[128,1536]{1,0:T(8,128)(2,1)S(1)}, u32[]{:S(2)}, u32[]{:S(2)}) %collective-permute-start.4) | collective-permute-done | bytes 393248 | tf_op jit(solution)/shard_map/ppermute | solution.py:75
  208.8 50.8 %shard_map.173 = (bf16[8,256,1536]{2,1,0:T(8,128)(2,1)}, bf16[8,256,1536]{2,1,0:T(8,128)(2,1)}, bf16[8,4,48,1024]{3,2,1,0:T(8,128)(2,1)}, bf16[4,128,1536]{2,1,0:T(8,128)(2,1)}) custom-call(bf16[256,1536]{1,0:T(8,128)(2,1)S(1)} %copy-done.1, bf16[256,1536]{1,0:T(8,128)(2,1)S(1)} %copy-done.10, bf16[256,1536]{1,0:T(8,128)(2,1)S(1)} %copy-done.12, ...), custom_call_target="tpu_custom_call" | custom-call | tf_op jit(solution)/shard_map/pallas_call | solution.py:381
  261.0 26.9 %shard_map.174 = (bf16[2048,512]{1,0:T(8,128)(2,1)S(1)}, bf16[2048,1024]{1,0:T(8,128)(2,1)}, bf16[1024,1536]{1,0:T(8,128)(2,1)}, bf16[1024,1536]{1,0:T(8,128)(2,1)}, bf16[2048,1536]{1,0:T(8,128)(2,1)}) custom-call(bf16[2048,1536]{1,0:T(8,128)(2,1)} %bitcast.83, bf16[2048,1536]{1,0:T(8,128)(2,1)} %bitcast.88, bf16[1536,1024]{1,0:T(8,128)(2,1)} %bitcast.93, ...), custom_call_target="tpu_custom_call" | custom-call | tf_op jit(solution)/shard_map/pallas_call | solution.py:425
  288.3 7.7 %convolution_convert_fusion.4.down_ref = bf16[512,1536]{1,0:T(8,128)(2,1)} fusion(bf16[2048,512]{1,0:T(8,128)(2,1)S(1)} %get-tuple-element.80, bf16[2048,1536]{1,0:T(8,128)(2,1)} %bitcast.89), kind=kOutput, calls=%fused_computation.9 | convolution fusion | flops 3222011904 | bytes 9961472 | tf_op jit(solution)/shard_map/dot_general | solution.py:20
  296.0 8.2 %convolution_convert_fusion.2.up_ref = bf16[1536,1024]{1,0:T(8,128)(2,1)} fusion(bf16[2048,1536]{1,0:T(8,128)(2,1)S(1)} %bitcast.86, bf16[2048,1024]{1,0:T(8,128)(2,1)S(1)} %copy-done.44), kind=kOutput, calls=%fused_computation.7 | convolution fusion | flops 6444023808 | bytes 13631488 | tf_op jit(solution)/shard_map/dot_general | solution.py:20
  305.8 46.4 %shard_map.175 = (f32[256,1536]{1,0:T(8,128)}, bf16[4,256,1536]{2,1,0:T(8,128)(2,1)}, bf16[1536,256]{1,0:T(8,128)(2,1)}, bf16[512,384]{1,0:T(8,128)(2,1)}, bf16[...) custom-call(bf16[4,256,1536]{2,1,0:T(8,128)(2,1)} %bitcast.92, ...), custom_call_target="tpu_custom_call" | custom-call | tf_op jit(solution)/shard_map/pallas_call | solution.py:566
  354.7 4.3 convolution_convert_fusion.5.refs_0_
  359.1 3.6 convolution_convert_fusion.1
  362.8 19.8 %shard_map.176 = (bf16[1024,384]{1,0:T(8,128)(2,1)S(1)}, bf16[256,1536]{1,0:T(8,128)(2,1)S(1)}, bf16[256,1536]{1,0:T(8,128)(2,1)S(1)}) custom-call(bf16[256,1536]{1,0:T(8,128)(2,1)S(1)} %convolution_convert_fusion.5.refs_0_, bf16[256,1536]{1,0:T(8,128)(2,1)S(1)} %get-tuple-element.113.refs_1_, bf16[256,1536]{1,0:T(8,128)(2,1)S(1)} %get-tuple-element.112.refs_2_), custom_call_target="tpu_custom_call" | custom-call | tf_op jit(solution)/shard_map/pallas_call | solution.py:290
  384.3 57.9 %shard_map.177 = (bf16[1024,1664]{1,0:T(8,128)(2,1)}, f32[8,128]{1,0:T(8,128)}, bf16[1536,256]{1,0:T(8,128)(2,1)}, bf16[512,384]{1,0:T(8,128)(2,1)}, bf16[1536,2...) custom-call(f32[1024,1664]{1,0:T(8,128)} %fusion.20.q_ref.k_ref.v_ref.gate_ref.small_ref, ...), custom_call_target="tpu_custom_call" | custom-call | tf_op jit(solution)/shard_map/pallas_call | solution.py:1135
  442.3 10.4 %convolution_convert_fusion.3.norm_ref = bf16[1024,1536]{1,0:T(8,128)(2,1)} fusion(bf16[1024,1664]{1,0:T(8,128)(2,1)} %get-tuple-element.92, bf16[1536,1664]{1,0:T(8,128)(2,1)} %bitcast.100), kind=kOutput, calls=%fused_computation.8 | convolution fusion | flops 5236064256 | bytes 11665408 | tf_op jit(solution)/shard_map/dot_general | solution.py:20
  452.7 7.8 %convolution_convert_fusion = bf16[1536,1664]{1,0:T(8,128)(2,1)} fusion(bf16[1024,1536]{1,0:T(8,128)(2,1)S(1)} %copy-done.31, bf16[1024,1664]{1,0:T(8,128)(2,1)S(1)} %copy-done.45), kind=kOutput, calls=%fused_computation | convolution fusion | flops 5237047296 | bytes 11665408 | tf_op jit(solution)/shard_map/dot_general | solution.py:20
  460.8 90.3 %shard_map.178 = (f32[256,1536]{1,0:T(8,128)S(1)}, bf16[4,192,512]{2,1,0:T(8,128)(2,1)S(1)}, f32[192,384]{1,0:T(8,128)S(1)}, bf16[192,2048]{1,0:T(8,128)(2,1)S(1)}, bf16[1,256,1536]{2,1,0:T(8,128)(2,1)S(1)}) custom-call(bf16[1024,1536]{1,0:T(8,128)(2,1)} %convolution_convert_fusion.3.norm_ref, bf16[8,192,1664]{2,1,0:T(8,128)(2,1)} %bitcast.90, ...), custom_call_target="tpu_custom_call" | custom-call | tf_op jit(solution)/shard_map/pallas_call | solution.py:758
  553.6 3.0 collective-permute-start.6
  560.0 11.4 %shard_map.179 = f32[32,128]{1,0:T(8,128)} custom-call(f32[32,128]{1,0:T(8,128)} %fusion.17.v_ref), custom_call_target="tpu_custom_call" | custom-call | tf_op jit(solution)/shard_map/pallas_call | solution.py:814
  575.9 2.6 convert_element_type.134
  581.6 4.1 fusion.8
  (166 shorter events, 47.3 us)
Async XLA Ops:
  3.9 117.1 %copy-start.43 = (s32[1,1024]{1,0:T(1,128)S(1)}, s32[1,1024]{1,0:T(1,128)}, u32[]{:S(2)}) copy-start(s32[1,1024]{1,0:T(1,128)} %param.18) | copy-start | bytes 12292
  103.6 18.1 %copy-start.40 = (f32[1536]{0:T(1024)S(1)}, f32[1536]{0:T(1024)}, u32[]{:S(2)}) copy-start(f32[1536]{0:T(1024)} %param.11) | copy-start | bytes 18436
  103.6 88.0 %collective-permute-start.1 = (bf16[8,48,1024]{2,1,0:T(8,128)(2,1)}, bf16[8,48,1024]{2,1,0:T(8,128)(2,1)}, u32[]{:S(2)}, u32[]{:S(2)}) collective-permute-start(bf16[8,48,1024]{2,1,0:T(8,128)(2,1)} %get-tuple-element.68.refs_5_), channel_id=1, source_target_pairs={{0,1},{1,0},{2,3},{3,2},{4,5},{5,4},{6,7},{7,6},{8,9},{9,8},{10,11... | collective-permute-start | bytes 2359304 | tf_op jit(solution)/shard_map/ppermute | solution.py:75
  116.5 75.1 %collective-permute-start = (bf16[8,48,1024]{2,1,0:T(8,128)(2,1)}, bf16[8,48,1024]{2,1,0:T(8,128)(2,1)}, u32[]{:S(2)}, u32[]{:S(2)}) collective-permute-start(bf16[8,48,1024]{2,1,0:T(8,128)(2,1)} %get-tuple-element.68.refs_5_), channel_id=1, source_target_pairs={{0,2},{2,0},{1,3},{3,1},{4,6},{6,4},{5,7},{7,5},{8,10},{10,8},{9,1... | collective-permute-start | bytes 2359304 | tf_op jit(solution)/shard_map/ppermute | solution.py:75
  119.3 70.6 %collective-permute-start.2 = (bf16[128,1536]{1,0:T(8,128)(2,1)}, bf16[128,1536]{1,0:T(8,128)(2,1)S(1)}, u32[]{:S(2)}, u32[]{:S(2)}) collective-permute-start(bf16[128,1536]{1,0:T(8,128)(2,1)} %param.17), channel_id=1, source_target_pairs={{0,0},{1,1},{2,4},{3,5},{4,8},{5,9},{6,12},{7,13},{8,16},{9,17},{1... | collective-permute-start | bytes 1179656 | tf_op jit(solution)/shard_map/ppermute | solution.py:1233
  126.8 59.0 %slice-start = ((s8[4718592]{0:T(1024)(128)(4,1)}), s8[4194304]{0:T(1024)(128)(4,1)S(1)}, s32[]{:S(2)}) async-start(s8[4718592]{0:T(1024)(128)(4,1)} %bitcast.79), calls=%async_computation | async-start | bytes 8388608
  138.4 47.4 %slice-start.1 = ((s8[4718592]{0:T(1024)(128)(4,1)}), s8[524288]{0:T(1024)(128)(4,1)S(1)}, s32[]{:S(2)}) async-start(s8[4718592]{0:T(1024)(128)(4,1)} %bitcast.79), calls=%async_computation.1 | async-start | bytes 1048576
  154.3 34.5 %copy-start.6 = (f32[1024,384]{1,0:T(8,128)}, f32[1024,384]{1,0:T(8,128)S(1)}, u32[]{:S(2)}) copy-start(f32[1024,384]{1,0:T(8,128)S(1)} %get-tuple-element.86.log_ref) | copy-start | bytes 4718596
  154.3 31.4 %copy-start.3 = (bf16[256,1536]{1,0:T(8,128)(2,1)S(1)}, bf16[256,1536]{1,0:T(8,128)(2,1)}, u32[]{:S(2)}) copy-start(bf16[256,1536]{1,0:T(8,128)(2,1)} %x_ref.1) | copy-start | bytes 2359300
  188.8 19.9 %copy-start.8 = (bf16[1,256,1536]{2,1,0:T(8,128)(2,1)S(1)}, bf16[1,256,1536]{2,1,0:T(8,128)(2,1)}, u32[]{:S(2)}) copy-start(bf16[1,256,1536]{2,1,0:T(8,128)(2,1)} %copy-done.7) | copy-start | bytes 2359300
  189.1 19.7 %copy-start.10 = (bf16[256,1536]{1,0:T(8,128)(2,1)S(1)}, bf16[256,1536]{1,0:T(8,128)(2,1)}, u32[]{:S(2)}) copy-start(bf16[256,1536]{1,0:T(8,128)(2,1)} %copy-done.9) | copy-start | bytes 2359300
  189.1 19.7 %copy-start.12 = (bf16[256,1536]{1,0:T(8,128)(2,1)S(1)}, bf16[256,1536]{1,0:T(8,128)(2,1)}, u32[]{:S(2)}) copy-start(bf16[256,1536]{1,0:T(8,128)(2,1)} %copy-done.11) | copy-start | bytes 2359300
  189.9 16.5 %collective-permute-start.4 = (bf16[128,1536]{1,0:T(8,128)(2,1)S(1)}, bf16[128,1536]{1,0:T(8,128)(2,1)S(1)}, u32[]{:S(2)}, u32[]{:S(2)}) collective-permute-start(bf16[128,1536]{1,0:T(8,128)(2,1)S(1)} %collective-permute-done.2.refs_8_), channel_id=1, source_target_pairs={{0,1},{1,0},{2,3},{3,2},{4,5},{5,4},{6,7},{7,6},{8,9},{9,8},{10,11... | collective-permute-start | bytes 1179656 | tf_op jit(solution)/shard_map/ppermute | solution.py:75
  189.9 18.8 %collective-permute-start.3 = (bf16[128,1536]{1,0:T(8,128)(2,1)S(1)}, bf16[128,1536]{1,0:T(8,128)(2,1)S(1)}, u32[]{:S(2)}, u32[]{:S(2)}) collective-permute-start(bf16[128,1536]{1,0:T(8,128)(2,1)S(1)} %collective-permute-done.2.refs_8_), channel_id=1, source_target_pairs={{0,2},{2,0},{1,3},{3,1},{4,6},{6,4},{5,7},{7,5},{8,10},{10,8},{9,1... | collective-permute-start | bytes 1179656 | tf_op jit(solution)/shard_map/ppermute | solution.py:75
  261.0 35.0 %slice-start.2 = ((s8[6291456]{0:T(1024)(128)(4,1)}), s8[2097152]{0:T(1024)(128)(4,1)S(1)}, s32[]{:S(2)}) async-start(s8[6291456]{0:T(1024)(128)(4,1)} %bitcast.84), calls=%async_computation.2 | async-start | bytes 4194304
  287.9 16.3 %collective-permute-start.5 = (bf16[4,256,1536]{2,1,0:T(8,128)(2,1)}, bf16[4,256,1536]{2,1,0:T(8,128)(2,1)S(1)}, u32[]{:S(2)}, u32[]{:S(2)}) collective-permute-start(bf16[4,256,1536]{2,1,0:T(8,128)(2,1)} %bitcast.101), channel_id=1, source_target_pairs={{0,4},{4,0},{8,12},{12,8},{16,20},{20,16},{24,28},{28,24},{1,5},{5... | collective-permute-start | bytes 9437192 | tf_op jit(solution)/shard_map/ppermute | solution.py:24
  305.8 46.5 %copy-start.27 = (f32[256,1536]{1,0:T(8,128)S(1)}, f32[256,1536]{1,0:T(8,128)}, u32[]{:S(2)}) copy-start(f32[256,1536]{1,0:T(8,128)} %get-tuple-element.123) | copy-start | bytes 4718596
  305.8 46.5 %copy-start.41 = (f32[1536]{0:T(1024)S(1)}, f32[1536]{0:T(1024)}, u32[]{:S(2)}) copy-start(f32[1536]{0:T(1024)} %param.15) | copy-start | bytes 18436
  384.3 57.9 %copy-start.15 = (bf16[256,1536]{1,0:T(8,128)(2,1)}, bf16[256,1536]{1,0:T(8,128)(2,1)S(1)}, u32[]{:S(2)}) copy-start(bf16[256,1536]{1,0:T(8,128)(2,1)S(1)} %get-tuple-element.83) | copy-start | bytes 2359300
  460.8 91.9 %copy-start.35 = (f32[512,384]{1,0:T(8,128)S(1)}, f32[512,384]{1,0:T(8,128)}, u32[]{:S(2)}) copy-start(f32[512,384]{1,0:T(8,128)} %get-tuple-element.102) | copy-start | bytes 2359300
  460.8 91.9 %copy-start.38 = (bf16[512,384]{1,0:T(8,128)(2,1)S(1)}, bf16[512,384]{1,0:T(8,128)(2,1)}, u32[]{:S(2)}) copy-start(bf16[512,384]{1,0:T(8,128)(2,1)} %get-tuple-element.104) | copy-start | bytes 1179652
  460.8 91.9 %copy-start.39 = (bf16[512,384]{1,0:T(8,128)(2,1)S(1)}, bf16[512,384]{1,0:T(8,128)(2,1)}, u32[]{:S(2)}) copy-start(bf16[512,384]{1,0:T(8,128)(2,1)} %get-tuple-element.103) | copy-start | bytes 1179652
  553.6 32.7 %collective-permute-start.6 = (bf16[256,384]{1,0:T(8,128)(2,1)}, bf16[256,384]{1,0:T(8,128)(2,1)}, u32[]{:S(2)}, u32[]{:S(2)}) collective-permute-start(bf16[256,384]{1,0:T(8,128)(2,1)} %get-tuple-element.116), channel_id=1, source_target_pairs={{0,0},{4,16},{8,4},{12,20},{16,8},{20,24},{24,12},{28,28},{1,1},{5... | collective-permute-start | bytes 589832 | tf_op jit(solution)/shard_map/ppermute | solution.py:1336
  556.6 29.7 %collective-permute-start.7 = (bf16[256,384]{1,0:T(8,128)(2,1)}, bf16[256,384]{1,0:T(8,128)(2,1)}, u32[]{:S(2)}, u32[]{:S(2)}) collective-permute-start(bf16[256,384]{1,0:T(8,128)(2,1)} %get-tuple-element.117), channel_id=1, source_target_pairs={{0,16},{4,0},{8,20},{12,4},{16,24},{20,8},{24,28},{28,12},{1,17},{... | collective-permute-start | bytes 589832 | tf_op jit(solution)/shard_map/ppermute | solution.py:1339
  (35 other events, 193.9 us)

commit v4 on v3

--- a/solution.py
+++ b/solution.py
@@ -147,12 +147,18 @@
             self.first[k].wait_recv()
             self.second[k].start()
 
-    def finish(self):
+    def received(self):
         self.first[1].wait_recv()
         for k in self.far:
             self.second[k].wait_recv()
+
+    def sent(self):
         for copy in list(self.first.values()) + list(self.second.values()):
             copy.wait_send()
+
+    def finish(self):
+        self.received()
+        self.sent()
 
 
 def gather_kernel(
@@ -924,25 +930,17 @@
     return running_sum(log_sigmoid(small_low.astype(F32)) - SEPARATE * (1.0 - cont), False)
 
 
-def forward_kernel(
-    heads, head_size, block, q_ref, k_ref, v_ref, gate_ref, small_ref, bias_ref, cont_ref,
-    mixed_ref, att_ref, log_ref, decay_scr,
+def forward_pair(
+    pair, heads, head_size, block, q_ref, k_ref, v_ref, gate_ref, small_low, cont, decay_all,
+    mixed_ref, att_ref, log_ref,
 ):
-    pair = pl.program_id(0)
-    cont = cont_ref[...]
-    small_low = small_columns(small_ref, bias_ref)
-
-    @pl.when(pair == 0)
-    def _():
-        decay_scr[...] = decay_of(small_low, cont)
-
     query, key, value_low, *unused = prologue(
         pair, heads, head_size, q_ref, k_ref, v_ref, small_low, cont
     )
     rows = query.shape[0]
     query = query.astype(BF16) * BF16(head_size**-0.5)
     key = key.astype(BF16)
-    decay = exact_dot(decay_scr[...], spread(2 * pair, head_size).astype(F32))
+    decay = exact_dot(decay_all, spread(2 * pair, head_size).astype(F32))
     decay_rows = decay.T
     lane = iota((1, LANES), 1)
     ones = jnp.ones((rows, LANES), BF16)
@@ -971,6 +969,31 @@
         mixed_ref[lo:hi, :] = (attended.astype(F32) * opened).astype(BF16)
 
 
+def forward_kernel(
+    heads, head_size, block, q_ref, k_ref, v_ref, gate_ref, small_ref, bias_ref, cont_ref,
+    mixed_ref, att_ref, log_ref, decay_scr,
+):
+    pair = pl.program_id(0)
+    cont = cont_ref[...]
+    small_low = small_columns(small_ref, bias_ref)
+
+    @pl.when(pair == 0)
+    def _():
+        decay_scr[...] = decay_of(small_low, cont)
+
+    forward_pair(
+        pair, heads, head_size, block, q_ref, k_ref, v_ref, gate_ref, small_low, cont,
+        decay_scr[...], mixed_ref, att_ref, log_ref,
+    )
+
+
+def share_of(ref, like, n):
+    size = like.shape[1]
+    if ref.shape[1] == size:
+        return ref
+    return ref.at[:, pl.ds(pl.multiple_of(n * size, size), size)]
+
+
 def backward_kernel(
     heads, head_size, block, q_ref, k_ref, v_ref, gate_ref, small_ref, bias_ref, cont_ref,
     att_ref, log_ref, grad_ref, up_src, down_src, up_one, down_one, out_ref, bias_grad_ref,
@@ -982,8 +1005,10 @@
     copies = [
         sender.plan(up_src, up_two_got, narrow_device(flipped(z, 2))),
         sender.plan(down_src, down_two_got, narrow_device(flipped(z, 2))),
-        sender.plan(up_one, up_one_got, narrow_device(flipped(z, 1))),
-        sender.plan(down_one, down_one_got, narrow_device(flipped(z, 1))),
+        sender.plan(share_of(up_one, up_src, flipped(z, 1)), up_one_got, narrow_device(flipped(z, 1))),
+        sender.plan(
+            share_of(down_one, down_src, flipped(z, 1)), down_one_got, narrow_device(flipped(z, 1))
+        ),
     ]
 
     @pl.when(pair == 0)
@@ -1145,7 +1170,7 @@
             jax.ShapeDtypeStruct((rows, columns), BF16),
             jax.ShapeDtypeStruct((8, LANES), F32),
         ]
-        + [jax.ShapeDtypeStruct(share.shape, BF16) for share in shares],
+        + [jax.ShapeDtypeStruct(share.shape, BF16) for share in shares[:2] * 2],
         scratch_shapes=[
             pltpu.VMEM((rows, LANES), F32),
             pltpu.VMEM((rows, LANES), F32),
@@ -1157,6 +1182,548 @@
             collective_id=collective_id, has_side_effects=True, vmem_limit_bytes=56 * 2**20
         ),
     )(*([projected] * 5), bias, cont, attended, logs, grad, *shares)
+
+
+def first_kernel(
+    wide, heads, head_size, block, x_ref, in_ref, out_ref, up_ref, grad_ref, down_ref, gain_one_ref,
+    gain_two_ref, bias_ref, cont_ref, normed_out, in_out, out_out, proj_out, att_ref, log_ref,
+    mixed_rows, middle_ref, normed_two_ref, up_out, up_two, up_one, down_got, grad_got, slot, in_buf,
+    out_buf, up_buf, normed, proj, mixed, decay_scr, send, recv, local,
+):
+    w, z = lax.axis_index("wide"), lax.axis_index("narrow")
+    line = [flipped(z, k) for k in range(4)]
+    rows, width = x_ref.shape
+    own_width = heads * head_size
+    part_rows = out_ref.shape[0]
+    is_middle = (z == 1) | (z == 2)
+    is_end = (z == 0) | (z == 3)
+    sender = Sender(send, recv)
+    used = []
+
+    def local_copy(src, dst):
+        copy = pltpu.make_async_copy(src, dst, local.at[len(used)])
+        used.append(copy)
+        return copy
+
+    def slot_rows(n):
+        return slot.at[pl.ds(pl.multiple_of(n * rows, rows), rows), :]
+
+    def weight_rows(ref, w_of, z_of):
+        at = (w_of * 4 + z_of) * part_rows
+        return ref.at[pl.ds(pl.multiple_of(at, 16), part_rows), :]
+
+    def wide_rows(ref, w_of):
+        at = w_of * 4 * part_rows
+        return ref.at[pl.ds(pl.multiple_of(at, 16), 4 * part_rows), :]
+
+    def by_rows(ref):
+        return (
+            (lambda k: wide_rows(ref, flipped(w, k))),
+            (lambda k, to: wide_rows(ref, flipped(w, k))),
+        )
+
+    own_in = local_copy(in_ref.at[z], weight_rows(in_buf, w, z))
+    own_out = local_copy(out_ref, weight_rows(out_buf, w, z))
+    own_x = local_copy(x_ref, slot_rows(z))
+    own_up = local_copy(up_ref.at[w], up_buf.at[w])
+    for copy in used:
+        copy.start()
+
+    index = w * 4 + z
+    down_wide = lax.div(lax.rem(index, 2 * wide), 2)
+    down_narrow = lax.rem(index, 2) + 2 * lax.div(index, 2 * wide)
+    from_index = 2 * wide * lax.div(z, 2) + 2 * w + lax.rem(z, 2)
+    from_wide_index, from_narrow_index = lax.div(from_index, 4), lax.rem(from_index, 4)
+    moves = jnp.logical_not((down_wide == w) & (down_narrow == z))
+    down_push = sender.plan(
+        down_ref, down_got, {"wide": down_wide, "narrow": down_narrow}
+    )
+    down_stay = local_copy(down_ref, down_got)
+
+    barrier = pltpu.get_barrier_semaphore()
+    partners = [narrow_device(line[k]) for k in (1, 2, 3)]
+    partners += [wide_device(flipped(w, k)) for k in range(1, wide)]
+    for device in partners:
+        pl.semaphore_signal(barrier, inc=1, device_id=device, device_id_type=MESH)
+
+    @pl.when(moves)
+    def _():
+        for device in (
+            {"wide": from_wide_index, "narrow": from_narrow_index},
+            {"wide": down_wide, "narrow": down_narrow},
+        ):
+            pl.semaphore_signal(barrier, inc=1, device_id=device, device_id_type=MESH)
+        pl.semaphore_wait(barrier, len(partners) + 2)
+
+    @pl.when(jnp.logical_not(moves))
+    def _():
+        pl.semaphore_wait(barrier, len(partners))
+
+    ins = [
+        sender.plan(in_ref.at[line[k]], weight_rows(in_buf, w, z), narrow_device(line[k]))
+        for k in (2, 3, 1)
+    ]
+    outs = [
+        sender.plan(out_ref, weight_rows(out_buf, w, z), narrow_device(line[k])) for k in (2, 3, 1)
+    ]
+    ups = [
+        sender.plan(up_ref.at[flipped(w, k)], up_buf.at[w], wide_device(flipped(w, k)))
+        for k in range(1, wide)
+    ]
+    grads = {
+        k: sender.plan(grad_ref, grad_got.at[k // 2 - 1], wide_device(flipped(w, k)))
+        for k in range(2, wide, 2)
+    }
+    two = sender.plan(x_ref, slot_rows(z), narrow_device(line[2]))
+    one = sender.plan(x_ref, slot_rows(z), narrow_device(line[1]))
+    middle = sender.plan(x_ref, slot_rows(z), narrow_device(line[3]))
+    relay = sender.plan(slot_rows(line[2]), slot_rows(line[2]), narrow_device(line[1]))
+    in_wide = WideGather(sender, w, wide, *by_rows(in_buf))
+    out_wide = WideGather(sender, w, wide, *by_rows(out_buf))
+    up_steps = [
+        sender.plan(up_buf, up_two, narrow_device(line[2])),
+        sender.plan(up_buf, up_one, narrow_device(line[1])),
+    ]
+    mixes = [
+        sender.plan(
+            mixed.at[pl.ds(pl.multiple_of(line[k] * rows, rows), rows), :],
+            mixed_rows.at[:, pl.ds(pl.multiple_of(z * own_width, LANES), own_width)],
+            narrow_device(line[k]),
+        )
+        for k in (2, 3, 1)
+    ]
+
+    for copy in ins + outs + ups:
+        copy.start()
+    own_in.wait()
+    for copy in ins:
+        copy.wait_recv()
+    in_wide.start()
+    two.start()
+    one.start()
+    own_out.wait()
+    for copy in outs:
+        copy.wait_recv()
+    out_wide.start()
+    in_wide.pass_on()
+    for k in diagonal_steps(wide):
+        grads[k].start()
+    two.wait_recv()
+
+    @pl.when(is_middle)
+    def _():
+        relay.start()
+        middle.start()
+
+    own_up.wait()
+    for copy in ups:
+        copy.wait_recv()
+    up_back = local_copy(up_buf, up_out)
+    up_back.start()
+    out_wide.pass_on()
+    in_wide.received()
+    in_back = local_copy(in_buf, in_out)
+    in_back.start()
+    one.wait_recv()
+    own_x.wait()
+
+    @pl.when(is_middle)
+    def _():
+        middle.wait_recv()
+
+    @pl.when(is_end)
+    def _():
+        relay.wait_recv()
+
+    for copy in up_steps:
+        copy.start()
+
+    @pl.when(moves)
+    def _():
+        down_push.start()
+
+    @pl.when(jnp.logical_not(moves))
+    def _():
+        down_stay.start()
+
+    for k in straight_steps(wide):
+        grads[k].start()
+
+    def project(n, carry):
+        at = pl.ds(pl.multiple_of(n * rows, rows), rows)
+        values = slot[at, :].astype(F32)
+        low = (values * rms_factor(values) * gain_one_ref[0:1, :]).astype(BF16)
+        normed[at, :] = low
+        proj[at, :] = dot_f32(low, in_buf[...])
+        return carry
+
+    lax.fori_loop(0, slot.shape[0] // rows, project, 0)
+    normed_back = local_copy(normed, normed_out)
+    proj_back = local_copy(proj, proj_out)
+    normed_back.start()
+    proj_back.start()
+
+    cont = cont_ref[...]
+    groups = own_width // LANES
+    small_low = small_columns(proj.at[:, pl.ds(4 * own_width, LANES)], bias_ref)
+    decay_scr[...] = decay_of(small_low, cont)
+
+    def attend(pair, carry):
+        def at(group):
+            return pl.ds(pl.multiple_of((group * groups + pair) * LANES, LANES), LANES)
+
+        forward_pair(
+            pair, heads, head_size, block, proj.at[:, at(0)], proj.at[:, at(1)], proj.at[:, at(2)],
+            proj.at[:, at(3)], small_low, cont, decay_scr[...], mixed.at[:, at(0)],
+            att_ref.at[:, at(0)], log_ref.at[:, at(0)],
+        )
+        return carry
+
+    lax.fori_loop(0, groups, attend, 0)
+    for copy in mixes:
+        copy.start()
+    mixed_rows[:, pl.ds(pl.multiple_of(z * own_width, LANES), own_width)] = mixed[
+        pl.ds(pl.multiple_of(z * rows, rows), rows), :
+    ]
+    out_wide.received()
+    out_back = local_copy(out_buf, out_out)
+    out_back.start()
+    for copy in mixes:
+        copy.wait_recv()
+    inputs = slot[pl.ds(pl.multiple_of(z * rows, rows), rows), :].astype(F32)
+    values = inputs + dot_f32(mixed_rows[...], out_buf[...])
+    middle_ref[...] = values
+    normed_two_ref[...] = (values * rms_factor(values) * gain_two_ref[0:1, :]).astype(BF16)
+
+    for copy in up_steps:
+        copy.wait()
+    for copy in grads.values():
+        copy.wait()
+
+    @pl.when(moves)
+    def _():
+        down_push.wait()
+
+    @pl.when(jnp.logical_not(moves))
+    def _():
+        down_stay.wait()
+
+    @pl.when(is_middle)
+    def _():
+        relay.wait_send()
+        middle.wait_send()
+
+    for copy in ins + outs + ups + [two, one] + mixes:
+        copy.wait_send()
+    in_wide.sent()
+    out_wide.sent()
+    for copy in (up_back, in_back, normed_back, proj_back, out_back):
+        copy.wait()
+
+
+def first_part(
+    tokens, in_parts, out_weight, up_parts, cotangent, down_weight, gain_one, gain_two, bias, cont,
+    heads, head_size, block, collective_id,
+):
+    wide = up_parts.shape[0]
+    rows, width = tokens.shape
+    slot, own_width, columns = 4 * rows, heads * head_size, in_parts.shape[2]
+    steps = 3 * wide + 2 * wide + 24
+    shape = jax.ShapeDtypeStruct
+    return pl.pallas_call(
+        functools.partial(first_kernel, wide, heads, head_size, block),
+        out_shape=[
+            shape((slot, width), BF16), shape((width, columns), BF16), shape((width, width), BF16),
+            shape((slot, columns), F32), shape((slot, own_width), BF16),
+            shape((slot, own_width), F32), shape((rows, width), BF16), shape((rows, width), F32),
+            shape((rows, width), BF16), shape(up_parts.shape, BF16), shape(up_parts.shape, BF16),
+            shape(up_parts.shape, BF16), shape(down_weight.shape, BF16),
+            shape((wide // 2 - 1, rows, width), BF16),
+        ],
+        in_specs=[ANY] * 6 + [VMEM] * 4,
+        out_specs=[ANY] * 4 + [VMEM] * 5 + [ANY] * 5,
+        scratch_shapes=[
+            pltpu.VMEM((slot, width), BF16), pltpu.VMEM((width, columns), BF16),
+            pltpu.VMEM((width, width), BF16), pltpu.VMEM(up_parts.shape, BF16),
+            pltpu.VMEM((slot, width), BF16), pltpu.VMEM((slot, columns), F32),
+            pltpu.VMEM((slot, own_width), BF16), pltpu.VMEM((slot, LANES), F32),
+            DMA((steps,)), DMA((steps,)), DMA((10,)),
+        ],
+        compiler_params=pltpu.CompilerParams(
+            collective_id=collective_id, has_side_effects=True, vmem_limit_bytes=60 * 2**20
+        ),
+    )(
+        tokens, in_parts, out_weight, up_parts, cotangent, down_weight,
+        jnp.broadcast_to(gain_one[None], (8, width)), jnp.broadcast_to(gain_two[None], (8, width)),
+        bias, cont,
+    )
+
+
+def second_kernel(
+    wide, src_ref, grad_ref, far_grads, up_ref, up_two, up_one, down_ref, norm_sum, branch_sum,
+    up_src, down_src, up_acc, down_acc, up_grad_out, down_grad_out, normed, grads, up_full,
+    down_full, hidden, mid, rows_buf, core_buf, far_buf, branch_buf, up_join, up_mid, down_join,
+    down_mid, up_grad, down_grad, send, recv, local,
+):
+    w, z = lax.axis_index("wide"), lax.axis_index("narrow")
+    line = [flipped(z, k) for k in range(4)]
+    rows, width = src_ref.shape
+    half = wide // 2
+    size = hidden.shape[1]
+    unit, part = up_src.shape[1], down_src.shape[1]
+    is_middle = (z == 1) | (z == 2)
+    is_end = (z == 0) | (z == 3)
+    sender = Sender(send, recv)
+    sibling = wide_device(flipped(w, 1))
+
+    def at_place(ref, place):
+        return ref.at[pl.ds(pl.multiple_of(place * rows, rows), rows), :]
+
+    up_at = lambda n: up_full.at[:, n]
+    down_at = lambda n: down_full.at[n]
+    moves = [
+        (src_ref, at_place(normed, 0)), (up_ref, up_at(z)), (up_two, up_at(line[2])),
+        (up_one, up_at(line[1])), (down_ref, down_at(z)), (grad_ref, at_place(grads, 0)),
+    ] + [(far_grads.at[n - 1], at_place(grads, n)) for n in range(1, half)]
+    own = [pltpu.make_async_copy(src, dst, local.at[n]) for n, (src, dst) in enumerate(moves)]
+    for copy in own:
+        copy.start()
+    greet(
+        [wide_device(flipped(w, k)) for k in wide_steps(wide)]
+        + [narrow_device(line[k]) for k in (1, 2, 3)]
+    )
+    gather = WideGather(
+        sender, w, wide, lambda k: src_ref if k == 0 else at_place(normed, place_of(k, wide)),
+        lambda k, to: at_place(normed, place_of(k ^ to, wide)),
+    )
+    middle = sender.plan(up_ref, up_at(z), narrow_device(line[3]))
+    relay = sender.plan(up_two, up_at(line[2]), narrow_device(line[1]))
+    down_two = sender.plan(down_ref, down_at(z), narrow_device(line[2]))
+    down_one = sender.plan(down_ref, down_at(z), narrow_device(line[1]))
+    down_middle = sender.plan(down_ref, down_at(z), narrow_device(line[3]))
+    down_relay = sender.plan(down_at(line[2]), down_at(line[2]), narrow_device(line[1]))
+    passed = [
+        sender.plan(
+            grad_ref if n == 0 else far_grads.at[n - 1], at_place(grads, half + n), sibling
+        )
+        for n in range(half)
+    ]
+    core = [
+        sender.plan(at_place(rows_buf, half + n), core_buf.at[n], sibling) for n in range(half)
+    ]
+    far = [
+        sender.plan(at_place(rows_buf, n), far_buf.at[n - 1], wide_device(flipped(w, 2 * n)))
+        for n in range(1, half)
+    ]
+    branch_core = [
+        sender.plan(at_place(normed, half + n), branch_buf.at[n], sibling) for n in range(half)
+    ]
+
+    def up_share(n):
+        return up_grad.at[:, pl.ds(pl.multiple_of(n * unit, unit), unit)]
+
+    def down_share(n):
+        return down_grad.at[:, pl.ds(pl.multiple_of(n * part, part), part)]
+
+    down_joined = sender.plan(down_share(line[3]), down_join, narrow_device(line[1]))
+    down_direct = sender.plan(down_share(line[3]), down_mid, narrow_device(line[3]))
+    up_joined = sender.plan(up_share(line[3]), up_join, narrow_device(line[1]))
+    up_direct = sender.plan(up_share(line[3]), up_mid, narrow_device(line[3]))
+
+    gather.start()
+    down_two.start()
+
+    @pl.when(is_middle)
+    def _():
+        relay.start()
+
+    down_two.wait_recv()
+
+    @pl.when(is_middle)
+    def _():
+        down_relay.start()
+        middle.start()
+        down_middle.start()
+
+    down_one.start()
+    for copy in passed:
+        copy.start()
+    gather.pass_on()
+    gather.received()
+    for copy in own:
+        copy.wait()
+    for copy in passed + [down_one]:
+        copy.wait_recv()
+
+    @pl.when(is_middle)
+    def _():
+        middle.wait_recv()
+        down_middle.wait_recv()
+
+    @pl.when(is_end)
+    def _():
+        relay.wait_recv()
+        down_relay.wait_recv()
+
+    up_shape = (width, 4 * unit)
+    down_shape = (size, width)
+
+    def block(t, carry):
+        place = lax.rem(t + half, wide) + jnp.where(t < half, 0, 1)
+        place = jnp.where(place == half, jnp.where(t < half, half, 0), place)
+        at = pl.ds(pl.multiple_of(place * rows, rows), rows)
+        gate_up = dot_f32(normed[at, :], up_full[...].reshape(up_shape))
+        grad_hidden = dot_f32(grads[at, :], down_full[...].reshape(down_shape), ((1,), (1,)))
+        gate, up = gate_up[:, :size], gate_up[:, size:]
+        opened = jax.nn.sigmoid(gate)
+        acted = gate * opened
+        hidden[at, :] = (acted * up).astype(BF16)
+        mid[at, :size] = (grad_hidden * up * (opened * (1.0 + gate * (1.0 - opened)))).astype(BF16)
+        mid[at, size:] = (grad_hidden * acted).astype(BF16)
+        rows_buf[at, :] = dot_f32(mid[at, :], up_full[...].reshape(up_shape), ((1,), (1,))).astype(
+            BF16
+        )
+        for n in range(half):
+
+            @pl.when(t == n)
+            def _():
+                core[n].start()
+
+        for n in range(half):
+
+            @pl.when(t == half + lax.rem(n + half - 1, half))
+            def _():
+                core[n].wait_recv()
+                total = rows_buf[n * rows : (n + 1) * rows, :].astype(F32) + core_buf[n].astype(F32)
+                rows_buf[n * rows : (n + 1) * rows, :] = total.astype(BF16)
+                if n > 0:
+                    far[n - 1].start()
+
+        return carry
+
+    lax.fori_loop(0, wide, block, 0)
+
+    step = min(256, size)
+    for n in range(size // step):
+        cut = slice(n * step, (n + 1) * step)
+        down_grad[cut, :] = dot_f32(hidden[:, cut], grads[...], ((0,), (0,))).astype(BF16)
+
+    @pl.when(is_end)
+    def _():
+        down_joined.start()
+
+    @pl.when(is_middle)
+    def _():
+        down_direct.start()
+
+    def up_rows(n, carry):
+        at = pl.ds(pl.multiple_of(n * 256, 256), 256)
+        up_grad[at, :] = dot_f32(normed[:, at], mid[...], ((0,), (0,))).astype(BF16)
+        return carry
+
+    lax.fori_loop(0, width // 256, up_rows, 0)
+
+    @pl.when(is_end)
+    def _():
+        up_joined.start()
+
+    @pl.when(is_middle)
+    def _():
+        up_direct.start()
+
+    backs = [
+        pltpu.make_async_copy(up_grad, up_grad_out, local.at[5 + half]),
+        pltpu.make_async_copy(down_grad, down_grad_out, local.at[6 + half]),
+        pltpu.make_async_copy(up_share(line[2]), up_src, local.at[7 + half]),
+        pltpu.make_async_copy(down_share(line[2]), down_src, local.at[8 + half]),
+    ]
+    for copy in backs:
+        copy.start()
+    gather.sent()
+
+    def branch(t, carry):
+        place = lax.rem(t + half, wide)
+        at = pl.ds(pl.multiple_of(place * rows, rows), rows)
+        normed[at, :] = dot_f32(hidden[at, :], down_full[...].reshape(down_shape)).astype(BF16)
+        for n in range(half):
+
+            @pl.when(t == n)
+            def _():
+                branch_core[n].start()
+
+        return carry
+
+    lax.fori_loop(0, wide, branch, 0)
+    for n in range(half):
+        branch_core[n].wait_recv()
+        total = normed[n * rows : (n + 1) * rows, :].astype(F32) + branch_buf[n].astype(F32)
+        branch_sum[n] = total.astype(BF16)
+
+    total = rows_buf[:rows, :].astype(F32)
+    for n in range(1, half):
+        far[n - 1].wait_recv()
+        total = total + far_buf[n - 1].astype(F32)
+    norm_sum[...] = total
+    for copy in backs:
+        copy.wait()
+    up_acc[...] = up_grad[:, pl.ds(pl.multiple_of(z * unit, unit), unit)]
+    down_acc[...] = down_grad[:, pl.ds(pl.multiple_of(z * part, part), part)]
+
+    @pl.when(is_middle)
+    def _():
+        down_joined.wait_recv()
+        down_src[...] = (down_src[...].astype(F32) + down_join[...].astype(F32)).astype(BF16)
+        up_joined.wait_recv()
+        up_src[...] = (up_src[...].astype(F32) + up_join[...].astype(F32)).astype(BF16)
+        down_direct.wait()
+        down_acc[...] = (down_acc[...].astype(F32) + down_mid[...].astype(F32)).astype(BF16)
+        up_direct.wait()
+        up_acc[...] = (up_acc[...].astype(F32) + up_mid[...].astype(F32)).astype(BF16)
+        for copy in (relay, middle, down_relay, down_middle):
+            copy.wait_send()
+
+    @pl.when(is_end)
+    def _():
+        down_joined.wait_send()
+        up_joined.wait_send()
+
+    for copy in passed + core + far + branch_core + [down_two, down_one]:
+        copy.wait_send()
+
+
+def second_part(normed, grad, far_grads, ups, down, collective_id):
+    rows, width = normed.shape
+    half = far_grads.shape[0] + 1
+    wide = 2 * half
+    wide_of_up, part_rows, mid_size = ups[0].shape
+    down_rows = down.shape[0]
+    size, unit, part = mid_size // 2, mid_size // 4, width // 4
+    steps = 6 + wide + 4 * half + 8
+    total = wide * rows
+    shape = jax.ShapeDtypeStruct
+    vmem = lambda *dims: pltpu.VMEM(dims, BF16)
+    return pl.pallas_call(
+        functools.partial(second_kernel, wide),
+        out_shape=[
+            shape((rows, width), F32), shape((half, rows, width), BF16),
+            shape((width, unit), BF16), shape((size, part), BF16),
+            shape((width, unit), BF16), shape((size, part), BF16),
+            shape((width, mid_size), BF16), shape((size, width), BF16),
+        ],
+        in_specs=[ANY] * 7,
+        out_specs=[VMEM] * 6 + [ANY] * 2,
+        scratch_shapes=[
+            vmem(total, width), vmem(total, width), vmem(wide, 4, part_rows, mid_size),
+            vmem(4, down_rows, width), vmem(total, size), vmem(total, mid_size), vmem(total, width),
+            vmem(half, rows, width), vmem(half - 1, rows, width), vmem(half, rows, width),
+            vmem(width, unit), vmem(width, unit), vmem(size, part), vmem(size, part),
+            vmem(width, mid_size), vmem(size, width),
+            DMA((steps,)), DMA((steps,)), DMA((9 + half,)),
+        ],
+        compiler_params=pltpu.CompilerParams(
+            collective_id=collective_id, has_side_effects=True, vmem_limit_bytes=63 * 2**20
+        ),
+    )(normed, grad, far_grads, *ups, down)
 
 
 def add_up(parts):
@@ -1224,28 +1791,6 @@
         up_parts = jnp.moveaxis(gate_up_weight.reshape(part_rows, 4, wide, unit), 2, 0)
         up_parts = up_parts.reshape(wide, part_rows, 4 * unit)
 
-    down_rows = down_weight.shape[0]
-    pairs = []
-    for i in range(wide * narrow):
-        to_wide = (i % (2 * wide)) // 2
-        to_narrow = i % 2 + 2 * (i // (2 * wide))
-        pairs.append((i, to_wide * narrow + to_narrow))
-    down_block = lax.ppermute(down_weight, ("wide", "narrow"), pairs)
-
-    slot_tokens, in_full, out_full, up_block, grad_far = gather_all(
-        tokens, in_parts, out_weight, up_parts, cotangent
-    )
-    slot_tokens = slot_tokens.reshape(slot, width)
-    in_full = in_full.reshape(width, columns)
-    out_full = out_full.reshape(width, width)
-
-    up_two = on_line(up_block, LINE_TWO)
-    up_one = on_line(up_block, LINE_ONE)
-
-    slot_floats = slot_tokens.astype(F32)
-    normed_one = (slot_floats * rms_factor(slot_floats) * gain_one).astype(BF16)
-    projected = dot_f32(normed_one, in_full)
-
     segments = segment_ids[0]
     joined = (segments[1:] == segments[:-1]).astype(F32)
     cont = jnp.concatenate([jnp.zeros((1,), F32), joined])
@@ -1253,10 +1798,6 @@
     own_bias = lax.dynamic_slice_in_dim(forget_bias, z * own_heads, own_heads)
     bias = jnp.broadcast_to(jnp.pad(own_bias, (0, LANES - own_heads))[None], (8, LANES))
     block = min(256, slot)
-    mixed, attended, logs = attention_forward(
-        projected, bias, cont, own_heads, head_size, block
-    )
-
     def row_block(ref, n):
         return ref.at[pl.ds(pl.multiple_of(n * rows, rows), rows), :]
 
@@ -1264,49 +1805,90 @@
         return ref.at[:, pl.ds(pl.multiple_of(n * own_width, LANES), own_width)]
 
     straight, diagonal = straight_steps(wide), diagonal_steps(wide)
-    mixed_rows, *grad_near = exchange(
-        mixed, row_block, column_block, (rows, width), straight, [cotangent] * len(straight), 1
-    )
-    grads = {0: cotangent}
-    grads.update({k: grad_near[n] for n, k in enumerate(straight)})
-    grads.update({k: grad_far[n] for n, k in enumerate(diagonal)})
-    grads = [grads[k] for k in range(0, wide, 2)]
-    down_block = follow(down_block, mixed_rows)
-    down_two = on_line(down_block, LINE_TWO)
-    down_one = on_line(down_block, LINE_ONE)
     inputs = tokens.astype(F32)
-    middle = inputs + dot_f32(mixed_rows, out_full)
-    normed_two = (middle * rms_factor(middle) * gain_two).astype(BF16)
-
     half = wide // 2
-    ups = [up_block] + [follow(piece, normed_two) for piece in (up_two, up_one)]
-    plane_normed, plane_grad, up_full, down_full = gather_rows(
-        normed_two, grads, ups, [down_block, down_two, down_one], 2
-    )
-    plane_normed = plane_normed.reshape(wide * rows, width)
-    plane_grad = plane_grad.reshape(wide * rows, width)
-    up_full = up_full.reshape(width, 4 * unit)
-    down_full = down_full.reshape(2 * unit, width)
-    hidden, gate_up_grad, norm_even, norm_odd, branch = feed_forward(
-        plane_normed, plane_grad, up_full, down_full, rows
-    )
-    grad_up_full = dot_f32(plane_normed, gate_up_grad, ((0,), (0,))).astype(BF16)
-    grad_down_full = dot_f32(hidden, plane_grad, ((0,), (0,))).astype(BF16)
-    if unit % LANES:
-        grouped = grad_up_full.reshape(width, 4, unit)
-        grad_up_full = jnp.pad(grouped, ((0, 0), (0, 0), (0, LANES - unit))).reshape(width, -1)
-    branch = branch.reshape(wide, rows, width)
-    fits = wide <= 8
-    norm_got = along_wide(norm_odd.reshape(half, rows, width), 1, wide)
-    (
-        grad_normed_two, branch_sum, up_src, down_src, up_one, down_one, up_acc, down_acc,
-    ) = middle_sums(
-        norm_even.reshape(half, rows, width), norm_got,
-        branch if fits else branch[:2, :16], grad_up_full, grad_down_full, 6,
-    )
-    if not fits:
-        received = along_wide(branch[half:], 1, wide)
-        branch_sum = (branch[:half].astype(F32) + received.astype(F32)).astype(BF16)
+    if aligned and part_rows % 16 == 0:
+        (
+            normed_one, in_full, out_full, projected, attended, logs, mixed_rows, middle, normed_two,
+            up_block, up_two, up_one, down_block, grad_got,
+        ) = first_part(
+            tokens, in_parts, out_weight, up_parts, cotangent, down_weight, gain_one, gain_two,
+            bias, cont, own_heads, head_size, block, 0,
+        )
+    else:
+        pairs = []
+        for i in range(wide * narrow):
+            to_wide = (i % (2 * wide)) // 2
+            to_narrow = i % 2 + 2 * (i // (2 * wide))
+            pairs.append((i, to_wide * narrow + to_narrow))
+        down_block = lax.ppermute(down_weight, ("wide", "narrow"), pairs)
+
+        slot_tokens, in_full, out_full, up_block, grad_far = gather_all(
+            tokens, in_parts, out_weight, up_parts, cotangent
+        )
+        slot_tokens = slot_tokens.reshape(slot, width)
+        in_full = in_full.reshape(width, columns)
+        out_full = out_full.reshape(width, width)
+
+        up_two = on_line(up_block, LINE_TWO)
+        up_one = on_line(up_block, LINE_ONE)
+
+        slot_floats = slot_tokens.astype(F32)
+        normed_one = (slot_floats * rms_factor(slot_floats) * gain_one).astype(BF16)
+        projected = dot_f32(normed_one, in_full)
+
+        mixed, attended, logs = attention_forward(
+            projected, bias, cont, own_heads, head_size, block
+        )
+
+        mixed_rows, *grad_near = exchange(
+            mixed, row_block, column_block, (rows, width), straight, [cotangent] * len(straight), 1
+        )
+        grads = {0: cotangent}
+        grads.update({k: grad_near[n] for n, k in enumerate(straight)})
+        grads.update({k: grad_far[n] for n, k in enumerate(diagonal)})
+        grads = [grads[k] for k in range(0, wide, 2)]
+        down_block = follow(down_block, mixed_rows)
+        down_two = on_line(down_block, LINE_TWO)
+        down_one = on_line(down_block, LINE_ONE)
+        middle = inputs + dot_f32(mixed_rows, out_full)
+        normed_two = (middle * rms_factor(middle) * gain_two).astype(BF16)
+
+    if aligned and part_rows % 16 == 0:
+        (
+            grad_normed_two, branch_sum, up_src, down_src, up_acc, down_acc, up_one, down_one,
+        ) = second_part(
+            normed_two, cotangent, grad_got, [up_block, up_two, up_one], down_block, 2
+        )
+    else:
+        ups = [up_block] + [follow(piece, normed_two) for piece in (up_two, up_one)]
+        plane_normed, plane_grad, up_full, down_full = gather_rows(
+            normed_two, grads, ups, [down_block, down_two, down_one], 2
+        )
+        plane_normed = plane_normed.reshape(wide * rows, width)
+        plane_grad = plane_grad.reshape(wide * rows, width)
+        up_full = up_full.reshape(width, 4 * unit)
+        down_full = down_full.reshape(2 * unit, width)
+        hidden, gate_up_grad, norm_even, norm_odd, branch = feed_forward(
+            plane_normed, plane_grad, up_full, down_full, rows
+        )
+        grad_up_full = dot_f32(plane_normed, gate_up_grad, ((0,), (0,))).astype(BF16)
+        grad_down_full = dot_f32(hidden, plane_grad, ((0,), (0,))).astype(BF16)
+        if unit % LANES:
+            grouped = grad_up_full.reshape(width, 4, unit)
+            grad_up_full = jnp.pad(grouped, ((0, 0), (0, 0), (0, LANES - unit))).reshape(width, -1)
+        branch = branch.reshape(wide, rows, width)
+        fits = wide <= 8
+        norm_got = along_wide(norm_odd.reshape(half, rows, width), 1, wide)
+        (
+            grad_normed_two, branch_sum, up_src, down_src, up_one, down_one, up_acc, down_acc,
+        ) = middle_sums(
+            norm_even.reshape(half, rows, width), norm_got,
+            branch if fits else branch[:2, :16], grad_up_full, grad_down_full, 6,
+        )
+        if not fits:
+            received = along_wide(branch[half:], 1, wide)
+            branch_sum = (branch[:half].astype(F32) + received.astype(F32)).astype(BF16)
     upstream = cotangent.astype(F32)
     grad_middle_norm, grad_gain_two = rms_back(middle, gain_two, grad_normed_two)
     grad_middle = upstream + grad_middle_norm
@@ -1327,8 +1909,8 @@
     wide_rows = width // wide
     out_part = dot_f32(mixed_rows, branch_one_grad, ((0,), (0,))).astype(BF16)
     late = lambda part: part.astype(F32)
-    up_part = (up_acc + late(up_one) + late(up_two)).astype(BF16)
-    grad_down = (down_acc + late(down_one) + late(down_two)).astype(BF16)
+    up_part = (late(up_acc) + late(up_one) + late(up_two)).astype(BF16)
+    grad_down = (late(down_acc) + late(down_one) + late(down_two)).astype(BF16)
     low_half, high_half = grad_down[:unit], grad_down[unit:]
     is_odd = lax.rem(w, 2) == 1
     first_send = jnp.where(is_odd, high_half, low_half)

time: 594 us -> 529 us (0.89)
  matrix products: 56.4 us -> 23.1 us
  starting transfers between devices: 22.2 us -> 3.99 us
  waiting for transfers between devices: 17.1 us -> 0.01 us
    dot_general x8 -> x4, matrix products: 56.4 us -> 23.1 us  [dot_f32(): lax.dot_general(left, right, (dims, ((), ())), preferred_element_type=F32)]
    pallas_call x2 -> x1, Pallas kernels: 50.3 us -> 20.1 us  [exchange(): pl.pallas_call(functools.partial(exchange_kernel, source, target, steps),...]
    pallas_call x5 -> x2, Pallas kernels: 234 us -> 263 us  [the longest x1 156 us: first_part(): pl.pallas_call(functools.partial(first_kernel, wide, heads, head_size, bl...]
    ppermute x6 -> x0, starting transfers between devices: 17.8 us -> none  [the longest x4 15.7 us: on_line(): return lax.ppermute(block, 'narrow', pairs)]
    ppermute x6 -> x0, waiting for transfers between devices: 17.1 us -> none  [the longest x4 17.1 us: on_line(): return lax.ppermute(block, 'narrow', pairs)]
    unnamed x108 -> x63, local copies, waits for them, and re-layouts: 16.4 us -> 12.1 us
  transfers between devices with their start and end apart: 8 -> 2, of which waited for: 2 -> 0; matrix products, arithmetic and copies ran while one was open for 9% -> 7% of each run, Pallas kernels for 10% -> 20%
where the time goes in v4:
time: 529 us; the launch traced here: 520 us
  Pallas kernels  445 us (84%)
  other arithmetic  24.6 us (5%)
  matrix products  23.1 us (4%)
  local copies, waits for them, and re-layouts  21.3 us (4%)
    pallas_call x1, Pallas kernels, first_part(): pl.pallas_call(functools.partial(first_kernel, wide, heads, head_size, bl...  156 us
    pallas_call x1, Pallas kernels, second_part(): pl.pallas_call(functools.partial(second_kernel, wide), out_shape=[shape((...  107 us
    pallas_call x1, Pallas kernels, last_transfers(): pl.pallas_call(functools.partial(last_kernel, wide, rows, own_width), out...  90.5 us
    pallas_call x1, Pallas kernels, attention_backward(): pl.pallas_call(functools.partial(backward_kernel, heads, head_size, block...  59.1 us
    dot_general x4, matrix products, dot_f32(): lax.dot_general(left, right, (dims, ((), ())), preferred_element_type=F32)  23.1 us
    pallas_call x1, Pallas kernels, exchange(): pl.pallas_call(functools.partial(exchange_kernel, source, target, steps),...  20.1 us
    unnamed x63, local copies, waits for them, and re-layouts  12.1 us
    pallas_call x1, Pallas kernels, total_of(): pl.pallas_call(functools.partial(total_kernel, wide), out_shape=jax.Shape...  11.4 us
  transfers between devices with their start and end apart: 2, of which 0 were waited for; matrix products, arithmetic and copies ran while one was open for 7% of the time, Pallas kernels for 20%

profile of v4, /device:TPU:0, one launch (start us, length us, event | category | flops | bytes accessed | tf_op | source)
XLA Modules:
  0.0 519.7 jit_solution(15297600321964814143)
XLA Ops:
  3.3 1.1 copy-done.1
  4.4 1.1 copy-done.11
  10.9 156.4 %shard_map.170 = (bf16[1024,1536]{1,0:T(8,128)(2,1)}, bf16[1536,1664]{1,0:T(8,128)(2,1)}, bf16[1536,1536]{1,0:T(8,128)(2,1)}, f32[1024,1664]{1,0:T(8,128)}, bf16...) custom-call(bf16[256,1536]{1,0:T(8,128)(2,1)} %x_ref.1, ...), custom_call_target="tpu_custom_call" | custom-call | tf_op jit(solution)/shard_map/pallas_call | solution.py:1433
  167.3 1.6 multiply_reduce_fusion.2
  168.9 106.9 %shard_map.171 = (f32[256,1536]{1,0:T(8,128)}, bf16[4,256,1536]{2,1,0:T(8,128)(2,1)}, bf16[1536,256]{1,0:T(8,128)(2,1)}, bf16[512,384]{1,0:T(8,128)(2,1)}, bf16[...) custom-call(bf16[256,1536]{1,0:T(8,128)(2,1)} %get-tuple-element.52.src, ...), custom_call_target="tpu_custom_call" | custom-call | tf_op jit(solution)/shard_map/pallas_call | solution.py:1705
  275.9 2.5 multiply_reduce_fusion
  278.4 3.2 multiply_add_fusion
  281.7 4.2 convolution_convert_fusion.3.refs_0_
  286.0 20.1 %shard_map.172 = (bf16[1024,384]{1,0:T(8,128)(2,1)S(1)}, bf16[256,1536]{1,0:T(8,128)(2,1)S(1)}, bf16[256,1536]{1,0:T(8,128)(2,1)S(1)}) custom-call(bf16[256,1536]{1,0:T(8,128)(2,1)S(1)} %convolution_convert_fusion.3.refs_0_, bf16[256,1536]{1,0:T(8,128)(2,1)S(1)} %get-tuple-element.95.refs_1_, bf16[256,1536]{1,0:T(8,128)(2,1)S(1)} %get-tuple-element.94.refs_2_), custom_call_target="tpu_custom_call" | custom-call | tf_op jit(solution)/shard_map/pallas_call | solution.py:296
  308.8 59.1 %shard_map.173 = (bf16[1024,1664]{1,0:T(8,128)(2,1)}, f32[8,128]{1,0:T(8,128)}, bf16[1536,256]{1,0:T(8,128)(2,1)}, bf16[512,384]{1,0:T(8,128)(2,1)}, bf16[1536,2...) custom-call(f32[1024,1664]{1,0:T(8,128)} %get-tuple-element.63.q_ref.k_ref.v_ref.gate_ref.small_ref, ...), custom_call_target="tpu_custom_call" | custom-call | tf_op jit(solution)/shard_map/pallas_call | solution.py:1160
  368.0 1.4 add_convert_fusion.1
  370.9 3.2 collective-permute-start
  374.2 3.8 convolution_convert_fusion.1
  378.3 7.7 %convolution_convert_fusion = bf16[1536,1664]{1,0:T(8,128)(2,1)} fusion(bf16[1024,1536]{1,0:T(8,128)(2,1)S(1)} %copy-done.26, bf16[1024,1664]{1,0:T(8,128)(2,1)S(1)} %copy-done.25), kind=kOutput, calls=%fused_computation | convolution fusion | flops 5237047296 | bytes 11665408 | tf_op jit(solution)/shard_map/dot_general | solution.py:20
  386.0 7.3 %convolution_convert_fusion.2.norm_ref = bf16[1024,1536]{1,0:T(8,128)(2,1)} fusion(bf16[1024,1664]{1,0:T(8,128)(2,1)S(1)} %copy-done.25, bf16[1536,1664]{1,0:T(8,128)(2,1)S(1)} %bitcast.55), kind=kOutput, calls=%fused_computation.2 | convolution fusion | flops 5236064256 | bytes 11665408 | tf_op jit(solution)/shard_map/dot_general | solution.py:20
  393.7 90.5 %shard_map.174 = (f32[256,1536]{1,0:T(8,128)S(1)}, bf16[4,192,512]{2,1,0:T(8,128)(2,1)S(1)}, f32[192,384]{1,0:T(8,128)S(1)}, bf16[192,2048]{1,0:T(8,128)(2,1)S(1)}, bf16[1,256,1536]{2,1,0:T(8,128)(2,1)S(1)}) custom-call(bf16[1024,1536]{1,0:T(8,128)(2,1)} %convolution_convert_fusion.2.norm_ref, bf16[8,192,1664]{2,1,0:T(8,128)(2,1)} %bitcast.49, ...), custom_call_target="tpu_custom_call" | custom-call | tf_op jit(solution)/shard_map/pallas_call | solution.py:764
  489.7 1.1 copy.24
  490.9 1.7 fusion.7
  494.0 11.4 %shard_map.175 = f32[32,128]{1,0:T(8,128)} custom-call(f32[32,128]{1,0:T(8,128)} %fusion.15.v_ref), custom_call_target="tpu_custom_call" | custom-call | tf_op jit(solution)/shard_map/pallas_call | solution.py:820
  505.4 1.2 slice.94
  506.6 1.3 convert_element_type.105
  508.6 2.4 dynamic-slice_convert_fusion
  511.0 5.0 fusion.6
  516.6 1.1 broadcast_select_fusion.3
  (98 shorter events, 22.9 us)
Async XLA Ops:
  0.6 9.0 %copy-start.23 = (f32[1536]{0:T(1024)S(1)}, f32[1536]{0:T(1024)}, u32[]{:S(2)}) copy-start(f32[1536]{0:T(1024)} %param.11) | copy-start | bytes 18436
  0.7 9.6 %copy-start.22 = (f32[1536]{0:T(1024)S(1)}, f32[1536]{0:T(1024)}, u32[]{:S(2)}) copy-start(f32[1536]{0:T(1024)} %param.15) | copy-start | bytes 18436
  3.3 1.1 copy-start.1
  4.4 1.1 copy-start.11
  275.8 2.5 copy-start.12
  275.8 2.5 copy-start.15
  278.4 3.2 copy-start.16
  308.8 59.2 %copy-start.21 = (bf16[512,384]{1,0:T(8,128)(2,1)S(1)}, bf16[512,384]{1,0:T(8,128)(2,1)}, u32[]{:S(2)}) copy-start(bf16[512,384]{1,0:T(8,128)(2,1)} %get-tuple-element.84) | copy-start | bytes 1179652
  367.9 6.2 %copy-start.13 = (f32[256,1536]{1,0:T(8,128)S(1)}, f32[256,1536]{1,0:T(8,128)}, u32[]{:S(2)}) copy-start(f32[256,1536]{1,0:T(8,128)} %multiply_add_fusion) | copy-start | bytes 4718596
  367.9 6.2 %copy-start.17 = (bf16[256,1536]{1,0:T(8,128)(2,1)S(1)}, bf16[256,1536]{1,0:T(8,128)(2,1)}, u32[]{:S(2)}) copy-start(bf16[256,1536]{1,0:T(8,128)(2,1)} %get-tuple-element.74) | copy-start | bytes 2359300
  370.2 146.4 %collective-permute-start.1 = (bf16[256,384]{1,0:T(8,128)(2,1)}, bf16[256,384]{1,0:T(8,128)(2,1)}, u32[]{:S(2)}, u32[]{:S(2)}) collective-permute-start(bf16[256,384]{1,0:T(8,128)(2,1)} %get-tuple-element.99), channel_id=1, source_target_pairs={{0,16},{4,0},{8,20},{12,4},{16,24},{20,8},{24,28},{28,12},{1,17},{... | collective-permute-start | bytes 589832 | tf_op jit(solution)/shard_map/ppermute | solution.py:1921
  370.9 145.6 %collective-permute-start = (bf16[256,384]{1,0:T(8,128)(2,1)}, bf16[256,384]{1,0:T(8,128)(2,1)}, u32[]{:S(2)}, u32[]{:S(2)}) collective-permute-start(bf16[256,384]{1,0:T(8,128)(2,1)} %get-tuple-element.98), channel_id=1, source_target_pairs={{0,0},{4,16},{8,4},{12,20},{16,8},{20,24},{24,12},{28,28},{1,1},{5... | collective-permute-start | bytes 589832 | tf_op jit(solution)/shard_map/ppermute | solution.py:1918
  374.2 3.9 copy-start.25
  374.2 4.1 copy-start.26
  374.2 11.8 %slice-start = ((s8[5111808]{0:T(1024)(128)(4,1)}), s8[4194304]{0:T(1024)(128)(4,1)S(1)}, s32[]{:S(2)}) async-start(s8[5111808]{0:T(1024)(128)(4,1)} %bitcast.54), calls=%async_computation | async-start | bytes 8388608
  378.3 7.7 %slice-start.1 = ((s8[5111808]{0:T(1024)(128)(4,1)}), s8[917504]{0:T(1024)(128)(4,1)S(1)}, s32[]{:S(2)}) async-start(s8[5111808]{0:T(1024)(128)(4,1)} %bitcast.54), calls=%async_computation.1 | async-start | bytes 1835008
  386.0 7.3 %copy-start.18 = (bf16[1536,256]{1,0:T(8,128)(2,1)S(1)}, bf16[1536,256]{1,0:T(8,128)(2,1)}, u32[]{:S(2)}) copy-start(bf16[1536,256]{1,0:T(8,128)(2,1)} %get-tuple-element.75) | copy-start | bytes 2359300
  386.0 7.3 %copy-start.19 = (bf16[1536,256]{1,0:T(8,128)(2,1)S(1)}, bf16[1536,256]{1,0:T(8,128)(2,1)}, u32[]{:S(2)}) copy-start(bf16[1536,256]{1,0:T(8,128)(2,1)} %get-tuple-element.77) | copy-start | bytes 2359300
  386.0 7.3 %copy-start.20 = (bf16[1536,256]{1,0:T(8,128)(2,1)S(1)}, bf16[1536,256]{1,0:T(8,128)(2,1)}, u32[]{:S(2)}) copy-start(bf16[1536,256]{1,0:T(8,128)(2,1)} %get-tuple-element.76) | copy-start | bytes 2359300
  393.6 93.7 %copy-start.14 = (bf16[256,1536]{1,0:T(8,128)(2,1)S(1)}, bf16[256,1536]{1,0:T(8,128)(2,1)}, u32[]{:S(2)}) copy-start(bf16[256,1536]{1,0:T(8,128)(2,1)} %x_ref.1) | copy-start | bytes 2359300
  489.0 17.6 %copy-start.3 = (bf16[192,2048]{1,0:T(8,128)(2,1)S(1)}, bf16[192,2048]{1,0:T(8,128)(2,1)}, u32[]{:S(2)}) copy-start(bf16[192,2048]{1,0:T(8,128)(2,1)} %copy-done.2) | copy-start | bytes 2359300
  507.9 3.0 copy-start.5
  507.9 3.0 copy-start.7
  511.0 5.0 copy-start.24
  (7 other events, 6.1 us)

commit v5 on v4

--- a/solution.py
+++ b/solution.py
@@ -594,16 +594,18 @@
 
 
 def last_kernel(
-    wide, rows, own_width, norm_ref, in_ref, out_ref, up_ref, branch_ref, norm_sum, in_got, out_sum,
-    up_got, branch_got,
-    join_buf, one_buf, mid_buf, two_buf, two_src, own_norm, in_core, in_own, in_far, in_sum,
-    out_core, out_own, out_far, out_low, out_buf, send, recv, local,
+    wide, rows, own_width, own_heads, norm_ref, in_ref, out_ref, up_parts, down_parts, branch_refs,
+    token_ref, middle_ref, grad_ref, gain_ref, small_ref, output, grad_tokens, grad_in, grad_out,
+    grad_up, grad_down, totals, join_buf, one_buf, mid_buf, two_buf, two_src, own_norm, norm_sum,
+    in_core, in_own, in_far, in_sum, in_got, out_own, out_buf, up_low, up_bufs, up_got, down_low,
+    down_bufs, down_got, branch_bufs, narrow_buf, wide_buf, sum_buf, send, recv, down_send, down_recv,
+    local,
 ):
     w, z = lax.axis_index("wide"), lax.axis_index("narrow")
     line = [flipped(z, k) for k in range(4)]
     half = wide // 2
-    unit = up_ref.shape[1]
-    wide_rows = up_got.shape[0]
+    unit = up_low.shape[1]
+    wide_rows, width = grad_in.shape[0], token_ref.shape[1]
     sender = Sender(send, recv)
     is_middle = (z == 1) | (z == 2)
     is_end = (z == 0) | (z == 3)
@@ -612,10 +614,10 @@
         return norm_ref.at[pl.ds(pl.multiple_of(n * rows, rows), rows), :]
 
     def out_columns(n):
-        return pl.ds(pl.multiple_of(n * own_width, LANES), own_width)
+        return out_ref.at[:, pl.ds(pl.multiple_of(n * own_width, LANES), own_width)]
 
     def up_rows(n):
-        return up_ref.at[pl.ds(pl.multiple_of(n * wide_rows, 16), wide_rows), :]
+        return up_low.at[pl.ds(pl.multiple_of(n * wide_rows, 16), wide_rows), :]
 
     def up_columns(n):
         return up_got.at[:, pl.ds(pl.multiple_of(n * unit, LANES), unit)]
@@ -624,10 +626,14 @@
         return in_sum.at[:, pl.ds(pl.multiple_of(n * own_width, LANES), own_width + LANES)]
 
     moves = [
-        (norm_block(line[2]), two_src), (norm_block(z), own_norm), (up_rows(w), up_columns(w)),
+        (norm_block(line[2]), two_src), (norm_block(z), own_norm), (out_columns(z), out_own),
     ]
     moves += [(in_ref.at[flipped(w, 2 * n)], in_own.at[n]) for n in range(half)]
-    moves += [(out_ref.at[flipped(w, 2 * n)], out_own.at[n]) for n in range(half)]
+    ffn_at = len(moves)
+    moves += [(ref, up_bufs.at[n]) for n, ref in enumerate(up_parts)]
+    moves += [(ref, down_bufs.at[n]) for n, ref in enumerate(down_parts)]
+    branch_at = len(moves)
+    moves += [(ref, branch_bufs.at[n]) for n, ref in enumerate(branch_refs)]
     own = [pltpu.make_async_copy(src, dst, local.at[n]) for n, (src, dst) in enumerate(moves)]
     for copy in own:
         copy.start()
@@ -636,43 +642,51 @@
         + [wide_device(flipped(w, k)) for k in range(1, wide)]
     )
     sibling = wide_device(flipped(w, 1))
-
-    def over_wide(ref, core_buf, own_buf, far_buf):
-        core = [
-            sender.plan(ref.at[flipped(w, 2 * n + 1)], core_buf.at[n], sibling)
-            for n in range(half)
-        ]
-        far = [
-            sender.plan(own_buf.at[n], far_buf.at[n - 1], wide_device(flipped(w, 2 * n)))
-            for n in range(1, half)
-        ]
-        return core, far
-
     joined = sender.plan(norm_block(line[3]), join_buf, narrow_device(line[1]))
     one = sender.plan(norm_block(line[1]), one_buf, narrow_device(line[1]))
     middle = sender.plan(norm_block(line[3]), mid_buf, narrow_device(line[3]))
     two = sender.plan(two_src, two_buf, narrow_device(line[2]))
-    in_steps = over_wide(in_ref, in_core, in_own, in_far)
-    out_steps = over_wide(out_ref, out_core, out_own, out_far)
+    core = [
+        sender.plan(in_ref.at[flipped(w, 2 * n + 1)], in_core.at[n], sibling) for n in range(half)
+    ]
+    far = [
+        sender.plan(in_own.at[n], in_far.at[n - 1], wide_device(flipped(w, 2 * n)))
+        for n in range(1, half)
+    ]
     sections = [
         sender.plan(section(line[k]), in_got.at[z], narrow_device(line[k])) for k in (2, 3, 1)
     ]
     outs = [
-        sender.plan(out_low.at[:, out_columns(line[k])], out_buf.at[k - 1], narrow_device(line[k]))
+        sender.plan(out_columns(line[k]), out_buf.at[k - 1], narrow_device(line[k]))
         for k in (1, 2, 3)
     ]
     ups = [
         sender.plan(up_rows(flipped(w, k)), up_columns(w), wide_device(flipped(w, k)))
         for k in range(1, wide)
     ]
-    branches = [
-        sender.plan(branch_ref.at[n], branch_got.at[n], wide_device(flipped(w, k)))
-        for n, k in enumerate(diagonal_steps(wide))
-    ]
+    first = [
+        sender.plan(sum_buf, narrow_buf.at[z], narrow_device(line[k])) for k in (1, 2, 3)
+    ]
+    second = [
+        sender.plan(sum_buf, wide_buf.at[w], wide_device(flipped(w, k))) for k in range(1, wide)
+    ]
+    parity, target = lax.rem(w, 2), lax.div(w, 2)
+    depth = down_low.shape[0] // 2
+    down_at = pl.ds(pl.multiple_of(parity * depth, 16), depth)
+    downs = []
+    for n in range(2):
+        owner = target + n * half
+        src, dst = down_low.at[pl.ds(n * depth, depth), :], down_got.at[down_at, :]
+        push = pltpu.make_async_remote_copy(
+            src_ref=src, dst_ref=dst, send_sem=down_send.at[n], recv_sem=down_recv.at[parity],
+            device_id=wide_device(owner), device_id_type=MESH,
+        )
+        stay = pltpu.make_async_copy(src, dst, local.at[len(moves) + 1 + n])
+        downs.append((owner == w, push, stay))
+
     order = list(range(1, half)) + [0]
-    for core in (in_steps[0], out_steps[0]):
-        for n in order:
-            core[n].start()
+    for n in order:
+        core[n].start()
 
     @pl.when(is_end)
     def _():
@@ -682,24 +696,13 @@
     def _():
         middle.start()
 
-    def between_cores(steps, core_buf, own_buf, first):
-        core, far = steps
-        for n in order:
-            core[n].wait_recv()
-            own[first + n].wait()
-            total = own_buf[n].astype(F32) + core_buf[n].astype(F32)
-            own_buf[n] = total.astype(BF16)
-            if n > 0:
-                far[n - 1].start()
-
-    def between_chips(steps, own_buf, far_buf):
-        total = own_buf[0].astype(F32)
-        for n in range(1, half):
-            steps[1][n - 1].wait_recv()
-            total = total + far_buf[n - 1].astype(F32)
-        return total.astype(BF16)
-
-    between_cores(in_steps, in_core, in_own, 3)
+    for n in order:
+        core[n].wait_recv()
+        own[3 + n].wait()
+        total = in_own[n].astype(F32) + in_core[n].astype(F32)
+        in_own[n] = total.astype(BF16)
+        if n > 0:
+            far[n - 1].start()
     own[0].wait()
 
     @pl.when(is_middle)
@@ -709,16 +712,32 @@
 
     two.start()
     one.start()
-    between_cores(out_steps, out_core, out_own, 3 + half)
-    for copy in branches:
+    for n in range(6):
+        own[ffn_at + n].wait()
+    up_low[...] = add_up([up_bufs[n] for n in range(3)]).astype(BF16)
+    down_low[...] = add_up([down_bufs[n] for n in range(3)]).astype(BF16)
+    for copy in ups:
         copy.start()
-    in_sum[...] = between_chips(in_steps, in_own, in_far)
-    mine = pltpu.make_async_copy(section(z), in_got.at[z], local.at[3 + 2 * half])
+    for stays, push, stay in downs:
+        pl.when(stays)(stay.start)
+        pl.when(jnp.logical_not(stays))(push.start)
+    up_got[:, pl.ds(pl.multiple_of(w * unit, LANES), unit)] = up_low[
+        pl.ds(pl.multiple_of(w * wide_rows, 16), wide_rows), :
+    ]
+    total = middle_ref[...]
+    for n in range(half):
+        own[branch_at + n].wait()
+        total = total + branch_bufs[n].astype(F32)
+    output[...] = total.astype(BF16)
+
+    total = in_own[0].astype(F32)
+    for n in range(1, half):
+        far[n - 1].wait_recv()
+        total = total + in_far[n - 1].astype(F32)
+    in_sum[...] = total.astype(BF16)
+    mine = pltpu.make_async_copy(section(z), in_got.at[z], local.at[len(moves)])
     mine.start()
-    for copy in sections:
-        copy.start()
-    out_low[...] = between_chips(out_steps, out_own, out_far)
-    for copy in outs + ups:
+    for copy in sections + outs:
         copy.start()
     own[1].wait()
     own[2].wait()
@@ -731,106 +750,126 @@
         norm_sum[...] += mid_buf[...].astype(F32)
 
     two.wait_recv()
-    norm_sum[...] += two_buf[...].astype(F32)
-    total = out_low[:, out_columns(z)].astype(F32)
-    for n in range(3):
-        outs[n].wait_recv()
-        total = total + out_buf[n].astype(F32)
-    out_sum[...] = total
-    for copy in sections + ups + branches:
-        copy.wait_recv()
-    mine.wait()
-
-    @pl.when(is_end)
-    def _():
-        joined.wait_send()
-
-    sent = [one, two] + in_steps[0] + in_steps[1] + out_steps[0] + out_steps[1]
-    for copy in sent + sections + outs + ups + branches:
-        copy.wait_send()
-
-
-def last_transfers(norm_part, in_part, out_part, up_part, branches, rows, own_width, collective_id):
-    wide, wide_rows, columns = in_part.shape
-    half = wide // 2
-    width = norm_part.shape[1]
-    unit = up_part.shape[1]
-    steps = 4 + 4 * half + 6 + 2 * wide
-    block = pltpu.VMEM((rows, width), BF16)
-    sums = lambda size: [
-        pltpu.VMEM((half, wide_rows, size), BF16), pltpu.VMEM((half, wide_rows, size), BF16),
-        pltpu.VMEM((half - 1, wide_rows, size), BF16), pltpu.VMEM((wide_rows, size), BF16),
-    ]
-    return pl.pallas_call(
-        functools.partial(last_kernel, wide, rows, own_width),
-        out_shape=[
-            jax.ShapeDtypeStruct((rows, width), F32),
-            jax.ShapeDtypeStruct((4, wide_rows, own_width + LANES), BF16),
-            jax.ShapeDtypeStruct((wide_rows, own_width), F32),
-            jax.ShapeDtypeStruct((wide_rows, wide * unit), BF16),
-            jax.ShapeDtypeStruct(branches.shape, BF16),
-        ],
-        in_specs=[ANY] * 5,
-        out_specs=[VMEM] * 5,
-        scratch_shapes=[
-            *[block] * 6, *sums(columns), *sums(width),
-            pltpu.VMEM((3, wide_rows, own_width), BF16),
-            DMA((steps,)), DMA((steps,)), DMA((4 + 2 * half,)),
-        ],
-        compiler_params=pltpu.CompilerParams(
-            collective_id=collective_id, has_side_effects=True, vmem_limit_bytes=48 * 2**20
-        ),
-    )(norm_part, in_part, out_part, up_part, branches)
-
-
-def total_kernel(wide, v_ref, out_ref, narrow_buf, wide_buf, sum_buf, send, recv):
-    w, z = lax.axis_index("wide"), lax.axis_index("narrow")
-    greet(
-        [narrow_device(flipped(z, k)) for k in (1, 2, 3)]
-        + [wide_device(flipped(w, k)) for k in range(1, wide)]
-    )
-    sender = Sender(send, recv)
-    first = [
-        sender.plan(v_ref, narrow_buf.at[z], narrow_device(flipped(z, k))) for k in (1, 2, 3)
-    ]
-    second = [
-        sender.plan(sum_buf, wide_buf.at[w], wide_device(flipped(w, k))) for k in range(1, wide)
-    ]
+    grads = norm_sum[...] + two_buf[...].astype(F32)
+    values = token_ref[...].astype(F32)
+    factor = rms_factor(values)
+    normed = values * factor
+    scaled = grads * gain_ref[0:1, :]
+    inner = jnp.mean(scaled * normed, axis=-1, keepdims=True)
+    grad_tokens[...] = grad_ref[...] + factor * (scaled - normed * inner)
+    narrow_buf[z] = small_ref[...]
+    narrow_buf[z, 0:1, :] = jnp.sum(grads * normed, axis=0, keepdims=True)
+    sum_buf[...] = narrow_buf[z]
     for copy in first:
         copy.start()
-    narrow_buf[z] = v_ref[...]
+
+    for copy in ups:
+        copy.wait_recv()
+    grad_up[...] = up_got[...].astype(F32)
+    for n, (stays, push, stay) in enumerate(downs):
+        pl.when(stays)(stay.wait)
+        pl.when(jnp.logical_not(stays))(push.wait_send)
+    for n in range(2):
+        source = lax.rem(2 * w + n, wide)
+        arrived = pltpu.make_async_remote_copy(
+            src_ref=down_low.at[pl.ds(0, depth), :], dst_ref=down_got.at[pl.ds(n * depth, depth), :],
+            send_sem=down_send.at[n], recv_sem=down_recv.at[n], device_id=sibling,
+            device_id_type=MESH,
+        )
+        pl.when(source != w)(arrived.wait_recv)
+    grad_down[...] = down_got[...].astype(F32)
+
     for copy in first:
         copy.wait()
     sum_buf[...] = narrow_buf[0] + narrow_buf[1] + narrow_buf[2] + narrow_buf[3]
     for copy in second:
         copy.start()
     wide_buf[w] = sum_buf[...]
+
+    total = out_own[...].astype(F32)
+    for n in range(3):
+        outs[n].wait_recv()
+        total = total + out_buf[n].astype(F32)
+    grad_out[...] = total
+    for copy in sections:
+        copy.wait_recv()
+    mine.wait()
+    row, lane = iota((LANES, LANES), 0), iota((LANES, LANES), 1)
+    last = jnp.zeros((wide_rows, LANES), F32)
+    for n in range(4):
+        group = lax.div(row, own_heads)
+        place = group * (4 * own_heads) + n * own_heads + row - group * own_heads
+        spot = ((lane == place) & (row < 3 * own_heads)).astype(BF16)
+        last = last + dot_f32(in_got[n, :, own_width:], spot)
+    after = jnp.where(z == 3, last, in_got[0, :, own_width:].astype(F32))
+    whole = jnp.concatenate(
+        [in_got[n, :, :own_width].astype(F32) for n in range(4)] + [after], axis=1
+    )
+    move = whole.shape[1] - (grad_in.shape[1] - width) * z
+    grad_in[...] = pltpu.roll(whole, lax.rem(move, whole.shape[1]), 1)[:, : grad_in.shape[1]]
+
     for copy in second:
         copy.wait()
     total = wide_buf[0]
     for n in range(1, wide):
         total = total + wide_buf[n]
-    out_ref[...] = total
-
-
-def total_of(values, wide, collective_id):
-    size = values.shape[0]
-    height = -(-size // (8 * LANES)) * 8
-    padded = jnp.pad(values, (0, height * LANES - size)).reshape(height, LANES)
-    total = pl.pallas_call(
-        functools.partial(total_kernel, wide),
-        out_shape=jax.ShapeDtypeStruct(padded.shape, F32),
-        in_specs=[VMEM],
-        out_specs=VMEM,
+    totals[...] = total
+
+    @pl.when(is_end)
+    def _():
+        joined.wait_send()
+
+    for copy in [one, two] + core + far + sections + outs + ups:
+        copy.wait_send()
+
+
+def grouped_last_kernel(wide, rows, own_width, own_heads, *refs):
+    half = wide // 2
+    last_kernel(
+        wide, rows, own_width, own_heads, *refs[:3], refs[3:6], refs[6:9], refs[9 : 9 + half],
+        *refs[9 + half :],
+    )
+
+
+def last_part(
+    norm_part, in_part, out_low, ups, downs, branches, tokens, middle, grad_middle, gain, small, own_width,
+    own_heads, shard, collective_id,
+):
+    wide, wide_rows, columns = in_part.shape
+    half = wide // 2
+    rows, width = tokens.shape
+    unit = ups[0].shape[1]
+    steps = 4 + 2 * half + 9 + 2 * wide
+    shape = jax.ShapeDtypeStruct
+    vmem = lambda *dims: pltpu.VMEM(dims, BF16)
+    return pl.pallas_call(
+        functools.partial(grouped_last_kernel, wide, rows, own_width, own_heads),
+        out_shape=[
+            shape((rows, width), BF16), shape((rows, width), F32), shape((wide_rows, shard), F32),
+            shape((wide_rows, own_width), F32), shape((wide_rows, wide * unit), F32),
+            shape(downs[0].shape, F32), shape(small.shape, F32),
+        ],
+        in_specs=[ANY] * (9 + half) + [VMEM] * 5,
+        out_specs=[VMEM] * 7,
         scratch_shapes=[
-            pltpu.VMEM((4,) + padded.shape, F32),
-            pltpu.VMEM((wide,) + padded.shape, F32),
-            pltpu.VMEM(padded.shape, F32),
-            DMA((wide + 2,)), DMA((wide + 2,)),
+            *[vmem(rows, width)] * 6, pltpu.VMEM((rows, width), F32),
+            vmem(half, wide_rows, columns), vmem(half, wide_rows, columns),
+            vmem(half - 1, wide_rows, columns), vmem(wide_rows, columns),
+            vmem(4, wide_rows, own_width + LANES), vmem(wide_rows, own_width),
+            vmem(3, wide_rows, own_width), vmem(*ups[0].shape), vmem(3, *ups[0].shape),
+            vmem(wide_rows, wide * unit), vmem(*downs[0].shape), vmem(3, *downs[0].shape),
+            vmem(*downs[0].shape), vmem(half, rows, width),
+            pltpu.VMEM((4,) + small.shape, F32), pltpu.VMEM((wide,) + small.shape, F32),
+            pltpu.VMEM(small.shape, F32),
+            DMA((steps,)), DMA((steps,)), DMA((2,)), DMA((2,)), DMA((12 + 2 * half,)),
         ],
-        compiler_params=pltpu.CompilerParams(collective_id=collective_id, has_side_effects=True),
-    )(padded)
-    return total.reshape(-1)[:size]
+        compiler_params=pltpu.CompilerParams(
+            collective_id=collective_id, has_side_effects=True, vmem_limit_bytes=60 * 2**20
+        ),
+    )(
+        norm_part, in_part, out_low, *ups, *downs, *branches, tokens, middle, grad_middle,
+        jnp.broadcast_to(gain[None], (8, width)), small,
+    )
 
 
 def rms_factor(values):
@@ -995,28 +1034,96 @@
 
 
 def backward_kernel(
-    heads, head_size, block, q_ref, k_ref, v_ref, gate_ref, small_ref, bias_ref, cont_ref,
-    att_ref, log_ref, grad_ref, up_src, down_src, up_one, down_one, out_ref, bias_grad_ref,
-    up_two_got, down_two_got, up_one_got, down_one_got, decay_scr, small_scr, dq_scr, send, recv,
+    heads, head_size, block, wide, *refs
 ):
+    q_ref, k_ref, v_ref, gate_ref, small_ref, bias_ref, cont_ref, att_ref, log_ref, grad_ref = refs[:10]
+    in_ref, normed_ref, up_src, down_src, up_one, down_one, part_ref, branch_ref = refs[10:18]
+    out_ref, bias_grad_ref, norm_ref, in_part_ref, part_sum = refs[18:23]
+    up_two_got, down_two_got, up_one_got, down_one_got, branch_got = refs[23:28]
+    decay_scr, small_scr, dq_scr, part_core, part_own, part_far, send, recv, local = refs[28:]
     pair = pl.program_id(0)
-    z = lax.axis_index("narrow")
+    pairs = heads * head_size // LANES
+    half = wide // 2
+    row_steps = out_ref.shape[0] // norm_ref.shape[0]
+    w, z = lax.axis_index("wide"), lax.axis_index("narrow")
     sender = Sender(send, recv)
+    one, two = flipped(z, 1), flipped(z, 2)
     copies = [
-        sender.plan(up_src, up_two_got, narrow_device(flipped(z, 2))),
-        sender.plan(down_src, down_two_got, narrow_device(flipped(z, 2))),
-        sender.plan(share_of(up_one, up_src, flipped(z, 1)), up_one_got, narrow_device(flipped(z, 1))),
-        sender.plan(
-            share_of(down_one, down_src, flipped(z, 1)), down_one_got, narrow_device(flipped(z, 1))
-        ),
+        sender.plan(up_src, up_two_got, narrow_device(two)),
+        sender.plan(down_src, down_two_got, narrow_device(two)),
+        sender.plan(share_of(up_one, up_src, one), up_one_got, narrow_device(one)),
+        sender.plan(share_of(down_one, down_src, one), down_one_got, narrow_device(one)),
+    ]
+    core = [
+        sender.plan(part_ref.at[flipped(w, 2 * n + 1)], part_core.at[n], wide_device(flipped(w, 1)))
+        for n in range(half)
+    ]
+    far = [
+        sender.plan(part_own.at[n], part_far.at[n - 1], wide_device(flipped(w, 2 * n)))
+        for n in range(1, half)
+    ]
+    branches = [
+        sender.plan(branch_ref.at[k // 2], branch_got.at[n], wide_device(flipped(w, k)))
+        for n, k in enumerate(diagonal_steps(wide))
+    ]
+    own = [
+        pltpu.make_async_copy(part_ref.at[flipped(w, 2 * n)], part_own.at[n], local.at[n])
+        for n in range(half)
     ]
 
     @pl.when(pair == 0)
     def _():
-        greet([narrow_device(flipped(z, 1)), narrow_device(flipped(z, 2))])
-        for copy in copies:
+        greet(
+            [narrow_device(one), narrow_device(two)]
+            + [wide_device(flipped(w, k)) for k in wide_steps(wide)]
+        )
+        for copy in copies + core + own + branches:
             copy.start()
 
+    @pl.when(pair == 1)
+    def _():
+        for n in range(half):
+            core[n].wait_recv()
+            own[n].wait()
+            part_own[n] = (part_own[n].astype(F32) + part_core[n].astype(F32)).astype(BF16)
+            if n > 0:
+                far[n - 1].start()
+
+    @pl.when(pair < pairs)
+    def _():
+        backward_pair(
+            pair, pairs, heads, head_size, block, q_ref, k_ref, v_ref, gate_ref, small_ref,
+            bias_ref, cont_ref, att_ref, log_ref, grad_ref, out_ref, bias_grad_ref, decay_scr,
+            small_scr, dq_scr,
+        )
+
+    @pl.when((pair >= pairs) & (pair < pairs + row_steps))
+    def _():
+        size = norm_ref.shape[0]
+        at = pl.ds(pl.multiple_of((pair - pairs) * size, size), size)
+        norm_ref[...] = dot_f32(out_ref[at, :], in_ref[...], ((1,), (1,))).astype(BF16)
+
+    @pl.when(pair >= pairs + row_steps)
+    def _():
+        in_part_ref[...] = dot_f32(normed_ref[...], out_ref[...], ((0,), (0,))).astype(BF16)
+
+    @pl.when(pair == pl.num_programs(0) - 1)
+    def _():
+        total = part_own[0].astype(F32)
+        for n in range(1, half):
+            far[n - 1].wait_recv()
+            total = total + part_far[n - 1].astype(F32)
+        part_sum[...] = total.astype(BF16)
+        for copy in copies + branches:
+            copy.wait()
+        for copy in core + far:
+            copy.wait_send()
+
+
+def backward_pair(
+    pair, pairs, heads, head_size, block, q_ref, k_ref, v_ref, gate_ref, small_ref, bias_ref, cont_ref,
+    att_ref, log_ref, grad_ref, out_ref, bias_grad_ref, decay_scr, small_scr, dq_scr,
+):
     cont = cont_ref[...]
     small_low = small_columns(small_ref, bias_ref)
     rows = cont.shape[0]
@@ -1110,7 +1217,7 @@
         + exact_dot(value_logit, collect(2 * heads + 2 * pair, head_size).astype(F32))
     )
 
-    @pl.when(pair == pl.num_programs(0) - 1)
+    @pl.when(pair == pairs - 1)
     def _():
         grads = small_scr[...]
         forget = running_sum(grads, True) * jax.nn.sigmoid(-small_low.astype(F32))
@@ -1119,19 +1226,17 @@
         bias_grad_ref[...] = jnp.broadcast_to(
             jnp.sum(result, axis=0, keepdims=True), bias_grad_ref.shape
         )
-        for copy in copies:
-            copy.wait()
 
 
 def attention_specs(rows, pairs):
     def block_at(group):
-        return pl.BlockSpec((rows, LANES), lambda p: (0, group * pairs + p))
+        return pl.BlockSpec((rows, LANES), lambda p: (0, group * pairs + jnp.minimum(p, pairs - 1)))
 
     def fixed(height, column=0):
         return pl.BlockSpec((height, LANES), lambda p: (0, column))
 
     base = [block_at(0), block_at(1), block_at(2), block_at(3), fixed(rows, 4 * pairs), fixed(8), fixed(rows)]
-    return base, pl.BlockSpec((rows, LANES), lambda p: (0, p))
+    return base, pl.BlockSpec((rows, LANES), lambda p: (0, jnp.minimum(p, pairs - 1)))
 
 
 def attention_forward(projected, bias, cont, heads, head_size, block):
@@ -1151,37 +1256,62 @@
 
 
 def attention_backward(
-    projected, bias, cont, attended, logs, grad, shares, heads, head_size, block, collective_id
+    projected, bias, cont, attended, logs, grad, in_full, normed_one, shares, out_part, branches, heads,
+    head_size, block, collective_id,
 ):
     rows = projected.shape[0]
+    width = normed_one.shape[1]
+    wide, wide_rows = out_part.shape[:2]
+    half = wide // 2
     pairs = heads * head_size // LANES
     base, own = attention_specs(rows, pairs)
     columns = 4 * heads * head_size + LANES
+    step = min(256, rows)
+    row_steps, in_steps = rows // step, width // 256
+    steps = 4 + 3 * wide
+    part = lambda count: pltpu.VMEM((count, wide_rows, width), BF16)
+    shape = jax.ShapeDtypeStruct
+
+    def later(first, count):
+        return lambda p: jnp.clip(p - first, 0, count - 1)
+
+    row_at, in_at = later(pairs, row_steps), later(pairs + row_steps, in_steps)
     return pl.pallas_call(
-        functools.partial(backward_kernel, heads, head_size, block),
-        grid=(pairs,),
-        in_specs=base + [own] * 3 + [ANY] * 4,
+        functools.partial(backward_kernel, heads, head_size, block, wide),
+        grid=(pairs + row_steps + in_steps,),
+        in_specs=base
+        + [own] * 3
+        + [
+            pl.BlockSpec(in_full.shape, lambda p: (0, 0), pipeline_mode=pl.Buffered(1)),
+            pl.BlockSpec((rows, 256), lambda p: (0, in_at(p))),
+        ]
+        + [ANY] * 6,
         out_specs=[
             pl.BlockSpec((rows, columns), lambda p: (0, 0)),
             pl.BlockSpec((8, LANES), lambda p: (0, 0)),
+            pl.BlockSpec((step, width), lambda p: (row_at(p), 0)),
+            pl.BlockSpec((256, columns), lambda p: (in_at(p), 0)),
+            pl.BlockSpec((wide_rows, width), lambda p: (0, 0)),
         ]
-        + [ANY] * 4,
+        + [ANY] * 5,
         out_shape=[
-            jax.ShapeDtypeStruct((rows, columns), BF16),
-            jax.ShapeDtypeStruct((8, LANES), F32),
-        ]
-        + [jax.ShapeDtypeStruct(share.shape, BF16) for share in shares[:2] * 2],
+            shape((rows, columns), BF16), shape((8, LANES), F32), shape((rows, width), BF16),
+            shape((width, columns), BF16), shape((wide_rows, width), BF16),
+            *[shape(share.shape, BF16) for share in shares[:2] * 2],
+            shape((len(diagonal_steps(wide)),) + branches.shape[1:], BF16),
+        ],
         scratch_shapes=[
-            pltpu.VMEM((rows, LANES), F32),
-            pltpu.VMEM((rows, LANES), F32),
-            pltpu.VMEM((rows, 2 * LANES), F32),
-            DMA((4,)),
-            DMA((4,)),
+            pltpu.VMEM((rows, LANES), F32), pltpu.VMEM((rows, LANES), F32),
+            pltpu.VMEM((rows, 2 * LANES), F32), part(half), part(half), part(half - 1),
+            DMA((steps,)), DMA((steps,)), DMA((half,)),
         ],
         compiler_params=pltpu.CompilerParams(
-            collective_id=collective_id, has_side_effects=True, vmem_limit_bytes=56 * 2**20
+            collective_id=collective_id, has_side_effects=True, vmem_limit_bytes=60 * 2**20
         ),
-    )(*([projected] * 5), bias, cont, attended, logs, grad, *shares)
+    )(
+        *([projected] * 5), bias, cont, attended, logs, grad, in_full, normed_one, *shares, out_part,
+        branches,
+    )
 
 
 def first_kernel(
@@ -1899,75 +2029,39 @@
         [branch_sum[k // 2] for k in straight], 3,
     )
 
-    projected_grad, bias_grad, up_two, down_two, up_one, down_one = attention_backward(
-        projected, bias, cont, attended, logs, slot_grad, [up_src, down_src, up_one, down_one],
-        own_heads, head_size, block, 7,
-    )
-    norm_part = dot_f32(projected_grad, in_full, ((1,), (1,))).astype(BF16)
-    in_part = dot_f32(normed_one, projected_grad, ((0,), (0,))).astype(BF16)
-
     wide_rows = width // wide
     out_part = dot_f32(mixed_rows, branch_one_grad, ((0,), (0,))).astype(BF16)
-    late = lambda part: part.astype(F32)
-    up_part = (late(up_acc) + late(up_one) + late(up_two)).astype(BF16)
-    grad_down = (late(down_acc) + late(down_one) + late(down_two)).astype(BF16)
-    low_half, high_half = grad_down[:unit], grad_down[unit:]
-    is_odd = lax.rem(w, 2) == 1
-    first_send = jnp.where(is_odd, high_half, low_half)
-    second_send = jnp.where(is_odd, low_half, high_half)
-    first_got = lax.ppermute(
-        first_send, "wide", [(i, i // 2 + (half if i % 2 else 0)) for i in range(wide)]
-    )
-    second_got = lax.ppermute(
-        second_send, "wide", [(i, i // 2 + (0 if i % 2 else half)) for i in range(wide)]
-    )
-    norm_sum, got, grad_out, grad_up, branch_far = last_transfers(
-        norm_part, in_part.reshape(wide, wide_rows, columns),
-        out_part.reshape(wide, wide_rows, width), up_part,
-        jnp.stack([branch_sum[k // 2] for k in diagonal]), rows, own_width, 4,
-    )
-    branch_far = [branch_far[n] for n in range(len(diagonal))]
-    output = (middle + add_up([branch_sum[0]] + branch_near + branch_far)).astype(BF16)
+    (
+        unused, bias_grad, norm_part, in_part, out_low, up_two, down_two, up_one, down_one,
+        branch_far,
+    ) = attention_backward(
+        projected, bias, cont, attended, logs, slot_grad, in_full, normed_one,
+        [up_src, down_src, up_one, down_one], out_part.reshape(wide, wide_rows, width), branch_sum,
+        own_heads, head_size, block, 7,
+    )
+    branches = [branch_sum[0]] + branch_near + [branch_far[n] for n in range(len(diagonal))]
+    all_bias = lax.dynamic_update_slice(
+        jnp.zeros((width,), F32), bias_grad[0, :own_heads], (z * own_heads,)
+    )
+    small = jnp.stack([jnp.zeros((width,), F32), grad_gain_two, all_bias])
+    small = jnp.pad(small, ((0, 5), (0, 0)))
+    low = lambda part: part.astype(BF16)
+    output, grad_tokens, grad_in, grad_out, grad_up, grad_down, totals = last_part(
+        norm_part, in_part.reshape(wide, wide_rows, columns), out_low, [low(up_acc), up_one, up_two],
+        [low(down_acc), down_one, down_two], branches, tokens, middle, grad_middle, gain_one, small,
+        own_width, own_heads, (base + 3 * heads) // narrow, 4,
+    )
     if not aligned:
         grad_up = grad_up.reshape(wide_rows, wide, LANES)[:, :, :unit]
         grad_up = grad_up.reshape(wide_rows, wide * unit)
-    first_got, second_got = follow(first_got, norm_sum), follow(second_got, norm_sum)
-    grad_up = grad_up.astype(F32)
-    grad_inputs, grad_gain_one = rms_back(inputs, gain_one, norm_sum)
-    grad_tokens = grad_middle + grad_inputs
-    in_low = w < half
-    grad_down = jnp.concatenate(
-        [
-            jnp.where(in_low, first_got, second_got),
-            jnp.where(in_low, second_got, first_got),
-        ],
-        axis=0,
-    ).astype(F32)
-
-    extra = 3 * heads
-    section = jnp.concatenate([got[n, :, :own_width] for n in range(narrow)], axis=1)
-    small_all = jnp.stack([got[n, :, own_width : own_width + 3 * own_heads] for n in range(narrow)])
-    small_all = small_all.reshape(narrow, wide_rows, 3, own_heads)
-    small_all = jnp.transpose(small_all, (1, 2, 0, 3)).reshape(wide_rows, extra)
-    next_first = got[0, :, own_width : own_width + extra]
-    tail = jnp.where(z == narrow - 1, small_all, next_first)
-    joined_columns = jnp.concatenate([section, tail], axis=1)
-    shard = (base + extra) // narrow
-    grad_in = lax.dynamic_slice_in_dim(joined_columns, z * (shard - width), shard, 1).astype(F32)
-
-    all_bias = lax.dynamic_update_slice(
-        jnp.zeros((heads,), F32), bias_grad[0, :own_heads], (z * own_heads,)
-    )
-    packed = jnp.concatenate([grad_gain_one, grad_gain_two, all_bias])
-    packed = total_of(packed, wide, 5)
     return (
         output,
         grad_tokens,
-        packed[:width],
+        totals[0],
         grad_in,
-        packed[2 * width :],
+        totals[2, :heads],
         grad_out,
-        packed[width : 2 * width],
+        totals[1],
         grad_up,
         grad_down,
     )

time: 529 us -> 492 us (0.930)
  other arithmetic: 24.6 us -> 5 us
  matrix products: 23.1 us -> 4.99 us
    dot_general x4 -> x2, matrix products: 23.1 us -> 4.99 us  [dot_f32(): lax.dot_general(left, right, (dims, ((), ())), preferred_element_type=F32)]
    convert_element_type x5 -> x0, other arithmetic: 6.31 us -> none  [the longest x1 2.36 us: on_device(): lax.dynamic_slice_in_dim(joined_columns, z * (shard - width), shard, 1)]
    unnamed x63 -> x52, local copies, waits for them, and re-layouts: 12.1 us -> 16.4 us
    pallas_call x2 -> x1, Pallas kernels: 102 us -> 100 us  [last_part(): pl.pallas_call(functools.partial(grouped_last_kernel, wide, rows, own_wid...]
  transfers between devices with their start and end apart: 2 -> 0, of which waited for: 0 -> 0; matrix products, arithmetic and copies ran while one was open for 7% -> 0% of each run, Pallas kernels for 20% -> 0%
where the time goes in v5:
time: 492 us; the launch traced here: 484 us
  Pallas kernels  447 us (91%)
  local copies, waits for them, and re-layouts  25.6 us (5%)
  other arithmetic  5 us (1%)
  matrix products  4.99 us (1%)
    pallas_call x1, Pallas kernels, first_part(): pl.pallas_call(functools.partial(first_kernel, wide, heads, head_size, bl...  156 us
    pallas_call x1, Pallas kernels, second_part(): pl.pallas_call(functools.partial(second_kernel, wide), out_shape=[shape((...  107 us
    pallas_call x1, Pallas kernels, last_part(): pl.pallas_call(functools.partial(grouped_last_kernel, wide, rows, own_wid...  100 us
    pallas_call x1, Pallas kernels, attention_backward(): pl.pallas_call(functools.partial(backward_kernel, heads, head_size, block...  62.6 us
    pallas_call x1, Pallas kernels, exchange(): pl.pallas_call(functools.partial(exchange_kernel, source, target, steps),...  19.9 us
    unnamed x52, local copies, waits for them, and re-layouts  16.4 us

profile of v5, /device:TPU:0, one launch (start us, length us, event | category | flops | bytes accessed | tf_op | source)
XLA Modules:
  0.0 483.6 jit_solution(8118152667569292584)
XLA Ops:
  3.0 1.1 copy-done.4
  4.2 1.1 copy-done.6
  6.0 0.9 copy-done.3
  7.9 1.0 broadcast_in_dim.11.cont_ref.refs_6_
  10.2 156.4 %shard_map.170 = (bf16[1024,1536]{1,0:T(8,128)(2,1)}, bf16[1536,1664]{1,0:T(8,128)(2,1)}, bf16[1536,1536]{1,0:T(8,128)(2,1)}, f32[1024,1664]{1,0:T(8,128)}, bf16...) custom-call(bf16[256,1536]{1,0:T(8,128)(2,1)} %refs_13_.1, ...), custom_call_target="tpu_custom_call" | custom-call | tf_op jit(solution)/shard_map/pallas_call | solution.py:1563
  166.6 106.8 %shard_map.171 = (f32[256,1536]{1,0:T(8,128)}, bf16[4,256,1536]{2,1,0:T(8,128)(2,1)}, bf16[1536,256]{1,0:T(8,128)(2,1)}, bf16[512,384]{1,0:T(8,128)(2,1)}, bf16[...) custom-call(bf16[256,1536]{1,0:T(8,128)(2,1)} %get-tuple-element.58.src, ...), custom_call_target="tpu_custom_call" | custom-call | tf_op jit(solution)/shard_map/pallas_call | solution.py:1835
  273.5 1.7 multiply_reduce_fusion.2
  275.3 2.0 multiply_reduce_fusion
  278.6 3.6 convolution_convert_fusion
  282.2 1.4 convolution_convert_fusion.1.refs_0_
  284.1 1.0 slice_bitcast_fusion
  285.1 19.9 %shard_map.172 = (bf16[1024,384]{1,0:T(8,128)(2,1)S(1)}, bf16[256,1536]{1,0:T(8,128)(2,1)S(1)}, bf16[256,1536]{1,0:T(8,128)(2,1)S(1)}) custom-call(bf16[256,1536]{1,0:T(8,128)(2,1)S(1)} %convolution_convert_fusion.1.refs_0_, bf16[256,1536]{1,0:T(8,128)(2,1)S(1)} %get-tuple-element.101.refs_1_, bf16[256,1536]{1,0:T(8,128)(2,1)S(1)} %get-tuple-element.100.refs_2_), custom_call_target="tpu_custom_call" | custom-call | tf_op jit(solution)/shard_map/pallas_call | solution.py:296
  305.0 0.9 copy-done
  305.9 0.9 copy-done.1
  306.8 0.9 copy-done.2
  307.7 62.6 %shard_map.173 = (bf16[1024,1664]{1,0:T(8,128)(2,1)}, f32[8,128]{1,0:T(8,128)}, bf16[1024,1536]{1,0:T(8,128)(2,1)}, bf16[1536,1664]{1,0:T(8,128)(2,1)}, bf16[192...) custom-call(f32[1024,1664]{1,0:T(8,128)} %get-tuple-element.54.refs_, ...), custom_call_target="tpu_custom_call" | custom-call | tf_op jit(solution)/shard_map/pallas_call | solution.py:1279
  371.7 100.1 %shard_map.174 = (bf16[256,1536]{1,0:T(8,128)(2,1)}, f32[256,1536]{1,0:T(8,128)}, f32[192,1554]{1,0:T(8,128)}, f32[192,384]{1,0:T(8,128)}, f32[192,2048]{1,0:T(8...) custom-call(bf16[1024,1536]{1,0:T(8,128)(2,1)} %get-tuple-element.75.refs_0_, bf16[8,192,1664]{2,1,0:T(8,128)(2,1)} %bitcast.18, ...), custom_call_target="tpu_custom_call" | custom-call | tf_op jit(solution)/shard_map/pallas_call | solution.py:845
  471.9 1.6 slice_reduce_fusion
  473.4 1.2 slice_bitcast_fusion.3
  474.6 2.1 copy.31
  476.7 1.1 copy.32
  478.6 1.0 copy.33
  480.6 1.1 copy.35
  482.2 0.9 copy.36
  (65 shorter events, 10.9 us)
Async XLA Ops:
  0.6 7.1 %copy-start.19 = (s32[1,1024]{1,0:T(1,128)S(1)}, s32[1,1024]{1,0:T(1,128)}, u32[]{:S(2)}) copy-start(s32[1,1024]{1,0:T(1,128)} %param.18) | copy-start | bytes 12292
  0.7 8.3 %copy-start.20 = (f32[1536]{0:T(1024)S(1)}, f32[1536]{0:T(1024)}, u32[]{:S(2)}) copy-start(f32[1536]{0:T(1024)} %param.11) | copy-start | bytes 18436
  0.7 8.9 %copy-start.18 = (f32[1536]{0:T(1024)S(1)}, f32[1536]{0:T(1024)}, u32[]{:S(2)}) copy-start(f32[1536]{0:T(1024)} %param.15) | copy-start | bytes 18436
  3.0 1.1 copy-start.4
  4.2 1.1 copy-start.6
  6.0 0.9 copy-start.3
  6.9 0.8 copy-start.5
  273.5 1.9 copy-start.7
  275.3 2.0 copy-start.10
  275.3 2.1 copy-start.11
  277.5 1.1 copy-start.12
  277.5 4.7 slice-start
  277.9 4.3 copy-start.8
  278.6 3.6 slice-start.1
  282.2 1.9 copy-start.9
  305.0 0.9 copy-start
  305.9 0.9 copy-start.1
  306.8 0.9 copy-start.2
  471.9 4.8 %copy-start.14 = (f32[256,1536]{1,0:T(8,128)S(1)}, f32[256,1536]{1,0:T(8,128)}, u32[]{:S(2)}) copy-start(f32[256,1536]{1,0:T(8,128)} %get-tuple-element.112) | copy-start | bytes 4718596
  476.7 1.9 copy-start.15
  478.6 1.1 copy-start.17
  478.6 2.0 copy-start.13
  480.6 1.7 copy-start.16

commit v6 on v5

--- a/solution.py
+++ b/solution.py
@@ -13,7 +13,7 @@
 BF16 = jnp.bfloat16
 LANES = 128
 EXACT = lax.Precision.HIGHEST
-ANY = pl.BlockSpec(memory_space=pl.ANY)
+ANY = pl.BlockSpec(memory_space=pltpu.HBM)
 
 
 def dot_f32(left, right, dims=((1,), (0,))):
@@ -594,11 +594,10 @@
 
 
 def last_kernel(
-    wide, rows, own_width, own_heads, norm_ref, in_ref, out_ref, up_parts, down_parts, branch_refs,
-    token_ref, middle_ref, grad_ref, gain_ref, small_ref, output, grad_tokens, grad_in, grad_out,
-    grad_up, grad_down, totals, join_buf, one_buf, mid_buf, two_buf, two_src, own_norm, norm_sum,
-    in_core, in_own, in_far, in_sum, in_got, out_own, out_buf, up_low, up_bufs, up_got, down_low,
-    down_bufs, down_got, branch_bufs, narrow_buf, wide_buf, sum_buf, send, recv, down_send, down_recv,
+    wide, rows, own_width, own_heads, norm_ref, in_ref, up_parts, down_parts, branch_refs, token_ref,
+    middle_ref, grad_ref, gain_ref, small_ref, output, grad_tokens, grad_in, up_got, down_got, totals, join_buf, one_buf, mid_buf, two_buf, two_src, own_norm, norm_sum,
+    in_core, in_own, in_far, in_sum, in_got, after_got, tail_buf, up_low, up_bufs, down_low,
+    down_bufs, branch_bufs, narrow_buf, wide_buf, sum_buf, send, recv, down_send, down_recv,
     local,
 ):
     w, z = lax.axis_index("wide"), lax.axis_index("narrow")
@@ -613,9 +612,6 @@
     def norm_block(n):
         return norm_ref.at[pl.ds(pl.multiple_of(n * rows, rows), rows), :]
 
-    def out_columns(n):
-        return out_ref.at[:, pl.ds(pl.multiple_of(n * own_width, LANES), own_width)]
-
     def up_rows(n):
         return up_low.at[pl.ds(pl.multiple_of(n * wide_rows, 16), wide_rows), :]
 
@@ -623,11 +619,12 @@
         return up_got.at[:, pl.ds(pl.multiple_of(n * unit, LANES), unit)]
 
     def section(n):
-        return in_sum.at[:, pl.ds(pl.multiple_of(n * own_width, LANES), own_width + LANES)]
-
-    moves = [
-        (norm_block(line[2]), two_src), (norm_block(z), own_norm), (out_columns(z), out_own),
-    ]
+        return in_sum.at[:, pl.ds(pl.multiple_of(n * own_width, LANES), own_width)]
+
+    def after_section(n):
+        return in_sum.at[:, pl.ds(pl.multiple_of((n + 1) * own_width, LANES), LANES)]
+
+    moves = [(norm_block(line[2]), two_src), (norm_block(z), own_norm)]
     moves += [(in_ref.at[flipped(w, 2 * n)], in_own.at[n]) for n in range(half)]
     ffn_at = len(moves)
     moves += [(ref, up_bufs.at[n]) for n, ref in enumerate(up_parts)]
@@ -656,9 +653,12 @@
     sections = [
         sender.plan(section(line[k]), in_got.at[z], narrow_device(line[k])) for k in (2, 3, 1)
     ]
-    outs = [
-        sender.plan(out_columns(line[k]), out_buf.at[k - 1], narrow_device(line[k]))
-        for k in (1, 2, 3)
+    afters = [
+        (
+            (z == 0) | (line[k] == 3), (line[k] == 0) | (z == 3),
+            sender.plan(after_section(line[k]), after_got.at[z], narrow_device(line[k])),
+        )
+        for k in (2, 3, 1)
     ]
     ups = [
         sender.plan(up_rows(flipped(w, k)), up_columns(w), wide_device(flipped(w, k)))
@@ -698,7 +698,7 @@
 
     for n in order:
         core[n].wait_recv()
-        own[3 + n].wait()
+        own[2 + n].wait()
         total = in_own[n].astype(F32) + in_core[n].astype(F32)
         in_own[n] = total.astype(BF16)
         if n > 0:
@@ -737,10 +737,7 @@
     in_sum[...] = total.astype(BF16)
     mine = pltpu.make_async_copy(section(z), in_got.at[z], local.at[len(moves)])
     mine.start()
-    for copy in sections + outs:
-        copy.start()
     own[1].wait()
-    own[2].wait()
     one.wait_recv()
     norm_sum[...] = own_norm[...].astype(F32) + one_buf[...].astype(F32)
 
@@ -750,6 +747,11 @@
         norm_sum[...] += mid_buf[...].astype(F32)
 
     two.wait_recv()
+    for copy in sections:
+        copy.start()
+    for sends, gets, copy in afters:
+        pl.when(sends)(copy.start)
+    after_got[z] = after_section(z)[...]
     grads = norm_sum[...] + two_buf[...].astype(F32)
     values = token_ref[...].astype(F32)
     factor = rms_factor(values)
@@ -765,7 +767,6 @@
 
     for copy in ups:
         copy.wait_recv()
-    grad_up[...] = up_got[...].astype(F32)
     for n, (stays, push, stay) in enumerate(downs):
         pl.when(stays)(stay.wait)
         pl.when(jnp.logical_not(stays))(push.wait_send)
@@ -777,7 +778,6 @@
             device_id_type=MESH,
         )
         pl.when(source != w)(arrived.wait_recv)
-    grad_down[...] = down_got[...].astype(F32)
 
     for copy in first:
         copy.wait()
@@ -786,25 +786,28 @@
         copy.start()
     wide_buf[w] = sum_buf[...]
 
-    total = out_own[...].astype(F32)
-    for n in range(3):
-        outs[n].wait_recv()
-        total = total + out_buf[n].astype(F32)
-    grad_out[...] = total
     for copy in sections:
         copy.wait_recv()
     mine.wait()
-    row, lane = iota((LANES, LANES), 0), iota((LANES, LANES), 1)
-    last = jnp.zeros((wide_rows, LANES), F32)
-    for n in range(4):
-        group = lax.div(row, own_heads)
-        place = group * (4 * own_heads) + n * own_heads + row - group * own_heads
-        spot = ((lane == place) & (row < 3 * own_heads)).astype(BF16)
-        last = last + dot_f32(in_got[n, :, own_width:], spot)
-    after = jnp.where(z == 3, last, in_got[0, :, own_width:].astype(F32))
-    whole = jnp.concatenate(
-        [in_got[n, :, :own_width].astype(F32) for n in range(4)] + [after], axis=1
-    )
+    for sends, gets, copy in afters:
+        pl.when(gets)(copy.wait_recv)
+
+    @pl.when(z == 3)
+    def _():
+        row, lane = iota((LANES, LANES), 0), iota((LANES, LANES), 1)
+        last = jnp.zeros((wide_rows, LANES), F32)
+        for n in range(4):
+            group = lax.div(row, own_heads)
+            place = group * (4 * own_heads) + n * own_heads + row - group * own_heads
+            spot = ((lane == place) & (row < 3 * own_heads)).astype(BF16)
+            last = last + dot_f32(after_got[n], spot)
+        tail_buf[...] = last
+
+    @pl.when(z != 3)
+    def _():
+        tail_buf[...] = after_got[0].astype(F32)
+
+    whole = jnp.concatenate([in_got[n].astype(F32) for n in range(4)] + [tail_buf[...]], axis=1)
     move = whole.shape[1] - (grad_in.shape[1] - width) * z
     grad_in[...] = pltpu.roll(whole, lax.rem(move, whole.shape[1]), 1)[:, : grad_in.shape[1]]
 
@@ -819,46 +822,48 @@
     def _():
         joined.wait_send()
 
-    for copy in [one, two] + core + far + sections + outs + ups:
+    for sends, gets, copy in afters:
+        pl.when(sends)(copy.wait_send)
+    for copy in [one, two] + core + far + sections + ups:
         copy.wait_send()
 
 
 def grouped_last_kernel(wide, rows, own_width, own_heads, *refs):
-    half = wide // 2
+    own, near, far = refs[8:11]
+    branches = [own.at[0]]
+    branches += [near.at[n] for n in range(near.shape[0])] + [far.at[n] for n in range(far.shape[0])]
     last_kernel(
-        wide, rows, own_width, own_heads, *refs[:3], refs[3:6], refs[6:9], refs[9 : 9 + half],
-        *refs[9 + half :],
+        wide, rows, own_width, own_heads, *refs[:2], refs[2:5], refs[5:8], branches, *refs[11:],
     )
 
 
 def last_part(
-    norm_part, in_part, out_low, ups, downs, branches, tokens, middle, grad_middle, gain, small, own_width,
-    own_heads, shard, collective_id,
+    norm_part, in_part, ups, downs, branches, tokens, middle, grad_middle, gain, small, own_width, own_heads,
+    shard, collective_id,
 ):
     wide, wide_rows, columns = in_part.shape
     half = wide // 2
     rows, width = tokens.shape
     unit = ups[0].shape[1]
-    steps = 4 + 2 * half + 9 + 2 * wide
+    steps = 4 + 2 * half + 12 + 2 * wide
     shape = jax.ShapeDtypeStruct
     vmem = lambda *dims: pltpu.VMEM(dims, BF16)
     return pl.pallas_call(
         functools.partial(grouped_last_kernel, wide, rows, own_width, own_heads),
         out_shape=[
             shape((rows, width), BF16), shape((rows, width), F32), shape((wide_rows, shard), F32),
-            shape((wide_rows, own_width), F32), shape((wide_rows, wide * unit), F32),
-            shape(downs[0].shape, F32), shape(small.shape, F32),
+            shape((wide_rows, wide * unit), BF16), shape(downs[0].shape, BF16),
+            shape(small.shape, F32),
         ],
-        in_specs=[ANY] * (9 + half) + [VMEM] * 5,
-        out_specs=[VMEM] * 7,
+        in_specs=[ANY] * 11 + [VMEM] * 5,
+        out_specs=[VMEM] * 6,
         scratch_shapes=[
             *[vmem(rows, width)] * 6, pltpu.VMEM((rows, width), F32),
             vmem(half, wide_rows, columns), vmem(half, wide_rows, columns),
             vmem(half - 1, wide_rows, columns), vmem(wide_rows, columns),
-            vmem(4, wide_rows, own_width + LANES), vmem(wide_rows, own_width),
-            vmem(3, wide_rows, own_width), vmem(*ups[0].shape), vmem(3, *ups[0].shape),
-            vmem(wide_rows, wide * unit), vmem(*downs[0].shape), vmem(3, *downs[0].shape),
-            vmem(*downs[0].shape), vmem(half, rows, width),
+            vmem(4, wide_rows, own_width), vmem(4, wide_rows, LANES),
+            pltpu.VMEM((wide_rows, LANES), F32), vmem(*ups[0].shape), vmem(3, *ups[0].shape),
+            vmem(*downs[0].shape), vmem(3, *downs[0].shape), vmem(half, rows, width),
             pltpu.VMEM((4,) + small.shape, F32), pltpu.VMEM((wide,) + small.shape, F32),
             pltpu.VMEM(small.shape, F32),
             DMA((steps,)), DMA((steps,)), DMA((2,)), DMA((2,)), DMA((12 + 2 * half,)),
@@ -867,7 +872,7 @@
             collective_id=collective_id, has_side_effects=True, vmem_limit_bytes=60 * 2**20
         ),
     )(
-        norm_part, in_part, out_low, *ups, *downs, *branches, tokens, middle, grad_middle,
+        norm_part, in_part, *ups, *downs, *branches, tokens, middle, grad_middle,
         jnp.broadcast_to(gain[None], (8, width)), small,
     )
 
@@ -1038,9 +1043,10 @@
 ):
     q_ref, k_ref, v_ref, gate_ref, small_ref, bias_ref, cont_ref, att_ref, log_ref, grad_ref = refs[:10]
     in_ref, normed_ref, up_src, down_src, up_one, down_one, part_ref, branch_ref = refs[10:18]
-    out_ref, bias_grad_ref, norm_ref, in_part_ref, part_sum = refs[18:23]
+    out_ref, bias_grad_ref, norm_ref, in_part_ref, grad_out = refs[18:23]
     up_two_got, down_two_got, up_one_got, down_one_got, branch_got = refs[23:28]
-    decay_scr, small_scr, dq_scr, part_core, part_own, part_far, send, recv, local = refs[28:]
+    decay_scr, small_scr, dq_scr, part_core, part_own, part_far, part_sum, part_got = refs[28:36]
+    send, recv, local = refs[36:]
     pair = pl.program_id(0)
     pairs = heads * head_size // LANES
     half = wide // 2
@@ -1070,14 +1076,23 @@
         pltpu.make_async_copy(part_ref.at[flipped(w, 2 * n)], part_own.at[n], local.at[n])
         for n in range(half)
     ]
+    own_width = heads * head_size
+
+    def part_columns(n):
+        return part_sum.at[:, pl.ds(pl.multiple_of(n * own_width, LANES), own_width)]
+
+    outs = [
+        sender.plan(part_columns(flipped(z, k)), part_got.at[k - 1], narrow_device(flipped(z, k)))
+        for k in (1, 2, 3)
+    ]
 
     @pl.when(pair == 0)
     def _():
         greet(
-            [narrow_device(one), narrow_device(two)]
+            [narrow_device(flipped(z, k)) for k in (1, 2, 3)]
             + [wide_device(flipped(w, k)) for k in wide_steps(wide)]
         )
-        for copy in copies + core + own + branches:
+        for copy in copies + core + own:
             copy.start()
 
     @pl.when(pair == 1)
@@ -1089,6 +1104,11 @@
             if n > 0:
                 far[n - 1].start()
 
+    @pl.when(pair == 2)
+    def _():
+        for copy in branches:
+            copy.start()
+
     @pl.when(pair < pairs)
     def _():
         backward_pair(
@@ -1103,19 +1123,28 @@
         at = pl.ds(pl.multiple_of((pair - pairs) * size, size), size)
         norm_ref[...] = dot_f32(out_ref[at, :], in_ref[...], ((1,), (1,))).astype(BF16)
 
-    @pl.when(pair >= pairs + row_steps)
-    def _():
-        in_part_ref[...] = dot_f32(normed_ref[...], out_ref[...], ((0,), (0,))).astype(BF16)
-
-    @pl.when(pair == pl.num_programs(0) - 1)
+    @pl.when(pair == pairs + row_steps)
     def _():
         total = part_own[0].astype(F32)
         for n in range(1, half):
             far[n - 1].wait_recv()
             total = total + part_far[n - 1].astype(F32)
         part_sum[...] = total.astype(BF16)
-        for copy in copies + branches:
+        for copy in outs:
+            copy.start()
+
+    @pl.when(pair >= pairs + row_steps)
+    def _():
+        in_part_ref[...] = dot_f32(normed_ref[...], out_ref[...], ((0,), (0,))).astype(BF16)
+
+    @pl.when(pair == pl.num_programs(0) - 1)
+    def _():
+        for copy in outs + copies + branches:
             copy.wait()
+        total = part_columns(z)[...].astype(F32)
+        for n in range(3):
+            total = total + part_got[n].astype(F32)
+        grad_out[...] = total
         for copy in core + far:
             copy.wait_send()
 
@@ -1268,7 +1297,7 @@
     columns = 4 * heads * head_size + LANES
     step = min(256, rows)
     row_steps, in_steps = rows // step, width // 256
-    steps = 4 + 3 * wide
+    steps = 8 + 3 * wide
     part = lambda count: pltpu.VMEM((count, wide_rows, width), BF16)
     shape = jax.ShapeDtypeStruct
 
@@ -1291,18 +1320,20 @@
             pl.BlockSpec((8, LANES), lambda p: (0, 0)),
             pl.BlockSpec((step, width), lambda p: (row_at(p), 0)),
             pl.BlockSpec((256, columns), lambda p: (in_at(p), 0)),
-            pl.BlockSpec((wide_rows, width), lambda p: (0, 0)),
+            pl.BlockSpec((wide_rows, heads * head_size), lambda p: (0, 0)),
         ]
         + [ANY] * 5,
         out_shape=[
             shape((rows, columns), BF16), shape((8, LANES), F32), shape((rows, width), BF16),
-            shape((width, columns), BF16), shape((wide_rows, width), BF16),
+            shape((width, columns), BF16), shape((wide_rows, heads * head_size), F32),
             *[shape(share.shape, BF16) for share in shares[:2] * 2],
             shape((len(diagonal_steps(wide)),) + branches.shape[1:], BF16),
         ],
         scratch_shapes=[
             pltpu.VMEM((rows, LANES), F32), pltpu.VMEM((rows, LANES), F32),
             pltpu.VMEM((rows, 2 * LANES), F32), part(half), part(half), part(half - 1),
+            pltpu.VMEM((wide_rows, width), BF16),
+            pltpu.VMEM((3, wide_rows, heads * head_size), BF16),
             DMA((steps,)), DMA((steps,)), DMA((half,)),
         ],
         compiler_params=pltpu.CompilerParams(
@@ -1315,7 +1346,7 @@
 
 
 def first_kernel(
-    wide, heads, head_size, block, x_ref, in_ref, out_ref, up_ref, grad_ref, down_ref, gain_one_ref,
+    wide, heads, head_size, block, x_ref, in_ref, small_ref, out_ref, up_ref, grad_ref, down_ref, gain_one_ref,
     gain_two_ref, bias_ref, cont_ref, normed_out, in_out, out_out, proj_out, att_ref, log_ref,
     mixed_rows, middle_ref, normed_two_ref, up_out, up_two, up_one, down_got, grad_got, slot, in_buf,
     out_buf, up_buf, normed, proj, mixed, decay_scr, send, recv, local,
@@ -1352,10 +1383,26 @@
             (lambda k, to: wide_rows(ref, flipped(w, k))),
         )
 
-    own_in = local_copy(in_ref.at[z], weight_rows(in_buf, w, z))
+    unit = up_buf.shape[2] // 4
+
+    def in_pieces(n):
+        target = lambda at, size: in_buf.at[
+            pl.ds(pl.multiple_of((w * 4 + z) * part_rows, 16), part_rows), pl.ds(at, size)
+        ]
+        for group in range(4):
+            at = pl.multiple_of(group * width + n * own_width, LANES)
+            yield in_ref.at[:, pl.ds(at, own_width)], target(group * own_width, own_width)
+        yield small_ref.at[n], target(4 * own_width, LANES)
+
+    def up_pieces(n):
+        for group in range(4):
+            at = pl.multiple_of((group * wide + n) * unit, LANES)
+            yield up_ref.at[:, pl.ds(at, unit)], up_buf.at[w, :, pl.ds(group * unit, unit)]
+
+    own_in = [local_copy(*piece) for piece in in_pieces(z)]
+    own_up = [local_copy(*piece) for piece in up_pieces(w)]
     own_out = local_copy(out_ref, weight_rows(out_buf, w, z))
     own_x = local_copy(x_ref, slot_rows(z))
-    own_up = local_copy(up_ref.at[w], up_buf.at[w])
     for copy in used:
         copy.start()
 
@@ -1390,15 +1437,15 @@
         pl.semaphore_wait(barrier, len(partners))
 
     ins = [
-        sender.plan(in_ref.at[line[k]], weight_rows(in_buf, w, z), narrow_device(line[k]))
-        for k in (2, 3, 1)
+        sender.plan(*piece, narrow_device(line[k])) for k in (2, 3, 1) for piece in in_pieces(line[k])
     ]
     outs = [
         sender.plan(out_ref, weight_rows(out_buf, w, z), narrow_device(line[k])) for k in (2, 3, 1)
     ]
     ups = [
-        sender.plan(up_ref.at[flipped(w, k)], up_buf.at[w], wide_device(flipped(w, k)))
+        sender.plan(*piece, wide_device(flipped(w, k)))
         for k in range(1, wide)
+        for piece in up_pieces(flipped(w, k))
     ]
     grads = {
         k: sender.plan(grad_ref, grad_got.at[k // 2 - 1], wide_device(flipped(w, k)))
@@ -1425,7 +1472,8 @@
 
     for copy in ins + outs + ups:
         copy.start()
-    own_in.wait()
+    for copy in own_in:
+        copy.wait()
     for copy in ins:
         copy.wait_recv()
     in_wide.start()
@@ -1445,41 +1493,50 @@
         relay.start()
         middle.start()
 
-    own_up.wait()
+    for copy in own_up:
+        copy.wait()
     for copy in ups:
         copy.wait_recv()
     up_back = local_copy(up_buf, up_out)
     up_back.start()
-    out_wide.pass_on()
     in_wide.received()
     in_back = local_copy(in_buf, in_out)
     in_back.start()
-    one.wait_recv()
     own_x.wait()
 
-    @pl.when(is_middle)
-    def _():
-        middle.wait_recv()
-
-    @pl.when(is_end)
-    def _():
-        relay.wait_recv()
-
-    for copy in up_steps:
-        copy.start()
-
-    @pl.when(moves)
-    def _():
-        down_push.start()
-
-    @pl.when(jnp.logical_not(moves))
-    def _():
-        down_stay.start()
-
-    for k in straight_steps(wide):
-        grads[k].start()
-
-    def project(n, carry):
+    def project(t, carry):
+        @pl.when(t == 2)
+        def _():
+            one.wait_recv()
+
+        @pl.when(t == 3)
+        def _():
+            out_wide.pass_on()
+
+        @pl.when((t == 3) & is_middle)
+        def _():
+            middle.wait_recv()
+
+        @pl.when((t == 3) & is_end)
+        def _():
+            relay.wait_recv()
+
+        @pl.when(t == 3)
+        def _():
+            for copy in up_steps:
+                copy.start()
+            for k in straight_steps(wide):
+                grads[k].start()
+
+        @pl.when((t == 3) & moves)
+        def _():
+            down_push.start()
+
+        @pl.when((t == 3) & jnp.logical_not(moves))
+        def _():
+            down_stay.start()
+
+        n = jnp.where(t == 0, z, jnp.where(t == 1, line[2], jnp.where(t == 2, line[1], line[3])))
         at = pl.ds(pl.multiple_of(n * rows, rows), rows)
         values = slot[at, :].astype(F32)
         low = (values * rms_factor(values) * gain_one_ref[0:1, :]).astype(BF16)
@@ -1487,7 +1544,7 @@
         proj[at, :] = dot_f32(low, in_buf[...])
         return carry
 
-    lax.fori_loop(0, slot.shape[0] // rows, project, 0)
+    lax.fori_loop(0, 4, project, 0)
     normed_back = local_copy(normed, normed_out)
     proj_back = local_copy(proj, proj_out)
     normed_back.start()
@@ -1552,13 +1609,14 @@
 
 
 def first_part(
-    tokens, in_parts, out_weight, up_parts, cotangent, down_weight, gain_one, gain_two, bias, cont,
-    heads, head_size, block, collective_id,
+    tokens, in_weight, small, out_weight, gate_up_weight, cotangent, down_weight, gain_one, gain_two, bias,
+    cont, wide, heads, head_size, block, collective_id,
 ):
-    wide = up_parts.shape[0]
     rows, width = tokens.shape
-    slot, own_width, columns = 4 * rows, heads * head_size, in_parts.shape[2]
-    steps = 3 * wide + 2 * wide + 24
+    slot, own_width = 4 * rows, heads * head_size
+    columns = 4 * own_width + LANES
+    steps = 8 * wide + 40
+    up_shape = (wide, gate_up_weight.shape[0], gate_up_weight.shape[1] // wide)
     shape = jax.ShapeDtypeStruct
     return pl.pallas_call(
         functools.partial(first_kernel, wide, heads, head_size, block),
@@ -1566,34 +1624,34 @@
             shape((slot, width), BF16), shape((width, columns), BF16), shape((width, width), BF16),
             shape((slot, columns), F32), shape((slot, own_width), BF16),
             shape((slot, own_width), F32), shape((rows, width), BF16), shape((rows, width), F32),
-            shape((rows, width), BF16), shape(up_parts.shape, BF16), shape(up_parts.shape, BF16),
-            shape(up_parts.shape, BF16), shape(down_weight.shape, BF16),
+            shape((rows, width), BF16), shape(up_shape, BF16), shape(up_shape, BF16),
+            shape(up_shape, BF16), shape(down_weight.shape, BF16),
             shape((wide // 2 - 1, rows, width), BF16),
         ],
-        in_specs=[ANY] * 6 + [VMEM] * 4,
+        in_specs=[ANY] * 7 + [VMEM] * 4,
         out_specs=[ANY] * 4 + [VMEM] * 5 + [ANY] * 5,
         scratch_shapes=[
             pltpu.VMEM((slot, width), BF16), pltpu.VMEM((width, columns), BF16),
-            pltpu.VMEM((width, width), BF16), pltpu.VMEM(up_parts.shape, BF16),
+            pltpu.VMEM((width, width), BF16), pltpu.VMEM(up_shape, BF16),
             pltpu.VMEM((slot, width), BF16), pltpu.VMEM((slot, columns), F32),
             pltpu.VMEM((slot, own_width), BF16), pltpu.VMEM((slot, LANES), F32),
-            DMA((steps,)), DMA((steps,)), DMA((10,)),
+            DMA((steps,)), DMA((steps,)), DMA((20,)),
         ],
         compiler_params=pltpu.CompilerParams(
             collective_id=collective_id, has_side_effects=True, vmem_limit_bytes=60 * 2**20
         ),
     )(
-        tokens, in_parts, out_weight, up_parts, cotangent, down_weight,
-        jnp.broadcast_to(gain_one[None], (8, width)), jnp.broadcast_to(gain_two[None], (8, width)),
-        bias, cont,
+        tokens, in_weight, small, out_weight, gate_up_weight, cotangent, down_weight, jnp.broadcast_to(gain_one[None], (8, width)),
+        jnp.broadcast_to(gain_two[None], (8, width)), bias, cont,
     )
 
 
 def second_kernel(
-    wide, src_ref, grad_ref, far_grads, up_ref, up_two, up_one, down_ref, norm_sum, branch_sum,
-    up_src, down_src, up_acc, down_acc, up_grad_out, down_grad_out, normed, grads, up_full,
-    down_full, hidden, mid, rows_buf, core_buf, far_buf, branch_buf, up_join, up_mid, down_join,
-    down_mid, up_grad, down_grad, send, recv, local,
+    wide, src_ref, grad_ref, far_grads, up_ref, up_two, up_one, down_ref, middle_ref, mixed_ref, out_ref,
+    gain_ref, grad_middle, gain_grad, slot_grad, branch_sum, up_src, down_src, up_acc, down_acc,
+    up_grad_out, down_grad_out, out_part, branch_near, normed, grads, up_full, down_full, hidden, mid,
+    rows_buf, core_buf, far_buf, branch_buf, up_join, up_mid, down_join, down_mid, up_grad, down_grad,
+    grad_mixed, mixed_buf, send, recv, local,
 ):
     w, z = lax.axis_index("wide"), lax.axis_index("narrow")
     line = [flipped(z, k) for k in range(4)]
@@ -1659,50 +1717,91 @@
     down_direct = sender.plan(down_share(line[3]), down_mid, narrow_device(line[3]))
     up_joined = sender.plan(up_share(line[3]), up_join, narrow_device(line[1]))
     up_direct = sender.plan(up_share(line[3]), up_mid, narrow_device(line[3]))
+    own_width = width // 4
+    mixes = [
+        sender.plan(
+            grad_mixed.at[:, pl.ds(pl.multiple_of(line[k] * own_width, LANES), own_width)],
+            slot_grad.at[pl.ds(pl.multiple_of(z * rows, rows), rows), :], narrow_device(line[k]),
+        )
+        for k in (2, 3, 1)
+    ]
+    near = [
+        sender.plan(branch_sum.at[k // 2], branch_near.at[n], wide_device(flipped(w, k)))
+        for n, k in enumerate(straight_steps(wide))
+    ]
 
     gather.start()
+
+    @pl.when(is_middle)
+    def _():
+        relay.start()
+        middle.start()
+
     down_two.start()
+    down_two.wait_recv()
 
     @pl.when(is_middle)
     def _():
-        relay.start()
-
-    down_two.wait_recv()
-
-    @pl.when(is_middle)
-    def _():
         down_relay.start()
-        middle.start()
         down_middle.start()
 
     down_one.start()
     for copy in passed:
         copy.start()
-    gather.pass_on()
-    gather.received()
-    for copy in own:
+    for copy in own[:4]:
+        copy.wait()
+
+    @pl.when(is_middle)
+    def _():
+        middle.wait_recv()
+
+    @pl.when(is_end)
+    def _():
+        relay.wait_recv()
+
+    up_shape = (width, 4 * unit)
+    down_shape = (size, width)
+
+    def arriving(t, carry):
+        @pl.when(t == 1)
+        def _():
+            gather.first[1].wait_recv()
+
+        for n, k in enumerate(gather.far):
+
+            @pl.when(t == 2 + n)
+            def _():
+                gather.first[k].wait_recv()
+                gather.second[k].start()
+
+            @pl.when(t == half + 1 + n)
+            def _():
+                gather.second[k].wait_recv()
+
+        place = jnp.where(t < 2, t * half, jnp.where(t < half + 1, t - 1, t))
+        at = pl.ds(pl.multiple_of(place * rows, rows), rows)
+        mid[at, :] = dot_f32(normed[at, :], up_full[...].reshape(up_shape)).astype(BF16)
+        return carry
+
+    lax.fori_loop(0, wide, arriving, 0)
+    for copy in own[4:]:
         copy.wait()
     for copy in passed + [down_one]:
         copy.wait_recv()
 
     @pl.when(is_middle)
     def _():
-        middle.wait_recv()
         down_middle.wait_recv()
 
     @pl.when(is_end)
     def _():
-        relay.wait_recv()
         down_relay.wait_recv()
-
-    up_shape = (width, 4 * unit)
-    down_shape = (size, width)
 
     def block(t, carry):
         place = lax.rem(t + half, wide) + jnp.where(t < half, 0, 1)
         place = jnp.where(place == half, jnp.where(t < half, half, 0), place)
         at = pl.ds(pl.multiple_of(place * rows, rows), rows)
-        gate_up = dot_f32(normed[at, :], up_full[...].reshape(up_shape))
+        gate_up = mid[at, :].astype(F32)
         grad_hidden = dot_f32(grads[at, :], down_full[...].reshape(down_shape), ((1,), (1,)))
         gate, up = gate_up[:, :size], gate_up[:, size:]
         opened = jax.nn.sigmoid(gate)
@@ -1746,6 +1845,15 @@
     def _():
         down_direct.start()
 
+    reloads = [
+        pltpu.make_async_copy(out_ref, grads.at[pl.ds(0, width), :], local.at[9 + half]),
+        pltpu.make_async_copy(grad_ref, grads.at[pl.ds(width, rows), :], local.at[10 + half]),
+        pltpu.make_async_copy(mixed_ref, mixed_buf, local.at[11 + half]),
+        pltpu.make_async_copy(middle_ref, grad_middle, local.at[12 + half]),
+    ]
+    for copy in reloads:
+        copy.start()
+
     def up_rows(n, carry):
         at = pl.ds(pl.multiple_of(n * 256, 256), 256)
         up_grad[at, :] = dot_f32(normed[:, at], mid[...], ((0,), (0,))).astype(BF16)
@@ -1793,7 +1901,34 @@
     for n in range(1, half):
         far[n - 1].wait_recv()
         total = total + far_buf[n - 1].astype(F32)
-    norm_sum[...] = total
+    for copy in core + far:
+        copy.wait_send()
+    for copy in reloads:
+        copy.wait()
+    values = grad_middle[...]
+    factor = rms_factor(values)
+    values = values * factor
+    gain_grad[...] = jnp.broadcast_to(
+        jnp.sum(total * values, axis=0, keepdims=True), gain_grad.shape
+    )
+    total = total * gain_ref[0:1, :]
+    inner = jnp.mean(total * values, axis=-1, keepdims=True)
+    total = grads[width : width + rows, :].astype(F32) + factor * (total - values * inner)
+    grad_middle[...] = total
+    branch_grad = total.astype(BF16)
+    grad_mixed[...] = dot_f32(branch_grad, grads[:width, :], ((1,), (1,))).astype(BF16)
+    for copy in mixes + near:
+        copy.start()
+    slot_grad[pl.ds(pl.multiple_of(z * rows, rows), rows), :] = grad_mixed[
+        :, pl.ds(pl.multiple_of(z * own_width, LANES), own_width)
+    ]
+    for n in range(width // 256):
+        cut = slice(n * 256, (n + 1) * 256)
+        rows_buf[cut, :] = dot_f32(mixed_buf[:, cut], branch_grad, ((0,), (0,))).astype(BF16)
+    out_back = pltpu.make_async_copy(
+        rows_buf.at[pl.ds(0, width), :], out_part, local.at[13 + half]
+    )
+    out_back.start()
     for copy in backs:
         copy.wait()
     up_acc[...] = up_grad[:, pl.ds(pl.multiple_of(z * unit, unit), unit)]
@@ -1817,43 +1952,53 @@
         down_joined.wait_send()
         up_joined.wait_send()
 
-    for copy in passed + core + far + branch_core + [down_two, down_one]:
+    for copy in mixes + near:
+        copy.wait()
+    out_back.wait()
+    for copy in passed + branch_core + [down_two, down_one]:
         copy.wait_send()
 
 
-def second_part(normed, grad, far_grads, ups, down, collective_id):
+def second_part(
+    normed, grad, far_grads, ups, down, middle, mixed_rows, out_full, gain, collective_id
+):
     rows, width = normed.shape
     half = far_grads.shape[0] + 1
     wide = 2 * half
     wide_of_up, part_rows, mid_size = ups[0].shape
     down_rows = down.shape[0]
     size, unit, part = mid_size // 2, mid_size // 4, width // 4
-    steps = 6 + wide + 4 * half + 8
+    steps = 9 + 2 * wide + 4 * half + 8
     total = wide * rows
     shape = jax.ShapeDtypeStruct
     vmem = lambda *dims: pltpu.VMEM(dims, BF16)
     return pl.pallas_call(
         functools.partial(second_kernel, wide),
         out_shape=[
-            shape((rows, width), F32), shape((half, rows, width), BF16),
+            shape((rows, width), F32), shape((8, width), F32), shape((4 * rows, part), BF16),
+            shape((half, rows, width), BF16),
             shape((width, unit), BF16), shape((size, part), BF16),
             shape((width, unit), BF16), shape((size, part), BF16),
             shape((width, mid_size), BF16), shape((size, width), BF16),
+            shape((width, width), BF16), shape((len(straight_steps(wide)), rows, width), BF16),
         ],
-        in_specs=[ANY] * 7,
-        out_specs=[VMEM] * 6 + [ANY] * 2,
+        in_specs=[ANY] * 10 + [VMEM],
+        out_specs=[VMEM] * 8 + [ANY] * 4,
         scratch_shapes=[
             vmem(total, width), vmem(total, width), vmem(wide, 4, part_rows, mid_size),
             vmem(4, down_rows, width), vmem(total, size), vmem(total, mid_size), vmem(total, width),
             vmem(half, rows, width), vmem(half - 1, rows, width), vmem(half, rows, width),
             vmem(width, unit), vmem(width, unit), vmem(size, part), vmem(size, part),
-            vmem(width, mid_size), vmem(size, width),
-            DMA((steps,)), DMA((steps,)), DMA((9 + half,)),
+            vmem(width, mid_size), vmem(size, width), vmem(rows, width), vmem(rows, width),
+            DMA((steps,)), DMA((steps,)), DMA((14 + half,)),
         ],
         compiler_params=pltpu.CompilerParams(
             collective_id=collective_id, has_side_effects=True, vmem_limit_bytes=63 * 2**20
         ),
-    )(normed, grad, far_grads, *ups, down)
+    )(
+        normed, grad, far_grads, *ups, down, middle, mixed_rows, out_full,
+        jnp.broadcast_to(gain[None], (8, width)),
+    )
 
 
 def add_up(parts):
@@ -1896,15 +2041,6 @@
                         targets[0].at[n, :, pl.ds(group * own_width, own_width)],
                     )
                 )
-        if aligned:
-            for n in range(wide):
-                for group in range(4):
-                    copies.append(
-                        (
-                            sources[2].at[:, pl.ds((group * wide + n) * unit, unit)],
-                            targets[1].at[n, :, pl.ds(group * unit, unit)],
-                        )
-                    )
         return copies
 
     shapes = [
@@ -1912,11 +2048,8 @@
         jax.ShapeDtypeStruct((wide, part_rows, 4 * unit), BF16),
     ]
     copies = 4 * narrow + 1
-    if aligned:
-        in_parts, up_parts = local_copies(
-            split_weights, copies + 4 * wide, [in_weight, small, gate_up_weight], shapes, False
-        )
-    else:
+    fused = aligned and part_rows % 16 == 0
+    if not fused:
         in_parts = local_copies(split_weights, copies, [in_weight, small], shapes[:1], False)[0]
         up_parts = jnp.moveaxis(gate_up_weight.reshape(part_rows, 4, wide, unit), 2, 0)
         up_parts = up_parts.reshape(wide, part_rows, 4 * unit)
@@ -1937,13 +2070,13 @@
     straight, diagonal = straight_steps(wide), diagonal_steps(wide)
     inputs = tokens.astype(F32)
     half = wide // 2
-    if aligned and part_rows % 16 == 0:
+    if fused:
         (
             normed_one, in_full, out_full, projected, attended, logs, mixed_rows, middle, normed_two,
             up_block, up_two, up_one, down_block, grad_got,
         ) = first_part(
-            tokens, in_parts, out_weight, up_parts, cotangent, down_weight, gain_one, gain_two,
-            bias, cont, own_heads, head_size, block, 0,
+            tokens, in_weight, small, out_weight, gate_up_weight, cotangent, down_weight, gain_one,
+            gain_two, bias, cont, wide, own_heads, head_size, block, 0,
         )
     else:
         pairs = []
@@ -1984,12 +2117,15 @@
         middle = inputs + dot_f32(mixed_rows, out_full)
         normed_two = (middle * rms_factor(middle) * gain_two).astype(BF16)
 
-    if aligned and part_rows % 16 == 0:
+    if fused:
         (
-            grad_normed_two, branch_sum, up_src, down_src, up_acc, down_acc, up_one, down_one,
+            grad_middle, grad_gain_two, slot_grad, branch_sum, up_src, down_src, up_acc, down_acc,
+            up_one, down_one, out_part, branch_near,
         ) = second_part(
-            normed_two, cotangent, grad_got, [up_block, up_two, up_one], down_block, 2
+            normed_two, cotangent, grad_got, [up_block, up_two, up_one], down_block, middle,
+            mixed_rows, out_full, gain_two, 2,
         )
+        grad_gain_two = grad_gain_two[0]
     else:
         ups = [up_block] + [follow(piece, normed_two) for piece in (up_two, up_one)]
         plane_normed, plane_grad, up_full, down_full = gather_rows(
@@ -2019,41 +2155,42 @@
         if not fits:
             received = along_wide(branch[half:], 1, wide)
             branch_sum = (branch[:half].astype(F32) + received.astype(F32)).astype(BF16)
-    upstream = cotangent.astype(F32)
-    grad_middle_norm, grad_gain_two = rms_back(middle, gain_two, grad_normed_two)
-    grad_middle = upstream + grad_middle_norm
-    branch_one_grad = grad_middle.astype(BF16)
-    grad_mixed = dot_f32(branch_one_grad, out_full, ((1,), (1,))).astype(BF16)
-    slot_grad, *branch_near = exchange(
-        grad_mixed, column_block, row_block, (slot, own_width), straight,
-        [branch_sum[k // 2] for k in straight], 3,
-    )
-
+        upstream = cotangent.astype(F32)
+        grad_middle_norm, grad_gain_two = rms_back(middle, gain_two, grad_normed_two)
+        grad_middle = upstream + grad_middle_norm
+        branch_one_grad = grad_middle.astype(BF16)
+        grad_mixed = dot_f32(branch_one_grad, out_full, ((1,), (1,))).astype(BF16)
+        slot_grad, *branch_near = exchange(
+            grad_mixed, column_block, row_block, (slot, own_width), straight,
+            [branch_sum[k // 2] for k in straight], 3,
+        )
+        branch_near = jnp.stack(branch_near)
+        out_part = dot_f32(mixed_rows, branch_one_grad, ((0,), (0,))).astype(BF16)
     wide_rows = width // wide
-    out_part = dot_f32(mixed_rows, branch_one_grad, ((0,), (0,))).astype(BF16)
     (
-        unused, bias_grad, norm_part, in_part, out_low, up_two, down_two, up_one, down_one,
+        unused, bias_grad, norm_part, in_part, grad_out, up_two, down_two, up_one, down_one,
         branch_far,
     ) = attention_backward(
         projected, bias, cont, attended, logs, slot_grad, in_full, normed_one,
         [up_src, down_src, up_one, down_one], out_part.reshape(wide, wide_rows, width), branch_sum,
         own_heads, head_size, block, 7,
     )
-    branches = [branch_sum[0]] + branch_near + [branch_far[n] for n in range(len(diagonal))]
+    branches = [branch_sum, branch_near, branch_far]
     all_bias = lax.dynamic_update_slice(
         jnp.zeros((width,), F32), bias_grad[0, :own_heads], (z * own_heads,)
     )
     small = jnp.stack([jnp.zeros((width,), F32), grad_gain_two, all_bias])
     small = jnp.pad(small, ((0, 5), (0, 0)))
     low = lambda part: part.astype(BF16)
-    output, grad_tokens, grad_in, grad_out, grad_up, grad_down, totals = last_part(
-        norm_part, in_part.reshape(wide, wide_rows, columns), out_low, [low(up_acc), up_one, up_two],
+    output, grad_tokens, grad_in, grad_up, grad_down, totals = last_part(
+        norm_part, in_part.reshape(wide, wide_rows, columns), [low(up_acc), up_one, up_two],
         [low(down_acc), down_one, down_two], branches, tokens, middle, grad_middle, gain_one, small,
         own_width, own_heads, (base + 3 * heads) // narrow, 4,
     )
     if not aligned:
         grad_up = grad_up.reshape(wide_rows, wide, LANES)[:, :, :unit]
         grad_up = grad_up.reshape(wide_rows, wide * unit)
+    grad_up, grad_down = grad_up.astype(F32), grad_down.astype(F32)
     return (
         output,
         grad_tokens,

time: 492 us -> 479 us (0.974)
  local copies, waits for them, and re-layouts: 25.6 us -> 14.7 us
  matrix products: 4.99 us -> 0 us
    pallas_call x1, Pallas kernels: 107 us -> 128 us  [second_part(): pl.pallas_call(functools.partial(second_kernel, wide), out_shape=[shape((...]
    pallas_call x2 -> x0, Pallas kernels: 20.7 us -> none  [the longest x1 19.9 us: exchange(): pl.pallas_call(functools.partial(exchange_kernel, source, target, steps),...]
    pallas_call x1, Pallas kernels: 62.6 us -> 78.8 us  [attention_backward(): pl.pallas_call(functools.partial(backward_kernel, heads, head_size, block...]
    pallas_call x1, Pallas kernels: 100 us -> 86 us  [last_part(): pl.pallas_call(functools.partial(grouped_last_kernel, wide, rows, own_wid...]
    unnamed x52 -> x14, local copies, waits for them, and re-layouts: 16.4 us -> 3.8 us
    dot_general x2 -> x0, matrix products: 4.99 us -> none  [dot_f32(): lax.dot_general(left, right, (dims, ((), ())), preferred_element_type=F32)]
where the time goes in v6:
time: 479 us; the launch traced here: 471 us
  Pallas kernels  450 us (94%)
  local copies, waits for them, and re-layouts  14.7 us (3%)
  other arithmetic  5.11 us (1%)
    pallas_call x1, Pallas kernels, first_part(): pl.pallas_call(functools.partial(first_kernel, wide, heads, head_size, bl...  157 us
    pallas_call x1, Pallas kernels, second_part(): pl.pallas_call(functools.partial(second_kernel, wide), out_shape=[shape((...  128 us
    pallas_call x1, Pallas kernels, last_part(): pl.pallas_call(functools.partial(grouped_last_kernel, wide, rows, own_wid...  86 us
    pallas_call x1, Pallas kernels, attention_backward(): pl.pallas_call(functools.partial(backward_kernel, heads, head_size, block...  78.8 us

profile of v6, /device:TPU:0, one launch (start us, length us, event | category | flops | bytes accessed | tf_op | source)
XLA Modules:
  0.0 470.7 jit_solution(13466743575132760823)
XLA Ops:
  0.6 0.7 dynamic_slice.3
  1.4 0.6 broadcast_in_dim.10.bias_ref.refs_5_
  2.0 0.9 compare_reduce_fusion
  2.9 1.0 broadcast_in_dim.11.cont_ref.refs_6_
  3.9 1.3 broadcast_in_dim.8.gain_one_ref.refs_14_
  5.2 1.3 broadcast_in_dim.9.gain_two_ref.gain_ref
  6.6 0.7 slice.26
  7.4 0.1 copy.22
  7.5 0.6 pad.12.small_ref
  8.2 157.3 %shard_map.169 = (bf16[1024,1536]{1,0:T(8,128)(2,1)}, bf16[1536,1664]{1,0:T(8,128)(2,1)}, bf16[1536,1536]{1,0:T(8,128)(2,1)}, f32[1024,1664]{1,0:T(8,128)}, bf16...) custom-call(bf16[256,1536]{1,0:T(8,128)(2,1)} %refs_11_.1, ...), custom_call_target="tpu_custom_call" | custom-call | tf_op jit(solution)/shard_map/pallas_call | solution.py:1621
  165.5 127.7 %shard_map.170 = (f32[256,1536]{1,0:T(8,128)}, f32[8,1536]{1,0:T(8,128)}, bf16[1024,384]{1,0:T(8,128)(2,1)}, bf16[4,256,1536]{2,1,0:T(8,128)(2,1)}, bf16[1536,25...) custom-call(bf16[256,1536]{1,0:T(8,128)(2,1)} %get-tuple-element.53., ...), custom_call_target="tpu_custom_call" | custom-call | tf_op jit(solution)/shard_map/pallas_call | solution.py:1975
  293.1 78.8 %shard_map.171 = (bf16[1024,1664]{1,0:T(8,128)(2,1)}, f32[8,128]{1,0:T(8,128)}, bf16[1024,1536]{1,0:T(8,128)(2,1)}, bf16[1536,1664]{1,0:T(8,128)(2,1)}, f32[192,...) custom-call(f32[1024,1664]{1,0:T(8,128)} %get-tuple-element.50.refs_, ...), custom_call_target="tpu_custom_call" | custom-call | tf_op jit(solution)/shard_map/pallas_call | solution.py:1308
  372.0 0.7 slice.30
  372.7 0.8 slice.29
  373.6 0.6 select_maximum_fusion.refs_15_
  374.2 86.0 %shard_map.172 = (bf16[256,1536]{1,0:T(8,128)(2,1)}, f32[256,1536]{1,0:T(8,128)}, f32[192,1554]{1,0:T(8,128)}, bf16[192,2048]{1,0:T(8,128)(2,1)}, bf16[512,384]{1,0:T(8,128)(2,1)}, /*index=5*/f32[8,1536]{1,0:T(8,128)}) custom-call(bf16[1024,1536]{1,0:T(8,128)(2,1)} %get-tuple-element.71.refs_0_, bf16[8,192,1664]{2,1,0:T(8,128)(2,1)} %bitcast.8, ...), custom_call_target="tpu_custom_call" | custom-call | tf_op jit(solution)/shard_map/pallas_call | solution.py:851
  460.2 2.6 convert_element_type.17
  462.8 0.9 convert_element_type.18
  463.8 1.5 slice_reduce_fusion
  465.3 1.2 slice_bitcast_fusion
  466.4 0.9 copy.29
  467.3 1.1 copy.30
  468.5 1.0 copy.31
  469.5 0.7 copy.32
  (18 shorter events, 0.3 us)
Async XLA Ops:
  460.2 2.6 copy-start.3
  460.2 6.3 %copy-start.2 = (bf16[256,1536]{1,0:T(8,128)(2,1)S(1)}, bf16[256,1536]{1,0:T(8,128)(2,1)}, u32[]{:S(2)}) copy-start(bf16[256,1536]{1,0:T(8,128)(2,1)} %get-tuple-element.102) | copy-start | bytes 2359300
  460.2 7.1 %copy-start = (f32[256,1536]{1,0:T(8,128)S(1)}, f32[256,1536]{1,0:T(8,128)}, u32[]{:S(2)}) copy-start(f32[256,1536]{1,0:T(8,128)} %get-tuple-element.103) | copy-start | bytes 4718596
  466.4 2.0 copy-start.1
  467.3 2.2 copy-start.4

commit v7 on v6

--- a/solution.py
+++ b/solution.py
@@ -1104,11 +1104,6 @@
             if n > 0:
                 far[n - 1].start()
 
-    @pl.when(pair == 2)
-    def _():
-        for copy in branches:
-            copy.start()
-
     @pl.when(pair < pairs)
     def _():
         backward_pair(
@@ -1130,7 +1125,7 @@
             far[n - 1].wait_recv()
             total = total + part_far[n - 1].astype(F32)
         part_sum[...] = total.astype(BF16)
-        for copy in outs:
+        for copy in outs + branches:
             copy.start()
 
     @pl.when(pair >= pairs + row_steps)
@@ -1798,8 +1793,8 @@
         down_relay.wait_recv()
 
     def block(t, carry):
-        place = lax.rem(t + half, wide) + jnp.where(t < half, 0, 1)
-        place = jnp.where(place == half, jnp.where(t < half, half, 0), place)
+        pick = half - 1 - lax.div(t, 2)
+        place = jnp.where(lax.rem(t, 2) == 0, half + pick, pick)
         at = pl.ds(pl.multiple_of(place * rows, rows), rows)
         gate_up = mid[at, :].astype(F32)
         grad_hidden = dot_f32(grads[at, :], down_full[...].reshape(down_shape), ((1,), (1,)))
@@ -1814,13 +1809,13 @@
         )
         for n in range(half):
 
-            @pl.when(t == n)
+            @pl.when(t == 2 * (half - 1 - n))
             def _():
                 core[n].start()
 
         for n in range(half):
 
-            @pl.when(t == half + lax.rem(n + half - 1, half))
+            @pl.when(t == 2 * (half - 1 - n) + 1)
             def _():
                 core[n].wait_recv()
                 total = rows_buf[n * rows : (n + 1) * rows, :].astype(F32) + core_buf[n].astype(F32)

time: 479 us -> 470 us (0.981)
  Pallas kernels: 450 us -> 440 us
    pallas_call x1, Pallas kernels: 128 us -> 123 us  [second_part(): pl.pallas_call(functools.partial(second_kernel, wide), out_shape=[shape((...]
where the time goes in v7:
time: 470 us; the launch traced here: 461 us
  Pallas kernels  440 us (94%)
  local copies, waits for them, and re-layouts  14.7 us (3%)
  other arithmetic  5.11 us (1%)
    pallas_call x1, Pallas kernels, first_part(): pl.pallas_call(functools.partial(first_kernel, wide, heads, head_size, bl...  157 us
    pallas_call x1, Pallas kernels, second_part(): pl.pallas_call(functools.partial(second_kernel, wide), out_shape=[shape((...  123 us
    pallas_call x1, Pallas kernels, last_part(): pl.pallas_call(functools.partial(grouped_last_kernel, wide, rows, own_wid...  83.3 us
    pallas_call x1, Pallas kernels, attention_backward(): pl.pallas_call(functools.partial(backward_kernel, heads, head_size, block...  76.5 us

profile of v7, /device:TPU:0, one launch (start us, length us, event | category | flops | bytes accessed | tf_op | source)
XLA Modules:
  0.0 460.8 jit_solution(3561039755935684150)
XLA Ops:
  0.6 0.7 dynamic_slice.3
  1.4 0.6 broadcast_in_dim.10.bias_ref.refs_5_
  2.0 0.9 compare_reduce_fusion
  2.9 1.0 broadcast_in_dim.11.cont_ref.refs_6_
  3.9 1.3 broadcast_in_dim.8.gain_one_ref.refs_14_
  5.2 1.3 broadcast_in_dim.9.gain_two_ref.gain_ref
  6.6 0.7 slice.26
  7.4 0.1 copy.22
  7.5 0.6 pad.12.small_ref
  8.2 157.3 %shard_map.169 = (bf16[1024,1536]{1,0:T(8,128)(2,1)}, bf16[1536,1664]{1,0:T(8,128)(2,1)}, bf16[1536,1536]{1,0:T(8,128)(2,1)}, f32[1024,1664]{1,0:T(8,128)}, bf16...) custom-call(bf16[256,1536]{1,0:T(8,128)(2,1)} %refs_11_.1, ...), custom_call_target="tpu_custom_call" | custom-call | tf_op jit(solution)/shard_map/pallas_call | solution.py:1616
  165.5 122.7 %shard_map.170 = (f32[256,1536]{1,0:T(8,128)}, f32[8,1536]{1,0:T(8,128)}, bf16[1024,384]{1,0:T(8,128)(2,1)}, bf16[4,256,1536]{2,1,0:T(8,128)(2,1)}, bf16[1536,25...) custom-call(bf16[256,1536]{1,0:T(8,128)(2,1)} %get-tuple-element.53., ...), custom_call_target="tpu_custom_call" | custom-call | tf_op jit(solution)/shard_map/pallas_call | solution.py:1970
  288.2 76.5 %shard_map.171 = (bf16[1024,1664]{1,0:T(8,128)(2,1)}, f32[8,128]{1,0:T(8,128)}, bf16[1024,1536]{1,0:T(8,128)(2,1)}, bf16[1536,1664]{1,0:T(8,128)(2,1)}, f32[192,...) custom-call(f32[1024,1664]{1,0:T(8,128)} %get-tuple-element.50.refs_, ...), custom_call_target="tpu_custom_call" | custom-call | tf_op jit(solution)/shard_map/pallas_call | solution.py:1303
  364.7 0.7 slice.30
  365.5 0.8 slice.29
  366.3 0.6 select_maximum_fusion.refs_15_
  367.0 83.3 %shard_map.172 = (bf16[256,1536]{1,0:T(8,128)(2,1)}, f32[256,1536]{1,0:T(8,128)}, f32[192,1554]{1,0:T(8,128)}, bf16[192,2048]{1,0:T(8,128)(2,1)}, bf16[512,384]{1,0:T(8,128)(2,1)}, /*index=5*/f32[8,1536]{1,0:T(8,128)}) custom-call(bf16[1024,1536]{1,0:T(8,128)(2,1)} %get-tuple-element.71.refs_0_, bf16[8,192,1664]{2,1,0:T(8,128)(2,1)} %bitcast.8, ...), custom_call_target="tpu_custom_call" | custom-call | tf_op jit(solution)/shard_map/pallas_call | solution.py:851
  450.3 2.6 convert_element_type.17
  452.9 0.9 convert_element_type.18
  453.9 1.5 slice_reduce_fusion
  455.4 1.2 slice_bitcast_fusion
  456.6 0.9 copy.29
  457.4 1.1 copy.30
  458.6 1.0 copy.31
  459.6 0.7 copy.32
  (18 shorter events, 0.3 us)
Async XLA Ops:
  450.3 2.6 copy-start.3
  450.3 6.3 %copy-start.2 = (bf16[256,1536]{1,0:T(8,128)(2,1)S(1)}, bf16[256,1536]{1,0:T(8,128)(2,1)}, u32[]{:S(2)}) copy-start(bf16[256,1536]{1,0:T(8,128)(2,1)} %get-tuple-element.102) | copy-start | bytes 2359300
  450.3 7.1 %copy-start = (f32[256,1536]{1,0:T(8,128)S(1)}, f32[256,1536]{1,0:T(8,128)}, u32[]{:S(2)}) copy-start(f32[256,1536]{1,0:T(8,128)} %get-tuple-element.103) | copy-start | bytes 4718596
  456.6 2.0 copy-start.1
  457.4 2.2 copy-start.4

commit v8 on v7

--- a/solution.py
+++ b/solution.py
@@ -595,9 +595,9 @@
 
 def last_kernel(
     wide, rows, own_width, own_heads, norm_ref, in_ref, up_parts, down_parts, branch_refs, token_ref,
-    middle_ref, grad_ref, gain_ref, small_ref, output, grad_tokens, grad_in, up_got, down_got, totals, join_buf, one_buf, mid_buf, two_buf, two_src, own_norm, norm_sum,
-    in_core, in_own, in_far, in_sum, in_got, after_got, tail_buf, up_low, up_bufs, down_low,
-    down_bufs, branch_bufs, narrow_buf, wide_buf, sum_buf, send, recv, down_send, down_recv,
+    middle_ref, grad_ref, gain_ref, small_ref, output, grad_tokens, grad_in, grad_up, grad_down, totals, join_buf, one_buf, mid_buf, two_buf, two_src, own_norm, norm_sum,
+    in_core, in_own, in_far, in_sum, in_got, after_got, tail_buf, up_low, up_bufs, up_got, down_low,
+    down_bufs, down_got, branch_bufs, narrow_buf, wide_buf, sum_buf, send, recv, down_send, down_recv,
     local,
 ):
     w, z = lax.axis_index("wide"), lax.axis_index("narrow")
@@ -756,7 +756,7 @@
     values = token_ref[...].astype(F32)
     factor = rms_factor(values)
     normed = values * factor
-    scaled = grads * gain_ref[0:1, :]
+    scaled = grads * gain_ref[...].reshape(1, width)
     inner = jnp.mean(scaled * normed, axis=-1, keepdims=True)
     grad_tokens[...] = grad_ref[...] + factor * (scaled - normed * inner)
     narrow_buf[z] = small_ref[...]
@@ -767,6 +767,7 @@
 
     for copy in ups:
         copy.wait_recv()
+    grad_up[...] = up_got[...].astype(F32)
     for n, (stays, push, stay) in enumerate(downs):
         pl.when(stays)(stay.wait)
         pl.when(jnp.logical_not(stays))(push.wait_send)
@@ -778,6 +779,7 @@
             device_id_type=MESH,
         )
         pl.when(source != w)(arrived.wait_recv)
+    grad_down[...] = down_got[...].astype(F32)
 
     for copy in first:
         copy.wait()
@@ -852,7 +854,7 @@
         functools.partial(grouped_last_kernel, wide, rows, own_width, own_heads),
         out_shape=[
             shape((rows, width), BF16), shape((rows, width), F32), shape((wide_rows, shard), F32),
-            shape((wide_rows, wide * unit), BF16), shape(downs[0].shape, BF16),
+            shape((wide_rows, wide * unit), F32), shape(downs[0].shape, F32),
             shape(small.shape, F32),
         ],
         in_specs=[ANY] * 11 + [VMEM] * 5,
@@ -863,7 +865,8 @@
             vmem(half - 1, wide_rows, columns), vmem(wide_rows, columns),
             vmem(4, wide_rows, own_width), vmem(4, wide_rows, LANES),
             pltpu.VMEM((wide_rows, LANES), F32), vmem(*ups[0].shape), vmem(3, *ups[0].shape),
-            vmem(*downs[0].shape), vmem(3, *downs[0].shape), vmem(half, rows, width),
+            vmem(wide_rows, wide * unit), vmem(*downs[0].shape), vmem(3, *downs[0].shape),
+            vmem(*downs[0].shape), vmem(half, rows, width),
             pltpu.VMEM((4,) + small.shape, F32), pltpu.VMEM((wide,) + small.shape, F32),
             pltpu.VMEM(small.shape, F32),
             DMA((steps,)), DMA((steps,)), DMA((2,)), DMA((2,)), DMA((12 + 2 * half,)),
@@ -873,7 +876,7 @@
         ),
     )(
         norm_part, in_part, *ups, *downs, *branches, tokens, middle, grad_middle,
-        jnp.broadcast_to(gain[None], (8, width)), small,
+        gain, small,
     )
 
 
@@ -1435,8 +1438,12 @@
         sender.plan(*piece, narrow_device(line[k])) for k in (2, 3, 1) for piece in in_pieces(line[k])
     ]
     outs = [
-        sender.plan(out_ref, weight_rows(out_buf, w, z), narrow_device(line[k])) for k in (2, 3, 1)
-    ]
+        sender.plan(out_ref, weight_rows(out_buf, w, z), narrow_device(line[k])) for k in (2, 1)
+    ]
+    out_middle = sender.plan(out_ref, weight_rows(out_buf, w, z), narrow_device(line[3]))
+    out_relay = sender.plan(
+        weight_rows(out_buf, w, line[2]), weight_rows(out_buf, w, line[2]), narrow_device(line[1])
+    )
     ups = [
         sender.plan(*piece, wide_device(flipped(w, k)))
         for k in range(1, wide)
@@ -1475,10 +1482,25 @@
     two.start()
     one.start()
     own_out.wait()
-    for copy in outs:
-        copy.wait_recv()
+    outs[0].wait_recv()
+
+    @pl.when(is_middle)
+    def _():
+        out_relay.start()
+        out_middle.start()
+
+    in_wide.pass_on()
+    outs[1].wait_recv()
+
+    @pl.when(is_middle)
+    def _():
+        out_middle.wait_recv()
+
+    @pl.when(is_end)
+    def _():
+        out_relay.wait_recv()
+
     out_wide.start()
-    in_wide.pass_on()
     for k in diagonal_steps(wide):
         grads[k].start()
     two.wait_recv()
@@ -1504,10 +1526,6 @@
         def _():
             one.wait_recv()
 
-        @pl.when(t == 3)
-        def _():
-            out_wide.pass_on()
-
         @pl.when((t == 3) & is_middle)
         def _():
             middle.wait_recv()
@@ -1534,7 +1552,7 @@
         n = jnp.where(t == 0, z, jnp.where(t == 1, line[2], jnp.where(t == 2, line[1], line[3])))
         at = pl.ds(pl.multiple_of(n * rows, rows), rows)
         values = slot[at, :].astype(F32)
-        low = (values * rms_factor(values) * gain_one_ref[0:1, :]).astype(BF16)
+        low = (values * rms_factor(values) * gain_one_ref[...].reshape(1, width)).astype(BF16)
         normed[at, :] = low
         proj[at, :] = dot_f32(low, in_buf[...])
         return carry
@@ -1564,6 +1582,7 @@
     lax.fori_loop(0, groups, attend, 0)
     for copy in mixes:
         copy.start()
+    out_wide.pass_on()
     mixed_rows[:, pl.ds(pl.multiple_of(z * own_width, LANES), own_width)] = mixed[
         pl.ds(pl.multiple_of(z * rows, rows), rows), :
     ]
@@ -1575,7 +1594,7 @@
     inputs = slot[pl.ds(pl.multiple_of(z * rows, rows), rows), :].astype(F32)
     values = inputs + dot_f32(mixed_rows[...], out_buf[...])
     middle_ref[...] = values
-    normed_two_ref[...] = (values * rms_factor(values) * gain_two_ref[0:1, :]).astype(BF16)
+    normed_two_ref[...] = (values * rms_factor(values) * gain_two_ref[...].reshape(1, width)).astype(BF16)
 
     for copy in up_steps:
         copy.wait()
@@ -1594,6 +1613,8 @@
     def _():
         relay.wait_send()
         middle.wait_send()
+        out_relay.wait_send()
+        out_middle.wait_send()
 
     for copy in ins + outs + ups + [two, one] + mixes:
         copy.wait_send()
@@ -1636,8 +1657,8 @@
             collective_id=collective_id, has_side_effects=True, vmem_limit_bytes=60 * 2**20
         ),
     )(
-        tokens, in_weight, small, out_weight, gate_up_weight, cotangent, down_weight, jnp.broadcast_to(gain_one[None], (8, width)),
-        jnp.broadcast_to(gain_two[None], (8, width)), bias, cont,
+        tokens, in_weight, small, out_weight, gate_up_weight, cotangent, down_weight, gain_one,
+        gain_two, bias, cont,
     )
 
 
@@ -1906,7 +1927,7 @@
     gain_grad[...] = jnp.broadcast_to(
         jnp.sum(total * values, axis=0, keepdims=True), gain_grad.shape
     )
-    total = total * gain_ref[0:1, :]
+    total = total * gain_ref[...].reshape(1, width)
     inner = jnp.mean(total * values, axis=-1, keepdims=True)
     total = grads[width : width + rows, :].astype(F32) + factor * (total - values * inner)
     grad_middle[...] = total
@@ -1992,7 +2013,7 @@
         ),
     )(
         normed, grad, far_grads, *ups, down, middle, mixed_rows, out_full,
-        jnp.broadcast_to(gain[None], (8, width)),
+        gain,
     )
 
 
@@ -2185,7 +2206,6 @@
     if not aligned:
         grad_up = grad_up.reshape(wide_rows, wide, LANES)[:, :, :unit]
         grad_up = grad_up.reshape(wide_rows, wide * unit)
-    grad_up, grad_down = grad_up.astype(F32), grad_down.astype(F32)
     return (
         output,
         grad_tokens,

time: 470 us -> 457 us (0.972)
  the two profiles are of different devices: /device:TPU:0 before, /device:TPU:17 now
where the time goes in v8:
time: 457 us; the launch traced here: 449 us
  Pallas kernels  431 us (94%)
  local copies, waits for them, and re-layouts  15.5 us (3%)
    pallas_call x1, Pallas kernels, first_part(): pl.pallas_call(functools.partial(first_kernel, wide, heads, head_size, bl...  152 us
    pallas_call x1, Pallas kernels, second_part(): pl.pallas_call(functools.partial(second_kernel, wide), out_shape=[shape((...  119 us
    pallas_call x1, Pallas kernels, last_part(): pl.pallas_call(functools.partial(grouped_last_kernel, wide, rows, own_wid...  85.5 us
    pallas_call x1, Pallas kernels, attention_backward(): pl.pallas_call(functools.partial(backward_kernel, heads, head_size, block...  74 us

profile of v8, /device:TPU:17, one launch (start us, length us, event | category | flops | bytes accessed | tf_op | source)
XLA Modules:
  0.0 448.8 jit_solution(2848264691476020825)
XLA Ops:
  0.6 0.7 dynamic_slice.3
  1.4 0.6 broadcast_in_dim.4.bias_ref.refs_5_
  2.0 0.9 compare_reduce_fusion
  2.9 1.0 broadcast_in_dim.5.cont_ref.refs_6_
  3.9 0.7 slice.26
  4.6 0.1 copy.20
  4.8 0.1 copy.22
  4.9 0.6 pad.12.small_ref
  5.5 151.8 %shard_map.169 = (bf16[1024,1536]{1,0:T(8,128)(2,1)}, bf16[1536,1664]{1,0:T(8,128)(2,1)}, bf16[1536,1536]{1,0:T(8,128)(2,1)}, f32[1024,1664]{1,0:T(8,128)}, bf16...) custom-call(bf16[256,1536]{1,0:T(8,128)(2,1)} %refs_11_.1, ...), custom_call_target="tpu_custom_call" | custom-call | tf_op jit(solution)/shard_map/pallas_call | solution.py:1637
  157.4 119.1 %shard_map.170 = (f32[256,1536]{1,0:T(8,128)}, f32[8,1536]{1,0:T(8,128)}, bf16[1024,384]{1,0:T(8,128)(2,1)}, bf16[4,256,1536]{2,1,0:T(8,128)(2,1)}, bf16[1536,25...) custom-call(bf16[256,1536]{1,0:T(8,128)(2,1)} %get-tuple-element.53., ...), custom_call_target="tpu_custom_call" | custom-call | tf_op jit(solution)/shard_map/pallas_call | solution.py:1991
  276.5 74.0 %shard_map.171 = (bf16[1024,1664]{1,0:T(8,128)(2,1)}, f32[8,128]{1,0:T(8,128)}, bf16[1024,1536]{1,0:T(8,128)(2,1)}, bf16[1536,1664]{1,0:T(8,128)(2,1)}, f32[192,...) custom-call(f32[1024,1664]{1,0:T(8,128)} %get-tuple-element.50.refs_, ...), custom_call_target="tpu_custom_call" | custom-call | tf_op jit(solution)/shard_map/pallas_call | solution.py:1306
  350.5 0.7 slice.30
  351.2 0.2 dynamic_update_slice.4
  351.4 0.8 slice.29
  352.2 0.6 select_maximum_fusion.refs_15_
  352.9 85.5 %shard_map.172 = (bf16[256,1536]{1,0:T(8,128)(2,1)}, f32[256,1536]{1,0:T(8,128)}, f32[192,1554]{1,0:T(8,128)}, f32[192,2048]{1,0:T(8,128)}, f32[512,384]{1,0:T(8,128)}, /*index=5*/f32[8,1536]{1,0:T(8,128)}) custom-call(bf16[1024,1536]{1,0:T(8,128)(2,1)} %get-tuple-element.71.refs_0_, bf16[8,192,1664]{2,1,0:T(8,128)(2,1)} %bitcast.8, ...), custom_call_target="tpu_custom_call" | custom-call | tf_op jit(solution)/shard_map/pallas_call | solution.py:853
  438.5 1.6 slice_reduce_fusion
  440.0 1.2 slice_bitcast_fusion
  441.2 2.2 copy.31
  443.4 1.1 copy.32
  444.5 1.0 copy.33
  445.6 0.7 copy.34
  446.3 1.1 copy.35
  447.5 0.9 copy.36
  (16 shorter events, 0.1 us)
Async XLA Ops:
  438.4 5.0 %copy-start.1 = (f32[256,1536]{1,0:T(8,128)S(1)}, f32[256,1536]{1,0:T(8,128)}, u32[]{:S(2)}) copy-start(f32[256,1536]{1,0:T(8,128)} %get-tuple-element.103) | copy-start | bytes 4718596
  441.2 3.3 copy-start.2
  443.4 2.2 copy-start.4
  443.4 2.9 copy-start
  445.6 1.9 copy-start.3

commit v9 on v8

--- a/solution.py
+++ b/solution.py
@@ -1049,7 +1049,7 @@
     out_ref, bias_grad_ref, norm_ref, in_part_ref, grad_out = refs[18:23]
     up_two_got, down_two_got, up_one_got, down_one_got, branch_got = refs[23:28]
     decay_scr, small_scr, dq_scr, part_core, part_own, part_far, part_sum, part_got = refs[28:36]
-    send, recv, local = refs[36:]
+    in_buf, send, recv, local = refs[36:]
     pair = pl.program_id(0)
     pairs = heads * head_size // LANES
     half = wide // 2
@@ -1079,6 +1079,7 @@
         pltpu.make_async_copy(part_ref.at[flipped(w, 2 * n)], part_own.at[n], local.at[n])
         for n in range(half)
     ]
+    in_copy = pltpu.make_async_copy(in_ref, in_buf, local.at[half])
     own_width = heads * head_size
 
     def part_columns(n):
@@ -1095,7 +1096,7 @@
             [narrow_device(flipped(z, k)) for k in (1, 2, 3)]
             + [wide_device(flipped(w, k)) for k in wide_steps(wide)]
         )
-        for copy in copies + core + own:
+        for copy in copies + core + own + [in_copy]:
             copy.start()
 
     @pl.when(pair == 1)
@@ -1115,11 +1116,15 @@
             small_scr, dq_scr,
         )
 
+    @pl.when(pair == pairs)
+    def _():
+        in_copy.wait()
+
     @pl.when((pair >= pairs) & (pair < pairs + row_steps))
     def _():
         size = norm_ref.shape[0]
         at = pl.ds(pl.multiple_of((pair - pairs) * size, size), size)
-        norm_ref[...] = dot_f32(out_ref[at, :], in_ref[...], ((1,), (1,))).astype(BF16)
+        norm_ref[...] = dot_f32(out_ref[at, :], in_buf[...], ((1,), (1,))).astype(BF16)
 
     @pl.when(pair == pairs + row_steps)
     def _():
@@ -1309,7 +1314,7 @@
         in_specs=base
         + [own] * 3
         + [
-            pl.BlockSpec(in_full.shape, lambda p: (0, 0), pipeline_mode=pl.Buffered(1)),
+            ANY,
             pl.BlockSpec((rows, 256), lambda p: (0, in_at(p))),
         ]
         + [ANY] * 6,
@@ -1332,7 +1337,8 @@
             pltpu.VMEM((rows, 2 * LANES), F32), part(half), part(half), part(half - 1),
             pltpu.VMEM((wide_rows, width), BF16),
             pltpu.VMEM((3, wide_rows, heads * head_size), BF16),
-            DMA((steps,)), DMA((steps,)), DMA((half,)),
+            pltpu.VMEM(in_full.shape, BF16),
+            DMA((steps,)), DMA((steps,)), DMA((half + 1,)),
         ],
         compiler_params=pltpu.CompilerParams(
             collective_id=collective_id, has_side_effects=True, vmem_limit_bytes=60 * 2**20
@@ -1472,14 +1478,13 @@
         for k in (2, 3, 1)
     ]
 
-    for copy in ins + outs + ups:
+    for copy in ins + outs + ups + [two]:
         copy.start()
     for copy in own_in:
         copy.wait()
     for copy in ins:
         copy.wait_recv()
     in_wide.start()
-    two.start()
     one.start()
     own_out.wait()
     outs[0].wait_recv()

time: 457 us -> 456 us (level)
  the two profiles are of different devices: /device:TPU:17 before, /device:TPU:0 now
where the time goes in v9:
time: 456 us; the launch traced here: 447 us
  Pallas kernels  428 us (94%)
  local copies, waits for them, and re-layouts  15.4 us (3%)
    pallas_call x1, Pallas kernels, first_part(): pl.pallas_call(functools.partial(first_kernel, wide, heads, head_size, bl...  156 us
    pallas_call x1, Pallas kernels, second_part(): pl.pallas_call(functools.partial(second_kernel, wide), out_shape=[shape((...  116 us
    pallas_call x1, Pallas kernels, last_part(): pl.pallas_call(functools.partial(grouped_last_kernel, wide, rows, own_wid...  84.7 us
    pallas_call x1, Pallas kernels, attention_backward(): pl.pallas_call(functools.partial(backward_kernel, heads, head_size, block...  72 us

profile of v9, /device:TPU:0, one launch (start us, length us, event | category | flops | bytes accessed | tf_op | source)
XLA Modules:
  0.0 446.6 jit_solution(4482373664127162525)
XLA Ops:
  0.6 0.7 dynamic_slice.3
  1.4 0.6 broadcast_in_dim.4.bias_ref.refs_5_
  2.0 0.9 compare_reduce_fusion
  2.9 1.0 broadcast_in_dim.5.cont_ref.refs_6_
  3.9 0.7 slice.26
  4.6 0.1 copy.20
  4.8 0.1 copy.22
  4.9 0.6 pad.12.small_ref
  5.5 155.8 %shard_map.169 = (bf16[1024,1536]{1,0:T(8,128)(2,1)}, bf16[1536,1664]{1,0:T(8,128)(2,1)}, bf16[1536,1536]{1,0:T(8,128)(2,1)}, f32[1024,1664]{1,0:T(8,128)}, bf16...) custom-call(bf16[256,1536]{1,0:T(8,128)(2,1)} %refs_11_.1, ...), custom_call_target="tpu_custom_call" | custom-call | tf_op jit(solution)/shard_map/pallas_call | solution.py:1642
  161.4 115.9 %shard_map.170 = (f32[256,1536]{1,0:T(8,128)}, f32[8,1536]{1,0:T(8,128)}, bf16[1024,384]{1,0:T(8,128)(2,1)}, bf16[4,256,1536]{2,1,0:T(8,128)(2,1)}, bf16[1536,25...) custom-call(bf16[256,1536]{1,0:T(8,128)(2,1)} %get-tuple-element.53., ...), custom_call_target="tpu_custom_call" | custom-call | tf_op jit(solution)/shard_map/pallas_call | solution.py:1996
  277.3 72.0 %shard_map.171 = (bf16[1024,1664]{1,0:T(8,128)(2,1)}, f32[8,128]{1,0:T(8,128)}, bf16[1024,1536]{1,0:T(8,128)(2,1)}, bf16[1536,1664]{1,0:T(8,128)(2,1)}, f32[192,...) custom-call(f32[1024,1664]{1,0:T(8,128)} %get-tuple-element.50.refs_, ...), custom_call_target="tpu_custom_call" | custom-call | tf_op jit(solution)/shard_map/pallas_call | solution.py:1311
  349.3 0.7 slice.30
  350.0 0.1 dynamic_update_slice.4
  350.1 0.8 slice.29
  350.9 0.6 select_maximum_fusion.refs_15_
  351.6 84.7 %shard_map.172 = (bf16[256,1536]{1,0:T(8,128)(2,1)}, f32[256,1536]{1,0:T(8,128)}, f32[192,1554]{1,0:T(8,128)}, f32[192,2048]{1,0:T(8,128)}, f32[512,384]{1,0:T(8,128)}, /*index=5*/f32[8,1536]{1,0:T(8,128)}) custom-call(bf16[1024,1536]{1,0:T(8,128)(2,1)} %get-tuple-element.71.refs_0_, bf16[8,192,1664]{2,1,0:T(8,128)(2,1)} %bitcast.8, ...), custom_call_target="tpu_custom_call" | custom-call | tf_op jit(solution)/shard_map/pallas_call | solution.py:853
  436.3 1.6 slice_reduce_fusion
  437.9 1.2 slice_bitcast_fusion
  439.1 2.2 copy.31
  441.2 1.1 copy.32
  442.4 1.0 copy.33
  443.4 0.7 copy.34
  444.1 1.1 copy.35
  445.3 0.9 copy.36
  (16 shorter events, 0.1 us)
Async XLA Ops:
  436.3 5.0 %copy-start.1 = (f32[256,1536]{1,0:T(8,128)S(1)}, f32[256,1536]{1,0:T(8,128)}, u32[]{:S(2)}) copy-start(f32[256,1536]{1,0:T(8,128)} %get-tuple-element.103) | copy-start | bytes 4718596
  439.1 3.3 copy-start.2
  441.2 2.2 copy-start.4
  441.2 2.9 copy-start
  443.4 1.9 copy-start.3

commit v10 on v9

--- a/solution.py
+++ b/solution.py
@@ -595,7 +595,7 @@
 
 def last_kernel(
     wide, rows, own_width, own_heads, norm_ref, in_ref, up_parts, down_parts, branch_refs, token_ref,
-    middle_ref, grad_ref, gain_ref, small_ref, output, grad_tokens, grad_in, grad_up, grad_down, totals, join_buf, one_buf, mid_buf, two_buf, two_src, own_norm, norm_sum,
+    middle_ref, grad_ref, gain_ref, gain_two_ref, bias_ref, output, grad_tokens, grad_in, grad_up, grad_down, totals, join_buf, one_buf, mid_buf, two_buf, two_src, own_norm, norm_sum,
     in_core, in_own, in_far, in_sum, in_got, after_got, tail_buf, up_low, up_bufs, up_got, down_low,
     down_bufs, down_got, branch_bufs, narrow_buf, wide_buf, sum_buf, send, recv, down_send, down_recv,
     local,
@@ -759,7 +759,11 @@
     scaled = grads * gain_ref[...].reshape(1, width)
     inner = jnp.mean(scaled * normed, axis=-1, keepdims=True)
     grad_tokens[...] = grad_ref[...] + factor * (scaled - normed * inner)
-    narrow_buf[z] = small_ref[...]
+    lane = iota((8, LANES), 1)
+    bias = jnp.where(lane < own_heads, bias_ref[...], 0.0)
+    narrow_buf[z] = jnp.zeros(sum_buf.shape, F32)
+    narrow_buf[z, 1:2, :] = gain_two_ref[0:1, :]
+    narrow_buf[z, 2:3, :LANES] = pltpu.roll(bias, z * own_heads, 1)[0:1, :]
     narrow_buf[z, 0:1, :] = jnp.sum(grads * normed, axis=0, keepdims=True)
     sum_buf[...] = narrow_buf[z]
     for copy in first:
@@ -840,7 +844,8 @@
 
 
 def last_part(
-    norm_part, in_part, ups, downs, branches, tokens, middle, grad_middle, gain, small, own_width, own_heads,
+    norm_part, in_part, ups, downs, branches, tokens, middle, grad_middle, gain, gain_two, bias, own_width,
+    own_heads,
     shard, collective_id,
 ):
     wide, wide_rows, columns = in_part.shape
@@ -855,9 +860,9 @@
         out_shape=[
             shape((rows, width), BF16), shape((rows, width), F32), shape((wide_rows, shard), F32),
             shape((wide_rows, wide * unit), F32), shape(downs[0].shape, F32),
-            shape(small.shape, F32),
+            shape(gain_two.shape, F32),
         ],
-        in_specs=[ANY] * 11 + [VMEM] * 5,
+        in_specs=[ANY] * 11 + [VMEM] * 6,
         out_specs=[VMEM] * 6,
         scratch_shapes=[
             *[vmem(rows, width)] * 6, pltpu.VMEM((rows, width), F32),
@@ -867,8 +872,8 @@
             pltpu.VMEM((wide_rows, LANES), F32), vmem(*ups[0].shape), vmem(3, *ups[0].shape),
             vmem(wide_rows, wide * unit), vmem(*downs[0].shape), vmem(3, *downs[0].shape),
             vmem(*downs[0].shape), vmem(half, rows, width),
-            pltpu.VMEM((4,) + small.shape, F32), pltpu.VMEM((wide,) + small.shape, F32),
-            pltpu.VMEM(small.shape, F32),
+            pltpu.VMEM((4,) + gain_two.shape, F32), pltpu.VMEM((wide,) + gain_two.shape, F32),
+            pltpu.VMEM(gain_two.shape, F32),
             DMA((steps,)), DMA((steps,)), DMA((2,)), DMA((2,)), DMA((12 + 2 * half,)),
         ],
         compiler_params=pltpu.CompilerParams(
@@ -876,7 +881,7 @@
         ),
     )(
         norm_part, in_part, *ups, *downs, *branches, tokens, middle, grad_middle,
-        gain, small,
+        gain, gain_two, bias,
     )
 
 
@@ -2146,7 +2151,6 @@
             normed_two, cotangent, grad_got, [up_block, up_two, up_one], down_block, middle,
             mixed_rows, out_full, gain_two, 2,
         )
-        grad_gain_two = grad_gain_two[0]
     else:
         ups = [up_block] + [follow(piece, normed_two) for piece in (up_two, up_one)]
         plane_normed, plane_grad, up_full, down_full = gather_rows(
@@ -2197,15 +2201,13 @@
         own_heads, head_size, block, 7,
     )
     branches = [branch_sum, branch_near, branch_far]
-    all_bias = lax.dynamic_update_slice(
-        jnp.zeros((width,), F32), bias_grad[0, :own_heads], (z * own_heads,)
-    )
-    small = jnp.stack([jnp.zeros((width,), F32), grad_gain_two, all_bias])
-    small = jnp.pad(small, ((0, 5), (0, 0)))
+    if not fused:
+        grad_gain_two = jnp.broadcast_to(grad_gain_two[None], (8, width))
     low = lambda part: part.astype(BF16)
     output, grad_tokens, grad_in, grad_up, grad_down, totals = last_part(
         norm_part, in_part.reshape(wide, wide_rows, columns), [low(up_acc), up_one, up_two],
-        [low(down_acc), down_one, down_two], branches, tokens, middle, grad_middle, gain_one, small,
+        [low(down_acc), down_one, down_two], branches, tokens, middle, grad_middle, gain_one, grad_gain_two,
+        bias_grad,
         own_width, own_heads, (base + 3 * heads) // narrow, 4,
     )
     if not aligned:

time: 456 us -> 453 us (level)
  the two profiles are of different devices: /device:TPU:0 before, /device:TPU:17 now
where the time goes in v10:
time: 453 us; the launch traced here: 445 us
  Pallas kernels  429 us (95%)
  local copies, waits for them, and re-layouts  13.9 us (3%)
    pallas_call x1, Pallas kernels, first_part(): pl.pallas_call(functools.partial(first_kernel, wide, heads, head_size, bl...  152 us
    pallas_call x1, Pallas kernels, second_part(): pl.pallas_call(functools.partial(second_kernel, wide), out_shape=[shape((...  119 us
    pallas_call x1, Pallas kernels, last_part(): pl.pallas_call(functools.partial(grouped_last_kernel, wide, rows, own_wid...  85.6 us
    pallas_call x1, Pallas kernels, attention_backward(): pl.pallas_call(functools.partial(backward_kernel, heads, head_size, block...  72.4 us

profile of v10, /device:TPU:17, one launch (start us, length us, event | category | flops | bytes accessed | tf_op | source)
XLA Modules:
  0.0 445.0 jit_solution(4243340645218511081)
XLA Ops:
  0.6 0.7 dynamic_slice.3
  1.4 0.9 compare_reduce_fusion
  2.2 0.1 add_convert_fusion
  2.3 0.6 broadcast_in_dim.4.bias_ref.refs_5_
  2.9 0.7 slice.20
  3.6 0.1 copy.20
  3.8 0.1 copy.22
  3.9 0.6 pad.8.small_ref
  4.5 1.0 broadcast_in_dim.5.cont_ref.refs_6_
  5.5 151.8 %shard_map.169 = (bf16[1024,1536]{1,0:T(8,128)(2,1)}, bf16[1536,1664]{1,0:T(8,128)(2,1)}, bf16[1536,1536]{1,0:T(8,128)(2,1)}, f32[1024,1664]{1,0:T(8,128)}, bf16...) custom-call(bf16[256,1536]{1,0:T(8,128)(2,1)} %refs_11_.1, ...), custom_call_target="tpu_custom_call" | custom-call | tf_op jit(solution)/shard_map/pallas_call | solution.py:1647
  157.4 119.1 %shard_map.170 = (f32[256,1536]{1,0:T(8,128)}, f32[8,1536]{1,0:T(8,128)}, bf16[1024,384]{1,0:T(8,128)(2,1)}, bf16[4,256,1536]{2,1,0:T(8,128)(2,1)}, bf16[1536,25...) custom-call(bf16[256,1536]{1,0:T(8,128)(2,1)} %get-tuple-element.53., ...), custom_call_target="tpu_custom_call" | custom-call | tf_op jit(solution)/shard_map/pallas_call | solution.py:2001
  276.5 72.4 %shard_map.171 = (bf16[1024,1664]{1,0:T(8,128)(2,1)}, f32[8,128]{1,0:T(8,128)}, bf16[1024,1536]{1,0:T(8,128)(2,1)}, bf16[1536,1664]{1,0:T(8,128)(2,1)}, f32[192,...) custom-call(f32[1024,1664]{1,0:T(8,128)} %get-tuple-element.50.refs_, ...), custom_call_target="tpu_custom_call" | custom-call | tf_op jit(solution)/shard_map/pallas_call | solution.py:1316
  348.9 85.6 %shard_map.172 = (bf16[256,1536]{1,0:T(8,128)(2,1)}, f32[256,1536]{1,0:T(8,128)}, f32[192,1554]{1,0:T(8,128)}, f32[192,2048]{1,0:T(8,128)}, f32[512,384]{1,0:T(8,128)}, /*index=5*/f32[8,1536]{1,0:T(8,128)}) custom-call(bf16[1024,1536]{1,0:T(8,128)(2,1)} %get-tuple-element.71.refs_0_, bf16[8,192,1664]{2,1,0:T(8,128)(2,1)} %bitcast.8, ...), custom_call_target="tpu_custom_call" | custom-call | tf_op jit(solution)/shard_map/pallas_call | solution.py:858
  434.6 0.0 copy-start.1
  434.6 1.3 slice_bitcast_fusion
  435.9 1.5 slice_reduce_fusion
  437.4 2.2 copy.29
  439.6 0.0 copy-done.1
  439.6 1.1 copy.30
  440.7 1.0 copy.31
  441.8 0.7 copy.32
  442.5 0.0 copy-done
  442.5 1.1 copy.33
  443.6 0.9 copy.34
  (10 shorter events, 0.0 us)
Async XLA Ops:
  434.6 5.0 %copy-start.1 = (f32[256,1536]{1,0:T(8,128)S(1)}, f32[256,1536]{1,0:T(8,128)}, u32[]{:S(2)}) copy-start(f32[256,1536]{1,0:T(8,128)} %get-tuple-element.103) | copy-start | bytes 4718596
  437.4 3.3 copy-start.2
  439.6 2.2 copy-start.4
  439.6 2.9 copy-start
  441.8 1.9 copy-start.3
